TPU v7x, 32 devices: a whole 2x2x4 slice. The times are simulated.
32 devices in a mesh: expert: 16 (over z, y, x), ffn: 2 (over core).
Axes of the slice: x: 2, y: 2, z: 4, core: 2. Of those that a mesh axis runs over, the one named last changes fastest.
Arguments:
- tokens: bfloat16 [4096, 768], P(('expert', 'ffn')), may hold values from -6 to 6
- norm_first: float32 [768], replicated, may hold values from 0.25 to 1.75
- w_query: bfloat16 [768, 768], replicated, may hold values from -0.21875 to 0.21875
- w_key: bfloat16 [768, 768], replicated, may hold values from -0.21875 to 0.21875
- w_value: bfloat16 [768, 768], replicated, may hold values from -0.21875 to 0.21875
- w_out: bfloat16 [768, 768], replicated, may hold values from -1.75 to 1.75
- bucket_bias_table: float32 [32, 12], replicated, may hold values from -4 to 4
- norm_second: float32 [768], replicated, may hold values from 0.25 to 1.75
- w_router: bfloat16 [768, 16], replicated, may hold values from -0.109375 to 0.109375
- w_in: bfloat16 [16, 768, 3072], P('expert', None, 'ffn'), may hold values from -0.21875 to 0.21875
- w_down: bfloat16 [16, 3072, 768], P('expert', 'ffn'), may hold values from -6 to 6
- expert_ids: int32 [4096], P(('expert', 'ffn')), may hold values from 0 to 15, as said below
- cotangent: bfloat16 [4096, 768], P(('expert', 'ffn')), may hold values from -6 to 6
Outputs:
- output: bfloat16 [4096, 768], P(('expert', 'ffn'))
- grad_input: float32 [4096, 768], P(('expert', 'ffn'))
- grad_norm_first: float32 [768], replicated
- grad_w_query: float32 [768, 768], replicated
- grad_w_key: float32 [768, 768], replicated
- grad_w_value: float32 [768, 768], replicated
- grad_w_out: float32 [768, 768], replicated
- grad_bias_table: float32 [32, 12], replicated
- grad_norm_second: float32 [768], replicated
- grad_router: float32 [768, 16], replicated
- grad_w_in: float32 [16, 768, 3072], P('expert', None, 'ffn')
- grad_w_down: float32 [16, 3072, 768], P('expert', 'ffn')
- expert_branch: float32 [4096, 768], P(('expert', 'ffn'))
Inputs may be any that keep to these rules, and one draw needn't show every extreme that they name: `expert_ids`: among the 128 rows of one device no expert is named more than 16 times, and one expert, the same on every device, is named exactly 16 times on each device.
All inputs are finite; a program needn't handle non-finite values.
Results may differ from a plain program's by a relative error of at most 0.018.
Values may be sent and summed in bfloat16 or wider, within the bound.
No kernel may reach another device: no remote copies, remote signals or barrier semaphores. Data moves between devices by JAX's collectives and lax.ppermute only.
A program may use at most 128 MiB of HBM per device.

v0:
```python
import math

import jax
import jax.numpy as jnp
import numpy as np
from jax import lax
from jax.sharding import PartitionSpec as P

REACH = 128


EPS = 1e-06
TOP_PRECISION = lax.Precision.HIGHEST


def prefix(x, axis, combine, identity):
    peers, mine = (lax.axis_size(axis), lax.axis_index(axis))
    everything = lax.all_gather(x, axis)
    start = jnp.broadcast_to(jnp.asarray(identity, x.dtype), x.shape)

    def turn(k, before):
        reached = k < mine
        new = combine(before, everything[k])
        return jnp.where(reached, new, before)

    return lax.fori_loop(0, peers, turn, start)


def bucket_onehot(length, buckets, reach):
    shift = np.arange(-(length - 1), length)
    distance = -shift
    half = buckets // 2
    exact = half // 2
    result = np.where(distance < 0, half, 0)
    magnitude = np.abs(distance)
    spread = exact + np.floor(
        np.log(np.maximum(magnitude, 1) / exact) / np.log(reach / exact) * (half - exact)
    )
    spread = np.minimum(spread, half - 1)
    result = result + np.where(magnitude < exact, magnitude, spread)
    return (result[None, :] == np.arange(buckets)[:, None]).astype(np.float32)


def bucket_select(length, buckets, reach):
    table = bucket_onehot(length, buckets, reach)
    offset_index = np.arange(length)[None, :] - np.arange(length)[:, None] + length - 1
    return table[:, offset_index]


def norm_apply(values, gain):
    return values * lax.rsqrt(jnp.mean(values * values, axis=-1, keepdims=True) + EPS) * gain


def contract_rows(left, right):
    return lax.dot_general(
        left, right, (((0,), (0,)), ((), ())), preferred_element_type=jnp.float32
    )


def contract_cols(left, right):
    return lax.dot_general(
        left, right, (((1,), (1,)), ((), ())), preferred_element_type=jnp.float32
    )


def gelu_grad(pre, grad_hidden):
    return jax.vjp(jax.nn.gelu, pre)[1](grad_hidden)[0]


def add_counts(earlier, later):
    return earlier + later


def shards(
    tokens,
    norm_first,
    w_query,
    w_key,
    w_value,
    w_out,
    bucket_bias_table,
    norm_second,
    w_router,
    w_in,
    w_down,
    expert_ids,
    cotangent,
):
    rows, width = tokens.shape
    buckets, heads = bucket_bias_table.shape
    head_size = width // heads
    pair = lax.axis_size("ffn")
    seq_len = rows * pair
    experts = w_router.shape[1]
    slots = 2 * rows // experts
    capacity = 5 * rows * pair // 4
    scale = 1.0 / math.sqrt(head_size)
    inputs = tokens.astype(jnp.float32)
    normed_first, norm_first_back = jax.vjp(norm_apply, inputs, norm_first)
    act_first = normed_first.astype(jnp.bfloat16)
    queries = jnp.dot(act_first, w_query, preferred_element_type=jnp.float32).astype(jnp.bfloat16)
    key_local = jnp.dot(act_first, w_key, preferred_element_type=jnp.float32).astype(jnp.bfloat16)
    value_local = jnp.dot(act_first, w_value, preferred_element_type=jnp.float32).astype(
        jnp.bfloat16
    )
    keys, values = (
        lax.all_gather(key_local, "ffn", axis=0, tiled=True),
        lax.all_gather(value_local, "ffn", axis=0, tiled=True),
    )
    select_whole = jnp.asarray(bucket_select(seq_len, buckets, REACH), dtype=jnp.float32)
    selected_rows = lax.dynamic_slice_in_dim(select_whole, lax.axis_index("ffn") * rows, rows, 1)
    position_bias = jnp.einsum(
        "ip,ifw->pfw", bucket_bias_table, selected_rows, precision=TOP_PRECISION
    )
    query_heads = queries.reshape(rows, heads, head_size)
    key_heads = keys.reshape(seq_len, heads, head_size)
    value_heads = values.reshape(seq_len, heads, head_size)

    def scores_of():
        raw = jnp.einsum("qhd,khd->hqk", query_heads, key_heads, preferred_element_type=jnp.float32)
        return raw * scale + position_bias

    scores = scores_of()
    peak = jnp.max(scores, axis=-1, keepdims=True)
    log_total = peak + jnp.log(jnp.sum(jnp.exp(scores - peak), axis=-1, keepdims=True))
    probs = jnp.exp(scores - log_total)
    mixed = jnp.einsum(
        "hqk,khd->qhd", probs.astype(jnp.bfloat16), value_heads, preferred_element_type=jnp.float32
    )
    mixed_low = mixed.reshape(rows, width).astype(jnp.bfloat16)
    middle = inputs + jnp.dot(mixed_low, w_out, preferred_element_type=jnp.float32)
    normed_second, norm_second_back = jax.vjp(norm_apply, middle, norm_second)
    act_second = normed_second.astype(jnp.bfloat16)
    logits = jnp.dot(act_second, w_router, preferred_element_type=jnp.float32)
    router_probs = jax.nn.softmax(logits, axis=-1)
    choose = expert_ids[:, None] == jnp.arange(experts, dtype=jnp.int32)[None, :]
    choose_float = choose.astype(jnp.float32)
    choose_int = choose.astype(jnp.int32)
    gate = jnp.sum(router_probs * choose_float, axis=1)
    row_index = jnp.arange(rows, dtype=jnp.int32)
    lower_mask = (row_index[:, None] > row_index[None, :]).astype(jnp.bfloat16)
    ranks = jnp.dot(lower_mask, choose.astype(jnp.bfloat16), preferred_element_type=jnp.float32)
    local_rank = jnp.sum(ranks * choose_float, axis=1).astype(jnp.int32)
    counts = jnp.sum(choose_int, axis=0)
    before = prefix(counts, ("expert", "ffn"), add_counts, jnp.zeros_like(counts))
    position = jnp.sum(before[None, :] * choose_int, axis=1) + local_rank
    keep = (position < capacity).astype(jnp.float32)
    target = expert_ids * slots + local_rank
    send_rows = jnp.where(keep[:, None] > 0.5, act_second, jnp.zeros_like(act_second))
    outgoing = (
        jnp.zeros((experts * slots, width), jnp.bfloat16)
        .at[target]
        .set(send_rows)
        .reshape(experts, slots, width)
    )
    arrived = lax.all_to_all(outgoing, "expert", split_axis=0, concat_axis=0, tiled=True)
    full_in, full_down = (
        lax.all_gather(w_in, "ffn", axis=2, tiled=True),
        lax.all_gather(w_down, "ffn", axis=1, tiled=True),
    )
    flat = arrived.reshape(-1, width)
    pre = jnp.dot(flat, full_in[0], preferred_element_type=jnp.float32)
    hidden = jax.nn.gelu(pre).astype(jnp.bfloat16)
    produced = jnp.dot(hidden, full_down[0], preferred_element_type=jnp.float32).reshape(
        arrived.shape
    )
    returned = lax.all_to_all(
        produced.astype(jnp.bfloat16), "expert", split_axis=0, concat_axis=0, tiled=True
    )
    expert_out = returned.reshape(-1, width)[target].astype(jnp.float32) * keep[:, None]
    expert_branch = gate[:, None] * expert_out
    output = (middle + expert_branch).astype(jnp.bfloat16)
    grad_result = cotangent.astype(jnp.float32)
    grad_gate = jnp.sum(grad_result * expert_out, axis=1)
    grad_produced = (grad_result * (gate * keep)[:, None]).astype(jnp.bfloat16)
    back_send = (
        jnp.zeros((experts * slots, width), jnp.bfloat16)
        .at[target]
        .set(grad_produced)
        .reshape(experts, slots, width)
    )
    back_arrived = lax.all_to_all(back_send, "expert", split_axis=0, concat_axis=0, tiled=True)
    back_flat = back_arrived.reshape(-1, width)
    grad_pre = gelu_grad(pre, contract_cols(back_flat, full_down[0])).astype(jnp.bfloat16)
    whole_in = contract_rows(flat, grad_pre)
    whole_down = contract_rows(hidden, back_flat)
    grad_w_in, grad_w_down = (
        lax.psum_scatter(
            whole_in[None].astype(jnp.bfloat16), "ffn", scatter_dimension=2, tiled=True
        ).astype(jnp.float32),
        lax.psum_scatter(
            whole_down[None].astype(jnp.bfloat16), "ffn", scatter_dimension=1, tiled=True
        ).astype(jnp.float32),
    )
    grad_slots = contract_cols(grad_pre, full_in[0]).reshape(arrived.shape)
    grad_back = lax.all_to_all(
        grad_slots.astype(jnp.bfloat16), "expert", split_axis=0, concat_axis=0, tiled=True
    )
    grad_from_expert = grad_back.reshape(-1, width)[target].astype(jnp.float32) * keep[:, None]
    grad_logits = ((grad_gate * gate)[:, None] * (choose_float - router_probs)).astype(jnp.bfloat16)
    grad_router_part = contract_rows(act_second, grad_logits)
    grad_act_second = contract_cols(grad_logits, w_router) + grad_from_expert
    grad_norm_path, grad_norm_second_part = norm_second_back(grad_act_second)
    grad_middle = grad_result + grad_norm_path
    grad_attended = grad_middle.astype(jnp.bfloat16)
    grad_w_out_part = contract_rows(mixed_low, grad_attended)
    grad_mixed = (
        contract_cols(grad_attended, w_out).astype(jnp.bfloat16).reshape(rows, heads, head_size)
    )
    probs = jnp.exp(scores_of() - log_total)
    grad_probs = jnp.einsum(
        "qhd,khd->hqk", grad_mixed, value_heads, preferred_element_type=jnp.float32
    )
    grad_value_terms = jnp.einsum(
        "hqk,qhd->khd", probs.astype(jnp.bfloat16), grad_mixed, preferred_element_type=jnp.float32
    )
    inner = jnp.sum(probs * grad_probs, axis=-1, keepdims=True)
    score_gradient = probs * (grad_probs - inner)
    table_gradient_piece = jnp.einsum(
        "yrd,wrd->wy", score_gradient, selected_rows, precision=TOP_PRECISION
    )
    grad_raw = (score_gradient * scale).astype(jnp.bfloat16)
    grad_queries = jnp.einsum(
        "hqk,khd->qhd", grad_raw, key_heads, preferred_element_type=jnp.float32
    )
    grad_queries = grad_queries.reshape(rows, width).astype(jnp.bfloat16)
    grad_key_terms = jnp.einsum(
        "hqk,qhd->khd", grad_raw, query_heads, preferred_element_type=jnp.float32
    )
    grad_key_sum, grad_value_sum = (
        lax.psum_scatter(
            grad_key_terms.reshape(seq_len, width).astype(jnp.bfloat16),
            "ffn",
            scatter_dimension=0,
            tiled=True,
        ).astype(jnp.float32),
        lax.psum_scatter(
            grad_value_terms.reshape(seq_len, width).astype(jnp.bfloat16),
            "ffn",
            scatter_dimension=0,
            tiled=True,
        ).astype(jnp.float32),
    )
    grad_keys = grad_key_sum.astype(jnp.bfloat16)
    grad_values = grad_value_sum.astype(jnp.bfloat16)
    grad_query_part = contract_rows(act_first, grad_queries)
    grad_key_part = contract_rows(act_first, grad_keys)
    grad_value_part = contract_rows(act_first, grad_values)
    grad_act_first = (
        contract_cols(grad_queries, w_query)
        + contract_cols(grad_keys, w_key)
        + contract_cols(grad_values, w_value)
    )
    grad_input_path, grad_norm_first_part = norm_first_back(grad_act_first)
    grad_input = grad_middle + grad_input_path
    summed = lax.psum(
        (
            grad_norm_first_part,
            grad_query_part,
            grad_key_part,
            grad_value_part,
            grad_w_out_part,
            table_gradient_piece,
            grad_norm_second_part,
            grad_router_part,
        ),
        ("expert", "ffn"),
    )
    return (
        output,
        grad_input,
        summed[0],
        summed[1],
        summed[2],
        summed[3],
        summed[4],
        summed[5],
        summed[6],
        summed[7],
        grad_w_in,
        grad_w_down,
        expert_branch,
    )


def solution(mesh):
    placed = (
        P(("expert", "ffn"), None),
        P(),
        P(),
        P(),
        P(),
        P(),
        P(),
        P(),
        P(),
        P("expert", None, "ffn"),
        P("expert", "ffn", None),
        P(("expert", "ffn")),
        P(("expert", "ffn"), None),
    )
    return jax.shard_map(
        shards,
        mesh=mesh,
        in_specs=placed,
        out_specs=(
            P(("expert", "ffn"), None),
            P(("expert", "ffn"), None),
            P(),
            P(),
            P(),
            P(),
            P(),
            P(),
            P(),
            P(),
            P("expert", None, "ffn"),
            P("expert", "ffn", None),
            P(("expert", "ffn"), None),
        ),
        check_vma=False,
    )
```

profile of v0, /device:TPU:0, one launch (start us, length us, event | category | flops | bytes accessed | tf_op | source)
XLA Modules:
  0.0 446.2 jit_solution(15715715489293951296)
XLA Ops:
  9.3 42.0 %all-reduce = s32[512]{0:T(512)S(1)} all-reduce(s32[512]{0:T(512)S(1)} %dynamic-update-slice), channel_id=2, replica_groups=mesh['expert'=16,'ffn'=2] {'expert','ffn'}, use_global_device_ids=true, to_apply=%add | all-reduce | flops 512 | bytes 4096
  54.9 2.1 all_gather.19
  57.5 2.1 all_gather.18
  60.8 4.1 fusion.2
  69.4 2.2 scatter_custom_fusion
  71.6 18.4 %all_to_all.20 = bf16[16,16,768]{2,1,0:T(8,128)(2,1)} all-to-all(bf16[16,16,768]{2,1,0:T(8,128)(2,1)} %bitcast.118), channel_id=1, replica_groups=mesh['expert'=16,'ffn'=2] {'expert'}, dimensions={0} | all-to-all | bytes 786432 | tf_op jit(solution)/shard_map/all_to_all | solution.py:156
  90.0 6.6 %multiply_convert_fusion = (bf16[256,3072]{1,0:T(8,128)(2,1)}, f32[256,3072]{1,0:T(8,128)}) fusion(bf16[256,768]{1,0:T(8,128)(2,1)} %bitcast.105, bf16[1,768,3072]{2,1,0:T(8,128)(2,1)} %all-gather.4.cloned.1.call-done), kind=kOutput, calls=%fused_computation.31 | convolution fusion | flops 1215037440 | bytes 9830400 | tf_op jit(solution)/shard_map/dot_general | solution.py:162
  96.6 4.9 %fusion.24 = bf16[16,16,768]{2,1,0:T(8,128)(2,1)} fusion(bf16[16,16,3072]{2,1,0:T(8,128)(2,1)} %bitcast.100, bf16[1,3072,768]{2,1,0:T(8,128)(2,1)} %all-gather.6.cloned.1.call-done), kind=kOutput, calls=%fused_computation.39 | convolution fusion | flops 1208156160 | bytes 6684672 | tf_op jit(solution)/shard_map/dot_general | solution.py:164
  101.6 4.2 all-to-all-start.1
  112.0 5.4 %all-to-all-done.1 = bf16[16,16,768]{2,1,0:T(8,128)(2,1)} async-done(((bf16[16,16,768]{2,1,0:T(8,128)(2,1)}), bf16[16,16,768]{2,1,0:T(8,128)(2,1)}, u32[]{:S(2)}, u32[]{:S(2)}) %all-to-all-start.1) | async-done | bytes 393248 | tf_op jit(solution)/shard_map/all_to_all | solution.py:167
  117.3 2.8 gather_fusion
  122.6 2.3 scatter_custom_fusion.1
  125.0 15.5 %all_to_all.21 = bf16[16,16,768]{2,1,0:T(8,128)(2,1)S(1)} all-to-all(bf16[16,16,768]{2,1,0:T(8,128)(2,1)} %bitcast.117), channel_id=1, replica_groups=mesh['expert'=16,'ffn'=2] {'expert'}, dimensions={0} | all-to-all | bytes 786432 | tf_op jit(solution)/shard_map/all_to_all | solution.py:182
  140.4 6.8 %fusion.20 = bf16[256,3072]{1,0:T(8,128)(2,1)S(1)} fusion(f32[256,3072]{1,0:T(8,128)} %get-tuple-element.140, bf16[256,768]{1,0:T(8,128)(2,1)S(1)} %bitcast.115, bf16[1,3072,768]{2,1,0:T(8,128)(2,1)} %all-gather.6.cloned.1.call-done), kind=kOutput, calls=%fused_computation.30 | convolution fusion | flops 1223688192 | bytes 9830400 | tf_op jit(solution)/shard_map/dot_general | solution.py:61
  148.8 15.0 %all_to_all.22 = bf16[16,16,768]{2,1,0:T(8,128)(2,1)} all-to-all(bf16[16,16,768]{2,1,0:T(8,128)(2,1)S(1)} %fusion.27), channel_id=1, replica_groups=mesh['expert'=16,'ffn'=2] {'expert'}, dimensions={0} | all-to-all | bytes 786432 | tf_op jit(solution)/shard_map/all_to_all | solution.py:196
  163.8 2.8 gather_fusion.1
  166.6 2.1 multiply_reduce_fusion.1
  169.3 2.1 add_convert_fusion
  175.1 2.1 convolution_convert_fusion.2
  177.3 1.9 copy.53
  183.6 1.9 copy.51
  185.6 3.6 fusion.13
  190.8 3.6 fusion.12
  197.9 2.0 fusion.76
  201.7 2.9 fusion.72
  204.7 2.9 fusion.74
  210.0 5.8 %fusion.31 = f32[32,12]{0,1:T(8,128)S(1)} fusion(f32[12,128,256]{2,1,0:T(8,128)S(1)} %copy-done.2, f32[32,256,256]{2,0,1:T(8,128)} %constant.84.clone, s32[]{:T(128)S(6)} %select_n.34), kind=kOutput, calls=%fused_computation.55 | convolution fusion | flops 150994944 | bytes 5768708 | tf_op jit(solution)/shard_map/yrd,wrd->wy/dot_general | solution.py:219
  218.3 41.1 %all-reduce.1 = (f32[768]{0:T(1024)}, f32[32,12]{0,1:T(8,128)}, f32[768]{0:T(1024)}, f32[768,16]{0,1:T(8,128)}) all-reduce(f32[768]{0:T(1024)S(1)} %get-tuple-element.110, f32[32,12]{0,1:T(8,128)S(1)} %fusion.31, f32[768]{0:T(1024)S(1)} %copy-done.38, f32[768,16]{0,1:T(8,128)S(1)} %copy-done.34), channel_id=1, replica_groups=mesh['expert'=16,'ffn'=2] {'expert','ffn'}, use_global_device_ids=true, to_apply=%region_21.22 | all-reduce | flops 14208 | bytes 113664 | tf_op jit(solution)/shard_map/psum | solution.py:256
  260.3 4.3 convert_element_type.191
  264.6 4.6 %convert_element_type.188 = f32[1,768,1536]{2,1,0:T(8,128)} convert(bf16[1,768,1536]{2,1,0:T(8,128)(2,1)} %reduce-scatter.9.cloned.1.call-done) | non-fusion elementwise | flops 1179648 | bytes 7077888 | tf_op jit(solution)/shard_map/convert_element_type | solution.py:190
  269.2 160.4 %all-reduce.5.cloned.1.call-done = (f32[768,768]{1,0:T(8,128)}, f32[768,768]{1,0:T(8,128)}, f32[768,768]{1,0:T(8,128)}, f32[768,768]{1,0:T(8,128)}) async-done(((f32[768,768]{1,0:T(8,128)}, f32[768,768]{1,0:T(8,128)}, f32[768,768]{1,0:T(8,128)}, f32[768,768]{1,0:T(8,128)}), (f32[768,768]{1,0:T(8,128)}, f32[768,768]{1,0:T(8,128)}, f32[768,768]{1,0:T(8,128)}, ...) | async-done | bytes 9437200 | tf_op jit(solution)/shard_map/psum | solution.py:256
  429.5 3.4 copy.71
  (204 shorter events, 50.1 us)
Async XLA Ops:
  7.2 50.0 %copy-start = (bf16[768,768]{1,0:T(8,128)(2,1)S(1)}, bf16[768,768]{1,0:T(8,128)(2,1)}, u32[]{:S(2)}) copy-start(bf16[768,768]{1,0:T(8,128)(2,1)} %param.20) | copy-start | bytes 3538948
  7.2 45.4 %copy-start.31 = (f32[768]{0:T(1024)S(1)}, f32[768]{0:T(1024)}, u32[]{:S(2)}) copy-start(f32[768]{0:T(1024)} %param.17) | copy-start | bytes 9220
  7.2 45.4 %copy-start.8 = (bf16[768,768]{1,0:T(8,128)(2,1)S(1)}, bf16[768,768]{1,0:T(8,128)(2,1)}, u32[]{:S(2)}) copy-start(bf16[768,768]{1,0:T(8,128)(2,1)} %param.18) | copy-start | bytes 3538948
  7.2 82.8 %all-gather.4.cloned.1.call-start = ((), (), s32[]{:S(2)}) async-start(), calls=%async_computation.8 | async-start | bytes 7077888 | tf_op jit(solution)/shard_map/all_gather | solution.py:158
  8.0 88.6 %all-gather.6.cloned.1.call-start = ((), (), s32[]{:S(2)}) async-start(), calls=%async_computation.9 | async-start | bytes 7077888 | tf_op jit(solution)/shard_map/all_gather | solution.py:159
  8.9 44.3 %copy-start.46 = (f32[128]{0:T(128)}, f32[128]{0:T(128)S(1)}, u32[]{:S(2)}) copy-start(f32[128]{0:T(128)S(1)} %fusion.44) | copy-start | bytes 1540
  8.9 48.2 %copy-start.36 = (f32[128]{0:T(128)}, f32[128]{0:T(128)S(1)}, u32[]{:S(2)}) copy-start(f32[128]{0:T(128)S(1)} %fusion.67) | copy-start | bytes 1540
  54.9 5.9 %copy-start.40 = (f32[32,12]{0,1:T(8,128)S(1)}, f32[32,12]{0,1:T(8,128)}, u32[]{:S(2)}) copy-start(f32[32,12]{0,1:T(8,128)} %param.22) | copy-start | bytes 4612
  57.1 7.7 %copy-start.12 = (bf16[256,768]{0,1:T(8,128)(2,1)}, bf16[256,768]{0,1:T(8,128)(2,1)S(1)}, u32[]{:S(2)}) copy-start(bf16[256,768]{0,1:T(8,128)(2,1)S(1)} %copy.47) | copy-start | bytes 1179652
  60.7 8.2 %copy-start.44 = (f32[128]{0:T(128)}, f32[128]{0:T(128)S(1)}, u32[]{:S(2)}) copy-start(f32[128]{0:T(128)S(1)} %fusion.36) | copy-start | bytes 1540
  60.8 8.1 %copy-start.45 = (s32[128]{0:T(128)}, s32[128]{0:T(128)S(1)}, u32[]{:S(2)}) copy-start(s32[128]{0:T(128)S(1)} %select_reduce_fusion) | copy-start | bytes 1540
  101.6 15.8 %all-to-all-start.1 = ((bf16[16,16,768]{2,1,0:T(8,128)(2,1)}), bf16[16,16,768]{2,1,0:T(8,128)(2,1)}, u32[]{:S(2)}, u32[]{:S(2)}) async-start(bf16[16,16,768]{2,1,0:T(8,128)(2,1)} %fusion.24), calls=%async_computation.1 | async-start | bytes 786432 | tf_op jit(solution)/shard_map/all_to_all | solution.py:167
  105.8 96.0 %reduce-scatter.15.cloned.1.call-start = ((), (), s32[]{:S(2)}) async-start(), calls=%async_computation.13 | async-start | bytes 589824
  125.0 22.3 %slice-start = ((s8[4718592]{0:T(1024)(128)(4,1)}), s8[4194304]{0:T(1024)(128)(4,1)S(1)}, s32[]{:S(2)}) async-start(s8[4718592]{0:T(1024)(128)(4,1)} %bitcast.122), calls=%async_computation.15 | async-start | bytes 8388608
  140.4 6.8 %copy-start.25 = (bf16[16,16,768]{2,1,0:T(8,128)(2,1)}, bf16[16,16,768]{2,1,0:T(8,128)(2,1)S(1)}, u32[]{:S(2)}) copy-start(bf16[16,16,768]{2,1,0:T(8,128)(2,1)S(1)} %all_to_all.21) | copy-start | bytes 1179652
  140.4 6.9 %slice-start.1 = ((s8[4718592]{0:T(1024)(128)(4,1)}), s8[524288]{0:T(1024)(128)(4,1)S(1)}, s32[]{:S(2)}) async-start(s8[4718592]{0:T(1024)(128)(4,1)} %bitcast.122), calls=%async_computation.16 | async-start | bytes 1048576
  166.6 5.5 %copy-start.7 = (bf16[768,768]{1,0:T(8,128)(2,1)S(1)}, bf16[768,768]{1,0:T(8,128)(2,1)}, u32[]{:S(2)}) copy-start(bf16[768,768]{1,0:T(8,128)(2,1)} %param.21) | copy-start | bytes 3538948
  173.3 5.9 %copy-start.14 = (bf16[256,768]{0,1:T(8,128)(2,1)S(1)}, bf16[256,768]{0,1:T(8,128)(2,1)}, u32[]{:S(2)}) copy-start(bf16[256,768]{0,1:T(8,128)(2,1)} %copy.45) | copy-start | bytes 1179652
  179.2 25.4 %reduce-scatter.13.cloned.1.call-start = ((), (), s32[]{:S(2)}) async-start(), calls=%async_computation.12 | async-start | bytes 589824
  182.6 3.0 copy-start.11
  182.6 3.0 copy-start.26
  185.6 74.7 %reduce-scatter.11.cloned.1.call-start = ((), (), s32[]{:S(2)}) async-start(), calls=%async_computation.11 | async-start | bytes 7077888 | tf_op jit(solution)/shard_map/reduce_scatter | solution.py:191
  189.3 75.3 %reduce-scatter.9.cloned.1.call-start = ((), (), s32[]{:S(2)}) async-start(), calls=%async_computation.10 | async-start | bytes 7077888 | tf_op jit(solution)/shard_map/reduce_scatter | solution.py:188
  194.4 3.5 copy-start.37
  194.5 5.4 %copy-start.5 = (f32[128,768]{1,0:T(8,128)S(1)}, f32[128,768]{1,0:T(8,128)}, u32[]{:S(2)}) copy-start(f32[128,768]{1,0:T(8,128)} %copy-done.4) | copy-start | bytes 1179652
  194.5 5.4 %copy-start.20 = (bf16[12,64,128]{2,1,0:T(8,128)(2,1)S(1)}, bf16[12,64,128]{2,1,0:T(8,128)(2,1)}, u32[]{:S(2)}) copy-start(bf16[12,64,128]{2,1,0:T(8,128)(2,1)} %copy-done.19) | copy-start | bytes 589828
  194.5 235.1 %all-reduce.5.cloned.1.call-start = ((), (), s32[]{:S(2)}) async-start(), calls=%async_computation.14 | async-start | bytes 18874368 | tf_op jit(solution)/shard_map/psum | solution.py:256
  210.0 5.9 %copy-start.9 = (bf16[768,768]{1,0:T(8,128)(2,1)S(1)}, bf16[768,768]{1,0:T(8,128)(2,1)}, u32[]{:S(2)}) copy-start(bf16[768,768]{1,0:T(8,128)(2,1)} %param.18) | copy-start | bytes 3538948
  210.0 5.9 %copy-start.22 = (bf16[12,64,128]{2,1,0:T(8,128)(2,1)S(1)}, bf16[12,64,128]{2,1,0:T(8,128)(2,1)}, u32[]{:S(2)}) copy-start(bf16[12,64,128]{2,1,0:T(8,128)(2,1)} %copy-done.21) | copy-start | bytes 589828
  210.0 6.4 %copy-start.30 = (bf16[128,768]{1,0:T(8,128)(2,1)S(1)}, bf16[128,768]{1,0:T(8,128)(2,1)}, u32[]{:S(2)}) copy-start(bf16[128,768]{1,0:T(8,128)(2,1)} %reduce-scatter.13.cloned.1.call-done) | copy-start | bytes 589828
  217.1 42.3 %copy-start.47 = (f32[128]{0:T(128)S(1)}, f32[128]{0:T(128)}, u32[]{:S(2)}) copy-start(f32[128]{0:T(128)} %copy-done.46) | copy-start | bytes 1540
  429.5 3.4 copy-start.17
  (27 other events, 35.9 us)
Sparse Core Ops, SparseCore 0:
  9.6 17.1 all-gather.3
  28.3 15.5 all-gather.5
  179.3 5.7 reduce-scatter.14
  187.3 8.9 reduce-scatter.12
  199.0 13.7 reduce-scatter.10
  215.7 13.7 reduce-scatter.8
  236.3 193.1 all-reduce.4
where the time goes:
time: 448 us; the launch traced here: 446 us
  waiting for transfers between devices  167 us (37%)
  blocking collectives  136 us (30%)
  matrix products  64.7 us (14%)
  local copies, waits for them, and re-layouts  31.6 us (7%)
  other arithmetic  26.2 us (6%)
  between operations  14.8 us (3%)
  starting transfers between devices  4.89 us (1%)
    psum x1, waiting for transfers between devices, shards(): lax.psum((grad_norm_first_part, grad_query_part, grad_key_part, grad_valu...  160 us
    unnamed x1, blocking collectives  42 us
    psum x1, blocking collectives, shards(): lax.psum((grad_norm_first_part, grad_query_part, grad_key_part, grad_valu...  41.1 us
    unnamed x110, local copies, waits for them, and re-layouts  22.8 us
    all_to_all x1, blocking collectives, shards(): lax.all_to_all(outgoing, 'expert', split_axis=0, concat_axis=0, tiled=True)  18.4 us
    dot_general x7, matrix products, contract_rows(): lax.dot_general(left, right, (((0,), (0,)), ((), ())), preferred_element_...  18.3 us
    all_to_all x1, blocking collectives, shards(): lax.all_to_all(back_send, 'expert', split_axis=0, concat_axis=0, tiled=True)  15.5 us
    all_to_all x1, blocking collectives, shards(): lax.all_to_all(grad_slots.astype(jnp.bfloat16), 'expert', split_axis=0, c...  15 us
  transfers between devices with their start and end apart: 8, of which 2 were waited for; matrix products, arithmetic and copies ran while one was open for 15% of the time, Pallas kernels for 0%

commit v1 on v0

v1 whole, which is shorter than its diff:
```python
import functools
import math

import jax
import jax.numpy as jnp
import numpy as np
from jax import lax
from jax.experimental import pallas as pl
from jax.experimental.pallas import tpu as pltpu
from jax.sharding import PartitionSpec as P

REACH = 128
EPS = 1e-06
TOP_PRECISION = lax.Precision.HIGHEST
LANES = 128
F32 = jnp.float32
BF16 = jnp.bfloat16


def bucket_of(distance, buckets, reach):
    half = buckets // 2
    exact = half // 2
    result = np.where(distance < 0, half, 0)
    magnitude = np.abs(distance)
    spread = exact + np.floor(
        np.log(np.maximum(magnitude, 1) / exact) / np.log(reach / exact) * (half - exact)
    )
    spread = np.minimum(spread, half - 1)
    return result + np.where(magnitude < exact, magnitude, spread)


def bucket_windows(rows, buckets, reach):
    lane = np.arange(2 * rows)
    offset = np.where(lane < rows, -lane, 2 * rows - lane)
    windows = []
    for shift in (0, rows, -rows):
        hot = bucket_of(offset + shift, buckets, reach)[None, :] == np.arange(buckets)[:, None]
        hot[:, rows] = False
        windows.append(hot)
    return np.concatenate(windows, axis=1).astype(np.float32)


def rows_by_rows(left, right):
    return lax.dot_general(left, right, (((0,), (0,)), ((), ())), preferred_element_type=F32)


def cols_by_cols(left, right):
    return lax.dot_general(left, right, (((1,), (1,)), ((), ())), preferred_element_type=F32)


def dot(left, right):
    return jnp.dot(left, right, preferred_element_type=F32)


def root_mean(x):
    return lax.rsqrt(jnp.mean(x * x, axis=-1, keepdims=True) + EPS)


def call(body, outs, args, vmem=48, flops=0, scratch=(), anys=(), nbytes=1000000):
    spec = pl.BlockSpec(memory_space=pltpu.VMEM)
    anywhere = pl.BlockSpec(memory_space=pl.ANY)
    return pl.pallas_call(
        body,
        out_shape=[jax.ShapeDtypeStruct(s, d) for s, d in outs],
        in_specs=[anywhere if i in anys else spec for i in range(len(args))],
        out_specs=[spec] * len(outs),
        scratch_shapes=list(scratch),
        compiler_params=pltpu.CompilerParams(vmem_limit_bytes=vmem * 2**20),
        cost_estimate=pl.CostEstimate(flops=flops, bytes_accessed=nbytes, transcendentals=0),
    )(*args)


def toeplitz(window, rows):
    wide = jnp.broadcast_to(window, (rows, 2 * rows))
    return pltpu.roll(wide, 0, 1, stride=1, stride_axis=0)[:, :rows]


def diagonal_sums(square, rows):
    wide = jnp.concatenate([square, jnp.zeros_like(square)], axis=1)
    height = rows
    while height > 1:
        height //= 2
        wide = wide[:height] + pltpu.roll(wide[height:], 2 * rows - height, 1)
    return wide


def prepare_kernel(
    experts, ids_ref, cot_ref, table_ref, hot_ref, place_ref, fetch_ref, choose_ref, out_ref, win_ref
):
    rows = ids_ref.shape[1]
    total, width = place_ref.shape[0], cot_ref.shape[1]
    slots = total // experts
    ids = ids_ref[...]
    choose = (lax.broadcasted_iota(jnp.int32, (experts, rows), 0) == ids).astype(F32)
    earlier = (
        lax.broadcasted_iota(jnp.int32, (rows, rows), 0)
        < lax.broadcasted_iota(jnp.int32, (rows, rows), 1)
    ).astype(F32)
    ranks = dot(choose.astype(BF16), earlier.astype(BF16))
    rank = jnp.sum(choose * ranks, axis=0, keepdims=True)
    target = ids * slots + rank.astype(jnp.int32)
    place = (lax.broadcasted_iota(jnp.int32, (total, rows), 0) == target).astype(F32)
    place_ref[...] = place.astype(BF16)
    fetch_ref[...] = place.T.astype(BF16)
    choose_ref[...] = choose.T
    out_ref[:, :width] = dot(place.astype(BF16), cot_ref[...]).astype(BF16)
    filled = jnp.sum(place, axis=1, keepdims=True)
    out_ref[:, width:] = jnp.broadcast_to(filled, (total, LANES)).astype(BF16)
    win_ref[...] = lax.dot_general(
        table_ref[...],
        hot_ref[...],
        (((0,), (0,)), ((), ())),
        precision=TOP_PRECISION,
        preferred_element_type=F32,
    )


def attend(query_pair, key_pair, scale, bias, side, low_half):
    own = jnp.where(low_half if side == 0 else jnp.logical_not(low_half), query_pair, 0)
    scores = cols_by_cols(own.astype(BF16), key_pair) * scale + bias
    grown = jnp.exp(scores - jnp.max(scores, axis=-1, keepdims=True))
    return grown / jnp.sum(grown, axis=-1, keepdims=True)


def forward_kernel(
    heads,
    own_ref,
    other_ref,
    gain_first_ref,
    wq_ref,
    wk_ref,
    wv_ref,
    wo_ref,
    win_ref,
    gain_second_ref,
    router_ref,
    choose_ref,
    place_ref,
    middle_ref,
    gate_ref,
    out_ref,
):
    rows, width = own_ref.shape
    size = width // heads
    scale = 1.0 / math.sqrt(size)
    core = lax.axis_index("ffn")
    x = own_ref[...].astype(F32)
    y = other_ref[...].astype(F32)
    gain = gain_first_ref[...]
    act_own = (x * root_mean(x) * gain).astype(BF16)
    act_other = (y * root_mean(y) * gain).astype(BF16)
    act = jnp.concatenate([act_own, act_other], axis=0)
    queries = dot(act_own, wq_ref[...]).astype(BF16)
    keys = dot(act, wk_ref[...]).astype(BF16)
    values = dot(act, wv_ref[...]).astype(BF16)
    low_half = lax.broadcasted_iota(jnp.int32, (rows, 2 * size), 1) < size
    windows = win_ref[...]
    same = windows[:, : 2 * rows]
    apart = jnp.where(core == 1, windows[:, 2 * rows : 4 * rows], windows[:, 4 * rows :])
    mixed = []
    for pair in range(heads // 2):
        lanes = slice(pair * 2 * size, (pair + 1) * 2 * size)
        outs = []
        for side in range(2):
            head = 2 * pair + side
            bias = jnp.concatenate(
                [
                    toeplitz(same[head : head + 1], rows),
                    toeplitz(apart[head : head + 1], rows),
                ],
                axis=1,
            )
            probs = attend(queries[:, lanes], keys[:, lanes], scale, bias, side, low_half)
            outs.append(dot(probs.astype(BF16), values[:, lanes]))
        mixed.append(jnp.where(low_half, outs[0], outs[1]).astype(BF16))
    middle = x + dot(jnp.concatenate(mixed, axis=1), wo_ref[...])
    middle_ref[...] = middle
    act_second = (middle * root_mean(middle) * gain_second_ref[...]).astype(BF16)
    logits = dot(act_second, router_ref[...])
    grown = jnp.exp(logits - jnp.max(logits, axis=-1, keepdims=True))
    gate = jnp.sum(grown * choose_ref[...], axis=-1, keepdims=True) / jnp.sum(
        grown, axis=-1, keepdims=True
    )
    gate_ref[...] = jnp.broadcast_to(gate, gate_ref.shape)
    out_ref[...] = dot(place_ref[...], act_second).astype(BF16)


def halves_kernel(
    heads,
    own_ref,
    other_ref,
    gain_first_ref,
    wq_ref,
    wk_ref,
    wv_ref,
    win_ref,
    act_ref,
    query_ref,
    key_ref,
    value_ref,
    probs_ref,
    mixed_ref,
    wq_half,
    wk_half,
    wv_half,
    sems,
):
    rows, width = own_ref.shape
    size = width // heads
    part = width // 2
    scale = 1.0 / math.sqrt(size)
    core = lax.axis_index("ffn")
    columns = pl.ds(pl.multiple_of(core * part, LANES), part)
    copies = [
        pltpu.make_async_copy(ref.at[:, columns], half, sems.at[i])
        for i, (ref, half) in enumerate(((wq_ref, wq_half), (wk_ref, wk_half), (wv_ref, wv_half)))
    ]
    for copy in copies:
        copy.start()
    x = own_ref[...].astype(F32)
    y = other_ref[...].astype(F32)
    gain = gain_first_ref[...]
    act = jnp.concatenate(
        [(x * root_mean(x) * gain).astype(BF16), (y * root_mean(y) * gain).astype(BF16)], axis=0
    )
    act_ref[...] = act
    for copy in copies:
        copy.wait()
    queries = dot(act, wq_half[...]).astype(BF16)
    keys = dot(act, wk_half[...]).astype(BF16)
    values = dot(act, wv_half[...]).astype(BF16)
    query_ref[...] = queries
    key_ref[...] = keys
    value_ref[...] = values
    low_half = lax.broadcasted_iota(jnp.int32, (2 * rows, 2 * size), 1) < size
    for pair in range(heads // 4):
        lanes = slice(pair * 2 * size, (pair + 1) * 2 * size)
        outs = []
        for side in range(2):
            head = 2 * pair + side
            window = win_ref[pl.ds(core * (heads // 2) + head, 1), :]
            same = toeplitz(window[:, : 2 * rows], rows)
            ahead = toeplitz(window[:, 2 * rows : 4 * rows], rows)
            behind = toeplitz(window[:, 4 * rows :], rows)
            first = jnp.where(core == 1, ahead, behind)
            second = jnp.where(core == 1, behind, ahead)
            bias = jnp.concatenate(
                [
                    jnp.concatenate([same, first], axis=1),
                    jnp.concatenate([second, same], axis=1),
                ],
                axis=0,
            )
            probs = attend(queries[:, lanes], keys[:, lanes], scale, bias, side, low_half)
            probs_ref[head] = probs
            outs.append(dot(probs.astype(BF16), values[:, lanes]))
        mixed_ref[:, lanes] = jnp.where(low_half, outs[0], outs[1]).astype(BF16)


def expert_kernel(
    capacity,
    chunk,
    flat_ref,
    back_ref,
    fill_ref,
    router_ref,
    in_own_ref,
    in_other_ref,
    down_own_ref,
    down_other_ref,
    hid_own_ref,
    hid_other_ref,
    pre_own_ref,
    pre_other_ref,
    grad_ref,
    sent_ref,
    produced_ref,
    router_grad_ref,
    in_vmem,
    down_vmem,
    sems,
):
    total, width = flat_ref.shape
    experts = router_ref.shape[1]
    slots = total // experts
    hidden = in_own_ref.shape[1]
    steps = hidden // chunk
    mine = lax.axis_index("expert")
    core = lax.axis_index("ffn")
    copies = []
    for side, (win, wdown) in enumerate(
        ((in_own_ref, down_own_ref), (in_other_ref, down_other_ref))
    ):
        for step in range(steps):
            i = side * steps + step
            span = pl.ds(step * chunk, chunk)
            copies.append(
                (
                    pltpu.make_async_copy(win.at[:, span], in_vmem.at[i], sems.at[0, i]),
                    pltpu.make_async_copy(wdown.at[span, :], down_vmem.at[i], sems.at[1, i]),
                )
            )
    for pair in copies:
        for copy in pair:
            copy.start()
    flat = flat_ref[...]
    cot = back_ref[:, :width]
    own = back_ref[:, width : width + 1].astype(F32)
    other = fill_ref[:, :1].astype(F32)
    row = lax.broadcasted_iota(jnp.int32, (total, total), 0)
    col = lax.broadcasted_iota(jnp.int32, (total, total), 1)
    shift = slots.bit_length() - 1
    row_block = jnp.right_shift(row, shift)
    col_block = jnp.right_shift(col, shift)
    before = (col_block < row_block).astype(BF16)
    upto = (col_block <= row_block).astype(BF16)
    ahead = jnp.where(core == 1, upto, before)
    filled_own = jnp.broadcast_to(own, (total, LANES)).astype(BF16)
    filled_other = jnp.broadcast_to(other, (total, LANES)).astype(BF16)
    position = dot(before, filled_own) + dot(ahead, filled_other)
    slot = jnp.bitwise_and(lax.broadcasted_iota(jnp.int32, (total, 1), 0), slots - 1)
    position = position[:, :1] + slot.astype(F32)
    keep = jnp.where(position < capacity, 1.0, 0.0)
    logits = dot(flat, router_ref[...])
    grown = jnp.exp(logits - jnp.max(logits, axis=-1, keepdims=True))
    router_probs = grown / jnp.sum(grown, axis=-1, keepdims=True)
    onehot = (lax.broadcasted_iota(jnp.int32, (total, experts), 1) == mine).astype(F32)
    gate = jnp.sum(router_probs * onehot, axis=-1, keepdims=True)
    sent = (cot.astype(F32) * (gate * keep)).astype(BF16)
    sent_ref[...] = sent
    produced = jnp.zeros((total, width), F32)
    grad = jnp.zeros((total, width), F32)
    inner = math.sqrt(2.0 / math.pi)
    for i, pair in enumerate(copies):
        hid_ref, pre_ref = (hid_own_ref, pre_own_ref) if i < steps else (hid_other_ref, pre_other_ref)
        span = pl.ds((i % steps) * chunk, chunk)
        for copy in pair:
            copy.wait()
        win, wdown = in_vmem[i], down_vmem[i]
        pre = dot(flat, win)
        square = pre * pre
        curve = jnp.tanh(inner * pre * (1.0 + 0.044715 * square))
        half_up = 0.5 + 0.5 * curve
        act = (pre * half_up).astype(BF16)
        slope = half_up + (0.5 * inner) * pre * (1.0 - curve * curve) * (
            1.0 + (3 * 0.044715) * square
        )
        grad_pre = (slope * cols_by_cols(sent, wdown)).astype(BF16)
        hid_ref[:, span] = act
        pre_ref[:, span] = grad_pre
        produced = produced + dot(act, wdown)
        grad = grad + cols_by_cols(grad_pre, win)
    produced_low = produced.astype(BF16)
    kept = produced_low.astype(F32) * keep
    produced_ref[...] = kept.astype(BF16)
    grad_gate = jnp.sum(cot.astype(F32) * kept, axis=-1, keepdims=True)
    grad_logits = ((grad_gate * gate) * (onehot - router_probs)).astype(BF16)
    grad_ref[...] = (grad * keep + cols_by_cols(grad_logits, router_ref[...])).astype(BF16)
    router_grad_ref[...] = rows_by_rows(flat, grad_logits)


def expert_weights_kernel(
    flat_own, flat_other, sent_own, sent_other, hid_own, hid_other, pre_own, pre_other, in_ref, down_ref
):
    in_ref[0] = rows_by_rows(flat_own[...], pre_own[...]) + rows_by_rows(
        flat_other[...], pre_other[...]
    )
    down_ref[0] = rows_by_rows(hid_own[...], sent_own[...]) + rows_by_rows(
        hid_other[...], sent_other[...]
    )


def expert_weights(flat, flat_other, sent, sent_other, hid, hid_other, pre, pre_other, chunk):
    total, width = flat.shape
    hidden = hid.shape[1]
    whole = pl.BlockSpec((total, width), lambda i: (0, 0))
    part = pl.BlockSpec((total, chunk), lambda i: (0, i))
    return pl.pallas_call(
        expert_weights_kernel,
        grid=(hidden // chunk,),
        out_shape=[
            jax.ShapeDtypeStruct((1, width, hidden), F32),
            jax.ShapeDtypeStruct((1, hidden, width), F32),
        ],
        in_specs=[whole] * 4 + [part] * 4,
        out_specs=[
            pl.BlockSpec((1, width, chunk), lambda i: (0, 0, i)),
            pl.BlockSpec((1, chunk, width), lambda i: (0, i, 0)),
        ],
        compiler_params=pltpu.CompilerParams(vmem_limit_bytes=32 * 2**20),
        cost_estimate=pl.CostEstimate(
            flops=8 * total * width * hidden, bytes_accessed=14000000, transcendentals=0
        ),
    )(flat, flat_other, sent, sent_other, hid, hid_other, pre, pre_other)


def middle_kernel(returned_ref, fetch_ref, middle_ref, gain_ref, cot_ref, grad_ref, low_ref, gain_grad_ref):
    grad = dot(fetch_ref[...], returned_ref[...])
    middle = middle_ref[...]
    root = root_mean(middle)
    scaled = middle * root
    gain_grad_ref[...] = jnp.sum(grad * scaled, axis=0, keepdims=True)
    up = gain_ref[...] * grad
    grad_middle = cot_ref[...].astype(F32) + root * (
        up - scaled * jnp.mean(up * scaled, axis=-1, keepdims=True)
    )
    grad_ref[...] = grad_middle
    low_ref[...] = grad_middle.astype(BF16)


def backward_kernel(
    heads,
    grad_own_ref,
    grad_other_ref,
    own_ref,
    other_ref,
    act_ref,
    query_ref,
    key_ref,
    value_ref,
    probs_ref,
    mixed_ref,
    hot_ref,
    wq_ref,
    wk_ref,
    wv_ref,
    wo_ref,
    packed_ref,
    input_own_ref,
    input_other_ref,
    gain_grad_ref,
    table_ref,
    wq_half,
    wk_half,
    wv_half,
    wo_half,
    sems,
):
    rows, width = own_ref.shape
    size = width // heads
    part = width // 2
    scale = 1.0 / math.sqrt(size)
    core = lax.axis_index("ffn")
    span = pl.ds(pl.multiple_of(core * part, LANES), part)
    copies = [
        pltpu.make_async_copy(src, half, sems.at[i])
        for i, (src, half) in enumerate(
            (
                (wo_ref.at[span, :], wo_half),
                (wq_ref.at[:, span], wq_half),
                (wk_ref.at[:, span], wk_half),
                (wv_ref.at[:, span], wv_half),
            )
        )
    ]
    for copy in copies:
        copy.start()
    grad_low = jnp.concatenate([grad_own_ref[...], grad_other_ref[...]], axis=0)
    grad_out = rows_by_rows(mixed_ref[...], grad_low).astype(BF16)
    packed_ref[3 * width : 3 * width + part] = grad_out[:, :part]
    packed_ref[3 * width + part :] = grad_out[:, part:]
    for copy in copies:
        copy.wait()
    grad_mixed = cols_by_cols(grad_low, wo_half[...]).astype(BF16)
    low_half = lax.broadcasted_iota(jnp.int32, (2 * rows, 2 * size), 1) < size
    grad_q, grad_k, grad_v = [], [], []
    same, ahead, behind = [], [], []
    for pair in range(heads // 4):
        lanes = slice(pair * 2 * size, (pair + 1) * 2 * size)
        query, key, value = query_ref[:, lanes], key_ref[:, lanes], value_ref[:, lanes]
        grad_pair = grad_mixed[:, lanes]
        got_q, got_k, got_v = [], [], []
        for side in range(2):
            probs = probs_ref[2 * pair + side]
            keep_lanes = low_half if side == 0 else jnp.logical_not(low_half)
            own_grad = jnp.where(keep_lanes, grad_pair, 0).astype(BF16)
            grad_probs = cols_by_cols(own_grad, value)
            got_v.append(rows_by_rows(probs.astype(BF16), grad_pair))
            inner = jnp.sum(probs * grad_probs, axis=-1, keepdims=True)
            grad_scores = probs * (grad_probs - inner)
            same.append(
                diagonal_sums(grad_scores[:rows, :rows] + grad_scores[rows:, rows:], rows)
            )
            first = diagonal_sums(grad_scores[:rows, rows:], rows)
            second = diagonal_sums(grad_scores[rows:, :rows], rows)
            ahead.append(jnp.where(core == 1, first, second))
            behind.append(jnp.where(core == 1, second, first))
            grad_raw = (grad_scores * scale).astype(BF16)
            got_q.append(dot(grad_raw, key))
            got_k.append(rows_by_rows(grad_raw, query))
        grad_q.append(jnp.where(low_half, got_q[0], got_q[1]).astype(BF16))
        grad_k.append(jnp.where(low_half, got_k[0], got_k[1]).astype(BF16))
        grad_v.append(jnp.where(low_half, got_v[0], got_v[1]).astype(BF16))
    grad_q = jnp.concatenate(grad_q, axis=1)
    grad_k = jnp.concatenate(grad_k, axis=1)
    grad_v = jnp.concatenate(grad_v, axis=1)
    act = act_ref[...]
    packed_ref[:width] = rows_by_rows(act, grad_q).astype(BF16)
    packed_ref[width : 2 * width] = rows_by_rows(act, grad_k).astype(BF16)
    packed_ref[2 * width : 3 * width] = rows_by_rows(act, grad_v).astype(BF16)
    sums = jnp.concatenate(
        [jnp.concatenate(part_sums, axis=0) for part_sums in (same, ahead, behind)], axis=1
    )
    table_ref[...] = lax.dot_general(
        sums,
        hot_ref[...],
        (((1,), (1,)), ((), ())),
        precision=TOP_PRECISION,
        preferred_element_type=F32,
    )
    grad_act = (
        cols_by_cols(grad_q, wq_half[...])
        + cols_by_cols(grad_k, wk_half[...])
        + cols_by_cols(grad_v, wv_half[...])
    )
    x = own_ref[...].astype(F32)
    y = other_ref[...].astype(F32)
    gain_grad_ref[...] = jnp.sum(
        grad_act[:rows] * (x * root_mean(x)) + grad_act[rows:] * (y * root_mean(y)),
        axis=0,
        keepdims=True,
    )
    input_own_ref[...] = grad_act[:rows]
    input_other_ref[...] = grad_act[rows:].astype(BF16)


def swap(x):
    return lax.ppermute(x, "ffn", [(0, 1), (1, 0)])


def flip(x, bit):
    peers = lax.axis_size("expert")
    return lax.ppermute(x, "expert", [(i, i ^ (1 << bit)) for i in range(peers)])


def scatter_sum(x, order):
    mine = lax.axis_index("expert")
    for bit in order:
        half = x.shape[0] // 2
        upper = (mine >> bit) & 1
        send = lax.dynamic_slice_in_dim(x, (1 - upper) * half, half, 0)
        keep = lax.dynamic_slice_in_dim(x, upper * half, half, 0)
        x = (keep.astype(F32) + flip(send, bit).astype(F32)).astype(BF16)
    return x


def gather_back(x, order):
    mine = lax.axis_index("expert")
    for bit in reversed(order):
        upper = (mine >> bit) & 1
        got = flip(x, bit)
        x = jnp.where(upper == 1, jnp.concatenate([got, x]), jnp.concatenate([x, got]))
    return x


def shards(
    tokens,
    norm_first,
    w_query,
    w_key,
    w_value,
    w_out,
    bucket_bias_table,
    norm_second,
    w_router,
    w_in,
    w_down,
    expert_ids,
    cotangent,
):
    rows, width = tokens.shape
    buckets, heads = bucket_bias_table.shape
    pair = lax.axis_size("ffn")
    experts = w_router.shape[1]
    total = 2 * rows
    capacity = 5 * rows * pair // 4
    hidden = w_in.shape[2]
    part = width // 2
    bits = experts.bit_length() - 1
    core = lax.axis_index("ffn")
    gain_first = norm_first.reshape(1, width)
    gain_second = norm_second.reshape(1, width)
    hot = jnp.asarray(bucket_windows(rows, buckets, REACH))

    other = swap(tokens)
    in_own, down_own = w_in[0], w_down[0]
    in_other, down_other = swap(in_own), swap(down_own)
    place, fetch, choose, cot_out, windows = call(
        functools.partial(prepare_kernel, experts),
        [
            ((total, rows), BF16),
            ((rows, total), BF16),
            ((rows, experts), F32),
            ((total, width + LANES), BF16),
            ((heads, 6 * rows), F32),
        ],
        (expert_ids.reshape(1, rows), cotangent, bucket_bias_table, hot),
        flops=100000000,
    )
    back = lax.all_to_all(cot_out, "expert", 0, 0, tiled=True)
    middle, gate, outgoing = call(
        functools.partial(forward_kernel, heads),
        [((rows, width), F32), ((rows, LANES), F32), ((total, width), BF16)],
        (
            tokens,
            other,
            gain_first,
            w_query,
            w_key,
            w_value,
            w_out,
            windows,
            gain_second,
            w_router,
            choose,
            place,
        ),
        flops=3000000000,
    )
    flat = lax.all_to_all(outgoing, "expert", 0, 0, tiled=True)
    act, queries, keys, values, probs, mixed = call(
        functools.partial(halves_kernel, heads),
        [
            ((2 * rows, width), BF16),
            ((2 * rows, part), BF16),
            ((2 * rows, part), BF16),
            ((2 * rows, part), BF16),
            ((heads // 2, 2 * rows, 2 * rows), F32),
            ((2 * rows, part), BF16),
        ],
        (tokens, other, gain_first, w_query, w_key, w_value, windows),
        flops=3000000000,
        anys=(3, 4, 5),
        scratch=[pltpu.VMEM((width, part), BF16)] * 3 + [pltpu.SemaphoreType.DMA((3,))],
    )
    fill_other = swap(back[:, width:])
    chunk = 512
    steps = 2 * hidden // chunk
    hid_own, hid_other, pre_own, pre_other, grad_slots, sent, produced, router_part = call(
        functools.partial(expert_kernel, capacity, chunk),
        [
            ((total, hidden), BF16),
            ((total, hidden), BF16),
            ((total, hidden), BF16),
            ((total, hidden), BF16),
            ((total, width), BF16),
            ((total, width), BF16),
            ((total, width), BF16),
            ((width, experts), F32),
        ],
        (flat, back, fill_other, w_router, in_own, in_other, down_own, down_other),
        flops=6000000000,
        anys=(4, 5, 6, 7),
        scratch=[
            pltpu.VMEM((steps, width, chunk), BF16),
            pltpu.VMEM((steps, chunk, width), BF16),
            pltpu.SemaphoreType.DMA((2, steps)),
        ],
    )
    grad_returned = lax.all_to_all(grad_slots, "expert", 0, 0, tiled=True)
    produced_returned = lax.all_to_all(produced, "expert", 0, 0, tiled=True)
    grad_w_in, grad_w_down = expert_weights(
        flat,
        swap(flat),
        sent,
        swap(sent),
        hid_own,
        swap(hid_other),
        pre_own,
        swap(pre_other),
        256,
    )
    grad_middle, grad_low, gain_second_part = call(
        middle_kernel,
        [((rows, width), F32), ((rows, width), BF16), ((1, width), F32)],
        (grad_returned, fetch, middle, gain_second, cotangent),
        flops=100000000,
    )
    packed, input_own, input_other, gain_first_part, table_part = call(
        functools.partial(backward_kernel, heads),
        [
            ((4 * width, part), BF16),
            ((rows, width), F32),
            ((rows, width), BF16),
            ((1, width), F32),
            ((heads // 2, buckets), F32),
        ],
        (
            grad_low,
            swap(grad_low),
            tokens,
            other,
            act,
            queries,
            keys,
            values,
            probs,
            mixed,
            hot,
            w_query,
            w_key,
            w_value,
            w_out,
        ),
        flops=4000000000,
        anys=(11, 12, 13, 14),
        scratch=[pltpu.VMEM((width, part), BF16)] * 3
        + [pltpu.VMEM((part, width), BF16), pltpu.SemaphoreType.DMA((4,))],
    )
    expert_branch = gate[:, :1] * dot(fetch, produced_returned)
    output = (middle + expert_branch).astype(BF16)
    inputs = tokens.astype(F32)
    root = root_mean(inputs)
    up = norm_first * (input_own + swap(input_other).astype(F32))
    grad_input = grad_middle + root * up - inputs * root**3 * jnp.mean(
        up * inputs, axis=-1, keepdims=True
    )
    table_full = lax.dynamic_update_slice_in_dim(
        jnp.zeros((buckets, heads), F32), table_part.T, core * (heads // 2), 1
    )
    small = jnp.concatenate(
        [
            gain_first_part.reshape(-1),
            gain_second_part.reshape(-1),
            table_full.reshape(-1),
            router_part.reshape(-1),
        ]
    )
    count = small.shape[0]
    small_rows = -(-count // (part * 128)) * 128
    small = jnp.pad(small, (0, small_rows * part - count)).reshape(small_rows, part).astype(BF16)
    third = 4 * width // 3
    orders = [list(range(bits)), [1, 2, 0] + list(range(3, bits)), [2, 0, 1] + list(range(3, bits))]
    pieces = [
        packed[:third],
        packed[third : 2 * third],
        jnp.concatenate([packed[2 * third :], small]),
    ]
    pieces = [scatter_sum(piece, order) for piece, order in zip(pieces, orders)]
    pieces = [gather_back(piece, order) for piece, order in zip(pieces, orders)]
    mine = jnp.concatenate(pieces)
    theirs = swap(mine)
    first = jnp.where(core == 0, mine, theirs)
    second = jnp.where(core == 0, theirs, mine)
    summed = []
    for i in range(3):
        span = slice(i * width, (i + 1) * width)
        summed.append(jnp.concatenate([first[span], second[span]], axis=1).astype(F32))
    blocks = [
        jnp.concatenate(
            [half[3 * width : 3 * width + part], half[3 * width + part : 4 * width]], axis=1
        )
        for half in (first, second)
    ]
    summed.append(jnp.concatenate(blocks, axis=0).astype(F32))
    tail = (first[4 * width :].astype(F32) + second[4 * width :].astype(F32)).reshape(-1)
    ends = np.cumsum([width, width, buckets * heads, width * experts])
    return (
        output,
        grad_input,
        tail[: ends[0]],
        summed[0],
        summed[1],
        summed[2],
        summed[3],
        tail[ends[1] : ends[2]].reshape(buckets, heads),
        tail[ends[0] : ends[1]],
        tail[ends[2] : ends[3]].reshape(width, experts),
        grad_w_in,
        grad_w_down,
        expert_branch,
    )


def solution(mesh):
    placed = (
        P(("expert", "ffn"), None),
        P(),
        P(),
        P(),
        P(),
        P(),
        P(),
        P(),
        P(),
        P("expert", None, "ffn"),
        P("expert", "ffn", None),
        P(("expert", "ffn")),
        P(("expert", "ffn"), None),
    )
    return jax.shard_map(
        shards,
        mesh=mesh,
        in_specs=placed,
        out_specs=(
            P(("expert", "ffn"), None),
            P(("expert", "ffn"), None),
            P(),
            P(),
            P(),
            P(),
            P(),
            P(),
            P(),
            P(),
            P("expert", None, "ffn"),
            P("expert", "ffn", None),
            P(("expert", "ffn"), None),
        ),
        check_vma=False,
    )
```

time: 448 us -> 237 us (0.53)
  blocking collectives: 136 us -> 0 us
  waiting for transfers between devices: 167 us -> 68.8 us
  matrix products: 64.7 us -> 2.02 us
  starting transfers between devices: 4.89 us -> 53.2 us
  Pallas kernels: 0 us -> 35.9 us
  local copies, waits for them, and re-layouts: 31.6 us -> 48.7 us
  between operations: 14.8 us -> 1.26 us
    psum x1 -> x0, waiting for transfers between devices: 160 us -> none  [shards(): lax.psum((grad_norm_first_part, grad_query_part, grad_key_part, grad_valu...]
    dot_general x30 -> x1, matrix products: 64.7 us -> 2.02 us  [dot(): return jnp.dot(left, right, preferred_element_type=F32)]
    all_to_all x3 -> x0, blocking collectives: 48.9 us -> none  [the longest x1 18.4 us: shards(): lax.all_to_all(outgoing, 'expert', split_axis=0, concat_axis=0, tiled=True)]
    unnamed x1 -> x0, blocking collectives: 42 us -> none
    psum x1 -> x0, blocking collectives: 41.1 us -> none  [shards(): lax.psum((grad_norm_first_part, grad_query_part, grad_key_part, grad_valu...]
    pallas_call x0 -> x7, Pallas kernels: none -> 35.9 us  [the longest x6 27.9 us: call(): pl.pallas_call(body, out_shape=[jax.ShapeDtypeStruct(s, d) for s, d in ou...]
    ppermute x0 -> x35, waiting for transfers between devices: none -> 32.5 us  [the longest x24 31.5 us: flip(): return lax.ppermute(x, 'expert', [(i, i ^ 1 << bit) for i in range(peers)])]
    ppermute x0 -> x35, starting transfers between devices: none -> 30.9 us  [the longest x24 28.8 us: flip(): return lax.ppermute(x, 'expert', [(i, i ^ 1 << bit) for i in range(peers)])]
  transfers between devices with their start and end apart: 8 -> 39, of which waited for: 2 -> 20; matrix products, arithmetic and copies ran while one was open for 15% -> 7% of each run, Pallas kernels for 0% -> 8%
where the time goes in v1:
time: 237 us; the launch traced here: 235 us
  waiting for transfers between devices  68.8 us (29%)
  starting transfers between devices  53.2 us (22%)
  local copies, waits for them, and re-layouts  48.7 us (21%)
  Pallas kernels  35.9 us (15%)
  other arithmetic  24.6 us (10%)
    unnamed x106, local copies, waits for them, and re-layouts  34.7 us
    ppermute x24, waiting for transfers between devices, flip(): return lax.ppermute(x, 'expert', [(i, i ^ 1 << bit) for i in range(peers)])  31.5 us
    ppermute x24, starting transfers between devices, flip(): return lax.ppermute(x, 'expert', [(i, i ^ 1 << bit) for i in range(peers)])  28.8 us
    pallas_call x6, Pallas kernels, call(): pl.pallas_call(body, out_shape=[jax.ShapeDtypeStruct(s, d) for s, d in ou...  27.9 us
    all_to_all x1, waiting for transfers between devices, shards(): grad_returned = lax.all_to_all(grad_slots, 'expert', 0, 0, tiled=True)  12 us
    all_to_all x1, waiting for transfers between devices, shards(): flat = lax.all_to_all(outgoing, 'expert', 0, 0, tiled=True)  11.8 us
    all_to_all x1, waiting for transfers between devices, shards(): produced_returned = lax.all_to_all(produced, 'expert', 0, 0, tiled=True)  11.3 us
    select_n x1, other arithmetic, shards(): first = jnp.where(core == 0, mine, theirs)  8.3 us
  transfers between devices with their start and end apart: 39, of which 20 were waited for; matrix products, arithmetic and copies ran while one was open for 7% of the time, Pallas kernels for 8%

profile of v1, /device:TPU:0, one launch (start us, length us, event | category | flops | bytes accessed | tf_op | source)
XLA Modules:
  0.0 234.6 jit_solution(17665923872865241379)
XLA Ops:
  5.7 8.3 %all-to-all-start.1 = ((bf16[16,16,896]{2,1,0:T(8,128)(2,1)}), bf16[16,16,896]{2,1,0:T(8,128)(2,1)S(1)}, u32[]{:S(2)}, u32[]{:S(2)}) async-start(bf16[16,16,896]{2,1,0:T(8,128)(2,1)} %bitcast.3), calls=%async_computation.1 | async-start | bytes 917504 | tf_op jit(solution)/shard_map/all_to_all | solution.py:600
  21.1 5.9 %shard_map.238 = (f32[128,768]{1,0:T(8,128)S(1)}, f32[128,128]{1,0:T(8,128)S(1)}, bf16[256,768]{1,0:T(8,128)(2,1)}) custom-call(bf16[128,768]{1,0:T(8,128)(2,1)S(1)} %copy-done, bf16[128,768]{1,0:T(8,128)(2,1)S(1)} %collective-permute-done.other_ref, f32[1,768]{1,0:T(1,128)S(1)} %reshape.93.gain_first_ref, bf16[768,768]{1,0:T(8,128)(2,1)S(1)} %copy-done.4, ...), custom_call_target="tpu_custom_call" | custom-call | flops 3000000000 | bytes 1000000 | tf_op jit(solution)/shard_map/pallas_call | solution.py:62
  28.1 5.7 %all-to-all-start = ((bf16[16,16,768]{2,1,0:T(8,128)(2,1)}), bf16[16,16,768]{2,1,0:T(8,128)(2,1)S(1)}, u32[]{:S(2)}, u32[]{:S(2)}) async-start(bf16[16,16,768]{2,1,0:T(8,128)(2,1)} %bitcast.1), calls=%async_computation | async-start | bytes 786432 | tf_op jit(solution)/shard_map/all_to_all | solution.py:620
  35.2 11.8 %all-to-all-done = bf16[16,16,768]{2,1,0:T(8,128)(2,1)S(1)} async-done(((bf16[16,16,768]{2,1,0:T(8,128)(2,1)}), bf16[16,16,768]{2,1,0:T(8,128)(2,1)S(1)}, u32[]{:S(2)}, u32[]{:S(2)}) %all-to-all-start) | async-done | bytes 393248 | tf_op jit(solution)/shard_map/all_to_all | solution.py:620
  47.0 9.6 %shard_map.239 = (bf16[256,1536]{1,0:T(8,128)(2,1)S(1)}, bf16[256,1536]{1,0:T(8,128)(2,1)S(1)}, bf16[256,1536]{1,0:T(8,128)(2,1)S(1)}, bf16[256,1536]{1,0:T(8,12...) custom-call(bf16[256,768]{1,0:T(8,128)(2,1)S(1)} %bitcast.17, ...), custom_call_target="tpu_custom_call" | custom-call | flops 6000000000 | bytes 1000000 | tf_op jit(solution)/shard_map/pallas_call | solution.py:62
  60.0 3.8 %all-to-all-start.3 = ((bf16[16,16,768]{2,1,0:T(8,128)(2,1)}), bf16[16,16,768]{2,1,0:T(8,128)(2,1)S(1)}, u32[]{:S(2)}, u32[]{:S(2)}) async-start(bf16[16,16,768]{2,1,0:T(8,128)(2,1)} %bitcast.9), calls=%async_computation.3 | async-start | bytes 786432 | tf_op jit(solution)/shard_map/all_to_all | solution.py:660
  63.8 12.0 %all-to-all-done.3 = bf16[16,16,768]{2,1,0:T(8,128)(2,1)S(1)} async-done(((bf16[16,16,768]{2,1,0:T(8,128)(2,1)}), bf16[16,16,768]{2,1,0:T(8,128)(2,1)S(1)}, u32[]{:S(2)}, u32[]{:S(2)}) %all-to-all-start.3) | async-done | bytes 393248 | tf_op jit(solution)/shard_map/all_to_all | solution.py:660
  81.5 3.2 %shard_map.241 = (bf16[256,768]{1,0:T(8,128)(2,1)S(1)}, bf16[256,384]{1,0:T(8,128)(2,1)S(1)}, bf16[256,384]{1,0:T(8,128)(2,1)S(1)}, bf16[256,384]{1,0:T(8,128)(2...) custom-call(bf16[128,768]{1,0:T(8,128)(2,1)S(1)} %copy-done.1, ...), custom_call_target="tpu_custom_call" | custom-call | flops 3000000000 | bytes 1000000 | tf_op jit(solution)/shard_map/pallas_call | solution.py:62
  88.0 1.7 reshape.99
  98.2 7.0 %shard_map.242 = (bf16[3072,384]{1,0:T(8,128)(2,1)}, f32[128,768]{1,0:T(8,128)S(1)}, bf16[128,768]{1,0:T(8,128)(2,1)S(1)}, f32[1,768]{1,0:T(1,128)S(1)}, f32[6,32]{1,0:T(8,128)S(1)}) custom-call(bf16[128,768]{1,0:T(8,128)(2,1)} %get-tuple-element.56.grad_own_ref, bf16[128,768]{1,0:T(8,128)(2,1)S(1)} %collective-permute-done.4.grad_other_ref, ...), custom_call_target="tpu_custom_call" | custom-call | flops 4000000000 | bytes 1000000 | tf_op jit(solution)/shard_map/pallas_call | solution.py:62
  106.5 2.7 %fusion.17 = (bf16[1024,384]{1,0:T(8,128)(2,1)}, bf16[1024,384]{1,0:T(8,128)(2,1)S(1)}, bf16[1024,384]{1,0:T(8,128)(2,1)S(1)}) fusion(bf16[3072,384]{1,0:T(8,128)(2,1)} %get-tuple-element.65), kind=kLoop, calls=%fused_computation.78 | loop fusion | bytes 4718592 | tf_op jit(solution)/shard_map/slice | solution.py:735
  117.2 5.7 %collective-permute-done.14 = bf16[512,384]{1,0:T(8,128)(2,1)} collective-permute-done((bf16[512,384]{1,0:T(8,128)(2,1)}, bf16[512,384]{1,0:T(8,128)(2,1)}, u32[]{:S(2)}, u32[]{:S(2)}) %collective-permute-start.14) | collective-permute-done | bytes 393248 | tf_op jit(solution)/shard_map/ppermute | solution.py:533
  128.0 2.0 collective-permute-done.22
  135.5 2.2 collective-permute-done.23
  140.5 1.6 collective-permute-start.9
  142.2 2.1 collective-permute-done.17
  145.6 1.7 collective-permute-done.9
  147.5 2.9 %collective-permute-start.25 = (bf16[72,384]{1,0:T(8,128)(2,1)S(1)}, bf16[72,384]{1,0:T(8,128)(2,1)S(1)}, u32[]{:S(2)}, u32[]{:S(2)}) collective-permute-start(bf16[72,384]{1,0:T(8,128)(2,1)S(1)} %constant_dynamic-slice_fusion), channel_id=1, source_target_pairs={{0,16},{2,18},{4,20},{6,22},{8,24},{10,26},{12,28},{14,30},{16,0},... | collective-permute-start | bytes 165896 | tf_op jit(solution)/shard_map/ppermute | solution.py:533
  153.1 3.1 %collective-permute-start.26 = (bf16[72,384]{1,0:T(8,128)(2,1)S(1)}, bf16[72,384]{1,0:T(8,128)(2,1)S(1)}, u32[]{:S(2)}, u32[]{:S(2)}) collective-permute-start(bf16[72,384]{1,0:T(8,128)(2,1)S(1)} %add_convert_fusion.10), channel_id=1, source_target_pairs={{0,16},{2,18},{4,20},{6,22},{8,24},{10,26},{12,28},{14,30},{16,0},... | collective-permute-start | bytes 165896 | tf_op jit(solution)/shard_map/ppermute | solution.py:533
  156.3 2.1 collective-permute-done.26
  160.6 3.8 %collective-permute-done.27 = bf16[144,384]{1,0:T(8,128)(2,1)S(1)} collective-permute-done((bf16[144,384]{1,0:T(8,128)(2,1)S(1)}, bf16[144,384]{1,0:T(8,128)(2,1)S(1)}, u32[]{:S(2)}, u32[]{:S(2)}) %collective-permute-start.27) | collective-permute-done | bytes 110624 | tf_op jit(solution)/shard_map/ppermute | solution.py:533
  164.4 2.5 %collective-permute-start.28 = (bf16[288,384]{1,0:T(8,128)(2,1)S(1)}, bf16[288,384]{1,0:T(8,128)(2,1)S(1)}, u32[]{:S(2)}, u32[]{:S(2)}) collective-permute-start(bf16[288,384]{1,0:T(8,128)(2,1)S(1)} %maximum_select_fusion.6), channel_id=1, source_target_pairs={{0,2},{2,0},{4,6},{6,4},{8,10},{10,8},{12,14},{14,12},{16,18},{18,... | collective-permute-start | bytes 663560 | tf_op jit(solution)/shard_map/ppermute | solution.py:533
  168.7 2.2 collective-permute-start.13
  171.9 3.0 %collective-permute-done.21 = bf16[512,384]{1,0:T(8,128)(2,1)S(1)} collective-permute-done((bf16[512,384]{1,0:T(8,128)(2,1)S(1)}, bf16[512,384]{1,0:T(8,128)(2,1)S(1)}, u32[]{:S(2)}, u32[]{:S(2)}) %collective-permute-start.21) | collective-permute-done | bytes 393248 | tf_op jit(solution)/shard_map/ppermute | solution.py:533
  177.0 2.4 %collective-permute-done.29 = bf16[576,384]{1,0:T(8,128)(2,1)S(1)} collective-permute-done((bf16[576,384]{1,0:T(8,128)(2,1)S(1)}, bf16[576,384]{1,0:T(8,128)(2,1)S(1)}, u32[]{:S(2)}, u32[]{:S(2)}) %collective-permute-start.29) | collective-permute-done | bytes 442400 | tf_op jit(solution)/shard_map/ppermute | solution.py:533
  179.9 1.7 pad_maximum_fusion
  181.6 4.5 %all-to-all-start.2 = ((bf16[16,16,768]{2,1,0:T(8,128)(2,1)}), bf16[16,16,768]{2,1,0:T(8,128)(2,1)}, u32[]{:S(2)}, u32[]{:S(2)}) async-start(bf16[16,16,768]{2,1,0:T(8,128)(2,1)} %bitcast.7), calls=%async_computation.2 | async-start | bytes 786432 | tf_op jit(solution)/shard_map/all_to_all | solution.py:661
  187.3 11.3 %all-to-all-done.2 = bf16[16,16,768]{2,1,0:T(8,128)(2,1)} async-done(((bf16[16,16,768]{2,1,0:T(8,128)(2,1)}), bf16[16,16,768]{2,1,0:T(8,128)(2,1)}, u32[]{:S(2)}, u32[]{:S(2)}) %all-to-all-start.2) | async-done | bytes 393248 | tf_op jit(solution)/shard_map/all_to_all | solution.py:661
  198.7 2.0 add_convert_fusion.6
  204.0 8.1 %shard_map.243 = (f32[1,768,1536]{2,1,0:T(8,128)}, f32[1,1536,768]{2,1,0:T(8,128)}) custom-call(bf16[256,768]{1,0:T(8,128)(2,1)S(1)} %bitcast.19, bf16[256,768]{1,0:T(8,128)(2,1)} %collective-permute-done.31.flat_other, bf16[256,768]{1,0:T(8,128)(2,1)S(1)} %copy-done.16, bf16[256,768]{1,0:T(8,128)(2,1)} %collective-permute-done.32.sent_other, ...), custom_call_target="tpu_custom_call" | custom-call | flops 2415919104 | bytes 14000000 | tf_op jit(solution)/shard_map/pallas_call | solution.py:378
  213.6 8.3 %broadcast_select_fusion.1 = (bf16[3200,384]{1,0:T(8,128)(2,1)S(1)}, bf16[3200,384]{1,0:T(8,128)(2,1)S(1)}) fusion(bf16[3200,384]{1,0:T(8,128)(2,1)} %collective-permute-done.30, pred[]{:T(512)S(6)} %eq.10, bf16[1152,384]{1,0:T(8,128)(2,1)S(1)} %copy-done.36, bf16[1024,384]{1,0:T(8,128)(2,1)S(1)} %copy-done.38, bf16[1024,384]{1,0:T(8,128)(2,1)S(1)} %copy-done.40), kind=kLoop, calls=%fused_computation.2 | loop fusion | flops 9830400 | bytes 9830401 | tf_op jit(solution)/shard_map/jit(_where)/select_n | solution.py:743
  227.2 2.6 %maximum_convert_fusion.2 = f32[768,768]{1,0:T(8,128)} fusion(bf16[768,384]{1,0:T(8,128)(2,1)} %get-tuple-element.130, bf16[768,384]{1,0:T(8,128)(2,1)S(1)} %get-tuple-element.113), kind=kLoop, calls=%fused_computation.5 | loop fusion | flops 2359296 | bytes 3538944 | tf_op jit(solution)/shard_map/convert_element_type | solution.py:748
  (231 shorter events, 85.8 us)
Async XLA Ops:
  0.6 46.4 %collective-permute-start.2 = (bf16[768,1536]{1,0:T(8,128)(2,1)}, bf16[768,1536]{1,0:T(8,128)(2,1)}, u32[]{:S(2)}, u32[]{:S(2)}) collective-permute-start(bf16[768,1536]{1,0:T(8,128)(2,1)} %bitcast.22), channel_id=1, source_target_pairs={{0,1},{1,0},{2,3},{3,2},{4,5},{5,4},{6,7},{7,6},{8,9},{9,8},{10,11... | collective-permute-start | bytes 7077896 | tf_op jit(solution)/shard_map/ppermute | solution.py:528
  1.2 45.9 %collective-permute-start.3 = (bf16[1536,768]{1,0:T(8,128)(2,1)}, bf16[1536,768]{1,0:T(8,128)(2,1)}, u32[]{:S(2)}, u32[]{:S(2)}) collective-permute-start(bf16[1536,768]{1,0:T(8,128)(2,1)} %bitcast.24), channel_id=1, source_target_pairs={{0,1},{1,0},{2,3},{3,2},{4,5},{5,4},{6,7},{7,6},{8,9},{9,8},{10,11... | collective-permute-start | bytes 7077896 | tf_op jit(solution)/shard_map/ppermute | solution.py:528
  5.7 22.4 %all-to-all-start.1 = ((bf16[16,16,896]{2,1,0:T(8,128)(2,1)}), bf16[16,16,896]{2,1,0:T(8,128)(2,1)S(1)}, u32[]{:S(2)}, u32[]{:S(2)}) async-start(bf16[16,16,896]{2,1,0:T(8,128)(2,1)} %bitcast.3), calls=%async_computation.1 | async-start | bytes 917504 | tf_op jit(solution)/shard_map/all_to_all | solution.py:600
  28.1 18.9 %all-to-all-start = ((bf16[16,16,768]{2,1,0:T(8,128)(2,1)}), bf16[16,16,768]{2,1,0:T(8,128)(2,1)S(1)}, u32[]{:S(2)}, u32[]{:S(2)}) async-start(bf16[16,16,768]{2,1,0:T(8,128)(2,1)} %bitcast.1), calls=%async_computation | async-start | bytes 786432 | tf_op jit(solution)/shard_map/all_to_all | solution.py:620
  60.0 15.8 %all-to-all-start.3 = ((bf16[16,16,768]{2,1,0:T(8,128)(2,1)}), bf16[16,16,768]{2,1,0:T(8,128)(2,1)S(1)}, u32[]{:S(2)}, u32[]{:S(2)}) async-start(bf16[16,16,768]{2,1,0:T(8,128)(2,1)} %bitcast.9), calls=%async_computation.3 | async-start | bytes 786432 | tf_op jit(solution)/shard_map/all_to_all | solution.py:660
  76.8 13.0 %collective-permute-start.4 = (bf16[128,768]{1,0:T(8,128)(2,1)}, bf16[128,768]{1,0:T(8,128)(2,1)S(1)}, u32[]{:S(2)}, u32[]{:S(2)}) collective-permute-start(bf16[128,768]{1,0:T(8,128)(2,1)} %get-tuple-element.56.grad_own_ref), channel_id=1, source_target_pairs={{0,1},{1,0},{2,3},{3,2},{4,5},{5,4},{6,7},{7,6},{8,9},{9,8},{10,11... | collective-permute-start | bytes 589832 | tf_op jit(solution)/shard_map/ppermute | solution.py:528
  110.9 12.0 %collective-permute-start.14 = (bf16[512,384]{1,0:T(8,128)(2,1)}, bf16[512,384]{1,0:T(8,128)(2,1)}, u32[]{:S(2)}, u32[]{:S(2)}) collective-permute-start(bf16[512,384]{1,0:T(8,128)(2,1)} %constant_dynamic-slice_fusion.6), channel_id=1, source_target_pairs={{0,4},{2,6},{4,0},{6,2},{8,12},{10,14},{12,8},{14,10},{16,20},{18,... | collective-permute-start | bytes 1179656 | tf_op jit(solution)/shard_map/ppermute | solution.py:533
  115.2 11.5 %collective-permute-start.6 = (bf16[512,384]{1,0:T(8,128)(2,1)S(1)}, bf16[512,384]{1,0:T(8,128)(2,1)S(1)}, u32[]{:S(2)}, u32[]{:S(2)}) collective-permute-start(bf16[512,384]{1,0:T(8,128)(2,1)S(1)} %constant_dynamic-slice_fusion.10), channel_id=1, source_target_pairs={{0,2},{2,0},{4,6},{6,4},{8,10},{10,8},{12,14},{14,12},{16,18},{18,... | collective-permute-start | bytes 1179656 | tf_op jit(solution)/shard_map/ppermute | solution.py:533
  117.0 13.1 %collective-permute-start.22 = (bf16[576,384]{1,0:T(8,128)(2,1)S(1)}, bf16[576,384]{1,0:T(8,128)(2,1)S(1)}, u32[]{:S(2)}, u32[]{:S(2)}) collective-permute-start(bf16[576,384]{1,0:T(8,128)(2,1)S(1)} %fusion), channel_id=1, source_target_pairs={{0,8},{2,10},{4,12},{6,14},{8,0},{10,2},{12,4},{14,6},{16,24},{18,... | collective-permute-start | bytes 1327112 | tf_op jit(solution)/shard_map/ppermute | solution.py:533
  124.0 9.4 %collective-permute-start.15 = (bf16[256,384]{1,0:T(8,128)(2,1)S(1)}, bf16[256,384]{1,0:T(8,128)(2,1)S(1)}, u32[]{:S(2)}, u32[]{:S(2)}) collective-permute-start(bf16[256,384]{1,0:T(8,128)(2,1)S(1)} %constant_dynamic-slice_fusion.5), channel_id=1, source_target_pairs={{0,8},{2,10},{4,12},{6,14},{8,0},{10,2},{12,4},{14,6},{16,24},{18,... | collective-permute-start | bytes 589832 | tf_op jit(solution)/shard_map/ppermute | solution.py:533
  126.8 8.2 %collective-permute-start.7 = (bf16[256,384]{1,0:T(8,128)(2,1)S(1)}, bf16[256,384]{1,0:T(8,128)(2,1)S(1)}, u32[]{:S(2)}, u32[]{:S(2)}) collective-permute-start(bf16[256,384]{1,0:T(8,128)(2,1)S(1)} %constant_dynamic-slice_fusion.9), channel_id=1, source_target_pairs={{0,4},{2,6},{4,0},{6,2},{8,12},{10,14},{12,8},{14,10},{16,20},{18,... | collective-permute-start | bytes 589832 | tf_op jit(solution)/shard_map/ppermute | solution.py:533
  130.6 7.1 %collective-permute-start.23 = (bf16[288,384]{1,0:T(8,128)(2,1)S(1)}, bf16[288,384]{1,0:T(8,128)(2,1)S(1)}, u32[]{:S(2)}, u32[]{:S(2)}) collective-permute-start(bf16[288,384]{1,0:T(8,128)(2,1)S(1)} %constant_dynamic-slice_fusion.2), channel_id=1, source_target_pairs={{0,2},{2,0},{4,6},{6,4},{8,10},{10,8},{12,14},{14,12},{16,18},{18,... | collective-permute-start | bytes 663560 | tf_op jit(solution)/shard_map/ppermute | solution.py:533
  137.8 9.7 %collective-permute-start.24 = (bf16[144,384]{1,0:T(8,128)(2,1)S(1)}, bf16[144,384]{1,0:T(8,128)(2,1)S(1)}, u32[]{:S(2)}, u32[]{:S(2)}) collective-permute-start(bf16[144,384]{1,0:T(8,128)(2,1)S(1)} %constant_dynamic-slice_fusion.1), channel_id=1, source_target_pairs={{0,4},{2,6},{4,0},{6,2},{8,12},{10,14},{12,8},{14,10},{16,20},{18,... | collective-permute-start | bytes 331784 | tf_op jit(solution)/shard_map/ppermute | solution.py:533
  140.5 6.8 %collective-permute-start.9 = (bf16[64,384]{1,0:T(8,128)(2,1)S(1)}, bf16[64,384]{1,0:T(8,128)(2,1)S(1)}, u32[]{:S(2)}, u32[]{:S(2)}) collective-permute-start(bf16[64,384]{1,0:T(8,128)(2,1)S(1)} %constant_dynamic-slice_fusion.7), channel_id=1, source_target_pairs={{0,16},{2,18},{4,20},{6,22},{8,24},{10,26},{12,28},{14,30},{16,0},... | collective-permute-start | bytes 147464 | tf_op jit(solution)/shard_map/ppermute | solution.py:533
  144.3 6.2 %collective-permute-start.18 = (bf16[64,384]{1,0:T(8,128)(2,1)S(1)}, bf16[64,384]{1,0:T(8,128)(2,1)S(1)}, u32[]{:S(2)}, u32[]{:S(2)}) collective-permute-start(bf16[64,384]{1,0:T(8,128)(2,1)S(1)} %add_convert_fusion.11), channel_id=1, source_target_pairs={{0,16},{2,18},{4,20},{6,22},{8,24},{10,26},{12,28},{14,30},{16,0},... | collective-permute-start | bytes 147464 | tf_op jit(solution)/shard_map/ppermute | solution.py:533
  147.5 5.5 %collective-permute-start.25 = (bf16[72,384]{1,0:T(8,128)(2,1)S(1)}, bf16[72,384]{1,0:T(8,128)(2,1)S(1)}, u32[]{:S(2)}, u32[]{:S(2)}) collective-permute-start(bf16[72,384]{1,0:T(8,128)(2,1)S(1)} %constant_dynamic-slice_fusion), channel_id=1, source_target_pairs={{0,16},{2,18},{4,20},{6,22},{8,24},{10,26},{12,28},{14,30},{16,0},... | collective-permute-start | bytes 165896 | tf_op jit(solution)/shard_map/ppermute | solution.py:533
  150.5 5.7 %collective-permute-start.19 = (bf16[128,384]{1,0:T(8,128)(2,1)S(1)}, bf16[128,384]{1,0:T(8,128)(2,1)S(1)}, u32[]{:S(2)}, u32[]{:S(2)}) collective-permute-start(bf16[128,384]{1,0:T(8,128)(2,1)S(1)} %maximum_select_fusion.11), channel_id=1, source_target_pairs={{0,2},{2,0},{4,6},{6,4},{8,10},{10,8},{12,14},{14,12},{16,18},{18,... | collective-permute-start | bytes 294920 | tf_op jit(solution)/shard_map/ppermute | solution.py:533
  152.5 7.2 %collective-permute-start.11 = (bf16[128,384]{1,0:T(8,128)(2,1)S(1)}, bf16[128,384]{1,0:T(8,128)(2,1)S(1)}, u32[]{:S(2)}, u32[]{:S(2)}) collective-permute-start(bf16[128,384]{1,0:T(8,128)(2,1)S(1)} %maximum_select_fusion.10), channel_id=1, source_target_pairs={{0,8},{2,10},{4,12},{6,14},{8,0},{10,2},{12,4},{14,6},{16,24},{18,... | collective-permute-start | bytes 294920 | tf_op jit(solution)/shard_map/ppermute | solution.py:533
  156.2 10.7 %collective-permute-start.20 = (bf16[256,384]{1,0:T(8,128)(2,1)S(1)}, bf16[256,384]{1,0:T(8,128)(2,1)S(1)}, u32[]{:S(2)}, u32[]{:S(2)}) collective-permute-start(bf16[256,384]{1,0:T(8,128)(2,1)S(1)} %maximum_select_fusion.8), channel_id=1, source_target_pairs={{0,8},{2,10},{4,12},{6,14},{8,0},{10,2},{12,4},{14,6},{16,24},{18,... | collective-permute-start | bytes 589832 | tf_op jit(solution)/shard_map/ppermute | solution.py:533
  158.4 6.0 %collective-permute-start.27 = (bf16[144,384]{1,0:T(8,128)(2,1)S(1)}, bf16[144,384]{1,0:T(8,128)(2,1)S(1)}, u32[]{:S(2)}, u32[]{:S(2)}) collective-permute-start(bf16[144,384]{1,0:T(8,128)(2,1)S(1)} %maximum_select_fusion.9), channel_id=1, source_target_pairs={{0,4},{2,6},{4,0},{6,2},{8,12},{10,14},{12,8},{14,10},{16,20},{18,... | collective-permute-start | bytes 331784 | tf_op jit(solution)/shard_map/ppermute | solution.py:533
  159.7 8.9 %collective-permute-start.12 = (bf16[256,384]{1,0:T(8,128)(2,1)S(1)}, bf16[256,384]{1,0:T(8,128)(2,1)S(1)}, u32[]{:S(2)}, u32[]{:S(2)}) collective-permute-start(bf16[256,384]{1,0:T(8,128)(2,1)S(1)} %maximum_select_fusion.7), channel_id=1, source_target_pairs={{0,4},{2,6},{4,0},{6,2},{8,12},{10,14},{12,8},{14,10},{16,20},{18,... | collective-permute-start | bytes 589832 | tf_op jit(solution)/shard_map/ppermute | solution.py:533
  164.4 6.5 %collective-permute-start.28 = (bf16[288,384]{1,0:T(8,128)(2,1)S(1)}, bf16[288,384]{1,0:T(8,128)(2,1)S(1)}, u32[]{:S(2)}, u32[]{:S(2)}) collective-permute-start(bf16[288,384]{1,0:T(8,128)(2,1)S(1)} %maximum_select_fusion.6), channel_id=1, source_target_pairs={{0,2},{2,0},{4,6},{6,4},{8,10},{10,8},{12,14},{14,12},{16,18},{18,... | collective-permute-start | bytes 663560 | tf_op jit(solution)/shard_map/ppermute | solution.py:533
  167.1 7.8 %collective-permute-start.21 = (bf16[512,384]{1,0:T(8,128)(2,1)S(1)}, bf16[512,384]{1,0:T(8,128)(2,1)S(1)}, u32[]{:S(2)}, u32[]{:S(2)}) collective-permute-start(bf16[512,384]{1,0:T(8,128)(2,1)S(1)} %maximum_select_fusion.5), channel_id=1, source_target_pairs={{0,4},{2,6},{4,0},{6,2},{8,12},{10,14},{12,8},{14,10},{16,20},{18,... | collective-permute-start | bytes 1179656 | tf_op jit(solution)/shard_map/ppermute | solution.py:533
  168.7 8.0 %collective-permute-start.13 = (bf16[512,384]{1,0:T(8,128)(2,1)S(1)}, bf16[512,384]{1,0:T(8,128)(2,1)S(1)}, u32[]{:S(2)}, u32[]{:S(2)}) collective-permute-start(bf16[512,384]{1,0:T(8,128)(2,1)S(1)} %maximum_select_fusion.4), channel_id=1, source_target_pairs={{0,2},{2,0},{4,6},{6,4},{8,10},{10,8},{12,14},{14,12},{16,18},{18,... | collective-permute-start | bytes 1179656 | tf_op jit(solution)/shard_map/ppermute | solution.py:533
  171.1 8.4 %collective-permute-start.29 = (bf16[576,384]{1,0:T(8,128)(2,1)S(1)}, bf16[576,384]{1,0:T(8,128)(2,1)S(1)}, u32[]{:S(2)}, u32[]{:S(2)}) collective-permute-start(bf16[576,384]{1,0:T(8,128)(2,1)S(1)} %maximum_select_fusion.3), channel_id=1, source_target_pairs={{0,8},{2,10},{4,12},{6,14},{8,0},{10,2},{12,4},{14,6},{16,24},{18,... | collective-permute-start | bytes 1327112 | tf_op jit(solution)/shard_map/ppermute | solution.py:533
  181.6 31.7 %collective-permute-start.30 = (bf16[3200,384]{1,0:T(8,128)(2,1)}, bf16[3200,384]{1,0:T(8,128)(2,1)}, u32[]{:S(2)}, u32[]{:S(2)}) collective-permute-start(bf16[3200,384]{1,0:T(8,128)(2,1)} %pad_maximum_fusion), channel_id=1, source_target_pairs={{0,1},{1,0},{2,3},{3,2},{4,5},{5,4},{6,7},{7,6},{8,9},{9,8},{10,11... | collective-permute-start | bytes 7372808 | tf_op jit(solution)/shard_map/ppermute | solution.py:528
  181.6 17.1 %all-to-all-start.2 = ((bf16[16,16,768]{2,1,0:T(8,128)(2,1)}), bf16[16,16,768]{2,1,0:T(8,128)(2,1)}, u32[]{:S(2)}, u32[]{:S(2)}) async-start(bf16[16,16,768]{2,1,0:T(8,128)(2,1)} %bitcast.7), calls=%async_computation.2 | async-start | bytes 786432 | tf_op jit(solution)/shard_map/all_to_all | solution.py:661
  186.1 14.6 %collective-permute-start.33 = (bf16[256,1536]{1,0:T(8,128)(2,1)S(1)}, bf16[256,1536]{1,0:T(8,128)(2,1)}, u32[]{:S(2)}, u32[]{:S(2)}) collective-permute-start(bf16[256,1536]{1,0:T(8,128)(2,1)S(1)} %copy-done.14), channel_id=1, source_target_pairs={{0,1},{1,0},{2,3},{3,2},{4,5},{5,4},{6,7},{7,6},{8,9},{9,8},{10,11... | collective-permute-start | bytes 2359304 | tf_op jit(solution)/shard_map/ppermute | solution.py:528
  186.7 14.1 %collective-permute-start.34 = (bf16[256,1536]{1,0:T(8,128)(2,1)S(1)}, bf16[256,1536]{1,0:T(8,128)(2,1)}, u32[]{:S(2)}, u32[]{:S(2)}) collective-permute-start(bf16[256,1536]{1,0:T(8,128)(2,1)S(1)} %get-tuple-element.74), channel_id=1, source_target_pairs={{0,1},{1,0},{2,3},{3,2},{4,5},{5,4},{6,7},{7,6},{8,9},{9,8},{10,11... | collective-permute-start | bytes 2359304 | tf_op jit(solution)/shard_map/ppermute | solution.py:528
  186.7 14.0 %collective-permute-start.31 = (bf16[256,768]{1,0:T(8,128)(2,1)S(1)}, bf16[256,768]{1,0:T(8,128)(2,1)}, u32[]{:S(2)}, u32[]{:S(2)}) collective-permute-start(bf16[256,768]{1,0:T(8,128)(2,1)S(1)} %bitcast.18), channel_id=1, source_target_pairs={{0,1},{1,0},{2,3},{3,2},{4,5},{5,4},{6,7},{7,6},{8,9},{9,8},{10,11... | collective-permute-start | bytes 1179656 | tf_op jit(solution)/shard_map/ppermute | solution.py:528
  187.2 13.6 %collective-permute-start.32 = (bf16[256,768]{1,0:T(8,128)(2,1)}, bf16[256,768]{1,0:T(8,128)(2,1)}, u32[]{:S(2)}, u32[]{:S(2)}) collective-permute-start(bf16[256,768]{1,0:T(8,128)(2,1)} %copy-done.15), channel_id=1, source_target_pairs={{0,1},{1,0},{2,3},{3,2},{4,5},{5,4},{6,7},{7,6},{8,9},{9,8},{10,11... | collective-permute-start | bytes 1179656 | tf_op jit(solution)/shard_map/ppermute | solution.py:528
  200.7 11.4 %collective-permute-start.5 = (bf16[128,768]{1,0:T(8,128)(2,1)}, bf16[128,768]{1,0:T(8,128)(2,1)S(1)}, u32[]{:S(2)}, u32[]{:S(2)}) collective-permute-start(bf16[128,768]{1,0:T(8,128)(2,1)} %copy-done.17), channel_id=1, source_target_pairs={{0,1},{1,0},{2,3},{3,2},{4,5},{5,4},{6,7},{7,6},{8,9},{9,8},{10,11... | collective-permute-start | bytes 589832 | tf_op jit(solution)/shard_map/ppermute | solution.py:528
  (58 other events, 228.0 us)

commit v2 on v1

v2 whole, which is shorter than its diff:
```python
import functools
import math

import jax
import jax.numpy as jnp
import numpy as np
from jax import lax
from jax.experimental import pallas as pl
from jax.experimental.pallas import tpu as pltpu
from jax.sharding import PartitionSpec as P

REACH = 128
EPS = 1e-06
TOP_PRECISION = lax.Precision.HIGHEST
LANES = 128
F32 = jnp.float32
BF16 = jnp.bfloat16


def bucket_of(distance, buckets, reach):
    half = buckets // 2
    exact = half // 2
    result = np.where(distance < 0, half, 0)
    magnitude = np.abs(distance)
    spread = exact + np.floor(
        np.log(np.maximum(magnitude, 1) / exact) / np.log(reach / exact) * (half - exact)
    )
    spread = np.minimum(spread, half - 1)
    return result + np.where(magnitude < exact, magnitude, spread)


def bucket_windows(rows, buckets, reach):
    lane = np.arange(2 * rows)
    offset = np.where(lane < rows, -lane, 2 * rows - lane)
    windows = []
    for shift in (0, rows, -rows):
        hot = bucket_of(offset + shift, buckets, reach)[None, :] == np.arange(buckets)[:, None]
        hot[:, rows] = False
        windows.append(hot)
    return np.concatenate(windows, axis=1).astype(np.float32)


def rows_by_rows(left, right):
    return lax.dot_general(left, right, (((0,), (0,)), ((), ())), preferred_element_type=F32)


def cols_by_cols(left, right):
    return lax.dot_general(left, right, (((1,), (1,)), ((), ())), preferred_element_type=F32)


def dot(left, right):
    return jnp.dot(left, right, preferred_element_type=F32)


def root_mean(x):
    return lax.rsqrt(jnp.mean(x * x, axis=-1, keepdims=True) + EPS)


def call(body, outs, args, modes, vmem=16, flops=0, scratch=(), aliases=None, nbytes=1000000):
    count, total = len(args), len(args) + len(outs)
    shapes = [(a.shape, a.dtype) for a in args] + list(outs)
    spaces = [pltpu.VMEM if m == "v" else pltpu.HBM for m in modes]
    moved = [i for i in range(total) if modes[i] in "hl"]
    buffers = [pltpu.VMEM(*shapes[i]) for i in moved]

    def kernel(*refs):
        bodies = list(refs[:total])
        for i, ref in zip(moved, refs[total : total + len(moved)]):
            bodies[i] = ref
        extra = refs[total + len(moved) : -1]
        sems = refs[-1]
        copies = {}
        for i in moved:
            ends = (refs[i], bodies[i]) if i < count else (bodies[i], refs[i])
            copies[i] = pltpu.make_async_copy(*ends, sems.at[i])
        for i in moved:
            if i < count:
                copies[i].start()
        flushed = set()

        def wait(i):
            copies[i].wait()

        def flush(i):
            flushed.add(i)
            copies[count + i].start()

        for i in moved:
            if i < count and modes[i] == "h":
                wait(i)
        body(wait, flush, *bodies, *extra)
        for i in moved:
            if i >= count and i - count not in flushed:
                copies[i].start()
        for i in moved:
            if i >= count:
                copies[i].wait()

    specs = [pl.BlockSpec(memory_space=space) for space in spaces]
    return pl.pallas_call(
        kernel,
        out_shape=[jax.ShapeDtypeStruct(s, d) for s, d in outs],
        in_specs=specs[:count],
        out_specs=specs[count:],
        scratch_shapes=buffers + list(scratch) + [pltpu.SemaphoreType.DMA((total,))],
        input_output_aliases=aliases or {},
        compiler_params=pltpu.CompilerParams(vmem_limit_bytes=vmem * 2**20),
        cost_estimate=pl.CostEstimate(flops=flops, bytes_accessed=nbytes, transcendentals=0),
    )(*args)


def toeplitz(window, rows):
    wide = jnp.broadcast_to(window, (rows, 2 * rows))
    return pltpu.roll(wide, 0, 1, stride=1, stride_axis=0)[:, :rows]


def diagonal_sums(square, rows):
    wide = jnp.concatenate([square, jnp.zeros_like(square)], axis=1)
    height = rows
    while height > 1:
        height //= 2
        wide = wide[:height] + pltpu.roll(wide[height:], 2 * rows - height, 1)
    return wide


def placement(ids, experts, total):
    rows = ids.shape[1]
    slots = total // experts
    choose = (lax.broadcasted_iota(jnp.int32, (experts, rows), 0) == ids).astype(F32)
    earlier = (
        lax.broadcasted_iota(jnp.int32, (rows, rows), 0)
        < lax.broadcasted_iota(jnp.int32, (rows, rows), 1)
    ).astype(F32)
    ranks = dot(choose.astype(BF16), earlier.astype(BF16))
    rank = jnp.sum(choose * ranks, axis=0, keepdims=True)
    target = ids * slots + rank.astype(jnp.int32)
    place = (lax.broadcasted_iota(jnp.int32, (total, rows), 0) == target).astype(F32)
    return choose, place


def attend(query_pair, key_pair, scale, bias, side, low_half):
    own = jnp.where(low_half if side == 0 else jnp.logical_not(low_half), query_pair, 0)
    scores = cols_by_cols(own.astype(BF16), key_pair) * scale + bias
    grown = jnp.exp(scores - jnp.max(scores, axis=-1, keepdims=True))
    return grown / jnp.sum(grown, axis=-1, keepdims=True)


def forward_kernel(
    heads,
    wait,
    flush,
    own_ref,
    other_ref,
    gain_first_ref,
    ids_ref,
    ids_other_ref,
    table_ref,
    hot_ref,
    wk,
    wv,
    wq,
    wo,
    gain_second_ref,
    router_ref,
    cot_ref,
    middle_ref,
    gate_ref,
    out_ref,
    mixed_ref,
    win_ref,
    fetch_ref,
    fetch_other_ref,
):
    rows, width = own_ref.shape
    size = width // heads
    scale = 1.0 / math.sqrt(size)
    core = lax.axis_index("ffn")
    total = out_ref.shape[0]
    experts = router_ref.shape[0]
    choose, place = placement(ids_ref[...], experts, total)
    _, place_other = placement(ids_other_ref[...], experts, total)
    fetch_ref[...] = place.T.astype(BF16)
    fetch_other_ref[...] = place_other.T.astype(BF16)
    choose = choose.T
    lane = lax.broadcasted_iota(jnp.int32, (total, LANES), 1)
    out_ref[:, 2 * width :] = jnp.where(
        lane == 0,
        jnp.sum(place, axis=1, keepdims=True),
        jnp.sum(place_other, axis=1, keepdims=True),
    ).astype(BF16)
    place = place.astype(BF16)
    windows = jnp.dot(
        table_ref[...], hot_ref[...], precision=TOP_PRECISION, preferred_element_type=F32
    )
    win_ref[...] = windows
    for i in (4, 5, 6):
        flush(i)
    x = own_ref[...].astype(F32)
    y = other_ref[...].astype(F32)
    gain = gain_first_ref[...].reshape(1, width)
    act_own = (x * root_mean(x) * gain).astype(BF16)
    act_other = (y * root_mean(y) * gain).astype(BF16)
    act = jnp.concatenate([act_own, act_other], axis=0)
    wait(7)
    keys = dot(act, wk[...]).astype(BF16)
    wait(8)
    values = dot(act, wv[...]).astype(BF16)
    wait(9)
    queries = dot(act_own, wq[...]).astype(BF16)
    low_half = lax.broadcasted_iota(jnp.int32, (rows, 2 * size), 1) < size
    same = windows[:, : 2 * rows]
    apart = jnp.where(core == 1, windows[:, 2 * rows : 4 * rows], windows[:, 4 * rows :])
    mixed = []
    for pair in range(heads // 2):
        lanes = slice(pair * 2 * size, (pair + 1) * 2 * size)
        outs = []
        for side in range(2):
            head = 2 * pair + side
            bias = jnp.concatenate(
                [
                    toeplitz(same[head : head + 1], rows),
                    toeplitz(apart[head : head + 1], rows),
                ],
                axis=1,
            )
            probs = attend(queries[:, lanes], keys[:, lanes], scale, bias, side, low_half)
            outs.append(dot(probs.astype(BF16), values[:, lanes]))
        mixed.append(jnp.where(low_half, outs[0], outs[1]).astype(BF16))
    mixed = jnp.concatenate(mixed, axis=1)
    mixed_ref[...] = mixed
    flush(3)
    for i in (10, 11, 12, 13):
        wait(i)
    out_ref[:, width : 2 * width] = dot(place, cot_ref[...]).astype(BF16)
    middle = x + dot(mixed, wo[...])
    middle_ref[...] = middle
    flush(0)
    gain_second = gain_second_ref[...].reshape(1, width)
    act_second = (middle * root_mean(middle) * gain_second).astype(BF16)
    logits = cols_by_cols(act_second, router_ref[...])
    grown = jnp.exp(logits - jnp.max(logits, axis=-1, keepdims=True))
    gate = jnp.sum(grown * choose, axis=-1, keepdims=True) / jnp.sum(
        grown, axis=-1, keepdims=True
    )
    gate_ref[...] = jnp.broadcast_to(gate, gate_ref.shape)
    out_ref[:, :width] = dot(place, act_second).astype(BF16)


def halves_kernel(
    heads,
    wait,
    flush,
    own_ref,
    other_ref,
    gain_first_ref,
    wq_ref,
    wk_ref,
    wv_ref,
    win_ref,
    after_ref,
    act_ref,
    query_ref,
    key_ref,
    value_ref,
    probs_ref,
    wq_half,
    wk_half,
    wv_half,
    sems,
):
    rows, width = own_ref.shape
    size = width // heads
    part = width // 2
    scale = 1.0 / math.sqrt(size)
    core = lax.axis_index("ffn")
    columns = pl.ds(pl.multiple_of(core * part, LANES), part)
    copies = [
        pltpu.make_async_copy(ref.at[:, columns], half, sems.at[i])
        for i, (ref, half) in enumerate(((wq_ref, wq_half), (wk_ref, wk_half), (wv_ref, wv_half)))
    ]
    for copy in copies:
        copy.start()
    x = own_ref[...].astype(F32)
    y = other_ref[...].astype(F32)
    gain = gain_first_ref[...].reshape(1, width)
    act = jnp.concatenate(
        [(x * root_mean(x) * gain).astype(BF16), (y * root_mean(y) * gain).astype(BF16)], axis=0
    )
    act_ref[...] = act
    for copy in copies:
        copy.wait()
    queries = dot(act, wq_half[...]).astype(BF16)
    keys = dot(act, wk_half[...]).astype(BF16)
    values = dot(act, wv_half[...]).astype(BF16)
    query_ref[...] = queries
    key_ref[...] = keys
    value_ref[...] = values
    for i in range(4):
        flush(i)
    low_half = lax.broadcasted_iota(jnp.int32, (2 * rows, 2 * size), 1) < size
    for pair in range(heads // 4):
        lanes = slice(pair * 2 * size, (pair + 1) * 2 * size)
        for side in range(2):
            head = 2 * pair + side
            window = win_ref[pl.ds(core * (heads // 2) + head, 1), :]
            same = toeplitz(window[:, : 2 * rows], rows)
            ahead = toeplitz(window[:, 2 * rows : 4 * rows], rows)
            behind = toeplitz(window[:, 4 * rows :], rows)
            first = jnp.where(core == 1, ahead, behind)
            second = jnp.where(core == 1, behind, ahead)
            bias = jnp.concatenate(
                [
                    jnp.concatenate([same, first], axis=1),
                    jnp.concatenate([second, same], axis=1),
                ],
                axis=0,
            )
            probs_ref[head] = attend(
                queries[:, lanes], keys[:, lanes], scale, bias, side, low_half
            )


def expert_kernel(
    capacity,
    chunk,
    wait,
    flush,
    arrived_ref,
    router_ref,
    in_own_ref,
    in_other_ref,
    down_own_ref,
    down_other_ref,
    after_ref,
    hid_own_ref,
    pre_own_ref,
    sent_ref,
    bundle_ref,
    grad_ref,
    produced_ref,
    router_grad_ref,
    in_vmem,
    down_vmem,
    sems,
):
    total = arrived_ref.shape[0]
    experts, width = router_ref.shape
    slots = total // experts
    hidden = in_own_ref.shape[1]
    steps = hidden // chunk
    mine = lax.axis_index("expert")
    core = lax.axis_index("ffn")
    copies = []
    for side, (win, wdown) in enumerate(
        ((in_own_ref, down_own_ref), (in_other_ref, down_other_ref))
    ):
        for step in range(steps):
            i = side * steps + step
            span = pl.ds(step * chunk, chunk)
            copies.append(
                (
                    pltpu.make_async_copy(win.at[:, span], in_vmem.at[i], sems.at[0, i]),
                    pltpu.make_async_copy(wdown.at[span, :], down_vmem.at[i], sems.at[1, i]),
                )
            )
    for pair in copies:
        for copy in pair:
            copy.start()
    flat = arrived_ref[:, :width]
    cot = arrived_ref[:, width : 2 * width]
    filled = arrived_ref[:, 2 * width :]
    row = lax.broadcasted_iota(jnp.int32, (total, total), 0)
    col = lax.broadcasted_iota(jnp.int32, (total, total), 1)
    shift = slots.bit_length() - 1
    row_block = jnp.right_shift(row, shift)
    col_block = jnp.right_shift(col, shift)
    before = (col_block < row_block).astype(F32).astype(BF16)
    ahead = (col_block < row_block + core).astype(F32).astype(BF16)
    slot = jnp.bitwise_and(lax.broadcasted_iota(jnp.int32, (total, 1), 0), slots - 1)
    position = dot(before, filled)[:, 0:1] + dot(ahead, filled)[:, 1:2] + slot.astype(F32)
    keep = jnp.where(position < capacity, 1.0, 0.0)
    logits = cols_by_cols(flat, router_ref[...])
    grown = jnp.exp(logits - jnp.max(logits, axis=-1, keepdims=True))
    router_probs = grown / jnp.sum(grown, axis=-1, keepdims=True)
    onehot = (lax.broadcasted_iota(jnp.int32, (total, experts), 1) == mine).astype(F32)
    gate = jnp.sum(router_probs * onehot, axis=-1, keepdims=True)
    sent = (cot.astype(F32) * (gate * keep)).astype(BF16)
    sent_ref[...] = sent
    bundle_ref[:, :width] = flat
    bundle_ref[:, width : 2 * width] = sent
    produced = jnp.zeros((total, width), F32)
    grad = jnp.zeros((total, width), F32)
    inner = math.sqrt(2.0 / math.pi)
    for i, pair in enumerate(copies):
        own_side = i < steps
        first = (i % steps) * chunk
        for copy in pair:
            copy.wait()
        win, wdown = in_vmem[i], down_vmem[i]
        pre = dot(flat, win)
        square = pre * pre
        curve = jnp.tanh(inner * pre * (1.0 + 0.044715 * square))
        half_up = 0.5 + 0.5 * curve
        act = (pre * half_up).astype(BF16)
        slope = half_up + (0.5 * inner) * pre * (1.0 - curve * curve) * (
            1.0 + (3 * 0.044715) * square
        )
        grad_pre = (slope * cols_by_cols(sent, wdown)).astype(BF16)
        if own_side:
            hid_own_ref[:, first : first + chunk] = act
            pre_own_ref[:, first : first + chunk] = grad_pre
        else:
            first += 2 * width
            bundle_ref[:, first : first + chunk] = act
            bundle_ref[:, first + hidden : first + hidden + chunk] = grad_pre
        produced = produced + dot(act, wdown)
        grad = grad + cols_by_cols(grad_pre, win)
    for i in range(4):
        flush(i)
    produced_low = produced.astype(BF16)
    kept = produced_low.astype(F32) * keep
    produced_ref[...] = kept.astype(BF16)
    grad_gate = jnp.sum(cot.astype(F32) * kept, axis=-1, keepdims=True)
    grad_logits = ((grad_gate * gate) * (onehot - router_probs)).astype(BF16)
    grad_ref[...] = (grad * keep + dot(grad_logits, router_ref[...])).astype(BF16)
    router_grad_ref[...] = rows_by_rows(grad_logits, flat)


def expert_weights_kernel(
    flat_own, sent_own, hid_own, pre_own, flat_other, sent_other, hid_other, pre_other, in_ref, down_ref
):
    in_ref[0] = rows_by_rows(flat_own[...], pre_own[...]) + rows_by_rows(
        flat_other[...], pre_other[...]
    )
    down_ref[0] = rows_by_rows(hid_own[...], sent_own[...]) + rows_by_rows(
        hid_other[...], sent_other[...]
    )


def expert_weights(flat, sent, hid, pre, bundle, chunk):
    total, width = sent.shape
    hidden = hid.shape[1]
    steps = hidden // chunk
    skip = 2 * width // chunk
    whole = pl.BlockSpec((total, width), lambda i: (0, 0))
    second = pl.BlockSpec((total, width), lambda i: (0, 1))
    part = pl.BlockSpec((total, chunk), lambda i: (0, i))
    return pl.pallas_call(
        expert_weights_kernel,
        grid=(steps,),
        out_shape=[
            jax.ShapeDtypeStruct((1, width, hidden), F32),
            jax.ShapeDtypeStruct((1, hidden, width), F32),
        ],
        in_specs=[
            whole,
            whole,
            part,
            part,
            whole,
            second,
            pl.BlockSpec((total, chunk), lambda i: (0, i + skip)),
            pl.BlockSpec((total, chunk), lambda i: (0, i + skip + steps)),
        ],
        out_specs=[
            pl.BlockSpec((1, width, chunk), lambda i: (0, 0, i)),
            pl.BlockSpec((1, chunk, width), lambda i: (0, i, 0)),
        ],
        compiler_params=pltpu.CompilerParams(vmem_limit_bytes=64 * 2**20),
        cost_estimate=pl.CostEstimate(
            flops=8 * total * width * hidden, bytes_accessed=14000000, transcendentals=0
        ),
    )(flat, sent, hid, pre, bundle, bundle, bundle, bundle)


def middle_back(returned, fetch, middle, gain, cot):
    grad = dot(fetch, returned)
    root = root_mean(middle)
    scaled = middle * root
    up = gain * grad
    grad_middle = cot.astype(F32) + root * (
        up - scaled * jnp.mean(up * scaled, axis=-1, keepdims=True)
    )
    return grad_middle, grad * scaled


def place_of(target, order):
    relative = jnp.bitwise_xor(target, lax.axis_index("expert"))
    place = 0
    for bit in order:
        place = place * 2 + jnp.bitwise_and(jnp.right_shift(relative, bit), 1)
    return place


def chunk_place(chunk, order, levels):
    target = sum((((chunk >> (levels - 1 - k)) & 1) << bit) for k, bit in enumerate(order[:levels]))
    return place_of(target, order[:levels])


def small_rows(experts):
    return [0, 2, 4, 16, 16 + experts, 16 + 2 * experts]


def small_height(experts, levels):
    return -(-(16 + 2 * experts) // (16 << levels)) * 16


def backward_kernel(
    heads,
    orders,
    levels,
    wait,
    flush,
    returned_ref,
    returned_other_ref,
    fetch_ref,
    fetch_other_ref,
    middle_ref,
    middle_other_ref,
    cot_ref,
    cot_other_ref,
    gain_second_ref,
    own_ref,
    other_ref,
    act_ref,
    query_ref,
    key_ref,
    value_ref,
    probs_ref,
    mixed_own_ref,
    mixed_other_ref,
    hot_ref,
    router_ref,
    after_ref,
    wq_ref,
    wk_ref,
    wv_ref,
    wo_ref,
    keep_0_ref,
    send_0_ref,
    keep_1_ref,
    send_1_ref,
    keep_2_ref,
    send_2_ref,
    input_own_ref,
    input_other_ref,
    grad_middle_ref,
    wq_half,
    wk_half,
    wv_half,
    wo_half,
    part_0,
    part_1,
    part_2,
    natural,
    sems,
):
    rows, width = own_ref.shape
    size = width // heads
    part = width // 2
    experts = router_ref.shape[0]
    scale = 1.0 / math.sqrt(size)
    core = lax.axis_index("ffn")
    span = pl.ds(pl.multiple_of(core * part, LANES), part)
    copies = [
        pltpu.make_async_copy(src, half, sems.at[i])
        for i, (src, half) in enumerate(
            (
                (wo_ref.at[span, :], wo_half),
                (wq_ref.at[:, span], wq_half),
                (wk_ref.at[:, span], wk_half),
                (wv_ref.at[:, span], wv_half),
            )
        )
    ]
    for copy in copies:
        copy.start()
    parts = (part_0, part_1, part_2)
    halves = ((keep_0_ref, send_0_ref), (keep_1_ref, send_1_ref), (keep_2_ref, send_2_ref))
    third = width // 3
    height = third >> levels
    writes = []
    for p, pair in enumerate(halves):
        rows_half = pair[0].shape[0]
        for i, ref in enumerate(pair):
            writes.append(
                pltpu.make_async_copy(
                    parts[p].at[pl.ds(i * rows_half, rows_half), :], ref, sems.at[4 + 2 * p + i]
                )
            )

    def pack(matrix, value):
        for p, ref in enumerate(parts):
            for chunk in range(2**levels):
                place = chunk_place(chunk, orders[p], levels)
                first = p * third + chunk * height
                step = ref.shape[0] >> levels
                at = pl.multiple_of(place * step + matrix * height, 16)
                ref[pl.ds(at, height), :] = value[first : first + height]

    gain = gain_second_ref[...].reshape(1, width)
    grad_own, gain_terms = middle_back(
        returned_ref[...], fetch_ref[...], middle_ref[...], gain, cot_ref[...]
    )
    grad_other, _ = middle_back(
        returned_other_ref[...], fetch_other_ref[...], middle_other_ref[...], gain, cot_other_ref[...]
    )
    gain_second = jnp.sum(gain_terms, axis=0, keepdims=True)
    grad_middle_ref[...] = grad_own
    flush(8)
    grad_low = jnp.concatenate([grad_own, grad_other], axis=0).astype(BF16)
    mixed = jnp.concatenate([mixed_own_ref[...], mixed_other_ref[...]], axis=0)
    grad_columns = jnp.where(core == 0, grad_low[:, :part], grad_low[:, part:])
    pack(3, rows_by_rows(mixed, grad_columns).astype(BF16))
    copies[0].wait()
    grad_mixed = cols_by_cols(grad_low, wo_half[...]).astype(BF16)
    low_half = lax.broadcasted_iota(jnp.int32, (2 * rows, 2 * size), 1) < size
    grad_q, grad_k, grad_v = [], [], []
    same, ahead, behind = [], [], []
    for pair in range(heads // 4):
        lanes = slice(pair * 2 * size, (pair + 1) * 2 * size)
        query, key, value = query_ref[:, lanes], key_ref[:, lanes], value_ref[:, lanes]
        grad_pair = grad_mixed[:, lanes]
        got_q, got_k, got_v = [], [], []
        for side in range(2):
            probs = probs_ref[2 * pair + side]
            keep_lanes = low_half if side == 0 else jnp.logical_not(low_half)
            own_grad = jnp.where(keep_lanes, grad_pair, 0).astype(BF16)
            grad_probs = cols_by_cols(own_grad, value)
            got_v.append(rows_by_rows(probs.astype(BF16), grad_pair))
            inner = jnp.sum(probs * grad_probs, axis=-1, keepdims=True)
            grad_scores = probs * (grad_probs - inner)
            same.append(
                diagonal_sums(grad_scores[:rows, :rows] + grad_scores[rows:, rows:], rows)
            )
            first = diagonal_sums(grad_scores[:rows, rows:], rows)
            second = diagonal_sums(grad_scores[rows:, :rows], rows)
            ahead.append(jnp.where(core == 1, first, second))
            behind.append(jnp.where(core == 1, second, first))
            grad_raw = (grad_scores * scale).astype(BF16)
            got_q.append(dot(grad_raw, key))
            got_k.append(rows_by_rows(grad_raw, query))
        grad_q.append(jnp.where(low_half, got_q[0], got_q[1]).astype(BF16))
        grad_k.append(jnp.where(low_half, got_k[0], got_k[1]).astype(BF16))
        grad_v.append(jnp.where(low_half, got_v[0], got_v[1]).astype(BF16))
    grad_q = jnp.concatenate(grad_q, axis=1)
    grad_k = jnp.concatenate(grad_k, axis=1)
    grad_v = jnp.concatenate(grad_v, axis=1)
    act = act_ref[...]
    pack(0, rows_by_rows(act, grad_q).astype(BF16))
    pack(1, rows_by_rows(act, grad_k).astype(BF16))
    pack(2, rows_by_rows(act, grad_v).astype(BF16))
    for write in writes[:4]:
        write.start()
    sums = jnp.concatenate(
        [jnp.concatenate(part_sums, axis=0) for part_sums in (same, ahead, behind)], axis=1
    )
    table = lax.dot_general(
        sums,
        hot_ref[...],
        (((1,), (1,)), ((), ())),
        precision=TOP_PRECISION,
        preferred_element_type=F32,
    )
    for copy in copies[1:]:
        copy.wait()
    grad_act = (
        cols_by_cols(grad_q, wq_half[...])
        + cols_by_cols(grad_k, wk_half[...])
        + cols_by_cols(grad_v, wv_half[...])
    )
    x = own_ref[...].astype(F32)
    y = other_ref[...].astype(F32)
    gain_first = jnp.sum(
        grad_act[:rows] * (x * root_mean(x)) + grad_act[rows:] * (y * root_mean(y)),
        axis=0,
        keepdims=True,
    )
    input_own_ref[...] = grad_act[:rows]
    input_other_ref[...] = grad_act[rows:].astype(BF16)
    at = small_rows(experts)
    natural[...] = jnp.zeros_like(natural)
    for i, value in enumerate((gain_first, gain_second)):
        natural[at[i] : at[i] + 1] = value[:, :part]
        natural[at[i] + 1 : at[i] + 2] = value[:, part:]
    natural[at[2] : at[2] + heads // 2, : table.shape[1]] = table
    natural[at[3] : at[4]] = router_ref[:, :part]
    natural[at[4] : at[5]] = router_ref[:, part:]
    step = part_2.shape[0] >> levels
    extra = step - 4 * height
    for chunk in range(2**levels):
        place = chunk_place(chunk, orders[2], levels)
        at = pl.multiple_of(place * step + 4 * height, 16)
        part_2[pl.ds(at, extra), :] = natural[chunk * extra : (chunk + 1) * extra].astype(BF16)
    for write in writes[4:]:
        write.start()
    for write in writes:
        write.wait()


def assemble_kernel(orders, levels, chosen, upper, last, wait, flush, *refs):
    arrays, refs = refs[: 2 * len(chosen)], refs[2 * len(chosen) :]
    if last is not None:
        experts, heads = last
        near_refs, refs = refs[:2], refs[2:]
    if upper:
        refs = refs[4:]
    outs, (wide, sems) = refs[:4], refs[-2:]
    if last is not None:
        gain_first_ref, gain_second_ref, table_ref, router_ref = refs[4:8]
    width = outs[0].shape[1]
    part = width // 2
    third = width // 3
    side = third // 2
    height = third >> levels
    half = 2 ** (levels - 1)
    core = lax.axis_index("ffn")
    mine = lax.axis_index("expert")
    own = pl.ds(pl.multiple_of(core * part, LANES), part)
    theirs = pl.ds(pl.multiple_of((1 - core) * part, LANES), part)
    writes = []
    for n, p in enumerate(chosen):
        order = orders[p]
        for i in (2 * n, 2 * n + 1):
            wait(i)
        for low in range(half):
            place = chunk_place(low, order, levels)
            place = jnp.bitwise_and(place, half - 1)
            step = arrays[2 * n].shape[0] // half
            for matrix in range(4):
                at = pl.ds(pl.multiple_of(place * step + matrix * height, 16), height)
                to = pl.ds(low * height, height)
                wide[n, matrix, to, own] = arrays[2 * n][at, :].astype(F32)
                wide[n, matrix, to, theirs] = arrays[2 * n + 1][at, :].astype(F32)
        bit = jnp.bitwise_and(jnp.right_shift(mine, order[0]), 1)
        if upper:
            bit = 1 - bit
        first = pl.multiple_of(p * third + bit * side, side)
        for matrix in range(4):
            write = pltpu.make_async_copy(
                wide.at[n, matrix], outs[matrix].at[pl.ds(first, side), :], sems.at[4 * n + matrix]
            )
            write.start()
            writes.append(write)
    if last is not None:
        at = small_rows(experts)
        extra = small_height(experts, levels)
        step = arrays[-1].shape[0] // half
        found = []
        for chunk in range(-(-at[5] // extra)):
            place = chunk_place(chunk, orders[2], levels)
            away = place >= half
            first = jnp.bitwise_and(place, half - 1) * step + 4 * height
            rows = pl.ds(pl.multiple_of(first, 16), extra)
            found.append(
                [
                    jnp.where(away, arrays[i - 2][rows, :].astype(F32), near_refs[i][rows, :].astype(F32))
                    for i in range(2)
                ]
            )
        mine = jnp.concatenate([a for a, _ in found], axis=0)
        other = jnp.concatenate([b for _, b in found], axis=0)
        both = mine + other
        gain_first_ref[...] = jnp.concatenate([both[0:1], both[1:2]], axis=1).reshape(width)
        gain_second_ref[...] = jnp.concatenate([both[2:3], both[3:4]], axis=1).reshape(width)
        buckets = table_ref.shape[1]
        low = mine[at[2] : at[2] + heads // 2, :buckets]
        high = other[at[2] : at[2] + heads // 2, :buckets]
        table_ref[...] = jnp.where(
            core == 0,
            jnp.concatenate([low, high], axis=0),
            jnp.concatenate([high, low], axis=0),
        )
        router_ref[...] = jnp.concatenate([both[at[3] : at[4]], both[at[4] : at[5]]], axis=1)
    for write in writes:
        write.wait()


def assemble(orders, levels, chosen, arrays, width, earlier=(), near=(), last=None):
    tail = []
    modes = "l" * len(arrays)
    if last is not None:
        experts, heads, buckets = last
        tail = [((width,), F32), ((width,), F32), ((heads, buckets), F32), ((experts, width), F32)]
        modes += "hh"
        last = (experts, heads)
    first = len(modes)
    modes += "r" * len(earlier)
    return call(
        functools.partial(assemble_kernel, orders, levels, chosen, bool(earlier), last),
        [((width, width), F32)] * 4 + tail,
        (*arrays, *near, *earlier),
        modes + "rrrr" + "h" * len(tail),
        vmem=64,
        aliases={first + i: i for i in range(len(earlier))},
        scratch=[
            pltpu.VMEM((len(chosen), 4, width // 6, width), F32),
            pltpu.SemaphoreType.DMA((4 * len(chosen),)),
        ],
        nbytes=8000000,
    )


def swap(x):
    return lax.ppermute(x, "ffn", [(0, 1), (1, 0)])


def flip(x, bit):
    peers = lax.axis_size("expert")
    return lax.ppermute(x, "expert", [(i, i ^ (1 << bit)) for i in range(peers)])


def add_low(left, right):
    return (left.astype(F32) + right.astype(F32)).astype(BF16)


def scatter_sum(keep, send, order, levels):
    for k, bit in enumerate(order):
        got = flip(send, bit)
        half = keep.shape[0] // 2
        if k + 2 == len(order):
            both = add_low(keep, got)
            send = both
            if k + 1 < levels:
                send = jnp.concatenate([both[half:], both[:half]])
            return add_low(both, flip(send, order[-1]))
        if k + 1 < levels:
            keep, send = add_low(keep[:half], got[:half]), add_low(keep[half:], got[half:])
        else:
            both = add_low(keep, got)
            upper = (lax.axis_index("expert") >> order[k + 1]) & 1
            keep = lax.dynamic_slice_in_dim(both, upper * half, half, 0)
            send = lax.dynamic_slice_in_dim(both, (1 - upper) * half, half, 0)


def gather_back(x, order, levels):
    for k, bit in reversed(list(enumerate(order[:-1]))):
        got = flip(x, bit)
        if k == 0:
            return x, got
        if k < levels:
            x = jnp.concatenate([x, got])
        else:
            upper = (lax.axis_index("expert") >> bit) & 1
            x = jnp.where(upper == 1, jnp.concatenate([got, x]), jnp.concatenate([x, got]))


def shards(
    tokens,
    norm_first,
    w_query,
    w_key,
    w_value,
    w_out,
    bucket_bias_table,
    norm_second,
    w_router,
    w_in,
    w_down,
    expert_ids,
    cotangent,
):
    rows, width = tokens.shape
    buckets, heads = bucket_bias_table.shape
    pair = lax.axis_size("ffn")
    experts = w_router.shape[1]
    total = 2 * rows
    capacity = 5 * rows * pair // 4
    hidden = w_in.shape[2]
    part = width // 2
    hot = jnp.asarray(bucket_windows(rows, buckets, REACH))
    router = w_router.T

    other = swap(tokens)
    ids = expert_ids.reshape(1, rows)
    ids_other = swap(ids)
    other, ids_other, w_in, w_down, cotangent = lax.optimization_barrier(
        (other, ids_other, w_in, w_down, cotangent)
    )
    in_own, down_own = w_in[0], w_down[0]
    in_other, down_other = swap(in_own), swap(down_own)
    cot_other = swap(cotangent)
    middle, gate, outgoing, mixed, windows, fetch, fetch_other = call(
        functools.partial(forward_kernel, heads),
        [
            ((rows, width), F32),
            ((rows, LANES), F32),
            ((total, 2 * width + LANES), BF16),
            ((rows, width), BF16),
            ((heads, 6 * rows), F32),
            ((rows, total), BF16),
            ((rows, total), BF16),
        ],
        (
            tokens,
            other,
            norm_first,
            ids,
            ids_other,
            bucket_bias_table.T,
            hot,
            w_key,
            w_value,
            w_query,
            w_out,
            norm_second,
            router,
            cotangent,
        ),
        "hhhhhhhlllllll" + "hhhhhhh",
        vmem=64,
        flops=3000000000,
    )
    arrived = lax.all_to_all(outgoing, "expert", 0, 0, tiled=True)
    mixed_other, middle_other = swap(mixed), swap(middle)
    act, queries, keys, values, probs = call(
        functools.partial(halves_kernel, heads),
        [
            ((2 * rows, width), BF16),
            ((2 * rows, part), BF16),
            ((2 * rows, part), BF16),
            ((2 * rows, part), BF16),
            ((heads // 2, 2 * rows, 2 * rows), F32),
        ],
        (tokens, other, norm_first, w_query, w_key, w_value, windows, gate),
        "hhhrrrhr" + "hhhhh",
        vmem=64,
        flops=3000000000,
        scratch=[pltpu.VMEM((width, part), BF16)] * 3 + [pltpu.SemaphoreType.DMA((3,))],
    )
    chunk = 512
    steps = 2 * hidden // chunk
    hid_own, pre_own, sent, bundle, grad_slots, produced, router_part = call(
        functools.partial(expert_kernel, capacity, chunk),
        [
            ((total, hidden), BF16),
            ((total, hidden), BF16),
            ((total, width), BF16),
            ((total, 2 * width + 2 * hidden), BF16),
            ((total, width), BF16),
            ((total, width), BF16),
            ((experts, width), F32),
        ],
        (arrived, router, in_own, in_other, down_own, down_other, act),
        "hhrrrrr" + "hhhhhhh",
        vmem=64,
        flops=6000000000,
        scratch=[
            pltpu.VMEM((steps, width, chunk), BF16),
            pltpu.VMEM((steps, chunk, width), BF16),
            pltpu.SemaphoreType.DMA((2, steps)),
        ],
    )
    bundle_other = swap(bundle)
    grad_returned = lax.all_to_all(grad_slots, "expert", 0, 0, tiled=True)
    grad_w_in, grad_w_down = expert_weights(arrived, sent, hid_own, pre_own, bundle_other, 256)
    produced, grad_returned, grad_w_in = lax.optimization_barrier(
        (produced, grad_returned, grad_w_in)
    )
    produced_returned = lax.all_to_all(produced, "expert", 0, 0, tiled=True)
    bits = experts.bit_length() - 1
    levels = min(bits, 4)
    rest = list(range(3, bits))
    orders = [[0, 1, 2] + rest, [1, 2, 0] + rest, [2, 0, 1] + rest]
    third = 4 * width // 3
    extra = small_height(experts, levels) << levels
    heights = [third, third, third + extra]
    *halves, input_own, input_other, grad_middle = call(
        functools.partial(backward_kernel, heads, orders, levels),
        [((height // 2, part), BF16) for height in heights for _ in range(2)]
        + [((rows, width), F32), ((rows, width), BF16), ((rows, width), F32)],
        (
            grad_returned,
            swap(grad_returned),
            fetch,
            fetch_other,
            middle,
            middle_other,
            cotangent,
            cot_other,
            norm_second,
            tokens,
            other,
            act,
            queries,
            keys,
            values,
            probs,
            mixed,
            mixed_other,
            hot,
            router_part,
            grad_w_in,
            w_query,
            w_key,
            w_value,
            w_out,
        ),
        "hhhhhhhhh" + "hhhhhhhhhhh" + "rrrrr" + "rrrrrrhhh",
        vmem=64,
        flops=4000000000,
        scratch=[pltpu.VMEM((width, part), BF16)] * 3
        + [
            pltpu.VMEM((part, width), BF16),
            *[pltpu.VMEM((height, part), BF16) for height in heights],
            pltpu.VMEM((extra, part), F32),
            pltpu.SemaphoreType.DMA((10,)),
        ],
    )
    halves, input_own, input_other, grad_middle, produced_returned = lax.optimization_barrier(
        (halves, input_own, input_other, grad_middle, produced_returned)
    )
    scattered = [
        scatter_sum(halves[2 * p], halves[2 * p + 1], order, levels)
        for p, order in enumerate(orders)
    ]
    inputs = tokens.astype(F32)
    root = root_mean(inputs)
    up = norm_first * (input_own + swap(input_other).astype(F32))
    grad_input = grad_middle + root * up - inputs * root**3 * jnp.mean(
        up * inputs, axis=-1, keepdims=True
    )
    expert_branch = gate[:, :1] * dot(fetch, produced_returned)
    output = (middle + expert_branch).astype(BF16)
    gathered = [gather_back(piece, order, levels) for piece, order in zip(scattered, orders)]
    near = []
    for kept, _ in gathered:
        near += [kept, swap(kept)]
    matrices = assemble(orders, levels, (0, 1, 2), near, width)
    got = [pair[1] for pair in gathered]
    got, matrices, output, expert_branch, grad_input = lax.optimization_barrier(
        (got, matrices, output, expert_branch, grad_input)
    )
    far = []
    for rows_got in got:
        far += [rows_got, swap(rows_got)]
    results = assemble(
        orders,
        levels,
        (0, 1, 2),
        far,
        width,
        matrices,
        near[4:],
        (experts, heads, buckets),
    )
    return (
        output,
        grad_input,
        results[4],
        results[0],
        results[1],
        results[2],
        results[3],
        results[6].T,
        results[5],
        results[7].T,
        grad_w_in,
        grad_w_down,
        expert_branch,
    )


def solution(mesh):
    placed = (
        P(("expert", "ffn"), None),
        P(),
        P(),
        P(),
        P(),
        P(),
        P(),
        P(),
        P(),
        P("expert", None, "ffn"),
        P("expert", "ffn", None),
        P(("expert", "ffn")),
        P(("expert", "ffn"), None),
    )
    return jax.shard_map(
        shards,
        mesh=mesh,
        in_specs=placed,
        out_specs=(
            P(("expert", "ffn"), None),
            P(("expert", "ffn"), None),
            P(),
            P(),
            P(),
            P(),
            P(),
            P(),
            P(),
            P(),
            P("expert", None, "ffn"),
            P("expert", "ffn", None),
            P(("expert", "ffn"), None),
        ),
        check_vma=False,
    )
```

time: 237 us -> 165 us (0.70)
  local copies, waits for them, and re-layouts: 48.7 us -> 2.29 us
  waiting for transfers between devices: 68.8 us -> 49.4 us
  other arithmetic: 24.6 us -> 5.33 us
  Pallas kernels: 35.9 us -> 52.8 us
  starting transfers between devices: 53.2 us -> 50.7 us
    unnamed x106 -> x18, local copies, waits for them, and re-layouts: 34.7 us -> 0.79 us
    pallas_call x7, Pallas kernels: 35.9 us -> 52.8 us  [the longest x6 43.9 us: call(): pl.pallas_call(kernel, out_shape=[jax.ShapeDtypeStruct(s, d) for s, d in...]
    all_to_all x1, waiting for transfers between devices: 11.3 us -> 0.01 us  [shards(): produced_returned = lax.all_to_all(produced, 'expert', 0, 0, tiled=True)]
    select_n x13 -> x0, other arithmetic: 9.92 us -> none  [the longest x1 8.3 us: shards(): first = jnp.where(core == 0, mine, theirs)]
    convert_element_type x16 -> x12, other arithmetic: 9.39 us -> 0.63 us  [add_low(): return (left.astype(F32) + right.astype(F32)).astype(BF16)]
    all_to_all x1, waiting for transfers between devices: 12 us -> 4.08 us  [shards(): grad_returned = lax.all_to_all(grad_slots, 'expert', 0, 0, tiled=True)]
    ppermute x24 -> x21, waiting for transfers between devices: 31.5 us -> 25.3 us  [flip(): return lax.ppermute(x, 'expert', [(i, i ^ 1 << bit) for i in range(peers)])]
    slice x9 -> x3, local copies, waits for them, and re-layouts: 6.21 us -> 0.04 us  [scatter_sum(): send = jnp.concatenate([both[half:], both[:half]])]
  transfers between devices with their start and end apart: 39 -> 40, of which waited for: 20 -> 20; matrix products, arithmetic and copies ran while one was open for 7% -> 5% of each run, Pallas kernels for 8% -> 23%
where the time goes in v2:
time: 165 us; the launch traced here: 164 us
  Pallas kernels  52.8 us (32%)
  starting transfers between devices  50.7 us (31%)
  waiting for transfers between devices  49.4 us (30%)
  other arithmetic  5.33 us (3%)
  local copies, waits for them, and re-layouts  2.29 us (1%)
  matrix products  2.17 us (1%)
    pallas_call x6, Pallas kernels, call(): pl.pallas_call(kernel, out_shape=[jax.ShapeDtypeStruct(s, d) for s, d in...  43.9 us
    ppermute x21, starting transfers between devices, flip(): return lax.ppermute(x, 'expert', [(i, i ^ 1 << bit) for i in range(peers)])  29.2 us
    ppermute x21, waiting for transfers between devices, flip(): return lax.ppermute(x, 'expert', [(i, i ^ 1 << bit) for i in range(peers)])  25.3 us
    all_to_all x1, waiting for transfers between devices, shards(): arrived = lax.all_to_all(outgoing, 'expert', 0, 0, tiled=True)  15.6 us
    pallas_call x1, Pallas kernels, expert_weights(): pl.pallas_call(expert_weights_kernel, grid=(steps,), out_shape=[jax.Shape...  8.89 us
    all_to_all x1, starting transfers between devices, shards(): arrived = lax.all_to_all(outgoing, 'expert', 0, 0, tiled=True)  8.29 us
    all_to_all x1, starting transfers between devices, shards(): grad_returned = lax.all_to_all(grad_slots, 'expert', 0, 0, tiled=True)  5.27 us
    all_to_all x1, starting transfers between devices, shards(): produced_returned = lax.all_to_all(produced, 'expert', 0, 0, tiled=True)  4.43 us
  transfers between devices with their start and end apart: 40, of which 20 were waited for; matrix products, arithmetic and copies ran while one was open for 5% of the time, Pallas kernels for 23%

profile of v2, /device:TPU:0, one launch (start us, length us, event | category | flops | bytes accessed | tf_op | source)
XLA Modules:
  0.0 163.8 jit_solution(15153945369562044864)
XLA Ops:
  3.1 7.9 %shard_map.237 = (f32[128,768]{1,0:T(8,128)}, f32[128,128]{1,0:T(8,128)}, bf16[256,1664]{1,0:T(8,128)(2,1)}, bf16[128,768]{1,0:T(8,128)(2,1)}, f32[12,768]{1,0:T...) custom-call(bf16[128,768]{1,0:T(8,128)(2,1)} %refs_9_.3, ...), custom_call_target="tpu_custom_call" | custom-call | flops 3000000000 | bytes 1000000 | tf_op jit(solution)/shard_map/pallas_call | solution.py:100
  11.0 8.3 %all-to-all-start = ((bf16[16,16,1664]{2,1,0:T(8,128)(2,1)}), bf16[16,16,1664]{2,1,0:T(8,128)(2,1)}, u32[]{:S(2)}, u32[]{:S(2)}) async-start(bf16[16,16,1664]{2,1,0:T(8,128)(2,1)} %bitcast.15), calls=%async_computation | async-start | bytes 1703936 | tf_op jit(solution)/shard_map/all_to_all | solution.py:914
  19.3 5.6 %shard_map.238 = (bf16[256,768]{1,0:T(8,128)(2,1)}, bf16[256,384]{1,0:T(8,128)(2,1)}, bf16[256,384]{1,0:T(8,128)(2,1)}, bf16[256,384]{1,0:T(8,128)(2,1)}, f32[6,256,256]{2,1,0:T(8,128)}) custom-call(bf16[128,768]{1,0:T(8,128)(2,1)} %refs_9_.3, bf16[128,768]{1,0:T(8,128)(2,1)} %collective-permute-done.refs_1_.refs_10_, f32[768]{0:T(1024)} %refs_2_.3, ...), custom_call_target="tpu_custom_call" | custom-call | flops 3000000000 | bytes 1000000 | tf_op jit(solution)/shard_map/pallas_call | solution.py:100
  24.9 15.6 %all-to-all-done = bf16[16,16,1664]{2,1,0:T(8,128)(2,1)} async-done(((bf16[16,16,1664]{2,1,0:T(8,128)(2,1)}), bf16[16,16,1664]{2,1,0:T(8,128)(2,1)}, u32[]{:S(2)}, u32[]{:S(2)}) %all-to-all-start) | async-done | bytes 852000 | tf_op jit(solution)/shard_map/all_to_all | solution.py:914
  40.5 10.6 %shard_map.239 = (bf16[256,1536]{1,0:T(8,128)(2,1)}, bf16[256,1536]{1,0:T(8,128)(2,1)}, bf16[256,768]{1,0:T(8,128)(2,1)}, bf16[256,4608]{1,0:T(8,128)(2,1)}, bf1...) custom-call(bf16[256,1664]{1,0:T(8,128)(2,1)} %bitcast.4.refs_0_.flat_own, ...), custom_call_target="tpu_custom_call" | custom-call | flops 6000000000 | bytes 1000000 | tf_op jit(solution)/shard_map/pallas_call | solution.py:100
  51.2 5.3 %all-to-all-start.1 = ((bf16[16,16,768]{2,1,0:T(8,128)(2,1)}), bf16[16,16,768]{2,1,0:T(8,128)(2,1)}, u32[]{:S(2)}, u32[]{:S(2)}) async-start(bf16[16,16,768]{2,1,0:T(8,128)(2,1)} %bitcast.17), calls=%async_computation.1 | async-start | bytes 786432 | tf_op jit(solution)/shard_map/all_to_all | solution.py:955
  56.8 8.9 %shard_map.240 = (f32[1,768,1536]{2,1,0:T(8,128)}, f32[1,1536,768]{2,1,0:T(8,128)}) custom-call(bf16[256,1664]{1,0:T(8,128)(2,1)} %bitcast.4.refs_0_.flat_own, bf16[256,768]{1,0:T(8,128)(2,1)} %get-tuple-element.94.sent_own, bf16[256,1536]{1,0:T(8,128)(2,1)} %get-tuple-element.95.hid_own, bf16[256,1536]{1,0:T(8,128)(2,1)} %get-tuple-element.96.pre_own, ...), custom_call_target="tpu_custom_call" | custom-call | flops 2415919104 | bytes 14000000 | tf_op jit(solution)/shard_map/pallas_call | solution.py:448
  65.7 4.1 %all-to-all-done.1 = bf16[16,16,768]{2,1,0:T(8,128)(2,1)} async-done(((bf16[16,16,768]{2,1,0:T(8,128)(2,1)}), bf16[16,16,768]{2,1,0:T(8,128)(2,1)}, u32[]{:S(2)}, u32[]{:S(2)}) %all-to-all-start.1) | async-done | bytes 393248 | tf_op jit(solution)/shard_map/all_to_all | solution.py:955
  69.7 4.4 %all-to-all-start.2 = ((bf16[16,16,768]{2,1,0:T(8,128)(2,1)}), bf16[16,16,768]{2,1,0:T(8,128)(2,1)}, u32[]{:S(2)}, u32[]{:S(2)}) async-start(bf16[16,16,768]{2,1,0:T(8,128)(2,1)} %bitcast.16), calls=%async_computation.2 | async-start | bytes 786432 | tf_op jit(solution)/shard_map/all_to_all | solution.py:960
  76.5 11.1 %shard_map.241 = (bf16[512,384]{1,0:T(8,128)(2,1)}, bf16[512,384]{1,0:T(8,128)(2,1)}, bf16[512,384]{1,0:T(8,128)(2,1)}, bf16[512,384]{1,0:T(8,128)(2,1)}, bf16[6...) custom-call(bf16[256,768]{1,0:T(8,128)(2,1)} %bitcast.8.refs_0_, ...), custom_call_target="tpu_custom_call" | custom-call | flops 4000000000 | bytes 1000000 | tf_op jit(solution)/shard_map/pallas_call | solution.py:100
  90.7 1.5 collective-permute-start.23
  92.2 2.2 %add_convert_fusion.2 = (bf16[128,768]{1,0:T(8,128)(2,1)}, f32[128,768]{1,0:T(8,128)}) fusion(f32[128,768]{1,0:T(8,128)} %get-tuple-element.102.refs_4_, bf16[128,256]{1,0:T(8,128)(2,1)} %get-tuple-element.100.refs_2_, bf16[256,768]{1,0:T(8,128)(2,1)} %bitcast.10, f32[128]{0:T(128)} %slice_reduce_fusion), kind=kOutput, calls=%fused_computation.14 | convolution fusion | flops 50626560 | bytes 1442304 | tf_op jit(solution)/shard_map/dot_general | solution.py:52
  95.6 3.8 %collective-permute-done.9 = bf16[512,384]{1,0:T(8,128)(2,1)S(1)} collective-permute-done((bf16[512,384]{1,0:T(8,128)(2,1)}, bf16[512,384]{1,0:T(8,128)(2,1)S(1)}, u32[]{:S(2)}, u32[]{:S(2)}) %collective-permute-start.9) | collective-permute-done | bytes 393248 | tf_op jit(solution)/shard_map/ppermute | solution.py:810
  101.1 1.6 collective-permute-start.17
  102.6 2.0 %collective-permute-done.23 = bf16[640,384]{1,0:T(8,128)(2,1)S(1)} collective-permute-done((bf16[640,384]{1,0:T(8,128)(2,1)}, bf16[640,384]{1,0:T(8,128)(2,1)S(1)}, u32[]{:S(2)}, u32[]{:S(2)}) %collective-permute-start.23) | collective-permute-done | bytes 491552 | tf_op jit(solution)/shard_map/ppermute | solution.py:810
  107.3 1.5 collective-permute-done.17
  109.0 1.6 collective-permute-done.11
  110.7 2.4 %collective-permute-start.12 = (bf16[128,384]{1,0:T(8,128)(2,1)S(1)}, bf16[128,384]{1,0:T(8,128)(2,1)S(1)}, u32[]{:S(2)}, u32[]{:S(2)}) collective-permute-start(bf16[128,384]{1,0:T(8,128)(2,1)S(1)} %pad_maximum_fusion.7), channel_id=1, source_target_pairs={{0,16},{2,18},{4,20},{6,22},{8,24},{10,26},{12,28},{14,30},{16,0},... | collective-permute-start | bytes 294920 | tf_op jit(solution)/shard_map/ppermute | solution.py:810
  113.7 2.6 %collective-permute-start.19 = (bf16[128,384]{1,0:T(8,128)(2,1)S(1)}, bf16[128,384]{1,0:T(8,128)(2,1)S(1)}, u32[]{:S(2)}, u32[]{:S(2)}) collective-permute-start(bf16[128,384]{1,0:T(8,128)(2,1)S(1)} %pad_maximum_fusion.8), channel_id=1, source_target_pairs={{0,16},{2,18},{4,20},{6,22},{8,24},{10,26},{12,28},{14,30},{16,0},... | collective-permute-start | bytes 294920 | tf_op jit(solution)/shard_map/ppermute | solution.py:810
  116.4 2.6 %collective-permute-done.12 = bf16[128,384]{1,0:T(8,128)(2,1)S(1)} collective-permute-done((bf16[128,384]{1,0:T(8,128)(2,1)S(1)}, bf16[128,384]{1,0:T(8,128)(2,1)S(1)}, u32[]{:S(2)}, u32[]{:S(2)}) %collective-permute-start.12) | collective-permute-done | bytes 98336 | tf_op jit(solution)/shard_map/ppermute | solution.py:810
  119.0 1.8 %collective-permute-start.13 = (bf16[128,384]{1,0:T(8,128)(2,1)S(1)}, bf16[128,384]{1,0:T(8,128)(2,1)S(1)}, u32[]{:S(2)}, u32[]{:S(2)}) collective-permute-start(bf16[128,384]{1,0:T(8,128)(2,1)S(1)} %add_convert_fusion.15), channel_id=1, source_target_pairs={{0,8},{2,10},{4,12},{6,14},{8,0},{10,2},{12,4},{14,6},{16,24},{18,... | collective-permute-start | bytes 294920 | tf_op jit(solution)/shard_map/ppermute | solution.py:810
  121.4 3.1 %collective-permute-start.26 = (bf16[160,384]{1,0:T(8,128)(2,1)S(1)}, bf16[160,384]{1,0:T(8,128)(2,1)S(1)}, u32[]{:S(2)}, u32[]{:S(2)}) collective-permute-start(bf16[160,384]{1,0:T(8,128)(2,1)S(1)} %pad_maximum_fusion.6), channel_id=1, source_target_pairs={{0,16},{2,18},{4,20},{6,22},{8,24},{10,26},{12,28},{14,30},{16,0},... | collective-permute-start | bytes 368648 | tf_op jit(solution)/shard_map/ppermute | solution.py:810
  124.5 2.4 %collective-permute-start.20 = (bf16[128,384]{1,0:T(8,128)(2,1)S(1)}, bf16[128,384]{1,0:T(8,128)(2,1)S(1)}, u32[]{:S(2)}, u32[]{:S(2)}) collective-permute-start(bf16[128,384]{1,0:T(8,128)(2,1)S(1)} %add_convert_fusion.11), channel_id=1, source_target_pairs={{0,2},{2,0},{4,6},{6,4},{8,10},{10,8},{12,14},{14,12},{16,18},{18,... | collective-permute-start | bytes 294920 | tf_op jit(solution)/shard_map/ppermute | solution.py:810
  126.9 1.7 %collective-permute-done.26 = bf16[160,384]{1,0:T(8,128)(2,1)S(1)} collective-permute-done((bf16[160,384]{1,0:T(8,128)(2,1)S(1)}, bf16[160,384]{1,0:T(8,128)(2,1)S(1)}, u32[]{:S(2)}, u32[]{:S(2)}) %collective-permute-start.26) | collective-permute-done | bytes 122912 | tf_op jit(solution)/shard_map/ppermute | solution.py:810
  128.7 2.4 %collective-permute-start.27 = (bf16[160,384]{1,0:T(8,128)(2,1)S(1)}, bf16[160,384]{1,0:T(8,128)(2,1)S(1)}, u32[]{:S(2)}, u32[]{:S(2)}) collective-permute-start(bf16[160,384]{1,0:T(8,128)(2,1)S(1)} %add_convert_fusion.7), channel_id=1, source_target_pairs={{0,4},{2,6},{4,0},{6,2},{8,12},{10,14},{12,8},{14,10},{16,20},{18,... | collective-permute-start | bytes 368648 | tf_op jit(solution)/shard_map/ppermute | solution.py:810
  131.3 2.6 %collective-permute-done.27 = bf16[160,384]{1,0:T(8,128)(2,1)S(1)} collective-permute-done((bf16[160,384]{1,0:T(8,128)(2,1)S(1)}, bf16[160,384]{1,0:T(8,128)(2,1)S(1)}, u32[]{:S(2)}, u32[]{:S(2)}) %collective-permute-start.27) | collective-permute-done | bytes 122912 | tf_op jit(solution)/shard_map/ppermute | solution.py:810
  134.0 2.2 %collective-permute-start.28 = (bf16[320,384]{1,0:T(8,128)(2,1)S(1)}, bf16[320,384]{1,0:T(8,128)(2,1)S(1)}, u32[]{:S(2)}, u32[]{:S(2)}) collective-permute-start(bf16[320,384]{1,0:T(8,128)(2,1)S(1)} %pad_maximum_fusion.3), channel_id=1, source_target_pairs={{0,2},{2,0},{4,6},{6,4},{8,10},{10,8},{12,14},{14,12},{16,18},{18,... | collective-permute-start | bytes 737288 | tf_op jit(solution)/shard_map/ppermute | solution.py:810
  142.6 1.9 %collective-permute-start.22 = (bf16[512,384]{1,0:T(8,128)(2,1)}, bf16[512,384]{1,0:T(8,128)(2,1)}, u32[]{:S(2)}, u32[]{:S(2)}) collective-permute-start(bf16[512,384]{1,0:T(8,128)(2,1)} %pad_maximum_fusion.2.refs_2_), channel_id=1, source_target_pairs={{0,4},{2,6},{4,0},{6,2},{8,12},{10,14},{12,8},{14,10},{16,20},{18,... | collective-permute-start | bytes 1179656 | tf_op jit(solution)/shard_map/ppermute | solution.py:810
  146.1 3.6 %shard_map.242 = (f32[768,768]{1,0:T(8,128)}, f32[768,768]{1,0:T(8,128)}, f32[768,768]{1,0:T(8,128)}, f32[768,768]{1,0:T(8,128)}) custom-call(bf16[512,384]{1,0:T(8,128)(2,1)} %pad_maximum_fusion.1.refs_0_, bf16[512,384]{1,0:T(8,128)(2,1)} %copy-done.3, bf16[512,384]{1,0:T(8,128)(2,1)} %pad_maximum_fusion.2.refs_2_, bf16[512,384]{1,0:T(8,128)(2,1)} %copy-done.4, ...), custom_call_target="tpu_custom_call" | custom-call | bytes 8000000 | tf_op jit(solution)/shard_map/pallas_call | solution.py:100
  149.7 4.4 %collective-permute-done.22.refs_2_ = bf16[512,384]{1,0:T(8,128)(2,1)} collective-permute-done((bf16[512,384]{1,0:T(8,128)(2,1)}, bf16[512,384]{1,0:T(8,128)(2,1)}, u32[]{:S(2)}, u32[]{:S(2)}) %collective-permute-start.22) | collective-permute-done | bytes 393248 | tf_op jit(solution)/shard_map/ppermute | solution.py:810
  155.7 2.3 %collective-permute-done.34.refs_1_ = bf16[512,384]{1,0:T(8,128)(2,1)} collective-permute-done((bf16[512,384]{1,0:T(8,128)(2,1)}, bf16[512,384]{1,0:T(8,128)(2,1)}, u32[]{:S(2)}, u32[]{:S(2)}) %collective-permute-start.34) | collective-permute-done | bytes 393248 | tf_op jit(solution)/shard_map/ppermute | solution.py:805
  158.5 5.1 %shard_map.243 = (f32[768,768]{1,0:T(8,128)}, f32[768,768]{1,0:T(8,128)}, f32[768,768]{1,0:T(8,128)}, f32[768,768]{1,0:T(8,128)}, f32[768]{0:T(1024)}, /*index=5...) custom-call(bf16[512,384]{1,0:T(8,128)(2,1)} %collective-permute-don, ...), custom_call_target="tpu_custom_call", output_to_operand_aliasing={{0}: (8, {}), {1}: (9, {}), {2}: (10, {}), {3}: (11, {})} | custom-call | bytes 8000000 | tf_op jit(solution)/shard_map/pallas_call | solution.py:100
  (103 shorter events, 25.6 us)
Async XLA Ops:
  2.6 38.0 %collective-permute-start.2 = (bf16[768,1536]{1,0:T(8,128)(2,1)}, bf16[768,1536]{1,0:T(8,128)(2,1)}, u32[]{:S(2)}, u32[]{:S(2)}) collective-permute-start(bf16[768,1536]{1,0:T(8,128)(2,1)} %bitcast.18), channel_id=1, source_target_pairs={{0,1},{1,0},{2,3},{3,2},{4,5},{5,4},{6,7},{7,6},{8,9},{9,8},{10,11... | collective-permute-start | bytes 7077896 | tf_op jit(solution)/shard_map/ppermute | solution.py:805
  3.0 37.6 %collective-permute-start.3 = (bf16[1536,768]{1,0:T(8,128)(2,1)}, bf16[1536,768]{1,0:T(8,128)(2,1)}, u32[]{:S(2)}, u32[]{:S(2)}) collective-permute-start(bf16[1536,768]{1,0:T(8,128)(2,1)} %bitcast.20), channel_id=1, source_target_pairs={{0,1},{1,0},{2,3},{3,2},{4,5},{5,4},{6,7},{7,6},{8,9},{9,8},{10,11... | collective-permute-start | bytes 7077896 | tf_op jit(solution)/shard_map/ppermute | solution.py:805
  11.0 29.5 %all-to-all-start = ((bf16[16,16,1664]{2,1,0:T(8,128)(2,1)}), bf16[16,16,1664]{2,1,0:T(8,128)(2,1)}, u32[]{:S(2)}, u32[]{:S(2)}) async-start(bf16[16,16,1664]{2,1,0:T(8,128)(2,1)} %bitcast.15), calls=%async_computation | async-start | bytes 1703936 | tf_op jit(solution)/shard_map/all_to_all | solution.py:914
  51.1 5.6 %collective-permute-start.4 = (bf16[256,4608]{1,0:T(8,128)(2,1)}, bf16[256,4608]{1,0:T(8,128)(2,1)}, u32[]{:S(2)}, u32[]{:S(2)}) collective-permute-start(bf16[256,4608]{1,0:T(8,128)(2,1)} %get-tuple-element.97), channel_id=1, source_target_pairs={{0,1},{1,0},{2,3},{3,2},{4,5},{5,4},{6,7},{7,6},{8,9},{9,8},{10,11... | collective-permute-start | bytes 7077896 | tf_op jit(solution)/shard_map/ppermute | solution.py:805
  51.2 18.5 %all-to-all-start.1 = ((bf16[16,16,768]{2,1,0:T(8,128)(2,1)}), bf16[16,16,768]{2,1,0:T(8,128)(2,1)}, u32[]{:S(2)}, u32[]{:S(2)}) async-start(bf16[16,16,768]{2,1,0:T(8,128)(2,1)} %bitcast.17), calls=%async_computation.1 | async-start | bytes 786432 | tf_op jit(solution)/shard_map/all_to_all | solution.py:955
  56.5 20.0 %collective-permute-start.6 = (f32[128,768]{1,0:T(8,128)}, f32[128,768]{1,0:T(8,128)}, u32[]{:S(2)}, u32[]{:S(2)}) collective-permute-start(f32[128,768]{1,0:T(8,128)} %get-tuple-element.102.refs_4_), channel_id=1, source_target_pairs={{0,1},{1,0},{2,3},{3,2},{4,5},{5,4},{6,7},{7,6},{8,9},{9,8},{10,11... | collective-permute-start | bytes 1179656 | tf_op jit(solution)/shard_map/ppermute | solution.py:805
  69.7 6.8 %collective-permute-start.5 = (bf16[256,768]{1,0:T(8,128)(2,1)}, bf16[256,768]{1,0:T(8,128)(2,1)}, u32[]{:S(2)}, u32[]{:S(2)}) collective-permute-start(bf16[256,768]{1,0:T(8,128)(2,1)} %bitcast.8.refs_0_), channel_id=1, source_target_pairs={{0,1},{1,0},{2,3},{3,2},{4,5},{5,4},{6,7},{7,6},{8,9},{9,8},{10,11... | collective-permute-start | bytes 1179656 | tf_op jit(solution)/shard_map/ppermute | solution.py:805
  69.7 17.9 %all-to-all-start.2 = ((bf16[16,16,768]{2,1,0:T(8,128)(2,1)}), bf16[16,16,768]{2,1,0:T(8,128)(2,1)}, u32[]{:S(2)}, u32[]{:S(2)}) async-start(bf16[16,16,768]{2,1,0:T(8,128)(2,1)} %bitcast.16), calls=%async_computation.2 | async-start | bytes 786432 | tf_op jit(solution)/shard_map/all_to_all | solution.py:960
  87.7 6.7 %collective-permute-start.33 = (bf16[128,768]{1,0:T(8,128)(2,1)}, bf16[128,768]{1,0:T(8,128)(2,1)S(1)}, u32[]{:S(2)}, u32[]{:S(2)}) collective-permute-start(bf16[128,768]{1,0:T(8,128)(2,1)} %get-tuple-element.133), channel_id=1, source_target_pairs={{0,1},{1,0},{2,3},{3,2},{4,5},{5,4},{6,7},{7,6},{8,9},{9,8},{10,11... | collective-permute-start | bytes 589832 | tf_op jit(solution)/shard_map/ppermute | solution.py:805
  88.0 11.5 %collective-permute-start.9 = (bf16[512,384]{1,0:T(8,128)(2,1)}, bf16[512,384]{1,0:T(8,128)(2,1)S(1)}, u32[]{:S(2)}, u32[]{:S(2)}) collective-permute-start(bf16[512,384]{1,0:T(8,128)(2,1)} %get-tuple-element.121), channel_id=1, source_target_pairs={{0,2},{2,0},{4,6},{6,4},{8,10},{10,8},{12,14},{14,12},{16,18},{18,... | collective-permute-start | bytes 1179656 | tf_op jit(solution)/shard_map/ppermute | solution.py:810
  89.3 11.7 %collective-permute-start.16 = (bf16[512,384]{1,0:T(8,128)(2,1)}, bf16[512,384]{1,0:T(8,128)(2,1)S(1)}, u32[]{:S(2)}, u32[]{:S(2)}) collective-permute-start(bf16[512,384]{1,0:T(8,128)(2,1)} %get-tuple-element.123), channel_id=1, source_target_pairs={{0,4},{2,6},{4,0},{6,2},{8,12},{10,14},{12,8},{14,10},{16,20},{18,... | collective-permute-start | bytes 1179656 | tf_op jit(solution)/shard_map/ppermute | solution.py:810
  90.7 13.9 %collective-permute-start.23 = (bf16[640,384]{1,0:T(8,128)(2,1)}, bf16[640,384]{1,0:T(8,128)(2,1)S(1)}, u32[]{:S(2)}, u32[]{:S(2)}) collective-permute-start(bf16[640,384]{1,0:T(8,128)(2,1)} %get-tuple-element.125), channel_id=1, source_target_pairs={{0,8},{2,10},{4,12},{6,14},{8,0},{10,2},{12,4},{14,6},{16,24},{18,... | collective-permute-start | bytes 1474568 | tf_op jit(solution)/shard_map/ppermute | solution.py:810
  99.6 6.3 %collective-permute-start.10 = (bf16[256,384]{1,0:T(8,128)(2,1)S(1)}, bf16[256,384]{1,0:T(8,128)(2,1)S(1)}, u32[]{:S(2)}, u32[]{:S(2)}) collective-permute-start(bf16[256,384]{1,0:T(8,128)(2,1)S(1)} %get-tuple-element.160), channel_id=1, source_target_pairs={{0,4},{2,6},{4,0},{6,2},{8,12},{10,14},{12,8},{14,10},{16,20},{18,... | collective-permute-start | bytes 589832 | tf_op jit(solution)/shard_map/ppermute | solution.py:810
  101.1 7.8 %collective-permute-start.17 = (bf16[256,384]{1,0:T(8,128)(2,1)S(1)}, bf16[256,384]{1,0:T(8,128)(2,1)S(1)}, u32[]{:S(2)}, u32[]{:S(2)}) collective-permute-start(bf16[256,384]{1,0:T(8,128)(2,1)S(1)} %get-tuple-element.158), channel_id=1, source_target_pairs={{0,8},{2,10},{4,12},{6,14},{8,0},{10,2},{12,4},{14,6},{16,24},{18,... | collective-permute-start | bytes 589832 | tf_op jit(solution)/shard_map/ppermute | solution.py:810
  104.7 11.5 %collective-permute-start.24 = (bf16[320,384]{1,0:T(8,128)(2,1)S(1)}, bf16[320,384]{1,0:T(8,128)(2,1)S(1)}, u32[]{:S(2)}, u32[]{:S(2)}) collective-permute-start(bf16[320,384]{1,0:T(8,128)(2,1)S(1)} %get-tuple-element.156), channel_id=1, source_target_pairs={{0,2},{2,0},{4,6},{6,4},{8,10},{10,8},{12,14},{14,12},{16,18},{18,... | collective-permute-start | bytes 737288 | tf_op jit(solution)/shard_map/ppermute | solution.py:810
  105.9 4.7 %collective-permute-start.11 = (bf16[128,384]{1,0:T(8,128)(2,1)S(1)}, bf16[128,384]{1,0:T(8,128)(2,1)S(1)}, u32[]{:S(2)}, u32[]{:S(2)}) collective-permute-start(bf16[128,384]{1,0:T(8,128)(2,1)S(1)} %add_convert_fusion.17), channel_id=1, source_target_pairs={{0,8},{2,10},{4,12},{6,14},{8,0},{10,2},{12,4},{14,6},{16,24},{18,... | collective-permute-start | bytes 294920 | tf_op jit(solution)/shard_map/ppermute | solution.py:810
  108.9 4.7 %collective-permute-start.18 = (bf16[128,384]{1,0:T(8,128)(2,1)S(1)}, bf16[128,384]{1,0:T(8,128)(2,1)S(1)}, u32[]{:S(2)}, u32[]{:S(2)}) collective-permute-start(bf16[128,384]{1,0:T(8,128)(2,1)S(1)} %add_convert_fusion.13), channel_id=1, source_target_pairs={{0,2},{2,0},{4,6},{6,4},{8,10},{10,8},{12,14},{14,12},{16,18},{18,... | collective-permute-start | bytes 294920 | tf_op jit(solution)/shard_map/ppermute | solution.py:810
  110.7 8.3 %collective-permute-start.12 = (bf16[128,384]{1,0:T(8,128)(2,1)S(1)}, bf16[128,384]{1,0:T(8,128)(2,1)S(1)}, u32[]{:S(2)}, u32[]{:S(2)}) collective-permute-start(bf16[128,384]{1,0:T(8,128)(2,1)S(1)} %pad_maximum_fusion.7), channel_id=1, source_target_pairs={{0,16},{2,18},{4,20},{6,22},{8,24},{10,26},{12,28},{14,30},{16,0},... | collective-permute-start | bytes 294920 | tf_op jit(solution)/shard_map/ppermute | solution.py:810
  113.7 10.8 %collective-permute-start.19 = (bf16[128,384]{1,0:T(8,128)(2,1)S(1)}, bf16[128,384]{1,0:T(8,128)(2,1)S(1)}, u32[]{:S(2)}, u32[]{:S(2)}) collective-permute-start(bf16[128,384]{1,0:T(8,128)(2,1)S(1)} %pad_maximum_fusion.8), channel_id=1, source_target_pairs={{0,16},{2,18},{4,20},{6,22},{8,24},{10,26},{12,28},{14,30},{16,0},... | collective-permute-start | bytes 294920 | tf_op jit(solution)/shard_map/ppermute | solution.py:810
  116.3 4.9 %collective-permute-start.25 = (bf16[160,384]{1,0:T(8,128)(2,1)S(1)}, bf16[160,384]{1,0:T(8,128)(2,1)S(1)}, u32[]{:S(2)}, u32[]{:S(2)}) collective-permute-start(bf16[160,384]{1,0:T(8,128)(2,1)S(1)} %add_convert_fusion.9), channel_id=1, source_target_pairs={{0,4},{2,6},{4,0},{6,2},{8,12},{10,14},{12,8},{14,10},{16,20},{18,... | collective-permute-start | bytes 368648 | tf_op jit(solution)/shard_map/ppermute | solution.py:810
  119.0 12.1 %collective-permute-start.13 = (bf16[128,384]{1,0:T(8,128)(2,1)S(1)}, bf16[128,384]{1,0:T(8,128)(2,1)S(1)}, u32[]{:S(2)}, u32[]{:S(2)}) collective-permute-start(bf16[128,384]{1,0:T(8,128)(2,1)S(1)} %add_convert_fusion.15), channel_id=1, source_target_pairs={{0,8},{2,10},{4,12},{6,14},{8,0},{10,2},{12,4},{14,6},{16,24},{18,... | collective-permute-start | bytes 294920 | tf_op jit(solution)/shard_map/ppermute | solution.py:810
  121.4 7.3 %collective-permute-start.26 = (bf16[160,384]{1,0:T(8,128)(2,1)S(1)}, bf16[160,384]{1,0:T(8,128)(2,1)S(1)}, u32[]{:S(2)}, u32[]{:S(2)}) collective-permute-start(bf16[160,384]{1,0:T(8,128)(2,1)S(1)} %pad_maximum_fusion.6), channel_id=1, source_target_pairs={{0,16},{2,18},{4,20},{6,22},{8,24},{10,26},{12,28},{14,30},{16,0},... | collective-permute-start | bytes 368648 | tf_op jit(solution)/shard_map/ppermute | solution.py:810
  124.5 6.7 %collective-permute-start.20 = (bf16[128,384]{1,0:T(8,128)(2,1)S(1)}, bf16[128,384]{1,0:T(8,128)(2,1)S(1)}, u32[]{:S(2)}, u32[]{:S(2)}) collective-permute-start(bf16[128,384]{1,0:T(8,128)(2,1)S(1)} %add_convert_fusion.11), channel_id=1, source_target_pairs={{0,2},{2,0},{4,6},{6,4},{8,10},{10,8},{12,14},{14,12},{16,18},{18,... | collective-permute-start | bytes 294920 | tf_op jit(solution)/shard_map/ppermute | solution.py:810
  128.7 5.3 %collective-permute-start.27 = (bf16[160,384]{1,0:T(8,128)(2,1)S(1)}, bf16[160,384]{1,0:T(8,128)(2,1)S(1)}, u32[]{:S(2)}, u32[]{:S(2)}) collective-permute-start(bf16[160,384]{1,0:T(8,128)(2,1)S(1)} %add_convert_fusion.7), channel_id=1, source_target_pairs={{0,4},{2,6},{4,0},{6,2},{8,12},{10,14},{12,8},{14,10},{16,20},{18,... | collective-permute-start | bytes 368648 | tf_op jit(solution)/shard_map/ppermute | solution.py:810
  131.1 5.7 %collective-permute-start.14 = (bf16[256,384]{1,0:T(8,128)(2,1)S(1)}, bf16[256,384]{1,0:T(8,128)(2,1)S(1)}, u32[]{:S(2)}, u32[]{:S(2)}) collective-permute-start(bf16[256,384]{1,0:T(8,128)(2,1)S(1)} %pad_maximum_fusion.4), channel_id=1, source_target_pairs={{0,4},{2,6},{4,0},{6,2},{8,12},{10,14},{12,8},{14,10},{16,20},{18,... | collective-permute-start | bytes 589832 | tf_op jit(solution)/shard_map/ppermute | solution.py:810
  131.2 10.0 %collective-permute-start.21 = (bf16[256,384]{1,0:T(8,128)(2,1)S(1)}, bf16[256,384]{1,0:T(8,128)(2,1)S(1)}, u32[]{:S(2)}, u32[]{:S(2)}) collective-permute-start(bf16[256,384]{1,0:T(8,128)(2,1)S(1)} %pad_maximum_fusion.5), channel_id=1, source_target_pairs={{0,8},{2,10},{4,12},{6,14},{8,0},{10,2},{12,4},{14,6},{16,24},{18,... | collective-permute-start | bytes 589832 | tf_op jit(solution)/shard_map/ppermute | solution.py:810
  134.0 6.4 %collective-permute-start.28 = (bf16[320,384]{1,0:T(8,128)(2,1)S(1)}, bf16[320,384]{1,0:T(8,128)(2,1)S(1)}, u32[]{:S(2)}, u32[]{:S(2)}) collective-permute-start(bf16[320,384]{1,0:T(8,128)(2,1)S(1)} %pad_maximum_fusion.3), channel_id=1, source_target_pairs={{0,2},{2,0},{4,6},{6,4},{8,10},{10,8},{12,14},{14,12},{16,18},{18,... | collective-permute-start | bytes 737288 | tf_op jit(solution)/shard_map/ppermute | solution.py:810
  137.6 4.9 %collective-permute-start.30 = (bf16[512,384]{1,0:T(8,128)(2,1)}, bf16[512,384]{1,0:T(8,128)(2,1)S(1)}, u32[]{:S(2)}, u32[]{:S(2)}) collective-permute-start(bf16[512,384]{1,0:T(8,128)(2,1)} %pad_maximum_fusion.1.refs_0_), channel_id=1, source_target_pairs={{0,1},{1,0},{2,3},{3,2},{4,5},{5,4},{6,7},{7,6},{8,9},{9,8},{10,11... | collective-permute-start | bytes 1179656 | tf_op jit(solution)/shard_map/ppermute | solution.py:805
  137.6 12.1 %collective-permute-start.15 = (bf16[512,384]{1,0:T(8,128)(2,1)}, bf16[512,384]{1,0:T(8,128)(2,1)}, u32[]{:S(2)}, u32[]{:S(2)}) collective-permute-start(bf16[512,384]{1,0:T(8,128)(2,1)} %pad_maximum_fusion.1.refs_0_), channel_id=1, source_target_pairs={{0,2},{2,0},{4,6},{6,4},{8,10},{10,8},{12,14},{14,12},{16,18},{18,... | collective-permute-start | bytes 1179656 | tf_op jit(solution)/shard_map/ppermute | solution.py:810
  141.2 4.9 %collective-permute-start.32 = (bf16[640,384]{1,0:T(8,128)(2,1)}, bf16[640,384]{1,0:T(8,128)(2,1)}, u32[]{:S(2)}, u32[]{:S(2)}) collective-permute-start(bf16[640,384]{1,0:T(8,128)(2,1)} %pad_maximum_fusion.refs_4_.refs_6_), channel_id=1, source_target_pairs={{0,1},{1,0},{2,3},{3,2},{4,5},{5,4},{6,7},{7,6},{8,9},{9,8},{10,11... | collective-permute-start | bytes 1474568 | tf_op jit(solution)/shard_map/ppermute | solution.py:805
  141.2 13.9 %collective-permute-start.29 = (bf16[640,384]{1,0:T(8,128)(2,1)}, bf16[640,384]{1,0:T(8,128)(2,1)}, u32[]{:S(2)}, u32[]{:S(2)}) collective-permute-start(bf16[640,384]{1,0:T(8,128)(2,1)} %pad_maximum_fusion.refs_4_.refs_6_), channel_id=1, source_target_pairs={{0,8},{2,10},{4,12},{6,14},{8,0},{10,2},{12,4},{14,6},{16,24},{18,... | collective-permute-start | bytes 1474568 | tf_op jit(solution)/shard_map/ppermute | solution.py:810
  142.6 11.5 %collective-permute-start.22 = (bf16[512,384]{1,0:T(8,128)(2,1)}, bf16[512,384]{1,0:T(8,128)(2,1)}, u32[]{:S(2)}, u32[]{:S(2)}) collective-permute-start(bf16[512,384]{1,0:T(8,128)(2,1)} %pad_maximum_fusion.2.refs_2_), channel_id=1, source_target_pairs={{0,4},{2,6},{4,0},{6,2},{8,12},{10,14},{12,8},{14,10},{16,20},{18,... | collective-permute-start | bytes 1179656 | tf_op jit(solution)/shard_map/ppermute | solution.py:810
  (17 other events, 157.7 us)

commit v3 on v2

--- a/solution.py
+++ b/solution.py
@@ -59,8 +59,7 @@
 def call(body, outs, args, modes, vmem=16, flops=0, scratch=(), aliases=None, nbytes=1000000):
     count, total = len(args), len(args) + len(outs)
     shapes = [(a.shape, a.dtype) for a in args] + list(outs)
-    spaces = [pltpu.VMEM if m == "v" else pltpu.HBM for m in modes]
-    moved = [i for i in range(total) if modes[i] in "hl"]
+    moved = [i for i in range(total) if modes[i] in "hls"]
     buffers = [pltpu.VMEM(*shapes[i]) for i in moved]
 
     def kernel(*refs):
@@ -74,12 +73,14 @@
             ends = (refs[i], bodies[i]) if i < count else (bodies[i], refs[i])
             copies[i] = pltpu.make_async_copy(*ends, sems.at[i])
         for i in moved:
-            if i < count:
+            if i < count and modes[i] != "s":
                 copies[i].start()
         flushed = set()
 
         def wait(i):
             copies[i].wait()
+
+        wait.start = lambda i: copies[i].start()
 
         def flush(i):
             flushed.add(i)
@@ -96,7 +97,7 @@
             if i >= count:
                 copies[i].wait()
 
-    specs = [pl.BlockSpec(memory_space=space) for space in spaces]
+    specs = [pl.BlockSpec(memory_space=pltpu.HBM)] * total
     return pl.pallas_call(
         kernel,
         out_shape=[jax.ShapeDtypeStruct(s, d) for s, d in outs],
@@ -142,7 +143,7 @@
     own = jnp.where(low_half if side == 0 else jnp.logical_not(low_half), query_pair, 0)
     scores = cols_by_cols(own.astype(BF16), key_pair) * scale + bias
     grown = jnp.exp(scores - jnp.max(scores, axis=-1, keepdims=True))
-    return grown / jnp.sum(grown, axis=-1, keepdims=True)
+    return grown * (1.0 / jnp.sum(grown, axis=-1, keepdims=True))
 
 
 def forward_kernel(
@@ -170,6 +171,8 @@
     win_ref,
     fetch_ref,
     fetch_other_ref,
+    root_ref,
+    bias,
 ):
     rows, width = own_ref.shape
     size = width // heads
@@ -195,10 +198,18 @@
     win_ref[...] = windows
     for i in (4, 5, 6):
         flush(i)
+    same = windows[:, : 2 * rows]
+    apart = jnp.where(core == 1, windows[:, 2 * rows : 4 * rows], windows[:, 4 * rows :])
+    for head in range(heads):
+        bias[head, :, :rows] = toeplitz(same[head : head + 1], rows)
+        bias[head, :, rows:] = toeplitz(apart[head : head + 1], rows)
     x = own_ref[...].astype(F32)
     y = other_ref[...].astype(F32)
     gain = gain_first_ref[...].reshape(1, width)
-    act_own = (x * root_mean(x) * gain).astype(BF16)
+    root = root_mean(x)
+    root_ref[...] = jnp.broadcast_to(root, root_ref.shape)
+    flush(7)
+    act_own = (x * root * gain).astype(BF16)
     act_other = (y * root_mean(y) * gain).astype(BF16)
     act = jnp.concatenate([act_own, act_other], axis=0)
     wait(7)
@@ -208,22 +219,14 @@
     wait(9)
     queries = dot(act_own, wq[...]).astype(BF16)
     low_half = lax.broadcasted_iota(jnp.int32, (rows, 2 * size), 1) < size
-    same = windows[:, : 2 * rows]
-    apart = jnp.where(core == 1, windows[:, 2 * rows : 4 * rows], windows[:, 4 * rows :])
     mixed = []
     for pair in range(heads // 2):
         lanes = slice(pair * 2 * size, (pair + 1) * 2 * size)
         outs = []
         for side in range(2):
-            head = 2 * pair + side
-            bias = jnp.concatenate(
-                [
-                    toeplitz(same[head : head + 1], rows),
-                    toeplitz(apart[head : head + 1], rows),
-                ],
-                axis=1,
+            probs = attend(
+                queries[:, lanes], keys[:, lanes], scale, bias[2 * pair + side], side, low_half
             )
-            probs = attend(queries[:, lanes], keys[:, lanes], scale, bias, side, low_half)
             outs.append(dot(probs.astype(BF16), values[:, lanes]))
         mixed.append(jnp.where(low_half, outs[0], outs[1]).astype(BF16))
     mixed = jnp.concatenate(mixed, axis=1)
@@ -341,6 +344,7 @@
     router_grad_ref,
     in_vmem,
     down_vmem,
+    bundle,
     sems,
 ):
     total = arrived_ref.shape[0]
@@ -363,7 +367,11 @@
                     pltpu.make_async_copy(wdown.at[span, :], down_vmem.at[i], sems.at[1, i]),
                 )
             )
-    for pair in copies:
+    for copy in copies[0]:
+        copy.start()
+    for i in (0, 1):
+        wait(i)
+    for pair in copies[1:]:
         for copy in pair:
             copy.start()
     flat = arrived_ref[:, :width]
@@ -386,8 +394,20 @@
     gate = jnp.sum(router_probs * onehot, axis=-1, keepdims=True)
     sent = (cot.astype(F32) * (gate * keep)).astype(BF16)
     sent_ref[...] = sent
-    bundle_ref[:, :width] = flat
-    bundle_ref[:, width : 2 * width] = sent
+    flush(2)
+    bundle[:, :width] = flat
+    bundle[:, width : 2 * width] = sent
+    writes = []
+
+    def forward(first, size):
+        span = pl.ds(first, size)
+        write = pltpu.make_async_copy(
+            bundle.at[:, span], bundle_ref.at[:, span], sems.at[2, len(writes)]
+        )
+        write.start()
+        writes.append(write)
+
+    forward(0, 2 * width)
     produced = jnp.zeros((total, width), F32)
     grad = jnp.zeros((total, width), F32)
     inner = math.sqrt(2.0 / math.pi)
@@ -411,19 +431,26 @@
             pre_own_ref[:, first : first + chunk] = grad_pre
         else:
             first += 2 * width
-            bundle_ref[:, first : first + chunk] = act
-            bundle_ref[:, first + hidden : first + hidden + chunk] = grad_pre
+            bundle[:, first : first + chunk] = act
+            bundle[:, first + hidden : first + hidden + chunk] = grad_pre
+            forward(first, chunk)
+            forward(first + hidden, chunk)
+        if i + 1 == steps:
+            flush(0)
+            flush(1)
         produced = produced + dot(act, wdown)
         grad = grad + cols_by_cols(grad_pre, win)
-    for i in range(4):
-        flush(i)
     produced_low = produced.astype(BF16)
     kept = produced_low.astype(F32) * keep
     produced_ref[...] = kept.astype(BF16)
+    flush(5)
     grad_gate = jnp.sum(cot.astype(F32) * kept, axis=-1, keepdims=True)
     grad_logits = ((grad_gate * gate) * (onehot - router_probs)).astype(BF16)
     grad_ref[...] = (grad * keep + dot(grad_logits, router_ref[...])).astype(BF16)
+    flush(4)
     router_grad_ref[...] = rows_by_rows(grad_logits, flat)
+    for write in writes:
+        write.wait()
 
 
 def expert_weights_kernel(
@@ -501,10 +528,6 @@
     return [0, 2, 4, 16, 16 + experts, 16 + 2 * experts]
 
 
-def small_height(experts, levels):
-    return -(-(16 + 2 * experts) // (16 << levels)) * 16
-
-
 def backward_kernel(
     heads,
     orders,
@@ -520,42 +543,43 @@
     cot_ref,
     cot_other_ref,
     gain_second_ref,
+    mixed_own_ref,
+    mixed_other_ref,
+    value_ref,
+    probs_ref,
+    key_ref,
+    query_ref,
+    act_ref,
+    hot_ref,
     own_ref,
     other_ref,
-    act_ref,
-    query_ref,
-    key_ref,
-    value_ref,
-    probs_ref,
-    mixed_own_ref,
-    mixed_other_ref,
-    hot_ref,
     router_ref,
     after_ref,
+    wo_ref,
     wq_ref,
     wk_ref,
     wv_ref,
-    wo_ref,
     keep_0_ref,
     send_0_ref,
     keep_1_ref,
     send_1_ref,
     keep_2_ref,
     send_2_ref,
+    grad_middle_ref,
+    small_ref,
     input_own_ref,
     input_other_ref,
-    grad_middle_ref,
+    wo_half,
     wq_half,
     wk_half,
     wv_half,
-    wo_half,
     part_0,
     part_1,
     part_2,
-    natural,
+    small,
     sems,
 ):
-    rows, width = own_ref.shape
+    rows, width = middle_ref.shape
     size = width // heads
     part = width // 2
     experts = router_ref.shape[0]
@@ -563,7 +587,7 @@
     core = lax.axis_index("ffn")
     span = pl.ds(pl.multiple_of(core * part, LANES), part)
     copies = [
-        pltpu.make_async_copy(src, half, sems.at[i])
+        pltpu.make_async_copy(src, half, sems.at[6 + i])
         for i, (src, half) in enumerate(
             (
                 (wo_ref.at[span, :], wo_half),
@@ -585,19 +609,24 @@
         for i, ref in enumerate(pair):
             writes.append(
                 pltpu.make_async_copy(
-                    parts[p].at[pl.ds(i * rows_half, rows_half), :], ref, sems.at[4 + 2 * p + i]
+                    parts[p].at[pl.ds(i * rows_half, rows_half), :], ref, sems.at[2 * p + i]
                 )
             )
+    places = [
+        [chunk_place(chunk, order, levels) * (4 * height) for chunk in range(2**levels)]
+        for order in orders
+    ]
 
     def pack(matrix, value):
         for p, ref in enumerate(parts):
             for chunk in range(2**levels):
-                place = chunk_place(chunk, orders[p], levels)
                 first = p * third + chunk * height
-                step = ref.shape[0] >> levels
-                at = pl.multiple_of(place * step + matrix * height, 16)
+                at = pl.multiple_of(places[p][chunk] + matrix * height, 16)
                 ref[pl.ds(at, height), :] = value[first : first + height]
 
+    for i in range(9):
+        wait(i)
+    copies[0].wait()
     gain = gain_second_ref[...].reshape(1, width)
     grad_own, gain_terms = middle_back(
         returned_ref[...], fetch_ref[...], middle_ref[...], gain, cot_ref[...]
@@ -607,13 +636,16 @@
     )
     gain_second = jnp.sum(gain_terms, axis=0, keepdims=True)
     grad_middle_ref[...] = grad_own
-    flush(8)
+    flush(6)
     grad_low = jnp.concatenate([grad_own, grad_other], axis=0).astype(BF16)
+    grad_mixed = cols_by_cols(grad_low, wo_half[...]).astype(BF16)
+    for i in range(9, 20):
+        wait(i)
+    for copy in copies[1:]:
+        copy.wait()
     mixed = jnp.concatenate([mixed_own_ref[...], mixed_other_ref[...]], axis=0)
     grad_columns = jnp.where(core == 0, grad_low[:, :part], grad_low[:, part:])
     pack(3, rows_by_rows(mixed, grad_columns).astype(BF16))
-    copies[0].wait()
-    grad_mixed = cols_by_cols(grad_low, wo_half[...]).astype(BF16)
     low_half = lax.broadcasted_iota(jnp.int32, (2 * rows, 2 * size), 1) < size
     grad_q, grad_k, grad_v = [], [], []
     same, ahead, behind = [], [], []
@@ -650,8 +682,24 @@
     pack(0, rows_by_rows(act, grad_q).astype(BF16))
     pack(1, rows_by_rows(act, grad_k).astype(BF16))
     pack(2, rows_by_rows(act, grad_v).astype(BF16))
-    for write in writes[:4]:
+    for write in writes:
         write.start()
+    grad_act = (
+        cols_by_cols(grad_q, wq_half[...])
+        + cols_by_cols(grad_k, wk_half[...])
+        + cols_by_cols(grad_v, wv_half[...])
+    )
+    input_other_ref[...] = grad_act[rows:].astype(BF16)
+    flush(9)
+    input_own_ref[...] = grad_act[:rows]
+    flush(8)
+    x = own_ref[...].astype(F32)
+    y = other_ref[...].astype(F32)
+    gain_first = jnp.sum(
+        grad_act[:rows] * (x * root_mean(x)) + grad_act[rows:] * (y * root_mean(y)),
+        axis=0,
+        keepdims=True,
+    )
     sums = jnp.concatenate(
         [jnp.concatenate(part_sums, axis=0) for part_sums in (same, ahead, behind)], axis=1
     )
@@ -662,38 +710,16 @@
         precision=TOP_PRECISION,
         preferred_element_type=F32,
     )
-    for copy in copies[1:]:
-        copy.wait()
-    grad_act = (
-        cols_by_cols(grad_q, wq_half[...])
-        + cols_by_cols(grad_k, wk_half[...])
-        + cols_by_cols(grad_v, wv_half[...])
-    )
-    x = own_ref[...].astype(F32)
-    y = other_ref[...].astype(F32)
-    gain_first = jnp.sum(
-        grad_act[:rows] * (x * root_mean(x)) + grad_act[rows:] * (y * root_mean(y)),
-        axis=0,
-        keepdims=True,
-    )
-    input_own_ref[...] = grad_act[:rows]
-    input_other_ref[...] = grad_act[rows:].astype(BF16)
     at = small_rows(experts)
-    natural[...] = jnp.zeros_like(natural)
+    small[: at[3]] = jnp.zeros((at[3], part), F32)
     for i, value in enumerate((gain_first, gain_second)):
-        natural[at[i] : at[i] + 1] = value[:, :part]
-        natural[at[i] + 1 : at[i] + 2] = value[:, part:]
-    natural[at[2] : at[2] + heads // 2, : table.shape[1]] = table
-    natural[at[3] : at[4]] = router_ref[:, :part]
-    natural[at[4] : at[5]] = router_ref[:, part:]
-    step = part_2.shape[0] >> levels
-    extra = step - 4 * height
-    for chunk in range(2**levels):
-        place = chunk_place(chunk, orders[2], levels)
-        at = pl.multiple_of(place * step + 4 * height, 16)
-        part_2[pl.ds(at, extra), :] = natural[chunk * extra : (chunk + 1) * extra].astype(BF16)
-    for write in writes[4:]:
-        write.start()
+        small[at[i] : at[i] + 1] = value[:, :part]
+        small[at[i] + 1 : at[i] + 2] = value[:, part:]
+    small[at[2] : at[2] + heads // 2, : table.shape[1]] = table
+    small[at[3] : at[4]] = router_ref[:, :part]
+    small[at[4] : at[5]] = router_ref[:, part:]
+    small_ref[...] = small[...].astype(BF16)
+    flush(7)
     for write in writes:
         write.wait()
 
@@ -702,7 +728,7 @@
     arrays, refs = refs[: 2 * len(chosen)], refs[2 * len(chosen) :]
     if last is not None:
         experts, heads = last
-        near_refs, refs = refs[:2], refs[2:]
+        (small_own_ref, small_other_ref), refs = refs[:2], refs[2:]
     if upper:
         refs = refs[4:]
     outs, (wide, sems) = refs[:4], refs[-2:]
@@ -726,9 +752,8 @@
         for low in range(half):
             place = chunk_place(low, order, levels)
             place = jnp.bitwise_and(place, half - 1)
-            step = arrays[2 * n].shape[0] // half
             for matrix in range(4):
-                at = pl.ds(pl.multiple_of(place * step + matrix * height, 16), height)
+                at = pl.ds(pl.multiple_of((place * 4 + matrix) * height, 16), height)
                 to = pl.ds(low * height, height)
                 wide[n, matrix, to, own] = arrays[2 * n][at, :].astype(F32)
                 wide[n, matrix, to, theirs] = arrays[2 * n + 1][at, :].astype(F32)
@@ -744,22 +769,7 @@
             writes.append(write)
     if last is not None:
         at = small_rows(experts)
-        extra = small_height(experts, levels)
-        step = arrays[-1].shape[0] // half
-        found = []
-        for chunk in range(-(-at[5] // extra)):
-            place = chunk_place(chunk, orders[2], levels)
-            away = place >= half
-            first = jnp.bitwise_and(place, half - 1) * step + 4 * height
-            rows = pl.ds(pl.multiple_of(first, 16), extra)
-            found.append(
-                [
-                    jnp.where(away, arrays[i - 2][rows, :].astype(F32), near_refs[i][rows, :].astype(F32))
-                    for i in range(2)
-                ]
-            )
-        mine = jnp.concatenate([a for a, _ in found], axis=0)
-        other = jnp.concatenate([b for _, b in found], axis=0)
+        mine, other = small_own_ref[...], small_other_ref[...]
         both = mine + other
         gain_first_ref[...] = jnp.concatenate([both[0:1], both[1:2]], axis=1).reshape(width)
         gain_second_ref[...] = jnp.concatenate([both[2:3], both[3:4]], axis=1).reshape(width)
@@ -776,7 +786,7 @@
         write.wait()
 
 
-def assemble(orders, levels, chosen, arrays, width, earlier=(), near=(), last=None):
+def assemble(orders, levels, chosen, arrays, width, earlier=(), smalls=(), last=None):
     tail = []
     modes = "l" * len(arrays)
     if last is not None:
@@ -789,9 +799,9 @@
     return call(
         functools.partial(assemble_kernel, orders, levels, chosen, bool(earlier), last),
         [((width, width), F32)] * 4 + tail,
-        (*arrays, *near, *earlier),
+        (*arrays, *smalls, *earlier),
         modes + "rrrr" + "h" * len(tail),
-        vmem=64,
+        vmem=16,
         aliases={first + i: i for i in range(len(earlier))},
         scratch=[
             pltpu.VMEM((len(chosen), 4, width // 6, width), F32),
@@ -814,35 +824,62 @@
     return (left.astype(F32) + right.astype(F32)).astype(BF16)
 
 
-def scatter_sum(keep, send, order, levels):
-    for k, bit in enumerate(order):
-        got = flip(send, bit)
-        half = keep.shape[0] // 2
-        if k + 2 == len(order):
-            both = add_low(keep, got)
-            send = both
-            if k + 1 < levels:
-                send = jnp.concatenate([both[half:], both[:half]])
-            return add_low(both, flip(send, order[-1]))
-        if k + 1 < levels:
-            keep, send = add_low(keep[:half], got[:half]), add_low(keep[half:], got[half:])
-        else:
-            both = add_low(keep, got)
-            upper = (lax.axis_index("expert") >> order[k + 1]) & 1
-            keep = lax.dynamic_slice_in_dim(both, upper * half, half, 0)
-            send = lax.dynamic_slice_in_dim(both, (1 - upper) * half, half, 0)
-
-
-def gather_back(x, order, levels):
-    for k, bit in reversed(list(enumerate(order[:-1]))):
-        got = flip(x, bit)
-        if k == 0:
-            return x, got
-        if k < levels:
-            x = jnp.concatenate([x, got])
-        else:
-            upper = (lax.axis_index("expert") >> bit) & 1
-            x = jnp.where(upper == 1, jnp.concatenate([got, x]), jnp.concatenate([x, got]))
+def sum_over_chips(keeps, sends, orders, levels, small, beside):
+    count = len(orders[0])
+    todo = set(orders[0])
+    ridden = set()
+
+    def exchange(phase, x, bit):
+        nonlocal small
+        if bit not in todo or phase in ridden or phase < 2 or phase > 2 * count - 3:
+            return flip(x, bit)
+        todo.discard(bit)
+        ridden.add(phase)
+        got = flip(jnp.concatenate([x, small.astype(BF16)]), bit)
+        rows = x.shape[0]
+        small = small.astype(F32) + got[rows:].astype(F32)
+        return got[:rows]
+
+    def mine(bit):
+        return (lax.axis_index("expert") >> bit) & 1
+
+    whole = [None] * len(orders)
+    for k in range(count - 1):
+        for p, order in enumerate(orders):
+            keep, got = keeps[p], exchange(k, sends[p], order[k])
+            half = keep.shape[0] // 2
+            if k + 2 == count:
+                whole[p] = add_low(keep, got)
+            elif k + 1 < levels:
+                keeps[p] = add_low(keep[:half], got[:half])
+                sends[p] = add_low(keep[half:], got[half:])
+            else:
+                both = add_low(keep, got)
+                upper = mine(order[k + 1])
+                keeps[p] = lax.dynamic_slice_in_dim(both, upper * half, half, 0)
+                sends[p] = lax.dynamic_slice_in_dim(both, (1 - upper) * half, half, 0)
+    whole, beside = lax.optimization_barrier((whole, beside))
+    for p, order in enumerate(orders):
+        x = whole[p]
+        whole[p] = add_low(x, exchange(count - 1, x, order[-1]))
+    got = [None] * len(orders)
+    for k in reversed(range(count - 1)):
+        for p, order in enumerate(orders):
+            x = whole[p]
+            got[p] = exchange(2 * count - 2 - k, x, order[k])
+            if k == 0:
+                continue
+            if k < levels:
+                whole[p] = jnp.concatenate([x, got[p]])
+            else:
+                whole[p] = jnp.where(
+                    mine(order[k]) == 1,
+                    jnp.concatenate([got[p], x]),
+                    jnp.concatenate([x, got[p]]),
+                )
+    for bit in sorted(todo):
+        small = small.astype(F32) + flip(small, bit).astype(F32)
+    return whole, got, small, beside
 
 
 def shards(
@@ -880,7 +917,7 @@
     in_own, down_own = w_in[0], w_down[0]
     in_other, down_other = swap(in_own), swap(down_own)
     cot_other = swap(cotangent)
-    middle, gate, outgoing, mixed, windows, fetch, fetch_other = call(
+    middle, gate, outgoing, mixed, windows, fetch, fetch_other, root = call(
         functools.partial(forward_kernel, heads),
         [
             ((rows, width), F32),
@@ -890,6 +927,7 @@
             ((heads, 6 * rows), F32),
             ((rows, total), BF16),
             ((rows, total), BF16),
+            ((rows, LANES), F32),
         ],
         (
             tokens,
@@ -907,9 +945,10 @@
             router,
             cotangent,
         ),
-        "hhhhhhhlllllll" + "hhhhhhh",
+        "hhhhhhhlllllll" + "hhhhhhhh",
         vmem=64,
         flops=3000000000,
+        scratch=[pltpu.VMEM((heads, rows, 2 * rows), F32)],
     )
     arrived = lax.all_to_all(outgoing, "expert", 0, 0, tiled=True)
     mixed_other, middle_other = swap(mixed), swap(middle)
@@ -928,7 +967,7 @@
         flops=3000000000,
         scratch=[pltpu.VMEM((width, part), BF16)] * 3 + [pltpu.SemaphoreType.DMA((3,))],
     )
-    chunk = 512
+    chunk = hidden // 2
     steps = 2 * hidden // chunk
     hid_own, pre_own, sent, bundle, grad_slots, produced, router_part = call(
         functools.partial(expert_kernel, capacity, chunk),
@@ -942,13 +981,14 @@
             ((experts, width), F32),
         ],
         (arrived, router, in_own, in_other, down_own, down_other, act),
-        "hhrrrrr" + "hhhhhhh",
+        "llrrrrr" + "hhhrhhh",
         vmem=64,
         flops=6000000000,
         scratch=[
             pltpu.VMEM((steps, width, chunk), BF16),
             pltpu.VMEM((steps, chunk, width), BF16),
-            pltpu.SemaphoreType.DMA((2, steps)),
+            pltpu.VMEM((total, 2 * width + 2 * hidden), BF16),
+            pltpu.SemaphoreType.DMA((3, steps + 1)),
         ],
     )
     bundle_other = swap(bundle)
@@ -959,16 +999,19 @@
     )
     produced_returned = lax.all_to_all(produced, "expert", 0, 0, tiled=True)
     bits = experts.bit_length() - 1
-    levels = min(bits, 4)
+    levels = min(bits - 1, 3)
     rest = list(range(3, bits))
     orders = [[0, 1, 2] + rest, [1, 2, 0] + rest, [2, 0, 1] + rest]
     third = 4 * width // 3
-    extra = small_height(experts, levels) << levels
-    heights = [third, third, third + extra]
-    *halves, input_own, input_other, grad_middle = call(
+    *halves, grad_middle, small, input_own, input_other = call(
         functools.partial(backward_kernel, heads, orders, levels),
-        [((height // 2, part), BF16) for height in heights for _ in range(2)]
-        + [((rows, width), F32), ((rows, width), BF16), ((rows, width), F32)],
+        [((third // 2, part), BF16)] * 6
+        + [
+            ((rows, width), F32),
+            ((16 + 2 * experts, part), BF16),
+            ((rows, width), F32),
+            ((rows, width), BF16),
+        ],
         (
             grad_returned,
             swap(grad_returned),
@@ -979,57 +1022,61 @@
             cotangent,
             cot_other,
             norm_second,
+            mixed,
+            mixed_other,
+            values,
+            probs,
+            keys,
+            queries,
+            act,
+            hot,
             tokens,
             other,
-            act,
-            queries,
-            keys,
-            values,
-            probs,
-            mixed,
-            mixed_other,
-            hot,
             router_part,
             grad_w_in,
+            w_out,
             w_query,
             w_key,
             w_value,
-            w_out,
         ),
-        "hhhhhhhhh" + "hhhhhhhhhhh" + "rrrrr" + "rrrrrrhhh",
-        vmem=64,
+        "l" * 20 + "rrrrr" + "rrrrrr" + "hhhh",
+        vmem=56,
         flops=4000000000,
-        scratch=[pltpu.VMEM((width, part), BF16)] * 3
-        + [
+        scratch=[
             pltpu.VMEM((part, width), BF16),
-            *[pltpu.VMEM((height, part), BF16) for height in heights],
-            pltpu.VMEM((extra, part), F32),
+            *[pltpu.VMEM((width, part), BF16)] * 3,
+            *[pltpu.VMEM((third, part), BF16)] * 3,
+            pltpu.VMEM((16 + 2 * experts, part), F32),
             pltpu.SemaphoreType.DMA((10,)),
         ],
     )
-    halves, input_own, input_other, grad_middle, produced_returned = lax.optimization_barrier(
-        (halves, input_own, input_other, grad_middle, produced_returned)
-    )
-    scattered = [
-        scatter_sum(halves[2 * p], halves[2 * p + 1], order, levels)
-        for p, order in enumerate(orders)
-    ]
-    inputs = tokens.astype(F32)
-    root = root_mean(inputs)
-    up = norm_first * (input_own + swap(input_other).astype(F32))
-    grad_input = grad_middle + root * up - inputs * root**3 * jnp.mean(
-        up * inputs, axis=-1, keepdims=True
+    halves, grad_middle, small, input_own, input_other, produced_returned = (
+        lax.optimization_barrier(
+            (halves, grad_middle, small, input_own, input_other, produced_returned)
+        )
+    )
+    beside = (grad_middle, input_own, swap(input_other), produced_returned)
+    kept, got, small, beside = sum_over_chips(
+        list(halves[0::2]), list(halves[1::2]), orders, levels, small, beside
+    )
+    grad_middle, input_own, input_swapped, produced_returned = beside
+    root = root[:, :1]
+    scaled = tokens.astype(F32) * root
+    up = norm_first * (input_own + input_swapped.astype(F32))
+    grad_input = grad_middle + root * (
+        up - scaled * jnp.mean(up * scaled, axis=-1, keepdims=True)
     )
     expert_branch = gate[:, :1] * dot(fetch, produced_returned)
     output = (middle + expert_branch).astype(BF16)
-    gathered = [gather_back(piece, order, levels) for piece, order in zip(scattered, orders)]
     near = []
-    for kept, _ in gathered:
-        near += [kept, swap(kept)]
+    for rows_kept in kept:
+        near += [rows_kept, swap(rows_kept)]
     matrices = assemble(orders, levels, (0, 1, 2), near, width)
-    got = [pair[1] for pair in gathered]
-    got, matrices, output, expert_branch, grad_input = lax.optimization_barrier(
-        (got, matrices, output, expert_branch, grad_input)
+    small_other = swap(small)
+    got, matrices, small, small_other, output, expert_branch, grad_input = (
+        lax.optimization_barrier(
+            (got, matrices, small, small_other, output, expert_branch, grad_input)
+        )
     )
     far = []
     for rows_got in got:
@@ -1041,7 +1088,7 @@
         far,
         width,
         matrices,
-        near[4:],
+        (small, small_other),
         (experts, heads, buckets),
     )
     return (

time: 165 us -> 160 us (0.970)
  waiting for transfers between devices: 49.4 us -> 59.4 us
  starting transfers between devices: 50.7 us -> 44.8 us
  Pallas kernels: 52.8 us -> 47.5 us
    ppermute x21, waiting for transfers between devices: 25.3 us -> 32.7 us  [flip(): return lax.ppermute(x, 'expert', [(i, i ^ 1 << bit) for i in range(peers)])]
    pallas_call x6, Pallas kernels: 43.9 us -> 38.6 us  [call(): pl.pallas_call(kernel, out_shape=[jax.ShapeDtypeStruct(s, d) for s, d in...]
    ppermute x21, starting transfers between devices: 29.2 us -> 24.5 us  [flip(): return lax.ppermute(x, 'expert', [(i, i ^ 1 << bit) for i in range(peers)])]
    concatenate x9, other arithmetic: 2.54 us -> 0.24 us  [the longest x5 0.16 us: sum_over_chips(): whole[p] = jnp.concatenate([x, got[p]])]
    convert_element_type x12, other arithmetic: 0.63 us -> 2.63 us  [add_low(): return (left.astype(F32) + right.astype(F32)).astype(BF16)]
    all_to_all x1, waiting for transfers between devices: 0.01 us -> 1.8 us  [shards(): produced_returned = lax.all_to_all(produced, 'expert', 0, 0, tiled=True)]
    ppermute x16 -> x17, waiting for transfers between devices: 4.41 us -> 5.26 us  [swap(): return lax.ppermute(x, 'ffn', [(0, 1), (1, 0)])]
    ppermute x16 -> x17, starting transfers between devices: 3.47 us -> 3 us  [swap(): return lax.ppermute(x, 'ffn', [(0, 1), (1, 0)])]
  transfers between devices with their start and end apart: 40 -> 41, of which waited for: 20 -> 23; matrix products, arithmetic and copies ran while one was open for 5% -> 3% of each run, Pallas kernels for 23% -> 21%
where the time goes in v3:
time: 160 us; the launch traced here: 159 us
  waiting for transfers between devices  59.4 us (37%)
  Pallas kernels  47.5 us (30%)
  starting transfers between devices  44.8 us (28%)
  other arithmetic  4.1 us (3%)
    pallas_call x6, Pallas kernels, call(): pl.pallas_call(kernel, out_shape=[jax.ShapeDtypeStruct(s, d) for s, d in...  38.6 us
    ppermute x21, waiting for transfers between devices, flip(): return lax.ppermute(x, 'expert', [(i, i ^ 1 << bit) for i in range(peers)])  32.7 us
    ppermute x21, starting transfers between devices, flip(): return lax.ppermute(x, 'expert', [(i, i ^ 1 << bit) for i in range(peers)])  24.5 us
    all_to_all x1, waiting for transfers between devices, shards(): arrived = lax.all_to_all(outgoing, 'expert', 0, 0, tiled=True)  15.6 us
    pallas_call x1, Pallas kernels, expert_weights(): pl.pallas_call(expert_weights_kernel, grid=(steps,), out_shape=[jax.Shape...  8.89 us
    all_to_all x1, starting transfers between devices, shards(): arrived = lax.all_to_all(outgoing, 'expert', 0, 0, tiled=True)  8.3 us
    ppermute x17, waiting for transfers between devices, swap(): return lax.ppermute(x, 'ffn', [(0, 1), (1, 0)])  5.26 us
    all_to_all x1, starting transfers between devices, shards(): grad_returned = lax.all_to_all(grad_slots, 'expert', 0, 0, tiled=True)  5.26 us
  transfers between devices with their start and end apart: 41, of which 23 were waited for; matrix products, arithmetic and copies ran while one was open for 3% of the time, Pallas kernels for 21%

profile of v3, /device:TPU:0, one launch (start us, length us, event | category | flops | bytes accessed | tf_op | source)
XLA Modules:
  0.0 159.2 jit_solution(535241572103038537)
XLA Ops:
  1.2 1.3 collective-permute-done.1.refs_4_
  3.1 7.2 %shard_map.237 = (f32[128,768]{1,0:T(8,128)}, f32[128,128]{1,0:T(8,128)}, bf16[256,1664]{1,0:T(8,128)(2,1)}, bf16[128,768]{1,0:T(8,128)(2,1)}, f32[12,768]{1,0:T...) custom-call(bf16[128,768]{1,0:T(8,128)(2,1)} %refs_17_.1, ...), custom_call_target="tpu_custom_call" | custom-call | flops 3000000000 | bytes 1000000 | tf_op jit(solution)/shard_map/pallas_call | solution.py:101
  10.3 8.3 %all-to-all-start = ((bf16[16,16,1664]{2,1,0:T(8,128)(2,1)}), bf16[16,16,1664]{2,1,0:T(8,128)(2,1)}, u32[]{:S(2)}, u32[]{:S(2)}) async-start(bf16[16,16,1664]{2,1,0:T(8,128)(2,1)} %bitcast.16), calls=%async_computation | async-start | bytes 1703936 | tf_op jit(solution)/shard_map/all_to_all | solution.py:953
  18.6 5.6 %shard_map.238 = (bf16[256,768]{1,0:T(8,128)(2,1)}, bf16[256,384]{1,0:T(8,128)(2,1)}, bf16[256,384]{1,0:T(8,128)(2,1)}, bf16[256,384]{1,0:T(8,128)(2,1)}, f32[6,256,256]{2,1,0:T(8,128)}) custom-call(bf16[128,768]{1,0:T(8,128)(2,1)} %refs_17_.1, bf16[128,768]{1,0:T(8,128)(2,1)} %collective-permute-done.refs_1_.refs_18_, f32[768]{0:T(1024)} %refs_2_.3, ...), custom_call_target="tpu_custom_call" | custom-call | flops 3000000000 | bytes 1000000 | tf_op jit(solution)/shard_map/pallas_call | solution.py:101
  24.2 15.6 %all-to-all-done = bf16[16,16,1664]{2,1,0:T(8,128)(2,1)} async-done(((bf16[16,16,1664]{2,1,0:T(8,128)(2,1)}), bf16[16,16,1664]{2,1,0:T(8,128)(2,1)}, u32[]{:S(2)}, u32[]{:S(2)}) %all-to-all-start) | async-done | bytes 852000 | tf_op jit(solution)/shard_map/all_to_all | solution.py:953
  39.8 9.3 %shard_map.239 = (bf16[256,1536]{1,0:T(8,128)(2,1)}, bf16[256,1536]{1,0:T(8,128)(2,1)}, bf16[256,768]{1,0:T(8,128)(2,1)}, bf16[256,4608]{1,0:T(8,128)(2,1)}, bf1...) custom-call(bf16[256,1664]{1,0:T(8,128)(2,1)} %bitcast.4.refs_0_.flat_own, ...), custom_call_target="tpu_custom_call" | custom-call | flops 6000000000 | bytes 1000000 | tf_op jit(solution)/shard_map/pallas_call | solution.py:101
  49.2 5.3 %all-to-all-start.1 = ((bf16[16,16,768]{2,1,0:T(8,128)(2,1)}), bf16[16,16,768]{2,1,0:T(8,128)(2,1)}, u32[]{:S(2)}, u32[]{:S(2)}) async-start(bf16[16,16,768]{2,1,0:T(8,128)(2,1)} %bitcast.18), calls=%async_computation.1 | async-start | bytes 786432 | tf_op jit(solution)/shard_map/all_to_all | solution.py:995
  54.8 8.9 %shard_map.240 = (f32[1,768,1536]{2,1,0:T(8,128)}, f32[1,1536,768]{2,1,0:T(8,128)}) custom-call(bf16[256,1664]{1,0:T(8,128)(2,1)} %bitcast.4.refs_0_.flat_own, bf16[256,768]{1,0:T(8,128)(2,1)} %get-tuple-element.106.sent_own, bf16[256,1536]{1,0:T(8,128)(2,1)} %get-tuple-element.107.hid_own, bf16[256,1536]{1,0:T(8,128)(2,1)} %get-tuple-element.108.pre_own, ...), custom_call_target="tpu_custom_call" | custom-call | flops 2415919104 | bytes 14000000 | tf_op jit(solution)/shard_map/pallas_call | solution.py:475
  63.7 4.1 %all-to-all-done.1 = bf16[16,16,768]{2,1,0:T(8,128)(2,1)} async-done(((bf16[16,16,768]{2,1,0:T(8,128)(2,1)}), bf16[16,16,768]{2,1,0:T(8,128)(2,1)}, u32[]{:S(2)}, u32[]{:S(2)}) %all-to-all-start.1) | async-done | bytes 393248 | tf_op jit(solution)/shard_map/all_to_all | solution.py:995
  67.7 3.8 %all-to-all-start.2 = ((bf16[16,16,768]{2,1,0:T(8,128)(2,1)}), bf16[16,16,768]{2,1,0:T(8,128)(2,1)S(1)}, u32[]{:S(2)}, u32[]{:S(2)}) async-start(bf16[16,16,768]{2,1,0:T(8,128)(2,1)} %bitcast.17), calls=%async_computation.2 | async-start | bytes 786432 | tf_op jit(solution)/shard_map/all_to_all | solution.py:1000
  74.6 8.2 %shard_map.241 = (bf16[512,384]{1,0:T(8,128)(2,1)}, bf16[512,384]{1,0:T(8,128)(2,1)}, bf16[512,384]{1,0:T(8,128)(2,1)}, bf16[512,384]{1,0:T(8,128)(2,1)}, bf16[5...) custom-call(bf16[256,768]{1,0:T(8,128)(2,1)} %bitcast.8.refs_0_, ...), custom_call_target="tpu_custom_call" | custom-call | flops 4000000000 | bytes 1000000 | tf_op jit(solution)/shard_map/pallas_call | solution.py:101
  82.8 1.8 %all-to-all-done.2 = bf16[16,16,768]{2,1,0:T(8,128)(2,1)S(1)} async-done(((bf16[16,16,768]{2,1,0:T(8,128)(2,1)}), bf16[16,16,768]{2,1,0:T(8,128)(2,1)S(1)}, u32[]{:S(2)}, u32[]{:S(2)}) %all-to-all-start.2) | async-done | bytes 393248 | tf_op jit(solution)/shard_map/all_to_all | solution.py:1000
  87.8 6.6 %collective-permute-done.9 = bf16[512,384]{1,0:T(8,128)(2,1)S(1)} collective-permute-done((bf16[512,384]{1,0:T(8,128)(2,1)}, bf16[512,384]{1,0:T(8,128)(2,1)S(1)}, u32[]{:S(2)}, u32[]{:S(2)}) %collective-permute-start.9) | collective-permute-done | bytes 393248 | tf_op jit(solution)/shard_map/ppermute | solution.py:820
  95.5 1.6 %collective-permute-start.10 = (bf16[256,384]{1,0:T(8,128)(2,1)S(1)}, bf16[256,384]{1,0:T(8,128)(2,1)S(1)}, u32[]{:S(2)}, u32[]{:S(2)}) collective-permute-start(bf16[256,384]{1,0:T(8,128)(2,1)S(1)} %get-tuple-element.182), channel_id=1, source_target_pairs={{0,4},{2,6},{4,0},{6,2},{8,12},{10,14},{12,8},{14,10},{16,20},{18,... | collective-permute-start | bytes 589832 | tf_op jit(solution)/shard_map/ppermute | solution.py:820
  98.3 1.5 collective-permute-start.13
  99.9 1.5 collective-permute-start.16
  101.5 1.4 collective-permute-start.11
  103.0 2.3 %collective-permute-done.13 = bf16[256,384]{1,0:T(8,128)(2,1)S(1)} collective-permute-done((bf16[256,384]{1,0:T(8,128)(2,1)S(1)}, bf16[256,384]{1,0:T(8,128)(2,1)S(1)}, u32[]{:S(2)}, u32[]{:S(2)}) %collective-permute-start.13) | collective-permute-done | bytes 196640 | tf_op jit(solution)/shard_map/ppermute | solution.py:820
  105.3 1.7 %collective-permute-start.14 = (bf16[128,384]{1,0:T(8,128)(2,1)S(1)}, bf16[128,384]{1,0:T(8,128)(2,1)S(1)}, u32[]{:S(2)}, u32[]{:S(2)}) collective-permute-start(bf16[128,384]{1,0:T(8,128)(2,1)S(1)} %add_convert_fusion.14), channel_id=1, source_target_pairs={{0,2},{2,0},{4,6},{6,4},{8,10},{10,8},{12,14},{14,12},{16,18},{18,... | collective-permute-start | bytes 294920 | tf_op jit(solution)/shard_map/ppermute | solution.py:820
  107.2 2.8 %collective-permute-done.14 = bf16[128,384]{1,0:T(8,128)(2,1)S(1)} collective-permute-done((bf16[128,384]{1,0:T(8,128)(2,1)S(1)}, bf16[128,384]{1,0:T(8,128)(2,1)S(1)}, u32[]{:S(2)}, u32[]{:S(2)}) %collective-permute-start.14) | collective-permute-done | bytes 98336 | tf_op jit(solution)/shard_map/ppermute | solution.py:820
  110.1 1.7 %collective-permute-done.17 = bf16[128,384]{1,0:T(8,128)(2,1)S(1)} collective-permute-done((bf16[128,384]{1,0:T(8,128)(2,1)S(1)}, bf16[128,384]{1,0:T(8,128)(2,1)S(1)}, u32[]{:S(2)}, u32[]{:S(2)}) %collective-permute-start.17) | collective-permute-done | bytes 98336 | tf_op jit(solution)/shard_map/ppermute | solution.py:820
  112.1 2.4 %collective-permute-start.21 = (bf16[128,384]{1,0:T(8,128)(2,1)S(1)}, bf16[128,384]{1,0:T(8,128)(2,1)S(1)}, u32[]{:S(2)}, u32[]{:S(2)}) collective-permute-start(bf16[128,384]{1,0:T(8,128)(2,1)S(1)} %add_convert_fusion.13), channel_id=1, source_target_pairs={{0,16},{2,18},{4,20},{6,22},{8,24},{10,26},{12,28},{14,30},{16,0},... | collective-permute-start | bytes 294920 | tf_op jit(solution)/shard_map/ppermute | solution.py:820
  115.2 2.4 %collective-permute-start.19 = (bf16[176,384]{1,0:T(8,128)(2,1)S(1)}, bf16[176,384]{1,0:T(8,128)(2,1)S(1)}, u32[]{:S(2)}, u32[]{:S(2)}) collective-permute-start(bf16[176,384]{1,0:T(8,128)(2,1)S(1)} %pad_maximum_fusion.7), channel_id=1, source_target_pairs={{0,16},{2,18},{4,20},{6,22},{8,24},{10,26},{12,28},{14,30},{16,0},... | collective-permute-start | bytes 405512 | tf_op jit(solution)/shard_map/ppermute | solution.py:820
  117.5 6.5 %collective-permute-done.27 = bf16[128,384]{1,0:T(8,128)(2,1)S(1)} collective-permute-done((bf16[128,384]{1,0:T(8,128)(2,1)S(1)}, bf16[128,384]{1,0:T(8,128)(2,1)S(1)}, u32[]{:S(2)}, u32[]{:S(2)}) %collective-permute-start.27) | collective-permute-done | bytes 98336 | tf_op jit(solution)/shard_map/ppermute | solution.py:820
  125.5 1.5 collective-permute-start.22
  127.1 1.6 %collective-permute-done.28 = bf16[128,384]{1,0:T(8,128)(2,1)S(1)} collective-permute-done((bf16[128,384]{1,0:T(8,128)(2,1)S(1)}, bf16[128,384]{1,0:T(8,128)(2,1)S(1)}, u32[]{:S(2)}, u32[]{:S(2)}) %collective-permute-start.28) | collective-permute-done | bytes 98336 | tf_op jit(solution)/shard_map/ppermute | solution.py:820
  128.8 1.5 collective-permute-start.29
  134.6 2.7 %collective-permute-done.25 = bf16[256,384]{1,0:T(8,128)(2,1)S(1)} collective-permute-done((bf16[256,384]{1,0:T(8,128)(2,1)S(1)}, bf16[256,384]{1,0:T(8,128)(2,1)S(1)}, u32[]{:S(2)}, u32[]{:S(2)}) %collective-permute-start.25) | collective-permute-done | bytes 196640 | tf_op jit(solution)/shard_map/ppermute | solution.py:820
  140.0 1.5 collective-permute-start.24
  142.7 3.6 %shard_map.242 = (f32[768,768]{1,0:T(8,128)}, f32[768,768]{1,0:T(8,128)}, f32[768,768]{1,0:T(8,128)}, f32[768,768]{1,0:T(8,128)}) custom-call(bf16[512,384]{1,0:T(8,128)(2,1)S(1)} %pad_maximum_fusion.refs_0_, bf16[512,384]{1,0:T(8,128)(2,1)S(1)} %collective-permute-done.31.refs_1_, bf16[512,384]{1,0:T(8,128)(2,1)S(1)} %pad_maximum_fusion.1.refs_2_, ...), custom_call_target="tpu_custom_call" | custom-call | bytes 8000000 | tf_op jit(solution)/shard_map/pallas_call | solution.py:101
  146.3 3.6 %collective-permute-done.30.refs_4_ = bf16[512,384]{1,0:T(8,128)(2,1)S(1)} collective-permute-done((bf16[512,384]{1,0:T(8,128)(2,1)S(1)}, bf16[512,384]{1,0:T(8,128)(2,1)S(1)}, u32[]{:S(2)}, u32[]{:S(2)}) %collective-permute-start.30) | collective-permute-done | bytes 393248 | tf_op jit(solution)/shard_map/ppermute | solution.py:820
  154.4 4.7 %shard_map.243 = (f32[768,768]{1,0:T(8,128)}, f32[768,768]{1,0:T(8,128)}, f32[768,768]{1,0:T(8,128)}, f32[768,768]{1,0:T(8,128)}, f32[768]{0:T(1024)}, /*index=5...) custom-call(bf16[512,384]{1,0:T(8,128)(2,1)S(1)} %collective-permute, ...), custom_call_target="tpu_custom_call", output_to_operand_aliasing={{0}: (8, {}), {1}: (9, {}), {2}: (10, {}), {3}: (11, {})} | custom-call | bytes 8000000 | tf_op jit(solution)/shard_map/pallas_call | solution.py:101
  (116 shorter events, 25.3 us)
Async XLA Ops:
  2.6 37.2 %collective-permute-start.2 = (bf16[768,1536]{1,0:T(8,128)(2,1)}, bf16[768,1536]{1,0:T(8,128)(2,1)}, u32[]{:S(2)}, u32[]{:S(2)}) collective-permute-start(bf16[768,1536]{1,0:T(8,128)(2,1)} %bitcast.19), channel_id=1, source_target_pairs={{0,1},{1,0},{2,3},{3,2},{4,5},{5,4},{6,7},{7,6},{8,9},{9,8},{10,11... | collective-permute-start | bytes 7077896 | tf_op jit(solution)/shard_map/ppermute | solution.py:815
  3.0 36.9 %collective-permute-start.3 = (bf16[1536,768]{1,0:T(8,128)(2,1)}, bf16[1536,768]{1,0:T(8,128)(2,1)}, u32[]{:S(2)}, u32[]{:S(2)}) collective-permute-start(bf16[1536,768]{1,0:T(8,128)(2,1)} %bitcast.21), channel_id=1, source_target_pairs={{0,1},{1,0},{2,3},{3,2},{4,5},{5,4},{6,7},{7,6},{8,9},{9,8},{10,11... | collective-permute-start | bytes 7077896 | tf_op jit(solution)/shard_map/ppermute | solution.py:815
  10.3 29.5 %all-to-all-start = ((bf16[16,16,1664]{2,1,0:T(8,128)(2,1)}), bf16[16,16,1664]{2,1,0:T(8,128)(2,1)}, u32[]{:S(2)}, u32[]{:S(2)}) async-start(bf16[16,16,1664]{2,1,0:T(8,128)(2,1)} %bitcast.16), calls=%async_computation | async-start | bytes 1703936 | tf_op jit(solution)/shard_map/all_to_all | solution.py:953
  49.1 5.6 %collective-permute-start.4 = (bf16[256,4608]{1,0:T(8,128)(2,1)}, bf16[256,4608]{1,0:T(8,128)(2,1)}, u32[]{:S(2)}, u32[]{:S(2)}) collective-permute-start(bf16[256,4608]{1,0:T(8,128)(2,1)} %get-tuple-element.109), channel_id=1, source_target_pairs={{0,1},{1,0},{2,3},{3,2},{4,5},{5,4},{6,7},{7,6},{8,9},{9,8},{10,11... | collective-permute-start | bytes 7077896 | tf_op jit(solution)/shard_map/ppermute | solution.py:815
  49.2 18.5 %all-to-all-start.1 = ((bf16[16,16,768]{2,1,0:T(8,128)(2,1)}), bf16[16,16,768]{2,1,0:T(8,128)(2,1)}, u32[]{:S(2)}, u32[]{:S(2)}) async-start(bf16[16,16,768]{2,1,0:T(8,128)(2,1)} %bitcast.18), calls=%async_computation.1 | async-start | bytes 786432 | tf_op jit(solution)/shard_map/all_to_all | solution.py:995
  54.5 19.3 %collective-permute-start.6 = (f32[128,768]{1,0:T(8,128)}, f32[128,768]{1,0:T(8,128)}, u32[]{:S(2)}, u32[]{:S(2)}) collective-permute-start(f32[128,768]{1,0:T(8,128)} %get-tuple-element.114.refs_4_), channel_id=1, source_target_pairs={{0,1},{1,0},{2,3},{3,2},{4,5},{5,4},{6,7},{7,6},{8,9},{9,8},{10,11... | collective-permute-start | bytes 1179656 | tf_op jit(solution)/shard_map/ppermute | solution.py:815
  67.7 6.0 %collective-permute-start.5 = (bf16[256,768]{1,0:T(8,128)(2,1)}, bf16[256,768]{1,0:T(8,128)(2,1)S(1)}, u32[]{:S(2)}, u32[]{:S(2)}) collective-permute-start(bf16[256,768]{1,0:T(8,128)(2,1)} %bitcast.8.refs_0_), channel_id=1, source_target_pairs={{0,1},{1,0},{2,3},{3,2},{4,5},{5,4},{6,7},{7,6},{8,9},{9,8},{10,11... | collective-permute-start | bytes 1179656 | tf_op jit(solution)/shard_map/ppermute | solution.py:815
  67.7 16.9 %all-to-all-start.2 = ((bf16[16,16,768]{2,1,0:T(8,128)(2,1)}), bf16[16,16,768]{2,1,0:T(8,128)(2,1)S(1)}, u32[]{:S(2)}, u32[]{:S(2)}) async-start(bf16[16,16,768]{2,1,0:T(8,128)(2,1)} %bitcast.17), calls=%async_computation.2 | async-start | bytes 786432 | tf_op jit(solution)/shard_map/all_to_all | solution.py:1000
  84.6 9.8 %collective-permute-start.9 = (bf16[512,384]{1,0:T(8,128)(2,1)}, bf16[512,384]{1,0:T(8,128)(2,1)S(1)}, u32[]{:S(2)}, u32[]{:S(2)}) collective-permute-start(bf16[512,384]{1,0:T(8,128)(2,1)} %get-tuple-element.134), channel_id=1, source_target_pairs={{0,2},{2,0},{4,6},{6,4},{8,10},{10,8},{12,14},{14,12},{16,18},{18,... | collective-permute-start | bytes 1179656 | tf_op jit(solution)/shard_map/ppermute | solution.py:820
  85.2 12.0 %collective-permute-start.12 = (bf16[512,384]{1,0:T(8,128)(2,1)}, bf16[512,384]{1,0:T(8,128)(2,1)S(1)}, u32[]{:S(2)}, u32[]{:S(2)}) collective-permute-start(bf16[512,384]{1,0:T(8,128)(2,1)} %get-tuple-element.137), channel_id=1, source_target_pairs={{0,4},{2,6},{4,0},{6,2},{8,12},{10,14},{12,8},{14,10},{16,20},{18,... | collective-permute-start | bytes 1179656 | tf_op jit(solution)/shard_map/ppermute | solution.py:820
  86.4 25.5 %collective-permute-start.18 = (bf16[128,768]{1,0:T(8,128)(2,1)}, bf16[128,768]{1,0:T(8,128)(2,1)S(1)}, u32[]{:S(2)}, u32[]{:S(2)}) collective-permute-start(bf16[128,768]{1,0:T(8,128)(2,1)} %get-tuple-element.142), channel_id=1, source_target_pairs={{0,1},{1,0},{2,3},{3,2},{4,5},{5,4},{6,7},{7,6},{8,9},{9,8},{10,11... | collective-permute-start | bytes 589832 | tf_op jit(solution)/shard_map/ppermute | solution.py:815
  86.5 13.4 %collective-permute-start.15 = (bf16[512,384]{1,0:T(8,128)(2,1)}, bf16[512,384]{1,0:T(8,128)(2,1)S(1)}, u32[]{:S(2)}, u32[]{:S(2)}) collective-permute-start(bf16[512,384]{1,0:T(8,128)(2,1)} %get-tuple-element.139), channel_id=1, source_target_pairs={{0,8},{2,10},{4,12},{6,14},{8,0},{10,2},{12,4},{14,6},{16,24},{18,... | collective-permute-start | bytes 1179656 | tf_op jit(solution)/shard_map/ppermute | solution.py:820
  95.5 5.9 %collective-permute-start.10 = (bf16[256,384]{1,0:T(8,128)(2,1)S(1)}, bf16[256,384]{1,0:T(8,128)(2,1)S(1)}, u32[]{:S(2)}, u32[]{:S(2)}) collective-permute-start(bf16[256,384]{1,0:T(8,128)(2,1)S(1)} %get-tuple-element.182), channel_id=1, source_target_pairs={{0,4},{2,6},{4,0},{6,2},{8,12},{10,14},{12,8},{14,10},{16,20},{18,... | collective-permute-start | bytes 589832 | tf_op jit(solution)/shard_map/ppermute | solution.py:820
  98.3 7.0 %collective-permute-start.13 = (bf16[256,384]{1,0:T(8,128)(2,1)S(1)}, bf16[256,384]{1,0:T(8,128)(2,1)S(1)}, u32[]{:S(2)}, u32[]{:S(2)}) collective-permute-start(bf16[256,384]{1,0:T(8,128)(2,1)S(1)} %get-tuple-element.180), channel_id=1, source_target_pairs={{0,8},{2,10},{4,12},{6,14},{8,0},{10,2},{12,4},{14,6},{16,24},{18,... | collective-permute-start | bytes 589832 | tf_op jit(solution)/shard_map/ppermute | solution.py:820
  99.9 7.1 %collective-permute-start.16 = (bf16[256,384]{1,0:T(8,128)(2,1)S(1)}, bf16[256,384]{1,0:T(8,128)(2,1)S(1)}, u32[]{:S(2)}, u32[]{:S(2)}) collective-permute-start(bf16[256,384]{1,0:T(8,128)(2,1)S(1)} %get-tuple-element.178), channel_id=1, source_target_pairs={{0,2},{2,0},{4,6},{6,4},{8,10},{10,8},{12,14},{14,12},{16,18},{18,... | collective-permute-start | bytes 589832 | tf_op jit(solution)/shard_map/ppermute | solution.py:820
  101.5 10.3 %collective-permute-start.11 = (bf16[176,384]{1,0:T(8,128)(2,1)S(1)}, bf16[176,384]{1,0:T(8,128)(2,1)S(1)}, u32[]{:S(2)}, u32[]{:S(2)}) collective-permute-start(bf16[176,384]{1,0:T(8,128)(2,1)S(1)} %pad_maximum_fusion.6), channel_id=1, source_target_pairs={{0,8},{2,10},{4,12},{6,14},{8,0},{10,2},{12,4},{14,6},{16,24},{18,... | collective-permute-start | bytes 405512 | tf_op jit(solution)/shard_map/ppermute | solution.py:820
  105.3 4.7 %collective-permute-start.14 = (bf16[128,384]{1,0:T(8,128)(2,1)S(1)}, bf16[128,384]{1,0:T(8,128)(2,1)S(1)}, u32[]{:S(2)}, u32[]{:S(2)}) collective-permute-start(bf16[128,384]{1,0:T(8,128)(2,1)S(1)} %add_convert_fusion.14), channel_id=1, source_target_pairs={{0,2},{2,0},{4,6},{6,4},{8,10},{10,8},{12,14},{14,12},{16,18},{18,... | collective-permute-start | bytes 294920 | tf_op jit(solution)/shard_map/ppermute | solution.py:820
  107.1 4.7 %collective-permute-start.17 = (bf16[128,384]{1,0:T(8,128)(2,1)S(1)}, bf16[128,384]{1,0:T(8,128)(2,1)S(1)}, u32[]{:S(2)}, u32[]{:S(2)}) collective-permute-start(bf16[128,384]{1,0:T(8,128)(2,1)S(1)} %add_convert_fusion.11), channel_id=1, source_target_pairs={{0,4},{2,6},{4,0},{6,2},{8,12},{10,14},{12,8},{14,10},{16,20},{18,... | collective-permute-start | bytes 294920 | tf_op jit(solution)/shard_map/ppermute | solution.py:820
  112.1 13.0 %collective-permute-start.21 = (bf16[128,384]{1,0:T(8,128)(2,1)S(1)}, bf16[128,384]{1,0:T(8,128)(2,1)S(1)}, u32[]{:S(2)}, u32[]{:S(2)}) collective-permute-start(bf16[128,384]{1,0:T(8,128)(2,1)S(1)} %add_convert_fusion.13), channel_id=1, source_target_pairs={{0,16},{2,18},{4,20},{6,22},{8,24},{10,26},{12,28},{14,30},{16,0},... | collective-permute-start | bytes 294920 | tf_op jit(solution)/shard_map/ppermute | solution.py:820
  114.5 9.5 %collective-permute-start.27 = (bf16[128,384]{1,0:T(8,128)(2,1)S(1)}, bf16[128,384]{1,0:T(8,128)(2,1)S(1)}, u32[]{:S(2)}, u32[]{:S(2)}) collective-permute-start(bf16[128,384]{1,0:T(8,128)(2,1)S(1)} %add_convert_fusion.10), channel_id=1, source_target_pairs={{0,16},{2,18},{4,20},{6,22},{8,24},{10,26},{12,28},{14,30},{16,0},... | collective-permute-start | bytes 294920 | tf_op jit(solution)/shard_map/ppermute | solution.py:820
  115.2 10.3 %collective-permute-start.19 = (bf16[176,384]{1,0:T(8,128)(2,1)S(1)}, bf16[176,384]{1,0:T(8,128)(2,1)S(1)}, u32[]{:S(2)}, u32[]{:S(2)}) collective-permute-start(bf16[176,384]{1,0:T(8,128)(2,1)S(1)} %pad_maximum_fusion.7), channel_id=1, source_target_pairs={{0,16},{2,18},{4,20},{6,22},{8,24},{10,26},{12,28},{14,30},{16,0},... | collective-permute-start | bytes 405512 | tf_op jit(solution)/shard_map/ppermute | solution.py:820
  124.1 4.7 %collective-permute-start.28 = (bf16[128,384]{1,0:T(8,128)(2,1)S(1)}, bf16[128,384]{1,0:T(8,128)(2,1)S(1)}, u32[]{:S(2)}, u32[]{:S(2)}) collective-permute-start(bf16[128,384]{1,0:T(8,128)(2,1)S(1)} %add_convert_fusion.7), channel_id=1, source_target_pairs={{0,4},{2,6},{4,0},{6,2},{8,12},{10,14},{12,8},{14,10},{16,20},{18,... | collective-permute-start | bytes 294920 | tf_op jit(solution)/shard_map/ppermute | solution.py:820
  125.5 6.1 %collective-permute-start.22 = (bf16[176,384]{1,0:T(8,128)(2,1)S(1)}, bf16[176,384]{1,0:T(8,128)(2,1)S(1)}, u32[]{:S(2)}, u32[]{:S(2)}) collective-permute-start(bf16[176,384]{1,0:T(8,128)(2,1)S(1)} %pad_maximum_fusion.8), channel_id=1, source_target_pairs={{0,2},{2,0},{4,6},{6,4},{8,10},{10,8},{12,14},{14,12},{16,18},{18,... | collective-permute-start | bytes 405512 | tf_op jit(solution)/shard_map/ppermute | solution.py:820
  127.0 5.7 %collective-permute-start.20 = (bf16[128,384]{1,0:T(8,128)(2,1)S(1)}, bf16[128,384]{1,0:T(8,128)(2,1)S(1)}, u32[]{:S(2)}, u32[]{:S(2)}) collective-permute-start(bf16[128,384]{1,0:T(8,128)(2,1)S(1)} %add_convert_fusion.9), channel_id=1, source_target_pairs={{0,8},{2,10},{4,12},{6,14},{8,0},{10,2},{12,4},{14,6},{16,24},{18,... | collective-permute-start | bytes 294920 | tf_op jit(solution)/shard_map/ppermute | solution.py:820
  128.8 5.7 %collective-permute-start.29 = (bf16[256,384]{1,0:T(8,128)(2,1)S(1)}, bf16[256,384]{1,0:T(8,128)(2,1)S(1)}, u32[]{:S(2)}, u32[]{:S(2)}) collective-permute-start(bf16[256,384]{1,0:T(8,128)(2,1)S(1)} %pad_maximum_fusion.5), channel_id=1, source_target_pairs={{0,2},{2,0},{4,6},{6,4},{8,10},{10,8},{12,14},{14,12},{16,18},{18,... | collective-permute-start | bytes 589832 | tf_op jit(solution)/shard_map/ppermute | solution.py:820
  131.6 5.7 %collective-permute-start.25 = (bf16[256,384]{1,0:T(8,128)(2,1)S(1)}, bf16[256,384]{1,0:T(8,128)(2,1)S(1)}, u32[]{:S(2)}, u32[]{:S(2)}) collective-permute-start(bf16[256,384]{1,0:T(8,128)(2,1)S(1)} %pad_maximum_fusion.4), channel_id=1, source_target_pairs={{0,8},{2,10},{4,12},{6,14},{8,0},{10,2},{12,4},{14,6},{16,24},{18,... | collective-permute-start | bytes 589832 | tf_op jit(solution)/shard_map/ppermute | solution.py:820
  132.8 7.0 %collective-permute-start.23 = (bf16[304,384]{1,0:T(8,128)(2,1)S(1)}, bf16[304,384]{1,0:T(8,128)(2,1)S(1)}, u32[]{:S(2)}, u32[]{:S(2)}) collective-permute-start(bf16[304,384]{1,0:T(8,128)(2,1)S(1)} %pad_maximum_fusion.3), channel_id=1, source_target_pairs={{0,4},{2,6},{4,0},{6,2},{8,12},{10,14},{12,8},{14,10},{16,20},{18,... | collective-permute-start | bytes 700424 | tf_op jit(solution)/shard_map/ppermute | solution.py:820
  134.6 5.5 %collective-permute-start.33 = (bf16[512,384]{1,0:T(8,128)(2,1)S(1)}, bf16[512,384]{1,0:T(8,128)(2,1)S(1)}, u32[]{:S(2)}, u32[]{:S(2)}) collective-permute-start(bf16[512,384]{1,0:T(8,128)(2,1)S(1)} %pad_maximum_fusion.2.refs_4_), channel_id=1, source_target_pairs={{0,1},{1,0},{2,3},{3,2},{4,5},{5,4},{6,7},{7,6},{8,9},{9,8},{10,11... | collective-permute-start | bytes 1179656 | tf_op jit(solution)/shard_map/ppermute | solution.py:815
  138.4 11.5 %collective-permute-start.30 = (bf16[512,384]{1,0:T(8,128)(2,1)S(1)}, bf16[512,384]{1,0:T(8,128)(2,1)S(1)}, u32[]{:S(2)}, u32[]{:S(2)}) collective-permute-start(bf16[512,384]{1,0:T(8,128)(2,1)S(1)} %pad_maximum_fusion.2.refs_4_), channel_id=1, source_target_pairs={{0,8},{2,10},{4,12},{6,14},{8,0},{10,2},{12,4},{14,6},{16,24},{18,... | collective-permute-start | bytes 1179656 | tf_op jit(solution)/shard_map/ppermute | solution.py:820
  139.2 11.2 %collective-permute-start.26 = (bf16[512,384]{1,0:T(8,128)(2,1)S(1)}, bf16[512,384]{1,0:T(8,128)(2,1)S(1)}, u32[]{:S(2)}, u32[]{:S(2)}) collective-permute-start(bf16[512,384]{1,0:T(8,128)(2,1)S(1)} %pad_maximum_fusion.1.refs_2_), channel_id=1, source_target_pairs={{0,4},{2,6},{4,0},{6,2},{8,12},{10,14},{12,8},{14,10},{16,20},{18,... | collective-permute-start | bytes 1179656 | tf_op jit(solution)/shard_map/ppermute | solution.py:820
  140.0 11.5 %collective-permute-start.24 = (bf16[512,384]{1,0:T(8,128)(2,1)S(1)}, bf16[512,384]{1,0:T(8,128)(2,1)S(1)}, u32[]{:S(2)}, u32[]{:S(2)}) collective-permute-start(bf16[512,384]{1,0:T(8,128)(2,1)S(1)} %pad_maximum_fusion.refs_0_), channel_id=1, source_target_pairs={{0,2},{2,0},{4,6},{6,4},{8,10},{10,8},{12,14},{14,12},{16,18},{18,... | collective-permute-start | bytes 1179656 | tf_op jit(solution)/shard_map/ppermute | solution.py:820
  141.6 4.8 %collective-permute-start.34 = (f32[48,384]{1,0:T(8,128)S(1)}, f32[48,384]{1,0:T(8,128)S(1)}, u32[]{:S(2)}, u32[]{:S(2)}) collective-permute-start(f32[48,384]{1,0:T(8,128)S(1)} %convert_add_fusion.refs_6_), channel_id=1, source_target_pairs={{0,1},{1,0},{2,3},{3,2},{4,5},{5,4},{6,7},{7,6},{8,9},{9,8},{10,11... | collective-permute-start | bytes 221192 | tf_op jit(solution)/shard_map/ppermute | solution.py:815
  (22 other events, 170.6 us)

commit v4 on v3

--- a/solution.py
+++ b/solution.py
@@ -724,8 +724,9 @@
         write.wait()
 
 
-def assemble_kernel(orders, levels, chosen, upper, last, wait, flush, *refs):
-    arrays, refs = refs[: 2 * len(chosen)], refs[2 * len(chosen) :]
+def assemble_kernel(orders, levels, sides, upper, last, wait, flush, *refs):
+    count = len(orders) * len(sides)
+    arrays, refs = refs[:count], refs[count:]
     if last is not None:
         experts, heads = last
         (small_own_ref, small_other_ref), refs = refs[:2], refs[2:]
@@ -737,34 +738,35 @@
     width = outs[0].shape[1]
     part = width // 2
     third = width // 3
-    side = third // 2
+    span = third // 2
     height = third >> levels
     half = 2 ** (levels - 1)
     core = lax.axis_index("ffn")
     mine = lax.axis_index("expert")
-    own = pl.ds(pl.multiple_of(core * part, LANES), part)
-    theirs = pl.ds(pl.multiple_of((1 - core) * part, LANES), part)
+    columns = [
+        pl.ds(pl.multiple_of((1 - core if side else core) * part, LANES), part) for side in sides
+    ]
     writes = []
-    for n, p in enumerate(chosen):
-        order = orders[p]
-        for i in (2 * n, 2 * n + 1):
-            wait(i)
+    for p, order in enumerate(orders):
+        for i in range(len(sides)):
+            wait(len(sides) * p + i)
         for low in range(half):
-            place = chunk_place(low, order, levels)
-            place = jnp.bitwise_and(place, half - 1)
+            place = jnp.bitwise_and(chunk_place(low, order, levels), half - 1)
             for matrix in range(4):
-                at = pl.ds(pl.multiple_of((place * 4 + matrix) * height, 16), height)
+                at = pl.ds(pl.multiple_of((place * 4 + matrix) * height, height), height)
                 to = pl.ds(low * height, height)
-                wide[n, matrix, to, own] = arrays[2 * n][at, :].astype(F32)
-                wide[n, matrix, to, theirs] = arrays[2 * n + 1][at, :].astype(F32)
+                for i in range(len(sides)):
+                    lanes = columns[i] if len(sides) == 2 else slice(None)
+                    wide[p, matrix, to, lanes] = arrays[len(sides) * p + i][at, :].astype(F32)
         bit = jnp.bitwise_and(jnp.right_shift(mine, order[0]), 1)
         if upper:
             bit = 1 - bit
-        first = pl.multiple_of(p * third + bit * side, side)
+        first = pl.multiple_of(p * third + bit * span, span)
         for matrix in range(4):
-            write = pltpu.make_async_copy(
-                wide.at[n, matrix], outs[matrix].at[pl.ds(first, side), :], sems.at[4 * n + matrix]
-            )
+            target = outs[matrix].at[pl.ds(first, span), :]
+            if len(sides) == 1:
+                target = outs[matrix].at[pl.ds(first, span), columns[0]]
+            write = pltpu.make_async_copy(wide.at[p, matrix], target, sems.at[4 * p + matrix])
             write.start()
             writes.append(write)
     if last is not None:
@@ -786,7 +788,7 @@
         write.wait()
 
 
-def assemble(orders, levels, chosen, arrays, width, earlier=(), smalls=(), last=None):
+def assemble(orders, levels, sides, arrays, width, earlier=(), smalls=(), last=None):
     tail = []
     modes = "l" * len(arrays)
     if last is not None:
@@ -796,16 +798,17 @@
         last = (experts, heads)
     first = len(modes)
     modes += "r" * len(earlier)
+    columns = width * len(sides) // 2
     return call(
-        functools.partial(assemble_kernel, orders, levels, chosen, bool(earlier), last),
+        functools.partial(assemble_kernel, orders, levels, sides, bool(earlier), last),
         [((width, width), F32)] * 4 + tail,
         (*arrays, *smalls, *earlier),
         modes + "rrrr" + "h" * len(tail),
         vmem=16,
         aliases={first + i: i for i in range(len(earlier))},
         scratch=[
-            pltpu.VMEM((len(chosen), 4, width // 6, width), F32),
-            pltpu.SemaphoreType.DMA((4 * len(chosen),)),
+            pltpu.VMEM((len(orders), 4, width // 6, columns), F32),
+            pltpu.SemaphoreType.DMA((4 * len(orders),)),
         ],
         nbytes=8000000,
     )
@@ -858,7 +861,6 @@
                 upper = mine(order[k + 1])
                 keeps[p] = lax.dynamic_slice_in_dim(both, upper * half, half, 0)
                 sends[p] = lax.dynamic_slice_in_dim(both, (1 - upper) * half, half, 0)
-    whole, beside = lax.optimization_barrier((whole, beside))
     for p, order in enumerate(orders):
         x = whole[p]
         whole[p] = add_low(x, exchange(count - 1, x, order[-1]))
@@ -1050,14 +1052,14 @@
             pltpu.SemaphoreType.DMA((10,)),
         ],
     )
-    halves, grad_middle, small, input_own, input_other, produced_returned = (
+    keeps, grad_middle, small, input_own, input_other, produced_returned = (
         lax.optimization_barrier(
-            (halves, grad_middle, small, input_own, input_other, produced_returned)
+            (halves[0::2], grad_middle, small, input_own, input_other, produced_returned)
         )
     )
     beside = (grad_middle, input_own, swap(input_other), produced_returned)
     kept, got, small, beside = sum_over_chips(
-        list(halves[0::2]), list(halves[1::2]), orders, levels, small, beside
+        list(keeps), list(halves[1::2]), orders, levels, small, beside
     )
     grad_middle, input_own, input_swapped, produced_returned = beside
     root = root[:, :1]
@@ -1071,20 +1073,19 @@
     near = []
     for rows_kept in kept:
         near += [rows_kept, swap(rows_kept)]
-    matrices = assemble(orders, levels, (0, 1, 2), near, width)
+    matrices = assemble(orders, levels, (0, 1), near, width)
     small_other = swap(small)
     got, matrices, small, small_other, output, expert_branch, grad_input = (
         lax.optimization_barrier(
             (got, matrices, small, small_other, output, expert_branch, grad_input)
         )
     )
-    far = []
-    for rows_got in got:
-        far += [rows_got, swap(rows_got)]
+    far = [swap(rows_got) for rows_got in got]
+    matrices = assemble(orders, levels, (0,), got, width, matrices)
     results = assemble(
         orders,
         levels,
-        (0, 1, 2),
+        (1,),
         far,
         width,
         matrices,

time: 160 us -> 154 us (0.963)
  waiting for transfers between devices: 59.4 us -> 52.1 us
  starting transfers between devices: 44.8 us -> 46.4 us
    ppermute x17, waiting for transfers between devices: 5.26 us -> 1.46 us  [swap(): return lax.ppermute(x, 'ffn', [(0, 1), (1, 0)])]
    all_to_all x1, waiting for transfers between devices: 1.8 us -> 0.01 us  [shards(): produced_returned = lax.all_to_all(produced, 'expert', 0, 0, tiled=True)]
    ppermute x21, waiting for transfers between devices: 32.7 us -> 30.9 us  [flip(): return lax.ppermute(x, 'expert', [(i, i ^ 1 << bit) for i in range(peers)])]
    pallas_call x6 -> x7, Pallas kernels: 38.6 us -> 39.3 us  [call(): pl.pallas_call(kernel, out_shape=[jax.ShapeDtypeStruct(s, d) for s, d in...]
  transfers between devices with their start and end apart: 41 -> 41, of which waited for: 23 -> 17; matrix products, arithmetic and copies ran while one was open for 3% -> 3% of each run, Pallas kernels for 21% -> 23%
where the time goes in v4:
time: 154 us; the launch traced here: 153 us
  waiting for transfers between devices  52.1 us (34%)
  Pallas kernels  48.2 us (31%)
  starting transfers between devices  46.4 us (30%)
  other arithmetic  3.05 us (2%)
    pallas_call x7, Pallas kernels, call(): pl.pallas_call(kernel, out_shape=[jax.ShapeDtypeStruct(s, d) for s, d in...  39.3 us
    ppermute x21, waiting for transfers between devices, flip(): return lax.ppermute(x, 'expert', [(i, i ^ 1 << bit) for i in range(peers)])  30.9 us
    ppermute x21, starting transfers between devices, flip(): return lax.ppermute(x, 'expert', [(i, i ^ 1 << bit) for i in range(peers)])  25.9 us
    all_to_all x1, waiting for transfers between devices, shards(): arrived = lax.all_to_all(outgoing, 'expert', 0, 0, tiled=True)  15.6 us
    pallas_call x1, Pallas kernels, expert_weights(): pl.pallas_call(expert_weights_kernel, grid=(steps,), out_shape=[jax.Shape...  8.89 us
    all_to_all x1, starting transfers between devices, shards(): arrived = lax.all_to_all(outgoing, 'expert', 0, 0, tiled=True)  8.3 us
    all_to_all x1, starting transfers between devices, shards(): grad_returned = lax.all_to_all(grad_slots, 'expert', 0, 0, tiled=True)  5.26 us
    all_to_all x1, waiting for transfers between devices, shards(): grad_returned = lax.all_to_all(grad_slots, 'expert', 0, 0, tiled=True)  4.08 us
  transfers between devices with their start and end apart: 41, of which 17 were waited for; matrix products, arithmetic and copies ran while one was open for 3% of the time, Pallas kernels for 23%

profile of v4, /device:TPU:0, one launch (start us, length us, event | category | flops | bytes accessed | tf_op | source)
XLA Modules:
  0.0 153.1 jit_solution(6001439845926563894)
XLA Ops:
  3.1 7.2 %shard_map.237 = (f32[128,768]{1,0:T(8,128)}, f32[128,128]{1,0:T(8,128)}, bf16[256,1664]{1,0:T(8,128)(2,1)}, bf16[128,768]{1,0:T(8,128)(2,1)}, f32[12,768]{1,0:T...) custom-call(bf16[128,768]{1,0:T(8,128)(2,1)} %refs_17_.1, ...), custom_call_target="tpu_custom_call" | custom-call | flops 3000000000 | bytes 1000000 | tf_op jit(solution)/shard_map/pallas_call | solution.py:101
  10.3 8.3 %all-to-all-start = ((bf16[16,16,1664]{2,1,0:T(8,128)(2,1)}), bf16[16,16,1664]{2,1,0:T(8,128)(2,1)}, u32[]{:S(2)}, u32[]{:S(2)}) async-start(bf16[16,16,1664]{2,1,0:T(8,128)(2,1)} %bitcast.16), calls=%async_computation | async-start | bytes 1703936 | tf_op jit(solution)/shard_map/all_to_all | solution.py:955
  18.6 5.6 %shard_map.238 = (bf16[256,768]{1,0:T(8,128)(2,1)}, bf16[256,384]{1,0:T(8,128)(2,1)}, bf16[256,384]{1,0:T(8,128)(2,1)}, bf16[256,384]{1,0:T(8,128)(2,1)}, f32[6,256,256]{2,1,0:T(8,128)}) custom-call(bf16[128,768]{1,0:T(8,128)(2,1)} %refs_17_.1, bf16[128,768]{1,0:T(8,128)(2,1)} %collective-permute-done.refs_1_.refs_18_, f32[768]{0:T(1024)} %refs_2_.3, ...), custom_call_target="tpu_custom_call" | custom-call | flops 3000000000 | bytes 1000000 | tf_op jit(solution)/shard_map/pallas_call | solution.py:101
  24.2 15.6 %all-to-all-done = bf16[16,16,1664]{2,1,0:T(8,128)(2,1)} async-done(((bf16[16,16,1664]{2,1,0:T(8,128)(2,1)}), bf16[16,16,1664]{2,1,0:T(8,128)(2,1)}, u32[]{:S(2)}, u32[]{:S(2)}) %all-to-all-start) | async-done | bytes 852000 | tf_op jit(solution)/shard_map/all_to_all | solution.py:955
  39.8 9.3 %shard_map.239 = (bf16[256,1536]{1,0:T(8,128)(2,1)}, bf16[256,1536]{1,0:T(8,128)(2,1)}, bf16[256,768]{1,0:T(8,128)(2,1)}, bf16[256,4608]{1,0:T(8,128)(2,1)}, bf1...) custom-call(bf16[256,1664]{1,0:T(8,128)(2,1)} %bitcast.4.refs_0_.flat_own, ...), custom_call_target="tpu_custom_call" | custom-call | flops 6000000000 | bytes 1000000 | tf_op jit(solution)/shard_map/pallas_call | solution.py:101
  49.2 5.3 %all-to-all-start.1 = ((bf16[16,16,768]{2,1,0:T(8,128)(2,1)}), bf16[16,16,768]{2,1,0:T(8,128)(2,1)}, u32[]{:S(2)}, u32[]{:S(2)}) async-start(bf16[16,16,768]{2,1,0:T(8,128)(2,1)} %bitcast.18), calls=%async_computation.1 | async-start | bytes 786432 | tf_op jit(solution)/shard_map/all_to_all | solution.py:997
  54.8 8.9 %shard_map.240 = (f32[1,768,1536]{2,1,0:T(8,128)}, f32[1,1536,768]{2,1,0:T(8,128)}) custom-call(bf16[256,1664]{1,0:T(8,128)(2,1)} %bitcast.4.refs_0_.flat_own, bf16[256,768]{1,0:T(8,128)(2,1)} %get-tuple-element.100.sent_own, bf16[256,1536]{1,0:T(8,128)(2,1)} %get-tuple-element.101.hid_own, bf16[256,1536]{1,0:T(8,128)(2,1)} %get-tuple-element.102.pre_own, ...), custom_call_target="tpu_custom_call" | custom-call | flops 2415919104 | bytes 14000000 | tf_op jit(solution)/shard_map/pallas_call | solution.py:475
  63.7 4.1 %all-to-all-done.1 = bf16[16,16,768]{2,1,0:T(8,128)(2,1)} async-done(((bf16[16,16,768]{2,1,0:T(8,128)(2,1)}), bf16[16,16,768]{2,1,0:T(8,128)(2,1)}, u32[]{:S(2)}, u32[]{:S(2)}) %all-to-all-start.1) | async-done | bytes 393248 | tf_op jit(solution)/shard_map/all_to_all | solution.py:997
  68.3 3.8 %all-to-all-start.2 = ((bf16[16,16,768]{2,1,0:T(8,128)(2,1)}), bf16[16,16,768]{2,1,0:T(8,128)(2,1)S(1)}, u32[]{:S(2)}, u32[]{:S(2)}) async-start(bf16[16,16,768]{2,1,0:T(8,128)(2,1)} %bitcast.17), calls=%async_computation.2 | async-start | bytes 786432 | tf_op jit(solution)/shard_map/all_to_all | solution.py:1002
  73.0 8.3 %shard_map.241 = (bf16[512,384]{1,0:T(8,128)(2,1)}, bf16[512,384]{1,0:T(8,128)(2,1)}, bf16[512,384]{1,0:T(8,128)(2,1)}, bf16[512,384]{1,0:T(8,128)(2,1)}, bf16[5...) custom-call(bf16[256,768]{1,0:T(8,128)(2,1)} %bitcast.8.refs_0_, ...), custom_call_target="tpu_custom_call" | custom-call | flops 4000000000 | bytes 1000000 | tf_op jit(solution)/shard_map/pallas_call | solution.py:101
  81.3 1.9 %collective-permute-start.9 = (bf16[512,384]{1,0:T(8,128)(2,1)}, bf16[512,384]{1,0:T(8,128)(2,1)S(1)}, u32[]{:S(2)}, u32[]{:S(2)}) collective-permute-start(bf16[512,384]{1,0:T(8,128)(2,1)} %get-tuple-element.125), channel_id=1, source_target_pairs={{0,2},{2,0},{4,6},{6,4},{8,10},{10,8},{12,14},{14,12},{16,18},{18,... | collective-permute-start | bytes 1179656 | tf_op jit(solution)/shard_map/ppermute | solution.py:823
  83.4 1.5 collective-permute-start.14
  84.9 1.5 collective-permute-start.23
  87.5 5.6 %collective-permute-done.9 = bf16[512,384]{1,0:T(8,128)(2,1)S(1)} collective-permute-done((bf16[512,384]{1,0:T(8,128)(2,1)}, bf16[512,384]{1,0:T(8,128)(2,1)S(1)}, u32[]{:S(2)}, u32[]{:S(2)}) %collective-permute-start.9) | collective-permute-done | bytes 393248 | tf_op jit(solution)/shard_map/ppermute | solution.py:823
  94.2 1.5 collective-permute-start.10
  95.8 1.4 collective-permute-start.15
  97.3 1.5 collective-permute-start.24
  99.1 1.8 %collective-permute-done.10 = bf16[256,384]{1,0:T(8,128)(2,1)S(1)} collective-permute-done((bf16[256,384]{1,0:T(8,128)(2,1)S(1)}, bf16[256,384]{1,0:T(8,128)(2,1)S(1)}, u32[]{:S(2)}, u32[]{:S(2)}) %collective-permute-start.10) | collective-permute-done | bytes 196640 | tf_op jit(solution)/shard_map/ppermute | solution.py:823
  101.7 1.7 %collective-permute-start.16 = (bf16[128,384]{1,0:T(8,128)(2,1)S(1)}, bf16[128,384]{1,0:T(8,128)(2,1)S(1)}, u32[]{:S(2)}, u32[]{:S(2)}) collective-permute-start(bf16[128,384]{1,0:T(8,128)(2,1)S(1)} %add_convert_fusion.13), channel_id=1, source_target_pairs={{0,2},{2,0},{4,6},{6,4},{8,10},{10,8},{12,14},{14,12},{16,18},{18,... | collective-permute-start | bytes 294920 | tf_op jit(solution)/shard_map/ppermute | solution.py:823
  104.8 1.6 %collective-permute-done.16 = bf16[128,384]{1,0:T(8,128)(2,1)S(1)} collective-permute-done((bf16[128,384]{1,0:T(8,128)(2,1)S(1)}, bf16[128,384]{1,0:T(8,128)(2,1)S(1)}, u32[]{:S(2)}, u32[]{:S(2)}) %collective-permute-start.16) | collective-permute-done | bytes 98336 | tf_op jit(solution)/shard_map/ppermute | solution.py:823
  106.4 2.6 %collective-permute-start.17 = (bf16[128,384]{1,0:T(8,128)(2,1)S(1)}, bf16[128,384]{1,0:T(8,128)(2,1)S(1)}, u32[]{:S(2)}, u32[]{:S(2)}) collective-permute-start(bf16[128,384]{1,0:T(8,128)(2,1)S(1)} %add_convert_fusion.12), channel_id=1, source_target_pairs={{0,16},{2,18},{4,20},{6,22},{8,24},{10,26},{12,28},{14,30},{16,0},... | collective-permute-start | bytes 294920 | tf_op jit(solution)/shard_map/ppermute | solution.py:823
  109.1 1.8 %collective-permute-start.26 = (bf16[128,384]{1,0:T(8,128)(2,1)S(1)}, bf16[128,384]{1,0:T(8,128)(2,1)S(1)}, u32[]{:S(2)}, u32[]{:S(2)}) collective-permute-start(bf16[128,384]{1,0:T(8,128)(2,1)S(1)} %add_convert_fusion.8), channel_id=1, source_target_pairs={{0,16},{2,18},{4,20},{6,22},{8,24},{10,26},{12,28},{14,30},{16,0},... | collective-permute-start | bytes 294920 | tf_op jit(solution)/shard_map/ppermute | solution.py:823
  112.2 7.9 %collective-permute-done.26 = bf16[128,384]{1,0:T(8,128)(2,1)S(1)} collective-permute-done((bf16[128,384]{1,0:T(8,128)(2,1)S(1)}, bf16[128,384]{1,0:T(8,128)(2,1)S(1)}, u32[]{:S(2)}, u32[]{:S(2)}) %collective-permute-start.26) | collective-permute-done | bytes 98336 | tf_op jit(solution)/shard_map/ppermute | solution.py:823
  122.0 1.5 collective-permute-start.18
  124.9 1.5 %collective-permute-start.28 = (bf16[256,384]{1,0:T(8,128)(2,1)S(1)}, bf16[256,384]{1,0:T(8,128)(2,1)S(1)}, u32[]{:S(2)}, u32[]{:S(2)}) collective-permute-start(bf16[256,384]{1,0:T(8,128)(2,1)S(1)} %pad_maximum_fusion.5), channel_id=1, source_target_pairs={{0,2},{2,0},{4,6},{6,4},{8,10},{10,8},{12,14},{14,12},{16,18},{18,... | collective-permute-start | bytes 589832 | tf_op jit(solution)/shard_map/ppermute | solution.py:823
  126.4 2.1 %collective-permute-done.18 = bf16[176,384]{1,0:T(8,128)(2,1)S(1)} collective-permute-done((bf16[176,384]{1,0:T(8,128)(2,1)S(1)}, bf16[176,384]{1,0:T(8,128)(2,1)S(1)}, u32[]{:S(2)}, u32[]{:S(2)}) %collective-permute-start.18) | collective-permute-done | bytes 135200 | tf_op jit(solution)/shard_map/ppermute | solution.py:823
  130.8 3.5 %collective-permute-done.21 = bf16[256,384]{1,0:T(8,128)(2,1)S(1)} collective-permute-done((bf16[256,384]{1,0:T(8,128)(2,1)S(1)}, bf16[256,384]{1,0:T(8,128)(2,1)S(1)}, u32[]{:S(2)}, u32[]{:S(2)}) %collective-permute-start.21) | collective-permute-done | bytes 196640 | tf_op jit(solution)/shard_map/ppermute | solution.py:823
  135.5 1.6 %collective-permute-start.20 = (bf16[512,384]{1,0:T(8,128)(2,1)S(1)}, bf16[512,384]{1,0:T(8,128)(2,1)S(1)}, u32[]{:S(2)}, u32[]{:S(2)}) collective-permute-start(bf16[512,384]{1,0:T(8,128)(2,1)S(1)} %pad_maximum_fusion.refs_0_), channel_id=1, source_target_pairs={{0,2},{2,0},{4,6},{6,4},{8,10},{10,8},{12,14},{14,12},{16,18},{18,... | collective-permute-start | bytes 1179656 | tf_op jit(solution)/shard_map/ppermute | solution.py:823
  138.2 3.6 %shard_map.242 = (f32[768,768]{1,0:T(8,128)}, f32[768,768]{1,0:T(8,128)}, f32[768,768]{1,0:T(8,128)}, f32[768,768]{1,0:T(8,128)}) custom-call(bf16[512,384]{1,0:T(8,128)(2,1)S(1)} %pad_maximum_fusion.refs_0_, bf16[512,384]{1,0:T(8,128)(2,1)S(1)} %collective-permute-done.30.refs_1_, bf16[512,384]{1,0:T(8,128)(2,1)S(1)} %pad_maximum_fusion.1.refs_2_, ...), custom_call_target="tpu_custom_call" | custom-call | bytes 8000000 | tf_op jit(solution)/shard_map/pallas_call | solution.py:101
  141.9 4.1 %collective-permute-done.29.refs_2_ = bf16[512,384]{1,0:T(8,128)(2,1)S(1)} collective-permute-done((bf16[512,384]{1,0:T(8,128)(2,1)S(1)}, bf16[512,384]{1,0:T(8,128)(2,1)S(1)}, u32[]{:S(2)}, u32[]{:S(2)}) %collective-permute-start.29) | collective-permute-done | bytes 393248 | tf_op jit(solution)/shard_map/ppermute | solution.py:823
  147.4 2.2 %shard_map.243 = (f32[768,768]{1,0:T(8,128)}, f32[768,768]{1,0:T(8,128)}, f32[768,768]{1,0:T(8,128)}, f32[768,768]{1,0:T(8,128)}) custom-call(bf16[512,384]{1,0:T(8,128)(2,1)S(1)} %collective-permute-done.20.refs_0_, bf16[512,384]{1,0:T(8,128)(2,1)S(1)} %collective-permute-done.22.refs_1_, ...), custom_call_target="tpu_custom_call", output_to_operand_aliasing={{0}: (3, {}), {1}: (4, {}), {2}: (5, {}), {3}: (6, {})} | custom-call | bytes 8000000 | tf_op jit(solution)/shard_map/pallas_call | solution.py:101
  149.8 3.1 %shard_map.244 = (f32[768,768]{1,0:T(8,128)}, f32[768,768]{1,0:T(8,128)}, f32[768,768]{1,0:T(8,128)}, f32[768,768]{1,0:T(8,128)}, f32[768]{0:T(1024)}, /*index=5...) custom-call(bf16[512,384]{1,0:T(8,128)(2,1)S(1)} %collective-permute, ...), custom_call_target="tpu_custom_call", output_to_operand_aliasing={{0}: (5, {}), {1}: (6, {}), {2}: (7, {}), {3}: (8, {})} | custom-call | bytes 8000000 | tf_op jit(solution)/shard_map/pallas_call | solution.py:101
  (119 shorter events, 19.8 us)
Async XLA Ops:
  2.6 37.2 %collective-permute-start.2 = (bf16[768,1536]{1,0:T(8,128)(2,1)}, bf16[768,1536]{1,0:T(8,128)(2,1)}, u32[]{:S(2)}, u32[]{:S(2)}) collective-permute-start(bf16[768,1536]{1,0:T(8,128)(2,1)} %bitcast.19), channel_id=1, source_target_pairs={{0,1},{1,0},{2,3},{3,2},{4,5},{5,4},{6,7},{7,6},{8,9},{9,8},{10,11... | collective-permute-start | bytes 7077896 | tf_op jit(solution)/shard_map/ppermute | solution.py:818
  3.0 36.8 %collective-permute-start.3 = (bf16[1536,768]{1,0:T(8,128)(2,1)}, bf16[1536,768]{1,0:T(8,128)(2,1)}, u32[]{:S(2)}, u32[]{:S(2)}) collective-permute-start(bf16[1536,768]{1,0:T(8,128)(2,1)} %bitcast.21), channel_id=1, source_target_pairs={{0,1},{1,0},{2,3},{3,2},{4,5},{5,4},{6,7},{7,6},{8,9},{9,8},{10,11... | collective-permute-start | bytes 7077896 | tf_op jit(solution)/shard_map/ppermute | solution.py:818
  10.3 29.5 %all-to-all-start = ((bf16[16,16,1664]{2,1,0:T(8,128)(2,1)}), bf16[16,16,1664]{2,1,0:T(8,128)(2,1)}, u32[]{:S(2)}, u32[]{:S(2)}) async-start(bf16[16,16,1664]{2,1,0:T(8,128)(2,1)} %bitcast.16), calls=%async_computation | async-start | bytes 1703936 | tf_op jit(solution)/shard_map/all_to_all | solution.py:955
  49.2 5.6 %collective-permute-start.4 = (bf16[256,4608]{1,0:T(8,128)(2,1)}, bf16[256,4608]{1,0:T(8,128)(2,1)}, u32[]{:S(2)}, u32[]{:S(2)}) collective-permute-start(bf16[256,4608]{1,0:T(8,128)(2,1)} %get-tuple-element.103), channel_id=1, source_target_pairs={{0,1},{1,0},{2,3},{3,2},{4,5},{5,4},{6,7},{7,6},{8,9},{9,8},{10,11... | collective-permute-start | bytes 7077896 | tf_op jit(solution)/shard_map/ppermute | solution.py:818
  49.2 18.5 %all-to-all-start.1 = ((bf16[16,16,768]{2,1,0:T(8,128)(2,1)}), bf16[16,16,768]{2,1,0:T(8,128)(2,1)}, u32[]{:S(2)}, u32[]{:S(2)}) async-start(bf16[16,16,768]{2,1,0:T(8,128)(2,1)} %bitcast.18), calls=%async_computation.1 | async-start | bytes 786432 | tf_op jit(solution)/shard_map/all_to_all | solution.py:997
  54.5 17.6 %collective-permute-start.6 = (f32[128,768]{1,0:T(8,128)}, f32[128,768]{1,0:T(8,128)}, u32[]{:S(2)}, u32[]{:S(2)}) collective-permute-start(f32[128,768]{1,0:T(8,128)} %get-tuple-element.108.refs_4_), channel_id=1, source_target_pairs={{0,1},{1,0},{2,3},{3,2},{4,5},{5,4},{6,7},{7,6},{8,9},{9,8},{10,11... | collective-permute-start | bytes 1179656 | tf_op jit(solution)/shard_map/ppermute | solution.py:818
  67.7 4.4 %collective-permute-start.5 = (bf16[256,768]{1,0:T(8,128)(2,1)}, bf16[256,768]{1,0:T(8,128)(2,1)S(1)}, u32[]{:S(2)}, u32[]{:S(2)}) collective-permute-start(bf16[256,768]{1,0:T(8,128)(2,1)} %bitcast.8.refs_0_), channel_id=1, source_target_pairs={{0,1},{1,0},{2,3},{3,2},{4,5},{5,4},{6,7},{7,6},{8,9},{9,8},{10,11... | collective-permute-start | bytes 1179656 | tf_op jit(solution)/shard_map/ppermute | solution.py:818
  68.3 18.1 %all-to-all-start.2 = ((bf16[16,16,768]{2,1,0:T(8,128)(2,1)}), bf16[16,16,768]{2,1,0:T(8,128)(2,1)S(1)}, u32[]{:S(2)}, u32[]{:S(2)}) async-start(bf16[16,16,768]{2,1,0:T(8,128)(2,1)} %bitcast.17), calls=%async_computation.2 | async-start | bytes 786432 | tf_op jit(solution)/shard_map/all_to_all | solution.py:1002
  81.3 11.8 %collective-permute-start.9 = (bf16[512,384]{1,0:T(8,128)(2,1)}, bf16[512,384]{1,0:T(8,128)(2,1)S(1)}, u32[]{:S(2)}, u32[]{:S(2)}) collective-permute-start(bf16[512,384]{1,0:T(8,128)(2,1)} %get-tuple-element.125), channel_id=1, source_target_pairs={{0,2},{2,0},{4,6},{6,4},{8,10},{10,8},{12,14},{14,12},{16,18},{18,... | collective-permute-start | bytes 1179656 | tf_op jit(solution)/shard_map/ppermute | solution.py:823
  83.4 12.3 %collective-permute-start.14 = (bf16[512,384]{1,0:T(8,128)(2,1)}, bf16[512,384]{1,0:T(8,128)(2,1)S(1)}, u32[]{:S(2)}, u32[]{:S(2)}) collective-permute-start(bf16[512,384]{1,0:T(8,128)(2,1)} %get-tuple-element.128), channel_id=1, source_target_pairs={{0,4},{2,6},{4,0},{6,2},{8,12},{10,14},{12,8},{14,10},{16,20},{18,... | collective-permute-start | bytes 1179656 | tf_op jit(solution)/shard_map/ppermute | solution.py:823
  84.9 12.3 %collective-permute-start.23 = (bf16[512,384]{1,0:T(8,128)(2,1)}, bf16[512,384]{1,0:T(8,128)(2,1)S(1)}, u32[]{:S(2)}, u32[]{:S(2)}) collective-permute-start(bf16[512,384]{1,0:T(8,128)(2,1)} %get-tuple-element.130), channel_id=1, source_target_pairs={{0,8},{2,10},{4,12},{6,14},{8,0},{10,2},{12,4},{14,6},{16,24},{18,... | collective-permute-start | bytes 1179656 | tf_op jit(solution)/shard_map/ppermute | solution.py:823
  86.4 12.5 %collective-permute-start.34 = (bf16[128,768]{1,0:T(8,128)(2,1)}, bf16[128,768]{1,0:T(8,128)(2,1)S(1)}, u32[]{:S(2)}, u32[]{:S(2)}) collective-permute-start(bf16[128,768]{1,0:T(8,128)(2,1)} %get-tuple-element.139), channel_id=1, source_target_pairs={{0,1},{1,0},{2,3},{3,2},{4,5},{5,4},{6,7},{7,6},{8,9},{9,8},{10,11... | collective-permute-start | bytes 589832 | tf_op jit(solution)/shard_map/ppermute | solution.py:818
  94.2 6.6 %collective-permute-start.10 = (bf16[256,384]{1,0:T(8,128)(2,1)S(1)}, bf16[256,384]{1,0:T(8,128)(2,1)S(1)}, u32[]{:S(2)}, u32[]{:S(2)}) collective-permute-start(bf16[256,384]{1,0:T(8,128)(2,1)S(1)} %get-tuple-element.170), channel_id=1, source_target_pairs={{0,4},{2,6},{4,0},{6,2},{8,12},{10,14},{12,8},{14,10},{16,20},{18,... | collective-permute-start | bytes 589832 | tf_op jit(solution)/shard_map/ppermute | solution.py:823
  95.8 5.9 %collective-permute-start.15 = (bf16[256,384]{1,0:T(8,128)(2,1)S(1)}, bf16[256,384]{1,0:T(8,128)(2,1)S(1)}, u32[]{:S(2)}, u32[]{:S(2)}) collective-permute-start(bf16[256,384]{1,0:T(8,128)(2,1)S(1)} %get-tuple-element.168), channel_id=1, source_target_pairs={{0,8},{2,10},{4,12},{6,14},{8,0},{10,2},{12,4},{14,6},{16,24},{18,... | collective-permute-start | bytes 589832 | tf_op jit(solution)/shard_map/ppermute | solution.py:823
  97.3 6.2 %collective-permute-start.24 = (bf16[256,384]{1,0:T(8,128)(2,1)S(1)}, bf16[256,384]{1,0:T(8,128)(2,1)S(1)}, u32[]{:S(2)}, u32[]{:S(2)}) collective-permute-start(bf16[256,384]{1,0:T(8,128)(2,1)S(1)} %get-tuple-element.166), channel_id=1, source_target_pairs={{0,2},{2,0},{4,6},{6,4},{8,10},{10,8},{12,14},{14,12},{16,18},{18,... | collective-permute-start | bytes 589832 | tf_op jit(solution)/shard_map/ppermute | solution.py:823
  100.9 10.0 %collective-permute-start.11 = (bf16[176,384]{1,0:T(8,128)(2,1)S(1)}, bf16[176,384]{1,0:T(8,128)(2,1)S(1)}, u32[]{:S(2)}, u32[]{:S(2)}) collective-permute-start(bf16[176,384]{1,0:T(8,128)(2,1)S(1)} %pad_maximum_fusion.6), channel_id=1, source_target_pairs={{0,8},{2,10},{4,12},{6,14},{8,0},{10,2},{12,4},{14,6},{16,24},{18,... | collective-permute-start | bytes 405512 | tf_op jit(solution)/shard_map/ppermute | solution.py:823
  101.7 4.7 %collective-permute-start.16 = (bf16[128,384]{1,0:T(8,128)(2,1)S(1)}, bf16[128,384]{1,0:T(8,128)(2,1)S(1)}, u32[]{:S(2)}, u32[]{:S(2)}) collective-permute-start(bf16[128,384]{1,0:T(8,128)(2,1)S(1)} %add_convert_fusion.13), channel_id=1, source_target_pairs={{0,2},{2,0},{4,6},{6,4},{8,10},{10,8},{12,14},{14,12},{16,18},{18,... | collective-permute-start | bytes 294920 | tf_op jit(solution)/shard_map/ppermute | solution.py:823
  103.5 5.5 %collective-permute-start.25 = (bf16[128,384]{1,0:T(8,128)(2,1)S(1)}, bf16[128,384]{1,0:T(8,128)(2,1)S(1)}, u32[]{:S(2)}, u32[]{:S(2)}) collective-permute-start(bf16[128,384]{1,0:T(8,128)(2,1)S(1)} %add_convert_fusion.9), channel_id=1, source_target_pairs={{0,4},{2,6},{4,0},{6,2},{8,12},{10,14},{12,8},{14,10},{16,20},{18,... | collective-permute-start | bytes 294920 | tf_op jit(solution)/shard_map/ppermute | solution.py:823
  106.4 14.8 %collective-permute-start.17 = (bf16[128,384]{1,0:T(8,128)(2,1)S(1)}, bf16[128,384]{1,0:T(8,128)(2,1)S(1)}, u32[]{:S(2)}, u32[]{:S(2)}) collective-permute-start(bf16[128,384]{1,0:T(8,128)(2,1)S(1)} %add_convert_fusion.12), channel_id=1, source_target_pairs={{0,16},{2,18},{4,20},{6,22},{8,24},{10,26},{12,28},{14,30},{16,0},... | collective-permute-start | bytes 294920 | tf_op jit(solution)/shard_map/ppermute | solution.py:823
  109.1 11.1 %collective-permute-start.26 = (bf16[128,384]{1,0:T(8,128)(2,1)S(1)}, bf16[128,384]{1,0:T(8,128)(2,1)S(1)}, u32[]{:S(2)}, u32[]{:S(2)}) collective-permute-start(bf16[128,384]{1,0:T(8,128)(2,1)S(1)} %add_convert_fusion.8), channel_id=1, source_target_pairs={{0,16},{2,18},{4,20},{6,22},{8,24},{10,26},{12,28},{14,30},{16,0},... | collective-permute-start | bytes 294920 | tf_op jit(solution)/shard_map/ppermute | solution.py:823
  111.0 10.9 %collective-permute-start.12 = (bf16[176,384]{1,0:T(8,128)(2,1)S(1)}, bf16[176,384]{1,0:T(8,128)(2,1)S(1)}, u32[]{:S(2)}, u32[]{:S(2)}) collective-permute-start(bf16[176,384]{1,0:T(8,128)(2,1)S(1)} %pad_maximum_fusion.7), channel_id=1, source_target_pairs={{0,16},{2,18},{4,20},{6,22},{8,24},{10,26},{12,28},{14,30},{16,0},... | collective-permute-start | bytes 405512 | tf_op jit(solution)/shard_map/ppermute | solution.py:823
  120.2 4.7 %collective-permute-start.27 = (bf16[128,384]{1,0:T(8,128)(2,1)S(1)}, bf16[128,384]{1,0:T(8,128)(2,1)S(1)}, u32[]{:S(2)}, u32[]{:S(2)}) collective-permute-start(bf16[128,384]{1,0:T(8,128)(2,1)S(1)} %add_convert_fusion.7), channel_id=1, source_target_pairs={{0,4},{2,6},{4,0},{6,2},{8,12},{10,14},{12,8},{14,10},{16,20},{18,... | collective-permute-start | bytes 294920 | tf_op jit(solution)/shard_map/ppermute | solution.py:823
  122.0 6.6 %collective-permute-start.18 = (bf16[176,384]{1,0:T(8,128)(2,1)S(1)}, bf16[176,384]{1,0:T(8,128)(2,1)S(1)}, u32[]{:S(2)}, u32[]{:S(2)}) collective-permute-start(bf16[176,384]{1,0:T(8,128)(2,1)S(1)} %pad_maximum_fusion.8), channel_id=1, source_target_pairs={{0,2},{2,0},{4,6},{6,4},{8,10},{10,8},{12,14},{14,12},{16,18},{18,... | collective-permute-start | bytes 405512 | tf_op jit(solution)/shard_map/ppermute | solution.py:823
  123.5 5.3 %collective-permute-start.13 = (bf16[128,384]{1,0:T(8,128)(2,1)S(1)}, bf16[128,384]{1,0:T(8,128)(2,1)S(1)}, u32[]{:S(2)}, u32[]{:S(2)}) collective-permute-start(bf16[128,384]{1,0:T(8,128)(2,1)S(1)} %add_convert_fusion.15), channel_id=1, source_target_pairs={{0,8},{2,10},{4,12},{6,14},{8,0},{10,2},{12,4},{14,6},{16,24},{18,... | collective-permute-start | bytes 294920 | tf_op jit(solution)/shard_map/ppermute | solution.py:823
  124.9 5.8 %collective-permute-start.28 = (bf16[256,384]{1,0:T(8,128)(2,1)S(1)}, bf16[256,384]{1,0:T(8,128)(2,1)S(1)}, u32[]{:S(2)}, u32[]{:S(2)}) collective-permute-start(bf16[256,384]{1,0:T(8,128)(2,1)S(1)} %pad_maximum_fusion.5), channel_id=1, source_target_pairs={{0,2},{2,0},{4,6},{6,4},{8,10},{10,8},{12,14},{14,12},{16,18},{18,... | collective-permute-start | bytes 589832 | tf_op jit(solution)/shard_map/ppermute | solution.py:823
  128.6 5.7 %collective-permute-start.21 = (bf16[256,384]{1,0:T(8,128)(2,1)S(1)}, bf16[256,384]{1,0:T(8,128)(2,1)S(1)}, u32[]{:S(2)}, u32[]{:S(2)}) collective-permute-start(bf16[256,384]{1,0:T(8,128)(2,1)S(1)} %pad_maximum_fusion.4), channel_id=1, source_target_pairs={{0,8},{2,10},{4,12},{6,14},{8,0},{10,2},{12,4},{14,6},{16,24},{18,... | collective-permute-start | bytes 589832 | tf_op jit(solution)/shard_map/ppermute | solution.py:823
  128.8 6.4 %collective-permute-start.19 = (bf16[304,384]{1,0:T(8,128)(2,1)S(1)}, bf16[304,384]{1,0:T(8,128)(2,1)S(1)}, u32[]{:S(2)}, u32[]{:S(2)}) collective-permute-start(bf16[304,384]{1,0:T(8,128)(2,1)S(1)} %pad_maximum_fusion.3), channel_id=1, source_target_pairs={{0,4},{2,6},{4,0},{6,2},{8,12},{10,14},{12,8},{14,10},{16,20},{18,... | collective-permute-start | bytes 700424 | tf_op jit(solution)/shard_map/ppermute | solution.py:823
  130.8 4.7 %collective-permute-start.32 = (bf16[512,384]{1,0:T(8,128)(2,1)S(1)}, bf16[512,384]{1,0:T(8,128)(2,1)S(1)}, u32[]{:S(2)}, u32[]{:S(2)}) collective-permute-start(bf16[512,384]{1,0:T(8,128)(2,1)S(1)} %pad_maximum_fusion.2.refs_4_), channel_id=1, source_target_pairs={{0,1},{1,0},{2,3},{3,2},{4,5},{5,4},{6,7},{7,6},{8,9},{9,8},{10,11... | collective-permute-start | bytes 1179656 | tf_op jit(solution)/shard_map/ppermute | solution.py:818
  134.5 11.5 %collective-permute-start.29 = (bf16[512,384]{1,0:T(8,128)(2,1)S(1)}, bf16[512,384]{1,0:T(8,128)(2,1)S(1)}, u32[]{:S(2)}, u32[]{:S(2)}) collective-permute-start(bf16[512,384]{1,0:T(8,128)(2,1)S(1)} %pad_maximum_fusion.2.refs_4_), channel_id=1, source_target_pairs={{0,8},{2,10},{4,12},{6,14},{8,0},{10,2},{12,4},{14,6},{16,24},{18,... | collective-permute-start | bytes 1179656 | tf_op jit(solution)/shard_map/ppermute | solution.py:823
  134.6 11.4 %collective-permute-start.22 = (bf16[512,384]{1,0:T(8,128)(2,1)S(1)}, bf16[512,384]{1,0:T(8,128)(2,1)S(1)}, u32[]{:S(2)}, u32[]{:S(2)}) collective-permute-start(bf16[512,384]{1,0:T(8,128)(2,1)S(1)} %pad_maximum_fusion.1.refs_2_), channel_id=1, source_target_pairs={{0,4},{2,6},{4,0},{6,2},{8,12},{10,14},{12,8},{14,10},{16,20},{18,... | collective-permute-start | bytes 1179656 | tf_op jit(solution)/shard_map/ppermute | solution.py:823
  135.5 11.5 %collective-permute-start.20 = (bf16[512,384]{1,0:T(8,128)(2,1)S(1)}, bf16[512,384]{1,0:T(8,128)(2,1)S(1)}, u32[]{:S(2)}, u32[]{:S(2)}) collective-permute-start(bf16[512,384]{1,0:T(8,128)(2,1)S(1)} %pad_maximum_fusion.refs_0_), channel_id=1, source_target_pairs={{0,2},{2,0},{4,6},{6,4},{8,10},{10,8},{12,14},{14,12},{16,18},{18,... | collective-permute-start | bytes 1179656 | tf_op jit(solution)/shard_map/ppermute | solution.py:823
  137.1 4.8 %collective-permute-start.33 = (f32[48,384]{1,0:T(8,128)S(1)}, f32[48,384]{1,0:T(8,128)S(1)}, u32[]{:S(2)}, u32[]{:S(2)}) collective-permute-start(f32[48,384]{1,0:T(8,128)S(1)} %convert_add_fusion.refs_3_), channel_id=1, source_target_pairs={{0,1},{1,0},{2,3},{3,2},{4,5},{5,4},{6,7},{7,6},{8,9},{9,8},{10,11... | collective-permute-start | bytes 221192 | tf_op jit(solution)/shard_map/ppermute | solution.py:818
  (23 other events, 169.6 us)

commit v5 on v4

--- a/solution.py
+++ b/solution.py
@@ -511,17 +511,16 @@
     return grad_middle, grad * scaled
 
 
-def place_of(target, order):
-    relative = jnp.bitwise_xor(target, lax.axis_index("expert"))
-    place = 0
-    for bit in order:
-        place = place * 2 + jnp.bitwise_and(jnp.right_shift(relative, bit), 1)
-    return place
-
-
-def chunk_place(chunk, order, levels):
-    target = sum((((chunk >> (levels - 1 - k)) & 1) << bit) for k, bit in enumerate(order[:levels]))
-    return place_of(target, order[:levels])
+def bit_of(step, other=0):
+    return jnp.where(lax.axis_index("ffn") == other, step[0], step[1])
+
+
+def chunk_place(chunk, order, levels, other=0):
+    chip = lax.axis_index("expert")
+    mine = 0
+    for step in order[:levels]:
+        mine = mine * 2 + jnp.bitwise_and(jnp.right_shift(chip, bit_of(step, other)), 1)
+    return jnp.bitwise_xor(mine, chunk)
 
 
 def small_rows(experts):
@@ -748,27 +747,30 @@
     ]
     writes = []
     for p, order in enumerate(orders):
-        for i in range(len(sides)):
-            wait(len(sides) * p + i)
-        for low in range(half):
-            place = jnp.bitwise_and(chunk_place(low, order, levels), half - 1)
+        for i, side in enumerate(sides):
+            n = len(sides) * p + i
+            wait(n)
+            bit = jnp.bitwise_and(jnp.right_shift(mine, bit_of(order[0], side)), 1)
+            if upper:
+                bit = 1 - bit
+            first = pl.multiple_of(p * third + bit * span, span)
+            places = [
+                jnp.bitwise_and(chunk_place(low, order, levels, side), half - 1)
+                for low in range(half)
+            ]
             for matrix in range(4):
-                at = pl.ds(pl.multiple_of((place * 4 + matrix) * height, height), height)
-                to = pl.ds(low * height, height)
-                for i in range(len(sides)):
-                    lanes = columns[i] if len(sides) == 2 else slice(None)
-                    wide[p, matrix, to, lanes] = arrays[len(sides) * p + i][at, :].astype(F32)
-        bit = jnp.bitwise_and(jnp.right_shift(mine, order[0]), 1)
-        if upper:
-            bit = 1 - bit
-        first = pl.multiple_of(p * third + bit * span, span)
-        for matrix in range(4):
-            target = outs[matrix].at[pl.ds(first, span), :]
-            if len(sides) == 1:
-                target = outs[matrix].at[pl.ds(first, span), columns[0]]
-            write = pltpu.make_async_copy(wide.at[p, matrix], target, sems.at[4 * p + matrix])
-            write.start()
-            writes.append(write)
+                for low in range(half):
+                    at = pl.multiple_of((places[low] * 4 + matrix) * height, height)
+                    wide[n, matrix, pl.ds(low * height, height)] = arrays[n][
+                        pl.ds(at, height), :
+                    ].astype(F32)
+                write = pltpu.make_async_copy(
+                    wide.at[n, matrix],
+                    outs[matrix].at[pl.ds(first, span), columns[i]],
+                    sems.at[4 * n + matrix],
+                )
+                write.start()
+                writes.append(write)
     if last is not None:
         at = small_rows(experts)
         mine, other = small_own_ref[...], small_other_ref[...]
@@ -798,7 +800,6 @@
         last = (experts, heads)
     first = len(modes)
     modes += "r" * len(earlier)
-    columns = width * len(sides) // 2
     return call(
         functools.partial(assemble_kernel, orders, levels, sides, bool(earlier), last),
         [((width, width), F32)] * 4 + tail,
@@ -807,8 +808,8 @@
         vmem=16,
         aliases={first + i: i for i in range(len(earlier))},
         scratch=[
-            pltpu.VMEM((len(orders), 4, width // 6, columns), F32),
-            pltpu.SemaphoreType.DMA((4 * len(orders),)),
+            pltpu.VMEM((len(arrays), 4, width // 6, width // 2), F32),
+            pltpu.SemaphoreType.DMA((4 * len(arrays),)),
         ],
         nbytes=8000000,
     )
@@ -818,9 +819,12 @@
     return lax.ppermute(x, "ffn", [(0, 1), (1, 0)])
 
 
-def flip(x, bit):
-    peers = lax.axis_size("expert")
-    return lax.ppermute(x, "expert", [(i, i ^ (1 << bit)) for i in range(peers)])
+def flip(x, step):
+    pairs = []
+    for chip in range(lax.axis_size("expert")):
+        for core in range(2):
+            pairs.append((chip * 2 + core, (chip ^ (1 << step[core])) * 2 + core))
+    return lax.ppermute(x, ("expert", "ffn"), pairs)
 
 
 def add_low(left, right):
@@ -829,22 +833,25 @@
 
 def sum_over_chips(keeps, sends, orders, levels, small, beside):
     count = len(orders[0])
-    todo = set(orders[0])
+    todo = [set(step[core] for step in orders[0]) for core in range(2)]
     ridden = set()
 
     def exchange(phase, x, bit):
         nonlocal small
-        if bit not in todo or phase in ridden or phase < 2 or phase > 2 * count - 3:
+        fresh = all(bit[core] in todo[core] for core in range(2))
+        if not fresh or phase in ridden or phase < 2 or phase > 2 * count - 3:
             return flip(x, bit)
-        todo.discard(bit)
+        for core in range(2):
+            todo[core].discard(bit[core])
         ridden.add(phase)
-        got = flip(jnp.concatenate([x, small.astype(BF16)]), bit)
+        sent = small.astype(BF16)
+        got = flip(jnp.concatenate([x, sent]), bit)
         rows = x.shape[0]
-        small = small.astype(F32) + got[rows:].astype(F32)
+        small = sent.astype(F32) + got[rows:].astype(F32)
         return got[:rows]
 
     def mine(bit):
-        return (lax.axis_index("expert") >> bit) & 1
+        return (lax.axis_index("expert") >> bit_of(bit)) & 1
 
     whole = [None] * len(orders)
     for k in range(count - 1):
@@ -879,8 +886,9 @@
                     jnp.concatenate([got[p], x]),
                     jnp.concatenate([x, got[p]]),
                 )
-    for bit in sorted(todo):
-        small = small.astype(F32) + flip(small, bit).astype(F32)
+    for bit in zip(sorted(todo[0]), sorted(todo[1])):
+        sent = small.astype(BF16)
+        small = sent.astype(F32) + flip(sent, bit).astype(F32)
     return whole, got, small, beside
 
 
@@ -1002,8 +1010,12 @@
     produced_returned = lax.all_to_all(produced, "expert", 0, 0, tiled=True)
     bits = experts.bit_length() - 1
     levels = min(bits - 1, 3)
-    rest = list(range(3, bits))
-    orders = [[0, 1, 2] + rest, [1, 2, 0] + rest, [2, 0, 1] + rest]
+    rest = [(bit, bit) for bit in range(3, bits)]
+    orders = [
+        [(0, 2), (1, 0), (2, 1)] + rest,
+        [(1, 0), (2, 1), (0, 2)] + rest,
+        [(2, 1), (0, 2), (1, 0)] + rest,
+    ]
     third = 4 * width // 3
     *halves, grad_middle, small, input_own, input_other = call(
         functools.partial(backward_kernel, heads, orders, levels),

time: 154 us -> 152 us (0.987)
  waiting for transfers between devices: 52.1 us -> 48 us
  starting transfers between devices: 46.4 us -> 48.7 us
    ppermute x21, waiting for transfers between devices: 30.9 us -> 26.9 us  [flip(): return lax.ppermute(x, ('expert', 'ffn'), pairs)]
  transfers between devices with their start and end apart: 41 -> 41, of which waited for: 17 -> 15; matrix products, arithmetic and copies ran while one was open for 3% -> 3% of each run, Pallas kernels for 23% -> 24%
where the time goes in v5:
time: 152 us; the launch traced here: 151 us
  starting transfers between devices  48.7 us (32%)
  Pallas kernels  48.1 us (32%)
  waiting for transfers between devices  48 us (32%)
  other arithmetic  3.03 us (2%)
    pallas_call x7, Pallas kernels, call(): pl.pallas_call(kernel, out_shape=[jax.ShapeDtypeStruct(s, d) for s, d in...  39.3 us
    ppermute x21, starting transfers between devices, flip(): return lax.ppermute(x, ('expert', 'ffn'), pairs)  27.3 us
    ppermute x21, waiting for transfers between devices, flip(): return lax.ppermute(x, ('expert', 'ffn'), pairs)  26.9 us
    all_to_all x1, waiting for transfers between devices, shards(): arrived = lax.all_to_all(outgoing, 'expert', 0, 0, tiled=True)  15.6 us
    pallas_call x1, Pallas kernels, expert_weights(): pl.pallas_call(expert_weights_kernel, grid=(steps,), out_shape=[jax.Shape...  8.89 us
    all_to_all x1, starting transfers between devices, shards(): arrived = lax.all_to_all(outgoing, 'expert', 0, 0, tiled=True)  8.3 us
    all_to_all x1, starting transfers between devices, shards(): grad_returned = lax.all_to_all(grad_slots, 'expert', 0, 0, tiled=True)  5.26 us
    all_to_all x1, waiting for transfers between devices, shards(): grad_returned = lax.all_to_all(grad_slots, 'expert', 0, 0, tiled=True)  4.08 us
  transfers between devices with their start and end apart: 41, of which 15 were waited for; matrix products, arithmetic and copies ran while one was open for 3% of the time, Pallas kernels for 24%

profile of v5, /device:TPU:0, one launch (start us, length us, event | category | flops | bytes accessed | tf_op | source)
XLA Modules:
  0.0 151.2 jit_solution(7513772327887758481)
XLA Ops:
  1.2 1.3 collective-permute-done.1.refs_4_
  3.1 7.2 %shard_map.237 = (f32[128,768]{1,0:T(8,128)}, f32[128,128]{1,0:T(8,128)}, bf16[256,1664]{1,0:T(8,128)(2,1)}, bf16[128,768]{1,0:T(8,128)(2,1)}, f32[12,768]{1,0:T...) custom-call(bf16[128,768]{1,0:T(8,128)(2,1)} %refs_17_.1, ...), custom_call_target="tpu_custom_call" | custom-call | flops 3000000000 | bytes 1000000 | tf_op jit(solution)/shard_map/pallas_call | solution.py:101
  10.3 8.3 %all-to-all-start = ((bf16[16,16,1664]{2,1,0:T(8,128)(2,1)}), bf16[16,16,1664]{2,1,0:T(8,128)(2,1)}, u32[]{:S(2)}, u32[]{:S(2)}) async-start(bf16[16,16,1664]{2,1,0:T(8,128)(2,1)} %bitcast.16), calls=%async_computation | async-start | bytes 1703936 | tf_op jit(solution)/shard_map/all_to_all | solution.py:963
  18.6 5.6 %shard_map.238 = (bf16[256,768]{1,0:T(8,128)(2,1)}, bf16[256,384]{1,0:T(8,128)(2,1)}, bf16[256,384]{1,0:T(8,128)(2,1)}, bf16[256,384]{1,0:T(8,128)(2,1)}, f32[6,256,256]{2,1,0:T(8,128)}) custom-call(bf16[128,768]{1,0:T(8,128)(2,1)} %refs_17_.1, bf16[128,768]{1,0:T(8,128)(2,1)} %collective-permute-done.refs_1_.refs_18_, f32[768]{0:T(1024)} %refs_2_.3, ...), custom_call_target="tpu_custom_call" | custom-call | flops 3000000000 | bytes 1000000 | tf_op jit(solution)/shard_map/pallas_call | solution.py:101
  24.2 15.6 %all-to-all-done = bf16[16,16,1664]{2,1,0:T(8,128)(2,1)} async-done(((bf16[16,16,1664]{2,1,0:T(8,128)(2,1)}), bf16[16,16,1664]{2,1,0:T(8,128)(2,1)}, u32[]{:S(2)}, u32[]{:S(2)}) %all-to-all-start) | async-done | bytes 852000 | tf_op jit(solution)/shard_map/all_to_all | solution.py:963
  39.8 9.3 %shard_map.239 = (bf16[256,1536]{1,0:T(8,128)(2,1)}, bf16[256,1536]{1,0:T(8,128)(2,1)}, bf16[256,768]{1,0:T(8,128)(2,1)}, bf16[256,4608]{1,0:T(8,128)(2,1)}, bf1...) custom-call(bf16[256,1664]{1,0:T(8,128)(2,1)} %bitcast.4.refs_0_.flat_own, ...), custom_call_target="tpu_custom_call" | custom-call | flops 6000000000 | bytes 1000000 | tf_op jit(solution)/shard_map/pallas_call | solution.py:101
  49.2 5.3 %all-to-all-start.1 = ((bf16[16,16,768]{2,1,0:T(8,128)(2,1)}), bf16[16,16,768]{2,1,0:T(8,128)(2,1)}, u32[]{:S(2)}, u32[]{:S(2)}) async-start(bf16[16,16,768]{2,1,0:T(8,128)(2,1)} %bitcast.18), calls=%async_computation.1 | async-start | bytes 786432 | tf_op jit(solution)/shard_map/all_to_all | solution.py:1005
  54.8 8.9 %shard_map.240 = (f32[1,768,1536]{2,1,0:T(8,128)}, f32[1,1536,768]{2,1,0:T(8,128)}) custom-call(bf16[256,1664]{1,0:T(8,128)(2,1)} %bitcast.4.refs_0_.flat_own, bf16[256,768]{1,0:T(8,128)(2,1)} %get-tuple-element.100.sent_own, bf16[256,1536]{1,0:T(8,128)(2,1)} %get-tuple-element.101.hid_own, bf16[256,1536]{1,0:T(8,128)(2,1)} %get-tuple-element.102.pre_own, ...), custom_call_target="tpu_custom_call" | custom-call | flops 2415919104 | bytes 14000000 | tf_op jit(solution)/shard_map/pallas_call | solution.py:475
  63.7 4.1 %all-to-all-done.1 = bf16[16,16,768]{2,1,0:T(8,128)(2,1)} async-done(((bf16[16,16,768]{2,1,0:T(8,128)(2,1)}), bf16[16,16,768]{2,1,0:T(8,128)(2,1)}, u32[]{:S(2)}, u32[]{:S(2)}) %all-to-all-start.1) | async-done | bytes 393248 | tf_op jit(solution)/shard_map/all_to_all | solution.py:1005
  68.3 3.8 %all-to-all-start.2 = ((bf16[16,16,768]{2,1,0:T(8,128)(2,1)}), bf16[16,16,768]{2,1,0:T(8,128)(2,1)S(1)}, u32[]{:S(2)}, u32[]{:S(2)}) async-start(bf16[16,16,768]{2,1,0:T(8,128)(2,1)} %bitcast.17), calls=%async_computation.2 | async-start | bytes 786432 | tf_op jit(solution)/shard_map/all_to_all | solution.py:1010
  73.0 8.3 %shard_map.241 = (bf16[512,384]{1,0:T(8,128)(2,1)}, bf16[512,384]{1,0:T(8,128)(2,1)}, bf16[512,384]{1,0:T(8,128)(2,1)}, bf16[512,384]{1,0:T(8,128)(2,1)}, bf16[5...) custom-call(bf16[256,768]{1,0:T(8,128)(2,1)} %bitcast.8.refs_0_, ...), custom_call_target="tpu_custom_call" | custom-call | flops 4000000000 | bytes 1000000 | tf_op jit(solution)/shard_map/pallas_call | solution.py:101
  81.3 1.9 %collective-permute-start.9 = (bf16[512,384]{1,0:T(8,128)(2,1)}, bf16[512,384]{1,0:T(8,128)(2,1)S(1)}, u32[]{:S(2)}, u32[]{:S(2)}) collective-permute-start(bf16[512,384]{1,0:T(8,128)(2,1)} %get-tuple-element.125), channel_id=1, source_target_pairs={{0,2},{1,9},{2,0},{3,11},{4,6},{5,13},{6,4},{7,15},{8,10},{9,1},{1... | collective-permute-start | bytes 1179656 | tf_op jit(solution)/shard_map/ppermute | solution.py:827
  83.4 1.5 %collective-permute-start.14 = (bf16[512,384]{1,0:T(8,128)(2,1)}, bf16[512,384]{1,0:T(8,128)(2,1)S(1)}, u32[]{:S(2)}, u32[]{:S(2)}) collective-permute-start(bf16[512,384]{1,0:T(8,128)(2,1)} %get-tuple-element.128), channel_id=1, source_target_pairs={{0,4},{1,3},{2,6},{3,1},{4,0},{5,7},{6,2},{7,5},{8,12},{9,11},{10,... | collective-permute-start | bytes 1179656 | tf_op jit(solution)/shard_map/ppermute | solution.py:827
  84.9 1.5 collective-permute-start.23
  87.5 5.2 %collective-permute-done.9 = bf16[512,384]{1,0:T(8,128)(2,1)S(1)} collective-permute-done((bf16[512,384]{1,0:T(8,128)(2,1)}, bf16[512,384]{1,0:T(8,128)(2,1)S(1)}, u32[]{:S(2)}, u32[]{:S(2)}) %collective-permute-start.9) | collective-permute-done | bytes 393248 | tf_op jit(solution)/shard_map/ppermute | solution.py:827
  93.9 2.2 %collective-permute-start.10 = (bf16[256,384]{1,0:T(8,128)(2,1)S(1)}, bf16[256,384]{1,0:T(8,128)(2,1)S(1)}, u32[]{:S(2)}, u32[]{:S(2)}) collective-permute-start(bf16[256,384]{1,0:T(8,128)(2,1)S(1)} %get-tuple-element.170), channel_id=1, source_target_pairs={{0,4},{1,3},{2,6},{3,1},{4,0},{5,7},{6,2},{7,5},{8,12},{9,11},{10,... | collective-permute-start | bytes 589832 | tf_op jit(solution)/shard_map/ppermute | solution.py:827
  96.2 1.6 %collective-permute-start.15 = (bf16[256,384]{1,0:T(8,128)(2,1)S(1)}, bf16[256,384]{1,0:T(8,128)(2,1)S(1)}, u32[]{:S(2)}, u32[]{:S(2)}) collective-permute-start(bf16[256,384]{1,0:T(8,128)(2,1)S(1)} %get-tuple-element.168), channel_id=1, source_target_pairs={{0,8},{1,5},{2,10},{3,7},{4,12},{5,1},{6,14},{7,3},{8,0},{9,13},{1... | collective-permute-start | bytes 589832 | tf_op jit(solution)/shard_map/ppermute | solution.py:827
  97.9 1.5 %collective-permute-start.24 = (bf16[256,384]{1,0:T(8,128)(2,1)S(1)}, bf16[256,384]{1,0:T(8,128)(2,1)S(1)}, u32[]{:S(2)}, u32[]{:S(2)}) collective-permute-start(bf16[256,384]{1,0:T(8,128)(2,1)S(1)} %get-tuple-element.166), channel_id=1, source_target_pairs={{0,2},{1,9},{2,0},{3,11},{4,6},{5,13},{6,4},{7,15},{8,10},{9,1},{1... | collective-permute-start | bytes 589832 | tf_op jit(solution)/shard_map/ppermute | solution.py:827
  99.6 2.2 %collective-permute-done.10 = bf16[256,384]{1,0:T(8,128)(2,1)S(1)} collective-permute-done((bf16[256,384]{1,0:T(8,128)(2,1)S(1)}, bf16[256,384]{1,0:T(8,128)(2,1)S(1)}, u32[]{:S(2)}, u32[]{:S(2)}) %collective-permute-start.10) | collective-permute-done | bytes 196640 | tf_op jit(solution)/shard_map/ppermute | solution.py:827
  101.9 1.9 %collective-permute-start.11 = (bf16[176,384]{1,0:T(8,128)(2,1)S(1)}, bf16[176,384]{1,0:T(8,128)(2,1)S(1)}, u32[]{:S(2)}, u32[]{:S(2)}) collective-permute-start(bf16[176,384]{1,0:T(8,128)(2,1)S(1)} %pad_maximum_fusion.6), channel_id=1, source_target_pairs={{0,8},{1,5},{2,10},{3,7},{4,12},{5,1},{6,14},{7,3},{8,0},{9,13},{1... | collective-permute-start | bytes 405512 | tf_op jit(solution)/shard_map/ppermute | solution.py:827
  105.0 1.4 collective-permute-start.25
  106.4 2.1 %collective-permute-done.16 = bf16[128,384]{1,0:T(8,128)(2,1)S(1)} collective-permute-done((bf16[128,384]{1,0:T(8,128)(2,1)S(1)}, bf16[128,384]{1,0:T(8,128)(2,1)S(1)}, u32[]{:S(2)}, u32[]{:S(2)}) %collective-permute-start.16) | collective-permute-done | bytes 98336 | tf_op jit(solution)/shard_map/ppermute | solution.py:827
  108.6 2.2 %collective-permute-start.17 = (bf16[128,384]{1,0:T(8,128)(2,1)S(1)}, bf16[128,384]{1,0:T(8,128)(2,1)S(1)}, u32[]{:S(2)}, u32[]{:S(2)}) collective-permute-start(bf16[128,384]{1,0:T(8,128)(2,1)S(1)} %add_convert_fusion.12), channel_id=1, source_target_pairs={{0,16},{1,17},{2,18},{3,19},{4,20},{5,21},{6,22},{7,23},{8,24},{9,... | collective-permute-start | bytes 294920 | tf_op jit(solution)/shard_map/ppermute | solution.py:827
  110.8 1.4 collective-permute-start.26
  112.3 1.7 %collective-permute-start.12 = (bf16[176,384]{1,0:T(8,128)(2,1)S(1)}, bf16[176,384]{1,0:T(8,128)(2,1)S(1)}, u32[]{:S(2)}, u32[]{:S(2)}) collective-permute-start(bf16[176,384]{1,0:T(8,128)(2,1)S(1)} %pad_maximum_fusion.7), channel_id=1, source_target_pairs={{0,16},{1,17},{2,18},{3,19},{4,20},{5,21},{6,22},{7,23},{8,24},{9,... | collective-permute-start | bytes 405512 | tf_op jit(solution)/shard_map/ppermute | solution.py:827
  114.0 6.3 %collective-permute-done.26 = bf16[128,384]{1,0:T(8,128)(2,1)S(1)} collective-permute-done((bf16[128,384]{1,0:T(8,128)(2,1)S(1)}, bf16[128,384]{1,0:T(8,128)(2,1)S(1)}, u32[]{:S(2)}, u32[]{:S(2)}) %collective-permute-start.26) | collective-permute-done | bytes 98336 | tf_op jit(solution)/shard_map/ppermute | solution.py:827
  123.1 1.8 %collective-permute-done.27 = bf16[128,384]{1,0:T(8,128)(2,1)S(1)} collective-permute-done((bf16[128,384]{1,0:T(8,128)(2,1)S(1)}, bf16[128,384]{1,0:T(8,128)(2,1)S(1)}, u32[]{:S(2)}, u32[]{:S(2)}) %collective-permute-start.27) | collective-permute-done | bytes 98336 | tf_op jit(solution)/shard_map/ppermute | solution.py:827
  128.9 3.6 %collective-permute-done.28 = bf16[256,384]{1,0:T(8,128)(2,1)S(1)} collective-permute-done((bf16[256,384]{1,0:T(8,128)(2,1)S(1)}, bf16[256,384]{1,0:T(8,128)(2,1)S(1)}, u32[]{:S(2)}, u32[]{:S(2)}) %collective-permute-start.28) | collective-permute-done | bytes 196640 | tf_op jit(solution)/shard_map/ppermute | solution.py:827
  137.4 3.6 %shard_map.242 = (f32[768,768]{1,0:T(8,128)}, f32[768,768]{1,0:T(8,128)}, f32[768,768]{1,0:T(8,128)}, f32[768,768]{1,0:T(8,128)}) custom-call(bf16[512,384]{1,0:T(8,128)(2,1)S(1)} %pad_maximum_fusion.refs_0_, bf16[512,384]{1,0:T(8,128)(2,1)S(1)} %collective-permute-done.30.refs_1_, bf16[512,384]{1,0:T(8,128)(2,1)S(1)} %pad_maximum_fusion.1.refs_2_, ...), custom_call_target="tpu_custom_call" | custom-call | bytes 8000000 | tf_op jit(solution)/shard_map/pallas_call | solution.py:101
  141.0 3.1 %collective-permute-done.29.refs_2_ = bf16[512,384]{1,0:T(8,128)(2,1)S(1)} collective-permute-done((bf16[512,384]{1,0:T(8,128)(2,1)S(1)}, bf16[512,384]{1,0:T(8,128)(2,1)S(1)}, u32[]{:S(2)}, u32[]{:S(2)}) %collective-permute-start.29) | collective-permute-done | bytes 393248 | tf_op jit(solution)/shard_map/ppermute | solution.py:827
  145.8 2.2 %shard_map.243 = (f32[768,768]{1,0:T(8,128)}, f32[768,768]{1,0:T(8,128)}, f32[768,768]{1,0:T(8,128)}, f32[768,768]{1,0:T(8,128)}) custom-call(bf16[512,384]{1,0:T(8,128)(2,1)S(1)} %collective-permute-done.20.refs_0_, bf16[512,384]{1,0:T(8,128)(2,1)S(1)} %collective-permute-done.22.refs_1_, ...), custom_call_target="tpu_custom_call", output_to_operand_aliasing={{0}: (3, {}), {1}: (4, {}), {2}: (5, {}), {3}: (6, {})} | custom-call | bytes 8000000 | tf_op jit(solution)/shard_map/pallas_call | solution.py:101
  148.0 3.1 %shard_map.244 = (f32[768,768]{1,0:T(8,128)}, f32[768,768]{1,0:T(8,128)}, f32[768,768]{1,0:T(8,128)}, f32[768,768]{1,0:T(8,128)}, f32[768]{0:T(1024)}, /*index=5...) custom-call(bf16[512,384]{1,0:T(8,128)(2,1)S(1)} %collective-permute, ...), custom_call_target="tpu_custom_call", output_to_operand_aliasing={{0}: (5, {}), {1}: (6, {}), {2}: (7, {}), {3}: (8, {})} | custom-call | bytes 8000000 | tf_op jit(solution)/shard_map/pallas_call | solution.py:101
  (119 shorter events, 20.3 us)
Async XLA Ops:
  2.6 37.2 %collective-permute-start.2 = (bf16[768,1536]{1,0:T(8,128)(2,1)}, bf16[768,1536]{1,0:T(8,128)(2,1)}, u32[]{:S(2)}, u32[]{:S(2)}) collective-permute-start(bf16[768,1536]{1,0:T(8,128)(2,1)} %bitcast.19), channel_id=1, source_target_pairs={{0,1},{1,0},{2,3},{3,2},{4,5},{5,4},{6,7},{7,6},{8,9},{9,8},{10,11... | collective-permute-start | bytes 7077896 | tf_op jit(solution)/shard_map/ppermute | solution.py:819
  3.0 36.8 %collective-permute-start.3 = (bf16[1536,768]{1,0:T(8,128)(2,1)}, bf16[1536,768]{1,0:T(8,128)(2,1)}, u32[]{:S(2)}, u32[]{:S(2)}) collective-permute-start(bf16[1536,768]{1,0:T(8,128)(2,1)} %bitcast.21), channel_id=1, source_target_pairs={{0,1},{1,0},{2,3},{3,2},{4,5},{5,4},{6,7},{7,6},{8,9},{9,8},{10,11... | collective-permute-start | bytes 7077896 | tf_op jit(solution)/shard_map/ppermute | solution.py:819
  10.3 29.5 %all-to-all-start = ((bf16[16,16,1664]{2,1,0:T(8,128)(2,1)}), bf16[16,16,1664]{2,1,0:T(8,128)(2,1)}, u32[]{:S(2)}, u32[]{:S(2)}) async-start(bf16[16,16,1664]{2,1,0:T(8,128)(2,1)} %bitcast.16), calls=%async_computation | async-start | bytes 1703936 | tf_op jit(solution)/shard_map/all_to_all | solution.py:963
  49.2 5.6 %collective-permute-start.4 = (bf16[256,4608]{1,0:T(8,128)(2,1)}, bf16[256,4608]{1,0:T(8,128)(2,1)}, u32[]{:S(2)}, u32[]{:S(2)}) collective-permute-start(bf16[256,4608]{1,0:T(8,128)(2,1)} %get-tuple-element.103), channel_id=1, source_target_pairs={{0,1},{1,0},{2,3},{3,2},{4,5},{5,4},{6,7},{7,6},{8,9},{9,8},{10,11... | collective-permute-start | bytes 7077896 | tf_op jit(solution)/shard_map/ppermute | solution.py:819
  49.2 18.5 %all-to-all-start.1 = ((bf16[16,16,768]{2,1,0:T(8,128)(2,1)}), bf16[16,16,768]{2,1,0:T(8,128)(2,1)}, u32[]{:S(2)}, u32[]{:S(2)}) async-start(bf16[16,16,768]{2,1,0:T(8,128)(2,1)} %bitcast.18), calls=%async_computation.1 | async-start | bytes 786432 | tf_op jit(solution)/shard_map/all_to_all | solution.py:1005
  54.5 17.6 %collective-permute-start.6 = (f32[128,768]{1,0:T(8,128)}, f32[128,768]{1,0:T(8,128)}, u32[]{:S(2)}, u32[]{:S(2)}) collective-permute-start(f32[128,768]{1,0:T(8,128)} %get-tuple-element.108.refs_4_), channel_id=1, source_target_pairs={{0,1},{1,0},{2,3},{3,2},{4,5},{5,4},{6,7},{7,6},{8,9},{9,8},{10,11... | collective-permute-start | bytes 1179656 | tf_op jit(solution)/shard_map/ppermute | solution.py:819
  67.7 4.4 %collective-permute-start.5 = (bf16[256,768]{1,0:T(8,128)(2,1)}, bf16[256,768]{1,0:T(8,128)(2,1)S(1)}, u32[]{:S(2)}, u32[]{:S(2)}) collective-permute-start(bf16[256,768]{1,0:T(8,128)(2,1)} %bitcast.8.refs_0_), channel_id=1, source_target_pairs={{0,1},{1,0},{2,3},{3,2},{4,5},{5,4},{6,7},{7,6},{8,9},{9,8},{10,11... | collective-permute-start | bytes 1179656 | tf_op jit(solution)/shard_map/ppermute | solution.py:819
  67.7 4.3 %collective-permute-start.8 = (bf16[128,768]{1,0:T(8,128)(2,1)}, bf16[128,768]{1,0:T(8,128)(2,1)S(1)}, u32[]{:S(2)}, u32[]{:S(2)}) collective-permute-start(bf16[128,768]{1,0:T(8,128)(2,1)} %get-tuple-element.109.refs_9_), channel_id=1, source_target_pairs={{0,1},{1,0},{2,3},{3,2},{4,5},{5,4},{6,7},{7,6},{8,9},{9,8},{10,11... | collective-permute-start | bytes 589832 | tf_op jit(solution)/shard_map/ppermute | solution.py:819
  68.3 18.1 %all-to-all-start.2 = ((bf16[16,16,768]{2,1,0:T(8,128)(2,1)}), bf16[16,16,768]{2,1,0:T(8,128)(2,1)S(1)}, u32[]{:S(2)}, u32[]{:S(2)}) async-start(bf16[16,16,768]{2,1,0:T(8,128)(2,1)} %bitcast.17), calls=%async_computation.2 | async-start | bytes 786432 | tf_op jit(solution)/shard_map/all_to_all | solution.py:1010
  81.3 11.4 %collective-permute-start.9 = (bf16[512,384]{1,0:T(8,128)(2,1)}, bf16[512,384]{1,0:T(8,128)(2,1)S(1)}, u32[]{:S(2)}, u32[]{:S(2)}) collective-permute-start(bf16[512,384]{1,0:T(8,128)(2,1)} %get-tuple-element.125), channel_id=1, source_target_pairs={{0,2},{1,9},{2,0},{3,11},{4,6},{5,13},{6,4},{7,15},{8,10},{9,1},{1... | collective-permute-start | bytes 1179656 | tf_op jit(solution)/shard_map/ppermute | solution.py:827
  83.4 12.7 %collective-permute-start.14 = (bf16[512,384]{1,0:T(8,128)(2,1)}, bf16[512,384]{1,0:T(8,128)(2,1)S(1)}, u32[]{:S(2)}, u32[]{:S(2)}) collective-permute-start(bf16[512,384]{1,0:T(8,128)(2,1)} %get-tuple-element.128), channel_id=1, source_target_pairs={{0,4},{1,3},{2,6},{3,1},{4,0},{5,7},{6,2},{7,5},{8,12},{9,11},{10,... | collective-permute-start | bytes 1179656 | tf_op jit(solution)/shard_map/ppermute | solution.py:827
  84.9 12.9 %collective-permute-start.23 = (bf16[512,384]{1,0:T(8,128)(2,1)}, bf16[512,384]{1,0:T(8,128)(2,1)S(1)}, u32[]{:S(2)}, u32[]{:S(2)}) collective-permute-start(bf16[512,384]{1,0:T(8,128)(2,1)} %get-tuple-element.130), channel_id=1, source_target_pairs={{0,8},{1,5},{2,10},{3,7},{4,12},{5,1},{6,14},{7,3},{8,0},{9,13},{1... | collective-permute-start | bytes 1179656 | tf_op jit(solution)/shard_map/ppermute | solution.py:827
  86.4 13.0 %collective-permute-start.34 = (bf16[128,768]{1,0:T(8,128)(2,1)}, bf16[128,768]{1,0:T(8,128)(2,1)S(1)}, u32[]{:S(2)}, u32[]{:S(2)}) collective-permute-start(bf16[128,768]{1,0:T(8,128)(2,1)} %get-tuple-element.139), channel_id=1, source_target_pairs={{0,1},{1,0},{2,3},{3,2},{4,5},{5,4},{6,7},{7,6},{8,9},{9,8},{10,11... | collective-permute-start | bytes 589832 | tf_op jit(solution)/shard_map/ppermute | solution.py:819
  93.9 8.0 %collective-permute-start.10 = (bf16[256,384]{1,0:T(8,128)(2,1)S(1)}, bf16[256,384]{1,0:T(8,128)(2,1)S(1)}, u32[]{:S(2)}, u32[]{:S(2)}) collective-permute-start(bf16[256,384]{1,0:T(8,128)(2,1)S(1)} %get-tuple-element.170), channel_id=1, source_target_pairs={{0,4},{1,3},{2,6},{3,1},{4,0},{5,7},{6,2},{7,5},{8,12},{9,11},{10,... | collective-permute-start | bytes 589832 | tf_op jit(solution)/shard_map/ppermute | solution.py:827
  96.2 7.6 %collective-permute-start.15 = (bf16[256,384]{1,0:T(8,128)(2,1)S(1)}, bf16[256,384]{1,0:T(8,128)(2,1)S(1)}, u32[]{:S(2)}, u32[]{:S(2)}) collective-permute-start(bf16[256,384]{1,0:T(8,128)(2,1)S(1)} %get-tuple-element.168), channel_id=1, source_target_pairs={{0,8},{1,5},{2,10},{3,7},{4,12},{5,1},{6,14},{7,3},{8,0},{9,13},{1... | collective-permute-start | bytes 589832 | tf_op jit(solution)/shard_map/ppermute | solution.py:827
  97.9 7.1 %collective-permute-start.24 = (bf16[256,384]{1,0:T(8,128)(2,1)S(1)}, bf16[256,384]{1,0:T(8,128)(2,1)S(1)}, u32[]{:S(2)}, u32[]{:S(2)}) collective-permute-start(bf16[256,384]{1,0:T(8,128)(2,1)S(1)} %get-tuple-element.166), channel_id=1, source_target_pairs={{0,2},{1,9},{2,0},{3,11},{4,6},{5,13},{6,4},{7,15},{8,10},{9,1},{1... | collective-permute-start | bytes 589832 | tf_op jit(solution)/shard_map/ppermute | solution.py:827
  101.9 10.3 %collective-permute-start.11 = (bf16[176,384]{1,0:T(8,128)(2,1)S(1)}, bf16[176,384]{1,0:T(8,128)(2,1)S(1)}, u32[]{:S(2)}, u32[]{:S(2)}) collective-permute-start(bf16[176,384]{1,0:T(8,128)(2,1)S(1)} %pad_maximum_fusion.6), channel_id=1, source_target_pairs={{0,8},{1,5},{2,10},{3,7},{4,12},{5,1},{6,14},{7,3},{8,0},{9,13},{1... | collective-permute-start | bytes 405512 | tf_op jit(solution)/shard_map/ppermute | solution.py:827
  103.8 4.7 %collective-permute-start.16 = (bf16[128,384]{1,0:T(8,128)(2,1)S(1)}, bf16[128,384]{1,0:T(8,128)(2,1)S(1)}, u32[]{:S(2)}, u32[]{:S(2)}) collective-permute-start(bf16[128,384]{1,0:T(8,128)(2,1)S(1)} %add_convert_fusion.13), channel_id=1, source_target_pairs={{0,2},{1,9},{2,0},{3,11},{4,6},{5,13},{6,4},{7,15},{8,10},{9,1},{1... | collective-permute-start | bytes 294920 | tf_op jit(solution)/shard_map/ppermute | solution.py:827
  105.0 5.8 %collective-permute-start.25 = (bf16[128,384]{1,0:T(8,128)(2,1)S(1)}, bf16[128,384]{1,0:T(8,128)(2,1)S(1)}, u32[]{:S(2)}, u32[]{:S(2)}) collective-permute-start(bf16[128,384]{1,0:T(8,128)(2,1)S(1)} %add_convert_fusion.9), channel_id=1, source_target_pairs={{0,4},{1,3},{2,6},{3,1},{4,0},{5,7},{6,2},{7,5},{8,12},{9,11},{10,... | collective-permute-start | bytes 294920 | tf_op jit(solution)/shard_map/ppermute | solution.py:827
  108.6 12.9 %collective-permute-start.17 = (bf16[128,384]{1,0:T(8,128)(2,1)S(1)}, bf16[128,384]{1,0:T(8,128)(2,1)S(1)}, u32[]{:S(2)}, u32[]{:S(2)}) collective-permute-start(bf16[128,384]{1,0:T(8,128)(2,1)S(1)} %add_convert_fusion.12), channel_id=1, source_target_pairs={{0,16},{1,17},{2,18},{3,19},{4,20},{5,21},{6,22},{7,23},{8,24},{9,... | collective-permute-start | bytes 294920 | tf_op jit(solution)/shard_map/ppermute | solution.py:827
  110.8 9.4 %collective-permute-start.26 = (bf16[128,384]{1,0:T(8,128)(2,1)S(1)}, bf16[128,384]{1,0:T(8,128)(2,1)S(1)}, u32[]{:S(2)}, u32[]{:S(2)}) collective-permute-start(bf16[128,384]{1,0:T(8,128)(2,1)S(1)} %add_convert_fusion.8), channel_id=1, source_target_pairs={{0,16},{1,17},{2,18},{3,19},{4,20},{5,21},{6,22},{7,23},{8,24},{9,... | collective-permute-start | bytes 294920 | tf_op jit(solution)/shard_map/ppermute | solution.py:827
  112.3 9.4 %collective-permute-start.12 = (bf16[176,384]{1,0:T(8,128)(2,1)S(1)}, bf16[176,384]{1,0:T(8,128)(2,1)S(1)}, u32[]{:S(2)}, u32[]{:S(2)}) collective-permute-start(bf16[176,384]{1,0:T(8,128)(2,1)S(1)} %pad_maximum_fusion.7), channel_id=1, source_target_pairs={{0,16},{1,17},{2,18},{3,19},{4,20},{5,21},{6,22},{7,23},{8,24},{9,... | collective-permute-start | bytes 405512 | tf_op jit(solution)/shard_map/ppermute | solution.py:827
  120.3 4.7 %collective-permute-start.27 = (bf16[128,384]{1,0:T(8,128)(2,1)S(1)}, bf16[128,384]{1,0:T(8,128)(2,1)S(1)}, u32[]{:S(2)}, u32[]{:S(2)}) collective-permute-start(bf16[128,384]{1,0:T(8,128)(2,1)S(1)} %add_convert_fusion.7), channel_id=1, source_target_pairs={{0,4},{1,3},{2,6},{3,1},{4,0},{5,7},{6,2},{7,5},{8,12},{9,11},{10,... | collective-permute-start | bytes 294920 | tf_op jit(solution)/shard_map/ppermute | solution.py:827
  121.8 5.1 %collective-permute-start.18 = (bf16[176,384]{1,0:T(8,128)(2,1)S(1)}, bf16[176,384]{1,0:T(8,128)(2,1)S(1)}, u32[]{:S(2)}, u32[]{:S(2)}) collective-permute-start(bf16[176,384]{1,0:T(8,128)(2,1)S(1)} %pad_maximum_fusion.8), channel_id=1, source_target_pairs={{0,2},{1,9},{2,0},{3,11},{4,6},{5,13},{6,4},{7,15},{8,10},{9,1},{1... | collective-permute-start | bytes 405512 | tf_op jit(solution)/shard_map/ppermute | solution.py:827
  123.1 4.7 %collective-permute-start.13 = (bf16[128,384]{1,0:T(8,128)(2,1)S(1)}, bf16[128,384]{1,0:T(8,128)(2,1)S(1)}, u32[]{:S(2)}, u32[]{:S(2)}) collective-permute-start(bf16[128,384]{1,0:T(8,128)(2,1)S(1)} %add_convert_fusion.15), channel_id=1, source_target_pairs={{0,8},{1,5},{2,10},{3,7},{4,12},{5,1},{6,14},{7,3},{8,0},{9,13},{1... | collective-permute-start | bytes 294920 | tf_op jit(solution)/shard_map/ppermute | solution.py:827
  125.0 7.5 %collective-permute-start.28 = (bf16[256,384]{1,0:T(8,128)(2,1)S(1)}, bf16[256,384]{1,0:T(8,128)(2,1)S(1)}, u32[]{:S(2)}, u32[]{:S(2)}) collective-permute-start(bf16[256,384]{1,0:T(8,128)(2,1)S(1)} %pad_maximum_fusion.5), channel_id=1, source_target_pairs={{0,2},{1,9},{2,0},{3,11},{4,6},{5,13},{6,4},{7,15},{8,10},{9,1},{1... | collective-permute-start | bytes 589832 | tf_op jit(solution)/shard_map/ppermute | solution.py:827
  126.9 5.8 %collective-permute-start.21 = (bf16[256,384]{1,0:T(8,128)(2,1)S(1)}, bf16[256,384]{1,0:T(8,128)(2,1)S(1)}, u32[]{:S(2)}, u32[]{:S(2)}) collective-permute-start(bf16[256,384]{1,0:T(8,128)(2,1)S(1)} %pad_maximum_fusion.4), channel_id=1, source_target_pairs={{0,8},{1,5},{2,10},{3,7},{4,12},{5,1},{6,14},{7,3},{8,0},{9,13},{1... | collective-permute-start | bytes 589832 | tf_op jit(solution)/shard_map/ppermute | solution.py:827
  127.8 6.9 %collective-permute-start.19 = (bf16[304,384]{1,0:T(8,128)(2,1)S(1)}, bf16[304,384]{1,0:T(8,128)(2,1)S(1)}, u32[]{:S(2)}, u32[]{:S(2)}) collective-permute-start(bf16[304,384]{1,0:T(8,128)(2,1)S(1)} %pad_maximum_fusion.3), channel_id=1, source_target_pairs={{0,4},{1,3},{2,6},{3,1},{4,0},{5,7},{6,2},{7,5},{8,12},{9,11},{10,... | collective-permute-start | bytes 700424 | tf_op jit(solution)/shard_map/ppermute | solution.py:827
  133.2 10.8 %collective-permute-start.29 = (bf16[512,384]{1,0:T(8,128)(2,1)S(1)}, bf16[512,384]{1,0:T(8,128)(2,1)S(1)}, u32[]{:S(2)}, u32[]{:S(2)}) collective-permute-start(bf16[512,384]{1,0:T(8,128)(2,1)S(1)} %pad_maximum_fusion.2.refs_4_), channel_id=1, source_target_pairs={{0,8},{1,5},{2,10},{3,7},{4,12},{5,1},{6,14},{7,3},{8,0},{9,13},{1... | collective-permute-start | bytes 1179656 | tf_op jit(solution)/shard_map/ppermute | solution.py:827
  133.7 10.7 %collective-permute-start.22 = (bf16[512,384]{1,0:T(8,128)(2,1)S(1)}, bf16[512,384]{1,0:T(8,128)(2,1)S(1)}, u32[]{:S(2)}, u32[]{:S(2)}) collective-permute-start(bf16[512,384]{1,0:T(8,128)(2,1)S(1)} %pad_maximum_fusion.1.refs_2_), channel_id=1, source_target_pairs={{0,4},{1,3},{2,6},{3,1},{4,0},{5,7},{6,2},{7,5},{8,12},{9,11},{10,... | collective-permute-start | bytes 1179656 | tf_op jit(solution)/shard_map/ppermute | solution.py:827
  135.1 10.1 %collective-permute-start.20 = (bf16[512,384]{1,0:T(8,128)(2,1)S(1)}, bf16[512,384]{1,0:T(8,128)(2,1)S(1)}, u32[]{:S(2)}, u32[]{:S(2)}) collective-permute-start(bf16[512,384]{1,0:T(8,128)(2,1)S(1)} %pad_maximum_fusion.refs_0_), channel_id=1, source_target_pairs={{0,2},{1,9},{2,0},{3,11},{4,6},{5,13},{6,4},{7,15},{8,10},{9,1},{1... | collective-permute-start | bytes 1179656 | tf_op jit(solution)/shard_map/ppermute | solution.py:827
  136.0 5.0 %collective-permute-start.33 = (f32[48,384]{1,0:T(8,128)S(1)}, f32[48,384]{1,0:T(8,128)S(1)}, u32[]{:S(2)}, u32[]{:S(2)}) collective-permute-start(f32[48,384]{1,0:T(8,128)S(1)} %convert_add_fusion.refs_3_), channel_id=1, source_target_pairs={{0,1},{1,0},{2,3},{3,2},{4,5},{5,4},{6,7},{7,6},{8,9},{9,8},{10,11... | collective-permute-start | bytes 221192 | tf_op jit(solution)/shard_map/ppermute | solution.py:819
  (23 other events, 172.9 us)

commit v6 on v5

--- a/solution.py
+++ b/solution.py
@@ -173,6 +173,8 @@
     fetch_other_ref,
     root_ref,
     bias,
+    staged,
+    sems,
 ):
     rows, width = own_ref.shape
     size = width // heads
@@ -180,13 +182,17 @@
     core = lax.axis_index("ffn")
     total = out_ref.shape[0]
     experts = router_ref.shape[0]
+    sends = [
+        pltpu.make_async_copy(staged.at[:, span], out_ref.at[:, span], sems.at[i])
+        for i, span in enumerate((pl.ds(width, width + LANES), pl.ds(0, width)))
+    ]
     choose, place = placement(ids_ref[...], experts, total)
     _, place_other = placement(ids_other_ref[...], experts, total)
     fetch_ref[...] = place.T.astype(BF16)
     fetch_other_ref[...] = place_other.T.astype(BF16)
     choose = choose.T
     lane = lax.broadcasted_iota(jnp.int32, (total, LANES), 1)
-    out_ref[:, 2 * width :] = jnp.where(
+    staged[:, 2 * width :] = jnp.where(
         lane == 0,
         jnp.sum(place, axis=1, keepdims=True),
         jnp.sum(place_other, axis=1, keepdims=True),
@@ -212,6 +218,9 @@
     act_own = (x * root * gain).astype(BF16)
     act_other = (y * root_mean(y) * gain).astype(BF16)
     act = jnp.concatenate([act_own, act_other], axis=0)
+    wait(13)
+    staged[:, width : 2 * width] = dot(place, cot_ref[...]).astype(BF16)
+    sends[0].start()
     wait(7)
     keys = dot(act, wk[...]).astype(BF16)
     wait(8)
@@ -232,9 +241,8 @@
     mixed = jnp.concatenate(mixed, axis=1)
     mixed_ref[...] = mixed
     flush(3)
-    for i in (10, 11, 12, 13):
+    for i in (10, 11, 12):
         wait(i)
-    out_ref[:, width : 2 * width] = dot(place, cot_ref[...]).astype(BF16)
     middle = x + dot(mixed, wo[...])
     middle_ref[...] = middle
     flush(0)
@@ -246,7 +254,11 @@
         grown, axis=-1, keepdims=True
     )
     gate_ref[...] = jnp.broadcast_to(gate, gate_ref.shape)
-    out_ref[:, :width] = dot(place, act_second).astype(BF16)
+    staged[:, :width] = dot(place, act_second).astype(BF16)
+    sends[1].start()
+    flush(1)
+    for send in sends:
+        send.wait()
 
 
 def halves_kernel(
@@ -729,6 +741,7 @@
     if last is not None:
         experts, heads = last
         (small_own_ref, small_other_ref), refs = refs[:2], refs[2:]
+        last_inputs = (count, count + 1)
     if upper:
         refs = refs[4:]
     outs, (wide, sems) = refs[:4], refs[-2:]
@@ -772,6 +785,8 @@
                 write.start()
                 writes.append(write)
     if last is not None:
+        for i in last_inputs:
+            wait(i)
         at = small_rows(experts)
         mine, other = small_own_ref[...], small_other_ref[...]
         both = mine + other
@@ -796,7 +811,7 @@
     if last is not None:
         experts, heads, buckets = last
         tail = [((width,), F32), ((width,), F32), ((heads, buckets), F32), ((experts, width), F32)]
-        modes += "hh"
+        modes += "ll"
         last = (experts, heads)
     first = len(modes)
     modes += "r" * len(earlier)
@@ -921,12 +936,6 @@
     other = swap(tokens)
     ids = expert_ids.reshape(1, rows)
     ids_other = swap(ids)
-    other, ids_other, w_in, w_down, cotangent = lax.optimization_barrier(
-        (other, ids_other, w_in, w_down, cotangent)
-    )
-    in_own, down_own = w_in[0], w_down[0]
-    in_other, down_other = swap(in_own), swap(down_own)
-    cot_other = swap(cotangent)
     middle, gate, outgoing, mixed, windows, fetch, fetch_other, root = call(
         functools.partial(forward_kernel, heads),
         [
@@ -955,12 +964,20 @@
             router,
             cotangent,
         ),
-        "hhhhhhhlllllll" + "hhhhhhhh",
+        "hhhhhhhlllllll" + "hhrhhhhh",
         vmem=64,
         flops=3000000000,
-        scratch=[pltpu.VMEM((heads, rows, 2 * rows), F32)],
+        scratch=[
+            pltpu.VMEM((heads, rows, 2 * rows), F32),
+            pltpu.VMEM((total, 2 * width + LANES), BF16),
+            pltpu.SemaphoreType.DMA((2,)),
+        ],
     )
     arrived = lax.all_to_all(outgoing, "expert", 0, 0, tiled=True)
+    gate, w_in, w_down, cot_own = lax.optimization_barrier((gate, w_in, w_down, cotangent))
+    in_own, down_own = w_in[0], w_down[0]
+    in_other, down_other = swap(in_own), swap(down_own)
+    cot_other = swap(cot_own)
     mixed_other, middle_other = swap(mixed), swap(middle)
     act, queries, keys, values, probs = call(
         functools.partial(halves_kernel, heads),
@@ -1085,36 +1102,30 @@
     near = []
     for rows_kept in kept:
         near += [rows_kept, swap(rows_kept)]
-    matrices = assemble(orders, levels, (0, 1), near, width)
     small_other = swap(small)
-    got, matrices, small, small_other, output, expert_branch, grad_input = (
-        lax.optimization_barrier(
-            (got, matrices, small, small_other, output, expert_branch, grad_input)
-        )
+    *matrices, gain_first, gain_second, table, router_sum = assemble(
+        orders,
+        levels,
+        (0, 1),
+        near,
+        width,
+        smalls=(small, small_other),
+        last=(experts, heads, buckets),
+    )
+    got, matrices, output, expert_branch, grad_input = lax.optimization_barrier(
+        (got, matrices, output, expert_branch, grad_input)
     )
     far = [swap(rows_got) for rows_got in got]
     matrices = assemble(orders, levels, (0,), got, width, matrices)
-    results = assemble(
-        orders,
-        levels,
-        (1,),
-        far,
-        width,
-        matrices,
-        (small, small_other),
-        (experts, heads, buckets),
-    )
+    matrices = assemble(orders, levels, (1,), far, width, matrices)
     return (
         output,
         grad_input,
-        results[4],
-        results[0],
-        results[1],
-        results[2],
-        results[3],
-        results[6].T,
-        results[5],
-        results[7].T,
+        gain_first,
+        *matrices,
+        table.T,
+        gain_second,
+        router_sum.T,
         grad_w_in,
         grad_w_down,
         expert_branch,

time: 152 us -> 151 us (level)
    ppermute x21, waiting for transfers between devices: 26.9 us -> 25 us  [flip(): return lax.ppermute(x, ('expert', 'ffn'), pairs)]
  transfers between devices with their start and end apart: 41 -> 41, of which waited for: 15 -> 17; matrix products, arithmetic and copies ran while one was open for 3% -> 3% of each run, Pallas kernels for 24% -> 20%
where the time goes in v6:
time: 151 us; the launch traced here: 150 us
  Pallas kernels  48.1 us (32%)
  starting transfers between devices  47.9 us (32%)
  waiting for transfers between devices  47.6 us (32%)
  other arithmetic  3.03 us (2%)
    pallas_call x7, Pallas kernels, call(): pl.pallas_call(kernel, out_shape=[jax.ShapeDtypeStruct(s, d) for s, d in...  39.2 us
    ppermute x21, starting transfers between devices, flip(): return lax.ppermute(x, ('expert', 'ffn'), pairs)  27.4 us
    ppermute x21, waiting for transfers between devices, flip(): return lax.ppermute(x, ('expert', 'ffn'), pairs)  25 us
    all_to_all x1, waiting for transfers between devices, shards(): arrived = lax.all_to_all(outgoing, 'expert', 0, 0, tiled=True)  15.6 us
    pallas_call x1, Pallas kernels, expert_weights(): pl.pallas_call(expert_weights_kernel, grid=(steps,), out_shape=[jax.Shape...  8.89 us
    all_to_all x1, starting transfers between devices, shards(): arrived = lax.all_to_all(outgoing, 'expert', 0, 0, tiled=True)  8.29 us
    all_to_all x1, starting transfers between devices, shards(): grad_returned = lax.all_to_all(grad_slots, 'expert', 0, 0, tiled=True)  5.26 us
    all_to_all x1, waiting for transfers between devices, shards(): grad_returned = lax.all_to_all(grad_slots, 'expert', 0, 0, tiled=True)  4.07 us
  transfers between devices with their start and end apart: 41, of which 17 were waited for; matrix products, arithmetic and copies ran while one was open for 3% of the time, Pallas kernels for 20%

profile of v6, /device:TPU:0, one launch (start us, length us, event | category | flops | bytes accessed | tf_op | source)
XLA Modules:
  0.0 150.0 jit_solution(11412929348571741945)
XLA Ops:
  2.6 7.2 %shard_map.237 = (f32[128,768]{1,0:T(8,128)}, f32[128,128]{1,0:T(8,128)}, bf16[256,1664]{1,0:T(8,128)(2,1)}, bf16[128,768]{1,0:T(8,128)(2,1)}, f32[12,768]{1,0:T...) custom-call(bf16[128,768]{1,0:T(8,128)(2,1)} %refs_17_.1, ...), custom_call_target="tpu_custom_call" | custom-call | flops 3000000000 | bytes 1000000 | tf_op jit(solution)/shard_map/pallas_call | solution.py:101
  10.3 8.3 %all-to-all-start = ((bf16[16,16,1664]{2,1,0:T(8,128)(2,1)}), bf16[16,16,1664]{2,1,0:T(8,128)(2,1)}, u32[]{:S(2)}, u32[]{:S(2)}) async-start(bf16[16,16,1664]{2,1,0:T(8,128)(2,1)} %bitcast.16), calls=%async_computation | async-start | bytes 1703936 | tf_op jit(solution)/shard_map/all_to_all | solution.py:976
  18.6 5.6 %shard_map.238 = (bf16[256,768]{1,0:T(8,128)(2,1)}, bf16[256,384]{1,0:T(8,128)(2,1)}, bf16[256,384]{1,0:T(8,128)(2,1)}, bf16[256,384]{1,0:T(8,128)(2,1)}, f32[6,256,256]{2,1,0:T(8,128)}) custom-call(bf16[128,768]{1,0:T(8,128)(2,1)} %refs_17_.1, bf16[128,768]{1,0:T(8,128)(2,1)} %collective-permute-done.refs_1_.refs_18_, f32[768]{0:T(1024)} %refs_2_.3, ...), custom_call_target="tpu_custom_call" | custom-call | flops 3000000000 | bytes 1000000 | tf_op jit(solution)/shard_map/pallas_call | solution.py:101
  24.2 15.6 %all-to-all-done = bf16[16,16,1664]{2,1,0:T(8,128)(2,1)} async-done(((bf16[16,16,1664]{2,1,0:T(8,128)(2,1)}), bf16[16,16,1664]{2,1,0:T(8,128)(2,1)}, u32[]{:S(2)}, u32[]{:S(2)}) %all-to-all-start) | async-done | bytes 852000 | tf_op jit(solution)/shard_map/all_to_all | solution.py:976
  39.8 9.3 %shard_map.239 = (bf16[256,1536]{1,0:T(8,128)(2,1)}, bf16[256,1536]{1,0:T(8,128)(2,1)}, bf16[256,768]{1,0:T(8,128)(2,1)}, bf16[256,4608]{1,0:T(8,128)(2,1)}, bf1...) custom-call(bf16[256,1664]{1,0:T(8,128)(2,1)} %bitcast.4.refs_0_.flat_own, ...), custom_call_target="tpu_custom_call" | custom-call | flops 6000000000 | bytes 1000000 | tf_op jit(solution)/shard_map/pallas_call | solution.py:101
  49.3 5.3 %all-to-all-start.1 = ((bf16[16,16,768]{2,1,0:T(8,128)(2,1)}), bf16[16,16,768]{2,1,0:T(8,128)(2,1)}, u32[]{:S(2)}, u32[]{:S(2)}) async-start(bf16[16,16,768]{2,1,0:T(8,128)(2,1)} %bitcast.18), calls=%async_computation.1 | async-start | bytes 786432 | tf_op jit(solution)/shard_map/all_to_all | solution.py:1022
  54.8 8.9 %shard_map.240 = (f32[1,768,1536]{2,1,0:T(8,128)}, f32[1,1536,768]{2,1,0:T(8,128)}) custom-call(bf16[256,1664]{1,0:T(8,128)(2,1)} %bitcast.4.refs_0_.flat_own, bf16[256,768]{1,0:T(8,128)(2,1)} %get-tuple-element.95.sent_own, bf16[256,1536]{1,0:T(8,128)(2,1)} %get-tuple-element.96.hid_own, bf16[256,1536]{1,0:T(8,128)(2,1)} %get-tuple-element.97.pre_own, ...), custom_call_target="tpu_custom_call" | custom-call | flops 2415919104 | bytes 14000000 | tf_op jit(solution)/shard_map/pallas_call | solution.py:487
  63.7 4.1 %all-to-all-done.1 = bf16[16,16,768]{2,1,0:T(8,128)(2,1)} async-done(((bf16[16,16,768]{2,1,0:T(8,128)(2,1)}), bf16[16,16,768]{2,1,0:T(8,128)(2,1)}, u32[]{:S(2)}, u32[]{:S(2)}) %all-to-all-start.1) | async-done | bytes 393248 | tf_op jit(solution)/shard_map/all_to_all | solution.py:1022
  68.3 3.8 %all-to-all-start.2 = ((bf16[16,16,768]{2,1,0:T(8,128)(2,1)}), bf16[16,16,768]{2,1,0:T(8,128)(2,1)S(1)}, u32[]{:S(2)}, u32[]{:S(2)}) async-start(bf16[16,16,768]{2,1,0:T(8,128)(2,1)} %bitcast.17), calls=%async_computation.2 | async-start | bytes 786432 | tf_op jit(solution)/shard_map/all_to_all | solution.py:1027
  73.0 8.3 %shard_map.241 = (bf16[512,384]{1,0:T(8,128)(2,1)}, bf16[512,384]{1,0:T(8,128)(2,1)}, bf16[512,384]{1,0:T(8,128)(2,1)}, bf16[512,384]{1,0:T(8,128)(2,1)}, bf16[5...) custom-call(bf16[256,768]{1,0:T(8,128)(2,1)} %bitcast.8.refs_0_, ...), custom_call_target="tpu_custom_call" | custom-call | flops 4000000000 | bytes 1000000 | tf_op jit(solution)/shard_map/pallas_call | solution.py:101
  81.4 1.9 %collective-permute-start.9 = (bf16[512,384]{1,0:T(8,128)(2,1)}, bf16[512,384]{1,0:T(8,128)(2,1)S(1)}, u32[]{:S(2)}, u32[]{:S(2)}) collective-permute-start(bf16[512,384]{1,0:T(8,128)(2,1)} %get-tuple-element.121), channel_id=1, source_target_pairs={{0,2},{1,9},{2,0},{3,11},{4,6},{5,13},{6,4},{7,15},{8,10},{9,1},{1... | collective-permute-start | bytes 1179656 | tf_op jit(solution)/shard_map/ppermute | solution.py:842
  83.4 1.5 %collective-permute-start.14 = (bf16[512,384]{1,0:T(8,128)(2,1)}, bf16[512,384]{1,0:T(8,128)(2,1)S(1)}, u32[]{:S(2)}, u32[]{:S(2)}) collective-permute-start(bf16[512,384]{1,0:T(8,128)(2,1)} %get-tuple-element.124), channel_id=1, source_target_pairs={{0,4},{1,3},{2,6},{3,1},{4,0},{5,7},{6,2},{7,5},{8,12},{9,11},{10,... | collective-permute-start | bytes 1179656 | tf_op jit(solution)/shard_map/ppermute | solution.py:842
  85.0 1.5 collective-permute-start.23
  87.6 5.2 %collective-permute-done.9 = bf16[512,384]{1,0:T(8,128)(2,1)S(1)} collective-permute-done((bf16[512,384]{1,0:T(8,128)(2,1)}, bf16[512,384]{1,0:T(8,128)(2,1)S(1)}, u32[]{:S(2)}, u32[]{:S(2)}) %collective-permute-start.9) | collective-permute-done | bytes 393248 | tf_op jit(solution)/shard_map/ppermute | solution.py:842
  93.9 2.2 %collective-permute-start.10 = (bf16[256,384]{1,0:T(8,128)(2,1)S(1)}, bf16[256,384]{1,0:T(8,128)(2,1)S(1)}, u32[]{:S(2)}, u32[]{:S(2)}) collective-permute-start(bf16[256,384]{1,0:T(8,128)(2,1)S(1)} %get-tuple-element.164), channel_id=1, source_target_pairs={{0,4},{1,3},{2,6},{3,1},{4,0},{5,7},{6,2},{7,5},{8,12},{9,11},{10,... | collective-permute-start | bytes 589832 | tf_op jit(solution)/shard_map/ppermute | solution.py:842
  96.3 1.6 %collective-permute-start.15 = (bf16[256,384]{1,0:T(8,128)(2,1)S(1)}, bf16[256,384]{1,0:T(8,128)(2,1)S(1)}, u32[]{:S(2)}, u32[]{:S(2)}) collective-permute-start(bf16[256,384]{1,0:T(8,128)(2,1)S(1)} %get-tuple-element.162), channel_id=1, source_target_pairs={{0,8},{1,5},{2,10},{3,7},{4,12},{5,1},{6,14},{7,3},{8,0},{9,13},{1... | collective-permute-start | bytes 589832 | tf_op jit(solution)/shard_map/ppermute | solution.py:842
  97.9 1.5 %collective-permute-start.24 = (bf16[256,384]{1,0:T(8,128)(2,1)S(1)}, bf16[256,384]{1,0:T(8,128)(2,1)S(1)}, u32[]{:S(2)}, u32[]{:S(2)}) collective-permute-start(bf16[256,384]{1,0:T(8,128)(2,1)S(1)} %get-tuple-element.160), channel_id=1, source_target_pairs={{0,2},{1,9},{2,0},{3,11},{4,6},{5,13},{6,4},{7,15},{8,10},{9,1},{1... | collective-permute-start | bytes 589832 | tf_op jit(solution)/shard_map/ppermute | solution.py:842
  99.7 2.2 %collective-permute-done.10 = bf16[256,384]{1,0:T(8,128)(2,1)S(1)} collective-permute-done((bf16[256,384]{1,0:T(8,128)(2,1)S(1)}, bf16[256,384]{1,0:T(8,128)(2,1)S(1)}, u32[]{:S(2)}, u32[]{:S(2)}) %collective-permute-start.10) | collective-permute-done | bytes 196640 | tf_op jit(solution)/shard_map/ppermute | solution.py:842
  102.0 1.8 %collective-permute-start.11 = (bf16[176,384]{1,0:T(8,128)(2,1)S(1)}, bf16[176,384]{1,0:T(8,128)(2,1)S(1)}, u32[]{:S(2)}, u32[]{:S(2)}) collective-permute-start(bf16[176,384]{1,0:T(8,128)(2,1)S(1)} %pad_maximum_fusion.6), channel_id=1, source_target_pairs={{0,8},{1,5},{2,10},{3,7},{4,12},{5,1},{6,14},{7,3},{8,0},{9,13},{1... | collective-permute-start | bytes 405512 | tf_op jit(solution)/shard_map/ppermute | solution.py:842
  105.0 1.4 collective-permute-start.25
  106.5 2.1 %collective-permute-done.16 = bf16[128,384]{1,0:T(8,128)(2,1)S(1)} collective-permute-done((bf16[128,384]{1,0:T(8,128)(2,1)S(1)}, bf16[128,384]{1,0:T(8,128)(2,1)S(1)}, u32[]{:S(2)}, u32[]{:S(2)}) %collective-permute-start.16) | collective-permute-done | bytes 98336 | tf_op jit(solution)/shard_map/ppermute | solution.py:842
  108.6 2.2 %collective-permute-start.17 = (bf16[128,384]{1,0:T(8,128)(2,1)S(1)}, bf16[128,384]{1,0:T(8,128)(2,1)S(1)}, u32[]{:S(2)}, u32[]{:S(2)}) collective-permute-start(bf16[128,384]{1,0:T(8,128)(2,1)S(1)} %add_convert_fusion.12), channel_id=1, source_target_pairs={{0,16},{1,17},{2,18},{3,19},{4,20},{5,21},{6,22},{7,23},{8,24},{9,... | collective-permute-start | bytes 294920 | tf_op jit(solution)/shard_map/ppermute | solution.py:842
  110.9 1.3 collective-permute-start.26
  112.3 1.7 %collective-permute-start.12 = (bf16[176,384]{1,0:T(8,128)(2,1)S(1)}, bf16[176,384]{1,0:T(8,128)(2,1)S(1)}, u32[]{:S(2)}, u32[]{:S(2)}) collective-permute-start(bf16[176,384]{1,0:T(8,128)(2,1)S(1)} %pad_maximum_fusion.7), channel_id=1, source_target_pairs={{0,16},{1,17},{2,18},{3,19},{4,20},{5,21},{6,22},{7,23},{8,24},{9,... | collective-permute-start | bytes 405512 | tf_op jit(solution)/shard_map/ppermute | solution.py:842
  114.0 6.3 %collective-permute-done.26 = bf16[128,384]{1,0:T(8,128)(2,1)S(1)} collective-permute-done((bf16[128,384]{1,0:T(8,128)(2,1)S(1)}, bf16[128,384]{1,0:T(8,128)(2,1)S(1)}, u32[]{:S(2)}, u32[]{:S(2)}) %collective-permute-start.26) | collective-permute-done | bytes 98336 | tf_op jit(solution)/shard_map/ppermute | solution.py:842
  123.2 1.8 %collective-permute-done.27 = bf16[128,384]{1,0:T(8,128)(2,1)S(1)} collective-permute-done((bf16[128,384]{1,0:T(8,128)(2,1)S(1)}, bf16[128,384]{1,0:T(8,128)(2,1)S(1)}, u32[]{:S(2)}, u32[]{:S(2)}) %collective-permute-start.27) | collective-permute-done | bytes 98336 | tf_op jit(solution)/shard_map/ppermute | solution.py:842
  128.9 3.6 %collective-permute-done.28 = bf16[256,384]{1,0:T(8,128)(2,1)S(1)} collective-permute-done((bf16[256,384]{1,0:T(8,128)(2,1)S(1)}, bf16[256,384]{1,0:T(8,128)(2,1)S(1)}, u32[]{:S(2)}, u32[]{:S(2)}) %collective-permute-start.28) | collective-permute-done | bytes 196640 | tf_op jit(solution)/shard_map/ppermute | solution.py:842
  133.4 1.7 %collective-permute-start.22 = (bf16[512,384]{1,0:T(8,128)(2,1)S(1)}, bf16[512,384]{1,0:T(8,128)(2,1)S(1)}, u32[]{:S(2)}, u32[]{:S(2)}) collective-permute-start(bf16[512,384]{1,0:T(8,128)(2,1)S(1)} %pad_maximum_fusion.1.refs_2_), channel_id=1, source_target_pairs={{0,4},{1,3},{2,6},{3,1},{4,0},{5,7},{6,2},{7,5},{8,12},{9,11},{10,... | collective-permute-start | bytes 1179656 | tf_op jit(solution)/shard_map/ppermute | solution.py:842
  138.1 4.5 %shard_map.242 = (f32[768,768]{1,0:T(8,128)}, f32[768,768]{1,0:T(8,128)}, f32[768,768]{1,0:T(8,128)}, f32[768,768]{1,0:T(8,128)}, f32[768]{0:T(1024)}, /*index=5...) custom-call(bf16[512,384]{1,0:T(8,128)(2,1)S(1)} %pad_maximum_fusion.refs_0_, ...), custom_call_target="tpu_custom_call" | custom-call | bytes 8000000 | tf_op jit(solution)/shard_map/pallas_call | solution.py:101
  142.6 1.6 %collective-permute-done.22.refs_1_ = bf16[512,384]{1,0:T(8,128)(2,1)S(1)} collective-permute-done((bf16[512,384]{1,0:T(8,128)(2,1)S(1)}, bf16[512,384]{1,0:T(8,128)(2,1)S(1)}, u32[]{:S(2)}, u32[]{:S(2)}) %collective-permute-start.22) | collective-permute-done | bytes 393248 | tf_op jit(solution)/shard_map/ppermute | solution.py:842
  145.4 2.2 %shard_map.243 = (f32[768,768]{1,0:T(8,128)}, f32[768,768]{1,0:T(8,128)}, f32[768,768]{1,0:T(8,128)}, f32[768,768]{1,0:T(8,128)}) custom-call(bf16[512,384]{1,0:T(8,128)(2,1)S(1)} %collective-permute-done.20.refs_0_, bf16[512,384]{1,0:T(8,128)(2,1)S(1)} %collective-permute-done.22.refs_1_, ...), custom_call_target="tpu_custom_call", output_to_operand_aliasing={{0}: (3, {}), {1}: (4, {}), {2}: (5, {}), {3}: (6, {})} | custom-call | bytes 8000000 | tf_op jit(solution)/shard_map/pallas_call | solution.py:101
  147.7 2.2 %shard_map.244 = (f32[768,768]{1,0:T(8,128)}, f32[768,768]{1,0:T(8,128)}, f32[768,768]{1,0:T(8,128)}, f32[768,768]{1,0:T(8,128)}) custom-call(bf16[512,384]{1,0:T(8,128)(2,1)S(1)} %collective-permute-done.35.refs_0_, bf16[512,384]{1,0:T(8,128)(2,1)S(1)} %collective-permute-done.36.refs_1_, ...), custom_call_target="tpu_custom_call", output_to_operand_aliasing={{0}: (3, {}), {1}: (4, {}), {2}: (5, {}), {3}: (6, {})} | custom-call | bytes 8000000 | tf_op jit(solution)/shard_map/pallas_call | solution.py:101
  (119 shorter events, 20.2 us)
Async XLA Ops:
  9.8 30.1 %collective-permute-start.2 = (bf16[768,1536]{1,0:T(8,128)(2,1)}, bf16[768,1536]{1,0:T(8,128)(2,1)}, u32[]{:S(2)}, u32[]{:S(2)}) collective-permute-start(bf16[768,1536]{1,0:T(8,128)(2,1)} %bitcast.19), channel_id=1, source_target_pairs={{0,1},{1,0},{2,3},{3,2},{4,5},{5,4},{6,7},{7,6},{8,9},{9,8},{10,11... | collective-permute-start | bytes 7077896 | tf_op jit(solution)/shard_map/ppermute | solution.py:834
  10.2 29.7 %collective-permute-start.3 = (bf16[1536,768]{1,0:T(8,128)(2,1)}, bf16[1536,768]{1,0:T(8,128)(2,1)}, u32[]{:S(2)}, u32[]{:S(2)}) collective-permute-start(bf16[1536,768]{1,0:T(8,128)(2,1)} %bitcast.21), channel_id=1, source_target_pairs={{0,1},{1,0},{2,3},{3,2},{4,5},{5,4},{6,7},{7,6},{8,9},{9,8},{10,11... | collective-permute-start | bytes 7077896 | tf_op jit(solution)/shard_map/ppermute | solution.py:834
  10.3 29.5 %all-to-all-start = ((bf16[16,16,1664]{2,1,0:T(8,128)(2,1)}), bf16[16,16,1664]{2,1,0:T(8,128)(2,1)}, u32[]{:S(2)}, u32[]{:S(2)}) async-start(bf16[16,16,1664]{2,1,0:T(8,128)(2,1)} %bitcast.16), calls=%async_computation | async-start | bytes 1703936 | tf_op jit(solution)/shard_map/all_to_all | solution.py:976
  49.2 5.6 %collective-permute-start.4 = (bf16[256,4608]{1,0:T(8,128)(2,1)}, bf16[256,4608]{1,0:T(8,128)(2,1)}, u32[]{:S(2)}, u32[]{:S(2)}) collective-permute-start(bf16[256,4608]{1,0:T(8,128)(2,1)} %get-tuple-element.98), channel_id=1, source_target_pairs={{0,1},{1,0},{2,3},{3,2},{4,5},{5,4},{6,7},{7,6},{8,9},{9,8},{10,11... | collective-permute-start | bytes 7077896 | tf_op jit(solution)/shard_map/ppermute | solution.py:834
  49.3 18.5 %all-to-all-start.1 = ((bf16[16,16,768]{2,1,0:T(8,128)(2,1)}), bf16[16,16,768]{2,1,0:T(8,128)(2,1)}, u32[]{:S(2)}, u32[]{:S(2)}) async-start(bf16[16,16,768]{2,1,0:T(8,128)(2,1)} %bitcast.18), calls=%async_computation.1 | async-start | bytes 786432 | tf_op jit(solution)/shard_map/all_to_all | solution.py:1022
  54.6 17.6 %collective-permute-start.6 = (f32[128,768]{1,0:T(8,128)}, f32[128,768]{1,0:T(8,128)}, u32[]{:S(2)}, u32[]{:S(2)}) collective-permute-start(f32[128,768]{1,0:T(8,128)} %get-tuple-element.103.refs_4_), channel_id=1, source_target_pairs={{0,1},{1,0},{2,3},{3,2},{4,5},{5,4},{6,7},{7,6},{8,9},{9,8},{10,11... | collective-permute-start | bytes 1179656 | tf_op jit(solution)/shard_map/ppermute | solution.py:834
  67.8 4.4 %collective-permute-start.5 = (bf16[256,768]{1,0:T(8,128)(2,1)}, bf16[256,768]{1,0:T(8,128)(2,1)S(1)}, u32[]{:S(2)}, u32[]{:S(2)}) collective-permute-start(bf16[256,768]{1,0:T(8,128)(2,1)} %bitcast.8.refs_0_), channel_id=1, source_target_pairs={{0,1},{1,0},{2,3},{3,2},{4,5},{5,4},{6,7},{7,6},{8,9},{9,8},{10,11... | collective-permute-start | bytes 1179656 | tf_op jit(solution)/shard_map/ppermute | solution.py:834
  67.8 4.3 %collective-permute-start.7 = (bf16[128,768]{1,0:T(8,128)(2,1)}, bf16[128,768]{1,0:T(8,128)(2,1)S(1)}, u32[]{:S(2)}, u32[]{:S(2)}) collective-permute-start(bf16[128,768]{1,0:T(8,128)(2,1)} %refs_6_.2), channel_id=1, source_target_pairs={{0,1},{1,0},{2,3},{3,2},{4,5},{5,4},{6,7},{7,6},{8,9},{9,8},{10,11... | collective-permute-start | bytes 589832 | tf_op jit(solution)/shard_map/ppermute | solution.py:834
  68.3 18.1 %all-to-all-start.2 = ((bf16[16,16,768]{2,1,0:T(8,128)(2,1)}), bf16[16,16,768]{2,1,0:T(8,128)(2,1)S(1)}, u32[]{:S(2)}, u32[]{:S(2)}) async-start(bf16[16,16,768]{2,1,0:T(8,128)(2,1)} %bitcast.17), calls=%async_computation.2 | async-start | bytes 786432 | tf_op jit(solution)/shard_map/all_to_all | solution.py:1027
  81.4 11.5 %collective-permute-start.9 = (bf16[512,384]{1,0:T(8,128)(2,1)}, bf16[512,384]{1,0:T(8,128)(2,1)S(1)}, u32[]{:S(2)}, u32[]{:S(2)}) collective-permute-start(bf16[512,384]{1,0:T(8,128)(2,1)} %get-tuple-element.121), channel_id=1, source_target_pairs={{0,2},{1,9},{2,0},{3,11},{4,6},{5,13},{6,4},{7,15},{8,10},{9,1},{1... | collective-permute-start | bytes 1179656 | tf_op jit(solution)/shard_map/ppermute | solution.py:842
  83.4 12.7 %collective-permute-start.14 = (bf16[512,384]{1,0:T(8,128)(2,1)}, bf16[512,384]{1,0:T(8,128)(2,1)S(1)}, u32[]{:S(2)}, u32[]{:S(2)}) collective-permute-start(bf16[512,384]{1,0:T(8,128)(2,1)} %get-tuple-element.124), channel_id=1, source_target_pairs={{0,4},{1,3},{2,6},{3,1},{4,0},{5,7},{6,2},{7,5},{8,12},{9,11},{10,... | collective-permute-start | bytes 1179656 | tf_op jit(solution)/shard_map/ppermute | solution.py:842
  85.0 12.9 %collective-permute-start.23 = (bf16[512,384]{1,0:T(8,128)(2,1)}, bf16[512,384]{1,0:T(8,128)(2,1)S(1)}, u32[]{:S(2)}, u32[]{:S(2)}) collective-permute-start(bf16[512,384]{1,0:T(8,128)(2,1)} %get-tuple-element.126), channel_id=1, source_target_pairs={{0,8},{1,5},{2,10},{3,7},{4,12},{5,1},{6,14},{7,3},{8,0},{9,13},{1... | collective-permute-start | bytes 1179656 | tf_op jit(solution)/shard_map/ppermute | solution.py:842
  86.5 13.0 %collective-permute-start.34 = (bf16[128,768]{1,0:T(8,128)(2,1)}, bf16[128,768]{1,0:T(8,128)(2,1)S(1)}, u32[]{:S(2)}, u32[]{:S(2)}) collective-permute-start(bf16[128,768]{1,0:T(8,128)(2,1)} %get-tuple-element.135), channel_id=1, source_target_pairs={{0,1},{1,0},{2,3},{3,2},{4,5},{5,4},{6,7},{7,6},{8,9},{9,8},{10,11... | collective-permute-start | bytes 589832 | tf_op jit(solution)/shard_map/ppermute | solution.py:834
  93.9 8.0 %collective-permute-start.10 = (bf16[256,384]{1,0:T(8,128)(2,1)S(1)}, bf16[256,384]{1,0:T(8,128)(2,1)S(1)}, u32[]{:S(2)}, u32[]{:S(2)}) collective-permute-start(bf16[256,384]{1,0:T(8,128)(2,1)S(1)} %get-tuple-element.164), channel_id=1, source_target_pairs={{0,4},{1,3},{2,6},{3,1},{4,0},{5,7},{6,2},{7,5},{8,12},{9,11},{10,... | collective-permute-start | bytes 589832 | tf_op jit(solution)/shard_map/ppermute | solution.py:842
  96.3 7.6 %collective-permute-start.15 = (bf16[256,384]{1,0:T(8,128)(2,1)S(1)}, bf16[256,384]{1,0:T(8,128)(2,1)S(1)}, u32[]{:S(2)}, u32[]{:S(2)}) collective-permute-start(bf16[256,384]{1,0:T(8,128)(2,1)S(1)} %get-tuple-element.162), channel_id=1, source_target_pairs={{0,8},{1,5},{2,10},{3,7},{4,12},{5,1},{6,14},{7,3},{8,0},{9,13},{1... | collective-permute-start | bytes 589832 | tf_op jit(solution)/shard_map/ppermute | solution.py:842
  97.9 7.1 %collective-permute-start.24 = (bf16[256,384]{1,0:T(8,128)(2,1)S(1)}, bf16[256,384]{1,0:T(8,128)(2,1)S(1)}, u32[]{:S(2)}, u32[]{:S(2)}) collective-permute-start(bf16[256,384]{1,0:T(8,128)(2,1)S(1)} %get-tuple-element.160), channel_id=1, source_target_pairs={{0,2},{1,9},{2,0},{3,11},{4,6},{5,13},{6,4},{7,15},{8,10},{9,1},{1... | collective-permute-start | bytes 589832 | tf_op jit(solution)/shard_map/ppermute | solution.py:842
  102.0 10.2 %collective-permute-start.11 = (bf16[176,384]{1,0:T(8,128)(2,1)S(1)}, bf16[176,384]{1,0:T(8,128)(2,1)S(1)}, u32[]{:S(2)}, u32[]{:S(2)}) collective-permute-start(bf16[176,384]{1,0:T(8,128)(2,1)S(1)} %pad_maximum_fusion.6), channel_id=1, source_target_pairs={{0,8},{1,5},{2,10},{3,7},{4,12},{5,1},{6,14},{7,3},{8,0},{9,13},{1... | collective-permute-start | bytes 405512 | tf_op jit(solution)/shard_map/ppermute | solution.py:842
  103.9 4.7 %collective-permute-start.16 = (bf16[128,384]{1,0:T(8,128)(2,1)S(1)}, bf16[128,384]{1,0:T(8,128)(2,1)S(1)}, u32[]{:S(2)}, u32[]{:S(2)}) collective-permute-start(bf16[128,384]{1,0:T(8,128)(2,1)S(1)} %add_convert_fusion.13), channel_id=1, source_target_pairs={{0,2},{1,9},{2,0},{3,11},{4,6},{5,13},{6,4},{7,15},{8,10},{9,1},{1... | collective-permute-start | bytes 294920 | tf_op jit(solution)/shard_map/ppermute | solution.py:842
  105.0 5.8 %collective-permute-start.25 = (bf16[128,384]{1,0:T(8,128)(2,1)S(1)}, bf16[128,384]{1,0:T(8,128)(2,1)S(1)}, u32[]{:S(2)}, u32[]{:S(2)}) collective-permute-start(bf16[128,384]{1,0:T(8,128)(2,1)S(1)} %add_convert_fusion.9), channel_id=1, source_target_pairs={{0,4},{1,3},{2,6},{3,1},{4,0},{5,7},{6,2},{7,5},{8,12},{9,11},{10,... | collective-permute-start | bytes 294920 | tf_op jit(solution)/shard_map/ppermute | solution.py:842
  108.6 13.0 %collective-permute-start.17 = (bf16[128,384]{1,0:T(8,128)(2,1)S(1)}, bf16[128,384]{1,0:T(8,128)(2,1)S(1)}, u32[]{:S(2)}, u32[]{:S(2)}) collective-permute-start(bf16[128,384]{1,0:T(8,128)(2,1)S(1)} %add_convert_fusion.12), channel_id=1, source_target_pairs={{0,16},{1,17},{2,18},{3,19},{4,20},{5,21},{6,22},{7,23},{8,24},{9,... | collective-permute-start | bytes 294920 | tf_op jit(solution)/shard_map/ppermute | solution.py:842
  110.9 9.4 %collective-permute-start.26 = (bf16[128,384]{1,0:T(8,128)(2,1)S(1)}, bf16[128,384]{1,0:T(8,128)(2,1)S(1)}, u32[]{:S(2)}, u32[]{:S(2)}) collective-permute-start(bf16[128,384]{1,0:T(8,128)(2,1)S(1)} %add_convert_fusion.8), channel_id=1, source_target_pairs={{0,16},{1,17},{2,18},{3,19},{4,20},{5,21},{6,22},{7,23},{8,24},{9,... | collective-permute-start | bytes 294920 | tf_op jit(solution)/shard_map/ppermute | solution.py:842
  112.3 9.4 %collective-permute-start.12 = (bf16[176,384]{1,0:T(8,128)(2,1)S(1)}, bf16[176,384]{1,0:T(8,128)(2,1)S(1)}, u32[]{:S(2)}, u32[]{:S(2)}) collective-permute-start(bf16[176,384]{1,0:T(8,128)(2,1)S(1)} %pad_maximum_fusion.7), channel_id=1, source_target_pairs={{0,16},{1,17},{2,18},{3,19},{4,20},{5,21},{6,22},{7,23},{8,24},{9,... | collective-permute-start | bytes 405512 | tf_op jit(solution)/shard_map/ppermute | solution.py:842
  120.3 4.7 %collective-permute-start.27 = (bf16[128,384]{1,0:T(8,128)(2,1)S(1)}, bf16[128,384]{1,0:T(8,128)(2,1)S(1)}, u32[]{:S(2)}, u32[]{:S(2)}) collective-permute-start(bf16[128,384]{1,0:T(8,128)(2,1)S(1)} %add_convert_fusion.7), channel_id=1, source_target_pairs={{0,4},{1,3},{2,6},{3,1},{4,0},{5,7},{6,2},{7,5},{8,12},{9,11},{10,... | collective-permute-start | bytes 294920 | tf_op jit(solution)/shard_map/ppermute | solution.py:842
  121.8 5.1 %collective-permute-start.18 = (bf16[176,384]{1,0:T(8,128)(2,1)S(1)}, bf16[176,384]{1,0:T(8,128)(2,1)S(1)}, u32[]{:S(2)}, u32[]{:S(2)}) collective-permute-start(bf16[176,384]{1,0:T(8,128)(2,1)S(1)} %pad_maximum_fusion.8), channel_id=1, source_target_pairs={{0,2},{1,9},{2,0},{3,11},{4,6},{5,13},{6,4},{7,15},{8,10},{9,1},{1... | collective-permute-start | bytes 405512 | tf_op jit(solution)/shard_map/ppermute | solution.py:842
  123.1 4.7 %collective-permute-start.13 = (bf16[128,384]{1,0:T(8,128)(2,1)S(1)}, bf16[128,384]{1,0:T(8,128)(2,1)S(1)}, u32[]{:S(2)}, u32[]{:S(2)}) collective-permute-start(bf16[128,384]{1,0:T(8,128)(2,1)S(1)} %add_convert_fusion.15), channel_id=1, source_target_pairs={{0,8},{1,5},{2,10},{3,7},{4,12},{5,1},{6,14},{7,3},{8,0},{9,13},{1... | collective-permute-start | bytes 294920 | tf_op jit(solution)/shard_map/ppermute | solution.py:842
  125.0 7.5 %collective-permute-start.28 = (bf16[256,384]{1,0:T(8,128)(2,1)S(1)}, bf16[256,384]{1,0:T(8,128)(2,1)S(1)}, u32[]{:S(2)}, u32[]{:S(2)}) collective-permute-start(bf16[256,384]{1,0:T(8,128)(2,1)S(1)} %pad_maximum_fusion.5), channel_id=1, source_target_pairs={{0,2},{1,9},{2,0},{3,11},{4,6},{5,13},{6,4},{7,15},{8,10},{9,1},{1... | collective-permute-start | bytes 589832 | tf_op jit(solution)/shard_map/ppermute | solution.py:842
  126.9 6.2 %collective-permute-start.21 = (bf16[256,384]{1,0:T(8,128)(2,1)S(1)}, bf16[256,384]{1,0:T(8,128)(2,1)S(1)}, u32[]{:S(2)}, u32[]{:S(2)}) collective-permute-start(bf16[256,384]{1,0:T(8,128)(2,1)S(1)} %pad_maximum_fusion.4), channel_id=1, source_target_pairs={{0,8},{1,5},{2,10},{3,7},{4,12},{5,1},{6,14},{7,3},{8,0},{9,13},{1... | collective-permute-start | bytes 589832 | tf_op jit(solution)/shard_map/ppermute | solution.py:842
  127.8 7.2 %collective-permute-start.19 = (bf16[304,384]{1,0:T(8,128)(2,1)S(1)}, bf16[304,384]{1,0:T(8,128)(2,1)S(1)}, u32[]{:S(2)}, u32[]{:S(2)}) collective-permute-start(bf16[304,384]{1,0:T(8,128)(2,1)S(1)} %pad_maximum_fusion.3), channel_id=1, source_target_pairs={{0,4},{1,3},{2,6},{3,1},{4,0},{5,7},{6,2},{7,5},{8,12},{9,11},{10,... | collective-permute-start | bytes 700424 | tf_op jit(solution)/shard_map/ppermute | solution.py:842
  132.7 9.9 %collective-permute-start.29 = (bf16[512,384]{1,0:T(8,128)(2,1)S(1)}, bf16[512,384]{1,0:T(8,128)(2,1)S(1)}, u32[]{:S(2)}, u32[]{:S(2)}) collective-permute-start(bf16[512,384]{1,0:T(8,128)(2,1)S(1)} %pad_maximum_fusion.2.refs_4_), channel_id=1, source_target_pairs={{0,8},{1,5},{2,10},{3,7},{4,12},{5,1},{6,14},{7,3},{8,0},{9,13},{1... | collective-permute-start | bytes 1179656 | tf_op jit(solution)/shard_map/ppermute | solution.py:842
  133.2 4.7 %collective-permute-start.31 = (bf16[512,384]{1,0:T(8,128)(2,1)S(1)}, bf16[512,384]{1,0:T(8,128)(2,1)S(1)}, u32[]{:S(2)}, u32[]{:S(2)}) collective-permute-start(bf16[512,384]{1,0:T(8,128)(2,1)S(1)} %pad_maximum_fusion.1.refs_2_), channel_id=1, source_target_pairs={{0,1},{1,0},{2,3},{3,2},{4,5},{5,4},{6,7},{7,6},{8,9},{9,8},{10,11... | collective-permute-start | bytes 1179656 | tf_op jit(solution)/shard_map/ppermute | solution.py:834
  133.4 10.8 %collective-permute-start.22 = (bf16[512,384]{1,0:T(8,128)(2,1)S(1)}, bf16[512,384]{1,0:T(8,128)(2,1)S(1)}, u32[]{:S(2)}, u32[]{:S(2)}) collective-permute-start(bf16[512,384]{1,0:T(8,128)(2,1)S(1)} %pad_maximum_fusion.1.refs_2_), channel_id=1, source_target_pairs={{0,4},{1,3},{2,6},{3,1},{4,0},{5,7},{6,2},{7,5},{8,12},{9,11},{10,... | collective-permute-start | bytes 1179656 | tf_op jit(solution)/shard_map/ppermute | solution.py:842
  136.6 8.2 %collective-permute-start.20 = (bf16[512,384]{1,0:T(8,128)(2,1)S(1)}, bf16[512,384]{1,0:T(8,128)(2,1)S(1)}, u32[]{:S(2)}, u32[]{:S(2)}) collective-permute-start(bf16[512,384]{1,0:T(8,128)(2,1)S(1)} %pad_maximum_fusion.refs_0_), channel_id=1, source_target_pairs={{0,2},{1,9},{2,0},{3,11},{4,6},{5,13},{6,4},{7,15},{8,10},{9,1},{1... | collective-permute-start | bytes 1179656 | tf_op jit(solution)/shard_map/ppermute | solution.py:842
  (23 other events, 171.8 us)

commit v7 on v6

--- a/solution.py
+++ b/solution.py
@@ -180,6 +180,7 @@
     size = width // heads
     scale = 1.0 / math.sqrt(size)
     core = lax.axis_index("ffn")
+    wait.start(10)
     total = out_ref.shape[0]
     experts = router_ref.shape[0]
     sends = [
@@ -248,14 +249,14 @@
     flush(0)
     gain_second = gain_second_ref[...].reshape(1, width)
     act_second = (middle * root_mean(middle) * gain_second).astype(BF16)
+    staged[:, :width] = dot(place, act_second).astype(BF16)
+    sends[1].start()
     logits = cols_by_cols(act_second, router_ref[...])
     grown = jnp.exp(logits - jnp.max(logits, axis=-1, keepdims=True))
     gate = jnp.sum(grown * choose, axis=-1, keepdims=True) / jnp.sum(
         grown, axis=-1, keepdims=True
     )
     gate_ref[...] = jnp.broadcast_to(gate, gate_ref.shape)
-    staged[:, :width] = dot(place, act_second).astype(BF16)
-    sends[1].start()
     flush(1)
     for send in sends:
         send.wait()
@@ -883,9 +884,14 @@
                 upper = mine(order[k + 1])
                 keeps[p] = lax.dynamic_slice_in_dim(both, upper * half, half, 0)
                 sends[p] = lax.dynamic_slice_in_dim(both, (1 - upper) * half, half, 0)
+    ended = [None] * len(orders)
     for p, order in enumerate(orders):
+        ended[p] = exchange(count - 1, whole[p], order[-1])
+    for p, ahead in ((1, None), (2, 1), (0, 1)):
         x = whole[p]
-        whole[p] = add_low(x, exchange(count - 1, x, order[-1]))
+        if ahead is not None:
+            x, whole[ahead] = lax.optimization_barrier((x, whole[ahead]))
+        whole[p] = add_low(x, ended[p])
     got = [None] * len(orders)
     for k in reversed(range(count - 1)):
         for p, order in enumerate(orders):
@@ -964,7 +970,7 @@
             router,
             cotangent,
         ),
-        "hhhhhhhlllllll" + "hhrhhhhh",
+        "hhhhhhhlllslll" + "hhrhhhhh",
         vmem=64,
         flops=3000000000,
         scratch=[

time: 151 us -> 149 us (0.987)
  waiting for transfers between devices: 47.6 us -> 44.5 us
  starting transfers between devices: 47.9 us -> 49.7 us
    ppermute x21, waiting for transfers between devices: 25 us -> 21.5 us  [flip(): return lax.ppermute(x, ('expert', 'ffn'), pairs)]
  transfers between devices with their start and end apart: 41 -> 41, of which waited for: 17 -> 19; matrix products, arithmetic and copies ran while one was open for 3% -> 3% of each run, Pallas kernels for 20% -> 20%
where the time goes in v7:
time: 149 us
  starting transfers between devices  49.7 us (33%)
  Pallas kernels  48 us (32%)
  waiting for transfers between devices  44.5 us (30%)
  other arithmetic  3.03 us (2%)
    pallas_call x7, Pallas kernels, call(): pl.pallas_call(kernel, out_shape=[jax.ShapeDtypeStruct(s, d) for s, d in...  39.1 us
    ppermute x21, starting transfers between devices, flip(): return lax.ppermute(x, ('expert', 'ffn'), pairs)  28.7 us
    ppermute x21, waiting for transfers between devices, flip(): return lax.ppermute(x, ('expert', 'ffn'), pairs)  21.5 us
    all_to_all x1, waiting for transfers between devices, shards(): arrived = lax.all_to_all(outgoing, 'expert', 0, 0, tiled=True)  15.6 us
    pallas_call x1, Pallas kernels, expert_weights(): pl.pallas_call(expert_weights_kernel, grid=(steps,), out_shape=[jax.Shape...  8.89 us
    all_to_all x1, starting transfers between devices, shards(): arrived = lax.all_to_all(outgoing, 'expert', 0, 0, tiled=True)  8.27 us
    all_to_all x1, starting transfers between devices, shards(): grad_returned = lax.all_to_all(grad_slots, 'expert', 0, 0, tiled=True)  5.44 us
    all_to_all x1, waiting for transfers between devices, shards(): grad_returned = lax.all_to_all(grad_slots, 'expert', 0, 0, tiled=True)  4.08 us
  transfers between devices with their start and end apart: 41, of which 19 were waited for; matrix products, arithmetic and copies ran while one was open for 3% of the time, Pallas kernels for 20%

profile of v7, /device:TPU:0, one launch (start us, length us, event | category | flops | bytes accessed | tf_op | source)
XLA Modules:
  0.0 148.6 jit_solution(18138396787015374138)
XLA Ops:
  2.6 7.1 %shard_map.237 = (f32[128,768]{1,0:T(8,128)}, f32[128,128]{1,0:T(8,128)}, bf16[256,1664]{1,0:T(8,128)(2,1)}, bf16[128,768]{1,0:T(8,128)(2,1)}, f32[12,768]{1,0:T...) custom-call(bf16[128,768]{1,0:T(8,128)(2,1)} %refs_17_.1, ...), custom_call_target="tpu_custom_call" | custom-call | flops 3000000000 | bytes 1000000 | tf_op jit(solution)/shard_map/pallas_call | solution.py:101
  10.2 8.3 %all-to-all-start = ((bf16[16,16,1664]{2,1,0:T(8,128)(2,1)}), bf16[16,16,1664]{2,1,0:T(8,128)(2,1)}, u32[]{:S(2)}, u32[]{:S(2)}) async-start(bf16[16,16,1664]{2,1,0:T(8,128)(2,1)} %bitcast.16), calls=%async_computation | async-start | bytes 1703936 | tf_op jit(solution)/shard_map/all_to_all | solution.py:982
  18.5 5.6 %shard_map.238 = (bf16[256,768]{1,0:T(8,128)(2,1)}, bf16[256,384]{1,0:T(8,128)(2,1)}, bf16[256,384]{1,0:T(8,128)(2,1)}, bf16[256,384]{1,0:T(8,128)(2,1)}, f32[6,256,256]{2,1,0:T(8,128)}) custom-call(bf16[128,768]{1,0:T(8,128)(2,1)} %refs_17_.1, bf16[128,768]{1,0:T(8,128)(2,1)} %collective-permute-done.refs_1_.refs_18_, f32[768]{0:T(1024)} %refs_2_.3, ...), custom_call_target="tpu_custom_call" | custom-call | flops 3000000000 | bytes 1000000 | tf_op jit(solution)/shard_map/pallas_call | solution.py:101
  24.1 15.6 %all-to-all-done = bf16[16,16,1664]{2,1,0:T(8,128)(2,1)} async-done(((bf16[16,16,1664]{2,1,0:T(8,128)(2,1)}), bf16[16,16,1664]{2,1,0:T(8,128)(2,1)}, u32[]{:S(2)}, u32[]{:S(2)}) %all-to-all-start) | async-done | bytes 852000 | tf_op jit(solution)/shard_map/all_to_all | solution.py:982
  39.7 9.3 %shard_map.239 = (bf16[256,1536]{1,0:T(8,128)(2,1)}, bf16[256,1536]{1,0:T(8,128)(2,1)}, bf16[256,768]{1,0:T(8,128)(2,1)}, bf16[256,4608]{1,0:T(8,128)(2,1)}, bf1...) custom-call(bf16[256,1664]{1,0:T(8,128)(2,1)} %bitcast.4.refs_0_.flat_own, ...), custom_call_target="tpu_custom_call" | custom-call | flops 6000000000 | bytes 1000000 | tf_op jit(solution)/shard_map/pallas_call | solution.py:101
  49.2 5.4 %all-to-all-start.1 = ((bf16[16,16,768]{2,1,0:T(8,128)(2,1)}), bf16[16,16,768]{2,1,0:T(8,128)(2,1)}, u32[]{:S(2)}, u32[]{:S(2)}) async-start(bf16[16,16,768]{2,1,0:T(8,128)(2,1)} %bitcast.18), calls=%async_computation.1 | async-start | bytes 786432 | tf_op jit(solution)/shard_map/all_to_all | solution.py:1028
  54.9 8.9 %shard_map.240 = (f32[1,768,1536]{2,1,0:T(8,128)}, f32[1,1536,768]{2,1,0:T(8,128)}) custom-call(bf16[256,1664]{1,0:T(8,128)(2,1)} %bitcast.4.refs_0_.flat_own, bf16[256,768]{1,0:T(8,128)(2,1)} %get-tuple-element.99.sent_own, bf16[256,1536]{1,0:T(8,128)(2,1)} %get-tuple-element.100.hid_own, bf16[256,1536]{1,0:T(8,128)(2,1)} %get-tuple-element.101.pre_own, ...), custom_call_target="tpu_custom_call" | custom-call | flops 2415919104 | bytes 14000000 | tf_op jit(solution)/shard_map/pallas_call | solution.py:488
  63.8 4.1 %all-to-all-done.1 = bf16[16,16,768]{2,1,0:T(8,128)(2,1)} async-done(((bf16[16,16,768]{2,1,0:T(8,128)(2,1)}), bf16[16,16,768]{2,1,0:T(8,128)(2,1)}, u32[]{:S(2)}, u32[]{:S(2)}) %all-to-all-start.1) | async-done | bytes 393248 | tf_op jit(solution)/shard_map/all_to_all | solution.py:1028
  68.4 3.7 %all-to-all-start.2 = ((bf16[16,16,768]{2,1,0:T(8,128)(2,1)}), bf16[16,16,768]{2,1,0:T(8,128)(2,1)S(1)}, u32[]{:S(2)}, u32[]{:S(2)}) async-start(bf16[16,16,768]{2,1,0:T(8,128)(2,1)} %bitcast.17), calls=%async_computation.2 | async-start | bytes 786432 | tf_op jit(solution)/shard_map/all_to_all | solution.py:1033
  73.0 8.3 %shard_map.241 = (bf16[512,384]{1,0:T(8,128)(2,1)}, bf16[512,384]{1,0:T(8,128)(2,1)}, bf16[512,384]{1,0:T(8,128)(2,1)}, bf16[512,384]{1,0:T(8,128)(2,1)}, bf16[5...) custom-call(bf16[256,768]{1,0:T(8,128)(2,1)} %bitcast.8.refs_0_, ...), custom_call_target="tpu_custom_call" | custom-call | flops 4000000000 | bytes 1000000 | tf_op jit(solution)/shard_map/pallas_call | solution.py:101
  81.3 2.0 %collective-permute-start.15 = (bf16[512,384]{1,0:T(8,128)(2,1)}, bf16[512,384]{1,0:T(8,128)(2,1)S(1)}, u32[]{:S(2)}, u32[]{:S(2)}) collective-permute-start(bf16[512,384]{1,0:T(8,128)(2,1)} %get-tuple-element.130), channel_id=1, source_target_pairs={{0,4},{1,3},{2,6},{3,1},{4,0},{5,7},{6,2},{7,5},{8,12},{9,11},{10,... | collective-permute-start | bytes 1179656 | tf_op jit(solution)/shard_map/ppermute | solution.py:843
  83.5 1.5 %collective-permute-start.12 = (bf16[512,384]{1,0:T(8,128)(2,1)}, bf16[512,384]{1,0:T(8,128)(2,1)S(1)}, u32[]{:S(2)}, u32[]{:S(2)}) collective-permute-start(bf16[512,384]{1,0:T(8,128)(2,1)} %get-tuple-element.128), channel_id=1, source_target_pairs={{0,8},{1,5},{2,10},{3,7},{4,12},{5,1},{6,14},{7,3},{8,0},{9,13},{1... | collective-permute-start | bytes 1179656 | tf_op jit(solution)/shard_map/ppermute | solution.py:843
  85.0 1.5 collective-permute-start.9
  87.6 5.1 %collective-permute-done.15 = bf16[512,384]{1,0:T(8,128)(2,1)S(1)} collective-permute-done((bf16[512,384]{1,0:T(8,128)(2,1)}, bf16[512,384]{1,0:T(8,128)(2,1)S(1)}, u32[]{:S(2)}, u32[]{:S(2)}) %collective-permute-start.15) | collective-permute-done | bytes 393248 | tf_op jit(solution)/shard_map/ppermute | solution.py:843
  93.8 2.4 %collective-permute-start.16 = (bf16[256,384]{1,0:T(8,128)(2,1)S(1)}, bf16[256,384]{1,0:T(8,128)(2,1)S(1)}, u32[]{:S(2)}, u32[]{:S(2)}) collective-permute-start(bf16[256,384]{1,0:T(8,128)(2,1)S(1)} %get-tuple-element.168), channel_id=1, source_target_pairs={{0,8},{1,5},{2,10},{3,7},{4,12},{5,1},{6,14},{7,3},{8,0},{9,13},{1... | collective-permute-start | bytes 589832 | tf_op jit(solution)/shard_map/ppermute | solution.py:843
  96.3 1.6 %collective-permute-start.13 = (bf16[256,384]{1,0:T(8,128)(2,1)S(1)}, bf16[256,384]{1,0:T(8,128)(2,1)S(1)}, u32[]{:S(2)}, u32[]{:S(2)}) collective-permute-start(bf16[256,384]{1,0:T(8,128)(2,1)S(1)} %get-tuple-element.170), channel_id=1, source_target_pairs={{0,2},{1,9},{2,0},{3,11},{4,6},{5,13},{6,4},{7,15},{8,10},{9,1},{1... | collective-permute-start | bytes 589832 | tf_op jit(solution)/shard_map/ppermute | solution.py:843
  98.0 1.5 %collective-permute-start.10 = (bf16[256,384]{1,0:T(8,128)(2,1)S(1)}, bf16[256,384]{1,0:T(8,128)(2,1)S(1)}, u32[]{:S(2)}, u32[]{:S(2)}) collective-permute-start(bf16[256,384]{1,0:T(8,128)(2,1)S(1)} %get-tuple-element.172), channel_id=1, source_target_pairs={{0,4},{1,3},{2,6},{3,1},{4,0},{5,7},{6,2},{7,5},{8,12},{9,11},{10,... | collective-permute-start | bytes 589832 | tf_op jit(solution)/shard_map/ppermute | solution.py:843
  99.8 2.1 %collective-permute-done.16 = bf16[256,384]{1,0:T(8,128)(2,1)S(1)} collective-permute-done((bf16[256,384]{1,0:T(8,128)(2,1)S(1)}, bf16[256,384]{1,0:T(8,128)(2,1)S(1)}, u32[]{:S(2)}, u32[]{:S(2)}) %collective-permute-start.16) | collective-permute-done | bytes 196640 | tf_op jit(solution)/shard_map/ppermute | solution.py:843
  104.7 1.5 %collective-permute-start.11 = (bf16[176,384]{1,0:T(8,128)(2,1)S(1)}, bf16[176,384]{1,0:T(8,128)(2,1)S(1)}, u32[]{:S(2)}, u32[]{:S(2)}) collective-permute-start(bf16[176,384]{1,0:T(8,128)(2,1)S(1)} %pad_maximum_fusion.6), channel_id=1, source_target_pairs={{0,8},{1,5},{2,10},{3,7},{4,12},{5,1},{6,14},{7,3},{8,0},{9,13},{1... | collective-permute-start | bytes 405512 | tf_op jit(solution)/shard_map/ppermute | solution.py:843
  106.6 2.7 %collective-permute-start.18 = (bf16[128,384]{1,0:T(8,128)(2,1)S(1)}, bf16[128,384]{1,0:T(8,128)(2,1)S(1)}, u32[]{:S(2)}, u32[]{:S(2)}) collective-permute-start(bf16[128,384]{1,0:T(8,128)(2,1)S(1)} %add_convert_fusion.10), channel_id=1, source_target_pairs={{0,16},{1,17},{2,18},{3,19},{4,20},{5,21},{6,22},{7,23},{8,24},{9,... | collective-permute-start | bytes 294920 | tf_op jit(solution)/shard_map/ppermute | solution.py:843
  111.6 1.6 %collective-permute-start.19 = (bf16[176,384]{1,0:T(8,128)(2,1)S(1)}, bf16[176,384]{1,0:T(8,128)(2,1)S(1)}, u32[]{:S(2)}, u32[]{:S(2)}) collective-permute-start(bf16[176,384]{1,0:T(8,128)(2,1)S(1)} %pad_maximum_fusion.7), channel_id=1, source_target_pairs={{0,16},{1,17},{2,18},{3,19},{4,20},{5,21},{6,22},{7,23},{8,24},{9,... | collective-permute-start | bytes 405512 | tf_op jit(solution)/shard_map/ppermute | solution.py:843
  113.2 2.9 %collective-permute-done.18 = bf16[128,384]{1,0:T(8,128)(2,1)S(1)} collective-permute-done((bf16[128,384]{1,0:T(8,128)(2,1)S(1)}, bf16[128,384]{1,0:T(8,128)(2,1)S(1)}, u32[]{:S(2)}, u32[]{:S(2)}) %collective-permute-start.18) | collective-permute-done | bytes 98336 | tf_op jit(solution)/shard_map/ppermute | solution.py:843
  116.2 2.5 %collective-permute-done.26 = bf16[128,384]{1,0:T(8,128)(2,1)S(1)} collective-permute-done((bf16[128,384]{1,0:T(8,128)(2,1)S(1)}, bf16[128,384]{1,0:T(8,128)(2,1)S(1)}, u32[]{:S(2)}, u32[]{:S(2)}) %collective-permute-start.26) | collective-permute-done | bytes 98336 | tf_op jit(solution)/shard_map/ppermute | solution.py:843
  118.7 1.7 %collective-permute-start.27 = (bf16[128,384]{1,0:T(8,128)(2,1)S(1)}, bf16[128,384]{1,0:T(8,128)(2,1)S(1)}, u32[]{:S(2)}, u32[]{:S(2)}) collective-permute-start(bf16[128,384]{1,0:T(8,128)(2,1)S(1)} %add_convert_fusion.7), channel_id=1, source_target_pairs={{0,4},{1,3},{2,6},{3,1},{4,0},{5,7},{6,2},{7,5},{8,12},{9,11},{10,... | collective-permute-start | bytes 294920 | tf_op jit(solution)/shard_map/ppermute | solution.py:843
  121.4 1.9 %collective-permute-done.27 = bf16[128,384]{1,0:T(8,128)(2,1)S(1)} collective-permute-done((bf16[128,384]{1,0:T(8,128)(2,1)S(1)}, bf16[128,384]{1,0:T(8,128)(2,1)S(1)}, u32[]{:S(2)}, u32[]{:S(2)}) %collective-permute-start.27) | collective-permute-done | bytes 98336 | tf_op jit(solution)/shard_map/ppermute | solution.py:843
  125.8 2.6 %collective-permute-start.22 = (bf16[304,384]{1,0:T(8,128)(2,1)S(1)}, bf16[304,384]{1,0:T(8,128)(2,1)S(1)}, u32[]{:S(2)}, u32[]{:S(2)}) collective-permute-start(bf16[304,384]{1,0:T(8,128)(2,1)S(1)} %pad_maximum_fusion.3), channel_id=1, source_target_pairs={{0,4},{1,3},{2,6},{3,1},{4,0},{5,7},{6,2},{7,5},{8,12},{9,11},{10,... | collective-permute-start | bytes 700424 | tf_op jit(solution)/shard_map/ppermute | solution.py:843
  128.4 1.8 %collective-permute-done.28 = bf16[256,384]{1,0:T(8,128)(2,1)S(1)} collective-permute-done((bf16[256,384]{1,0:T(8,128)(2,1)S(1)}, bf16[256,384]{1,0:T(8,128)(2,1)S(1)}, u32[]{:S(2)}, u32[]{:S(2)}) %collective-permute-start.28) | collective-permute-done | bytes 196640 | tf_op jit(solution)/shard_map/ppermute | solution.py:843
  132.0 2.0 %collective-permute-start.25 = (bf16[512,384]{1,0:T(8,128)(2,1)S(1)}, bf16[512,384]{1,0:T(8,128)(2,1)S(1)}, u32[]{:S(2)}, u32[]{:S(2)}) collective-permute-start(bf16[512,384]{1,0:T(8,128)(2,1)S(1)} %pad_maximum_fusion.1.refs_2_), channel_id=1, source_target_pairs={{0,4},{1,3},{2,6},{3,1},{4,0},{5,7},{6,2},{7,5},{8,12},{9,11},{10,... | collective-permute-start | bytes 1179656 | tf_op jit(solution)/shard_map/ppermute | solution.py:843
  137.2 4.5 %shard_map.242 = (f32[768,768]{1,0:T(8,128)}, f32[768,768]{1,0:T(8,128)}, f32[768,768]{1,0:T(8,128)}, f32[768,768]{1,0:T(8,128)}, f32[768]{0:T(1024)}, /*index=5...) custom-call(bf16[512,384]{1,0:T(8,128)(2,1)S(1)} %pad_maximum_fusion.refs_0_, ...), custom_call_target="tpu_custom_call" | custom-call | bytes 8000000 | tf_op jit(solution)/shard_map/pallas_call | solution.py:101
  141.8 1.6 %collective-permute-done.23.refs_0_ = bf16[512,384]{1,0:T(8,128)(2,1)S(1)} collective-permute-done((bf16[512,384]{1,0:T(8,128)(2,1)S(1)}, bf16[512,384]{1,0:T(8,128)(2,1)S(1)}, u32[]{:S(2)}, u32[]{:S(2)}) %collective-permute-start.23) | collective-permute-done | bytes 393248 | tf_op jit(solution)/shard_map/ppermute | solution.py:843
  143.9 2.2 %shard_map.243 = (f32[768,768]{1,0:T(8,128)}, f32[768,768]{1,0:T(8,128)}, f32[768,768]{1,0:T(8,128)}, f32[768,768]{1,0:T(8,128)}) custom-call(bf16[512,384]{1,0:T(8,128)(2,1)S(1)} %collective-permute-done.23.refs_0_, bf16[512,384]{1,0:T(8,128)(2,1)S(1)} %collective-permute-done.25.refs_1_, ...), custom_call_target="tpu_custom_call", output_to_operand_aliasing={{0}: (3, {}), {1}: (4, {}), {2}: (5, {}), {3}: (6, {})} | custom-call | bytes 8000000 | tf_op jit(solution)/shard_map/pallas_call | solution.py:101
  146.2 2.2 %shard_map.244 = (f32[768,768]{1,0:T(8,128)}, f32[768,768]{1,0:T(8,128)}, f32[768,768]{1,0:T(8,128)}, f32[768,768]{1,0:T(8,128)}) custom-call(bf16[512,384]{1,0:T(8,128)(2,1)S(1)} %collective-permute-done.35.refs_0_, bf16[512,384]{1,0:T(8,128)(2,1)S(1)} %collective-permute-done.36.refs_1_, ...), custom_call_target="tpu_custom_call", output_to_operand_aliasing={{0}: (3, {}), {1}: (4, {}), {2}: (5, {}), {3}: (6, {})} | custom-call | bytes 8000000 | tf_op jit(solution)/shard_map/pallas_call | solution.py:101
  (119 shorter events, 21.7 us)
Async XLA Ops:
  9.6 30.1 %collective-permute-start.2 = (bf16[768,1536]{1,0:T(8,128)(2,1)}, bf16[768,1536]{1,0:T(8,128)(2,1)}, u32[]{:S(2)}, u32[]{:S(2)}) collective-permute-start(bf16[768,1536]{1,0:T(8,128)(2,1)} %bitcast.19), channel_id=1, source_target_pairs={{0,1},{1,0},{2,3},{3,2},{4,5},{5,4},{6,7},{7,6},{8,9},{9,8},{10,11... | collective-permute-start | bytes 7077896 | tf_op jit(solution)/shard_map/ppermute | solution.py:835
  10.1 29.6 %collective-permute-start.3 = (bf16[1536,768]{1,0:T(8,128)(2,1)}, bf16[1536,768]{1,0:T(8,128)(2,1)}, u32[]{:S(2)}, u32[]{:S(2)}) collective-permute-start(bf16[1536,768]{1,0:T(8,128)(2,1)} %bitcast.21), channel_id=1, source_target_pairs={{0,1},{1,0},{2,3},{3,2},{4,5},{5,4},{6,7},{7,6},{8,9},{9,8},{10,11... | collective-permute-start | bytes 7077896 | tf_op jit(solution)/shard_map/ppermute | solution.py:835
  10.2 29.5 %all-to-all-start = ((bf16[16,16,1664]{2,1,0:T(8,128)(2,1)}), bf16[16,16,1664]{2,1,0:T(8,128)(2,1)}, u32[]{:S(2)}, u32[]{:S(2)}) async-start(bf16[16,16,1664]{2,1,0:T(8,128)(2,1)} %bitcast.16), calls=%async_computation | async-start | bytes 1703936 | tf_op jit(solution)/shard_map/all_to_all | solution.py:982
  49.1 5.8 %collective-permute-start.4 = (bf16[256,4608]{1,0:T(8,128)(2,1)}, bf16[256,4608]{1,0:T(8,128)(2,1)}, u32[]{:S(2)}, u32[]{:S(2)}) collective-permute-start(bf16[256,4608]{1,0:T(8,128)(2,1)} %get-tuple-element.102), channel_id=1, source_target_pairs={{0,1},{1,0},{2,3},{3,2},{4,5},{5,4},{6,7},{7,6},{8,9},{9,8},{10,11... | collective-permute-start | bytes 7077896 | tf_op jit(solution)/shard_map/ppermute | solution.py:835
  49.2 18.7 %all-to-all-start.1 = ((bf16[16,16,768]{2,1,0:T(8,128)(2,1)}), bf16[16,16,768]{2,1,0:T(8,128)(2,1)}, u32[]{:S(2)}, u32[]{:S(2)}) async-start(bf16[16,16,768]{2,1,0:T(8,128)(2,1)} %bitcast.18), calls=%async_computation.1 | async-start | bytes 786432 | tf_op jit(solution)/shard_map/all_to_all | solution.py:1028
  54.6 17.5 %collective-permute-start.6 = (f32[128,768]{1,0:T(8,128)}, f32[128,768]{1,0:T(8,128)}, u32[]{:S(2)}, u32[]{:S(2)}) collective-permute-start(f32[128,768]{1,0:T(8,128)} %get-tuple-element.107.refs_4_), channel_id=1, source_target_pairs={{0,1},{1,0},{2,3},{3,2},{4,5},{5,4},{6,7},{7,6},{8,9},{9,8},{10,11... | collective-permute-start | bytes 1179656 | tf_op jit(solution)/shard_map/ppermute | solution.py:835
  67.8 4.3 %collective-permute-start.5 = (bf16[256,768]{1,0:T(8,128)(2,1)}, bf16[256,768]{1,0:T(8,128)(2,1)S(1)}, u32[]{:S(2)}, u32[]{:S(2)}) collective-permute-start(bf16[256,768]{1,0:T(8,128)(2,1)} %bitcast.8.refs_0_), channel_id=1, source_target_pairs={{0,1},{1,0},{2,3},{3,2},{4,5},{5,4},{6,7},{7,6},{8,9},{9,8},{10,11... | collective-permute-start | bytes 1179656 | tf_op jit(solution)/shard_map/ppermute | solution.py:835
  68.4 18.2 %all-to-all-start.2 = ((bf16[16,16,768]{2,1,0:T(8,128)(2,1)}), bf16[16,16,768]{2,1,0:T(8,128)(2,1)S(1)}, u32[]{:S(2)}, u32[]{:S(2)}) async-start(bf16[16,16,768]{2,1,0:T(8,128)(2,1)} %bitcast.17), calls=%async_computation.2 | async-start | bytes 786432 | tf_op jit(solution)/shard_map/all_to_all | solution.py:1033
  81.3 11.4 %collective-permute-start.15 = (bf16[512,384]{1,0:T(8,128)(2,1)}, bf16[512,384]{1,0:T(8,128)(2,1)S(1)}, u32[]{:S(2)}, u32[]{:S(2)}) collective-permute-start(bf16[512,384]{1,0:T(8,128)(2,1)} %get-tuple-element.130), channel_id=1, source_target_pairs={{0,4},{1,3},{2,6},{3,1},{4,0},{5,7},{6,2},{7,5},{8,12},{9,11},{10,... | collective-permute-start | bytes 1179656 | tf_op jit(solution)/shard_map/ppermute | solution.py:843
  83.5 12.7 %collective-permute-start.12 = (bf16[512,384]{1,0:T(8,128)(2,1)}, bf16[512,384]{1,0:T(8,128)(2,1)S(1)}, u32[]{:S(2)}, u32[]{:S(2)}) collective-permute-start(bf16[512,384]{1,0:T(8,128)(2,1)} %get-tuple-element.128), channel_id=1, source_target_pairs={{0,8},{1,5},{2,10},{3,7},{4,12},{5,1},{6,14},{7,3},{8,0},{9,13},{1... | collective-permute-start | bytes 1179656 | tf_op jit(solution)/shard_map/ppermute | solution.py:843
  85.0 12.9 %collective-permute-start.9 = (bf16[512,384]{1,0:T(8,128)(2,1)}, bf16[512,384]{1,0:T(8,128)(2,1)S(1)}, u32[]{:S(2)}, u32[]{:S(2)}) collective-permute-start(bf16[512,384]{1,0:T(8,128)(2,1)} %get-tuple-element.125), channel_id=1, source_target_pairs={{0,2},{1,9},{2,0},{3,11},{4,6},{5,13},{6,4},{7,15},{8,10},{9,1},{1... | collective-permute-start | bytes 1179656 | tf_op jit(solution)/shard_map/ppermute | solution.py:843
  86.5 13.0 %collective-permute-start.34 = (bf16[128,768]{1,0:T(8,128)(2,1)}, bf16[128,768]{1,0:T(8,128)(2,1)S(1)}, u32[]{:S(2)}, u32[]{:S(2)}) collective-permute-start(bf16[128,768]{1,0:T(8,128)(2,1)} %get-tuple-element.143), channel_id=1, source_target_pairs={{0,1},{1,0},{2,3},{3,2},{4,5},{5,4},{6,7},{7,6},{8,9},{9,8},{10,11... | collective-permute-start | bytes 589832 | tf_op jit(solution)/shard_map/ppermute | solution.py:835
  93.8 8.0 %collective-permute-start.16 = (bf16[256,384]{1,0:T(8,128)(2,1)S(1)}, bf16[256,384]{1,0:T(8,128)(2,1)S(1)}, u32[]{:S(2)}, u32[]{:S(2)}) collective-permute-start(bf16[256,384]{1,0:T(8,128)(2,1)S(1)} %get-tuple-element.168), channel_id=1, source_target_pairs={{0,8},{1,5},{2,10},{3,7},{4,12},{5,1},{6,14},{7,3},{8,0},{9,13},{1... | collective-permute-start | bytes 589832 | tf_op jit(solution)/shard_map/ppermute | solution.py:843
  96.3 6.9 %collective-permute-start.13 = (bf16[256,384]{1,0:T(8,128)(2,1)S(1)}, bf16[256,384]{1,0:T(8,128)(2,1)S(1)}, u32[]{:S(2)}, u32[]{:S(2)}) collective-permute-start(bf16[256,384]{1,0:T(8,128)(2,1)S(1)} %get-tuple-element.170), channel_id=1, source_target_pairs={{0,2},{1,9},{2,0},{3,11},{4,6},{5,13},{6,4},{7,15},{8,10},{9,1},{1... | collective-permute-start | bytes 589832 | tf_op jit(solution)/shard_map/ppermute | solution.py:843
  98.0 6.6 %collective-permute-start.10 = (bf16[256,384]{1,0:T(8,128)(2,1)S(1)}, bf16[256,384]{1,0:T(8,128)(2,1)S(1)}, u32[]{:S(2)}, u32[]{:S(2)}) collective-permute-start(bf16[256,384]{1,0:T(8,128)(2,1)S(1)} %get-tuple-element.172), channel_id=1, source_target_pairs={{0,4},{1,3},{2,6},{3,1},{4,0},{5,7},{6,2},{7,5},{8,12},{9,11},{10,... | collective-permute-start | bytes 589832 | tf_op jit(solution)/shard_map/ppermute | solution.py:843
  101.9 4.7 %collective-permute-start.17 = (bf16[128,384]{1,0:T(8,128)(2,1)S(1)}, bf16[128,384]{1,0:T(8,128)(2,1)S(1)}, u32[]{:S(2)}, u32[]{:S(2)}) collective-permute-start(bf16[128,384]{1,0:T(8,128)(2,1)S(1)} %add_convert_fusion.11), channel_id=1, source_target_pairs={{0,2},{1,9},{2,0},{3,11},{4,6},{5,13},{6,4},{7,15},{8,10},{9,1},{1... | collective-permute-start | bytes 294920 | tf_op jit(solution)/shard_map/ppermute | solution.py:843
  103.2 6.1 %collective-permute-start.14 = (bf16[128,384]{1,0:T(8,128)(2,1)S(1)}, bf16[128,384]{1,0:T(8,128)(2,1)S(1)}, u32[]{:S(2)}, u32[]{:S(2)}) collective-permute-start(bf16[128,384]{1,0:T(8,128)(2,1)S(1)} %add_convert_fusion.14), channel_id=1, source_target_pairs={{0,4},{1,3},{2,6},{3,1},{4,0},{5,7},{6,2},{7,5},{8,12},{9,11},{10,... | collective-permute-start | bytes 294920 | tf_op jit(solution)/shard_map/ppermute | solution.py:843
  104.7 6.8 %collective-permute-start.11 = (bf16[176,384]{1,0:T(8,128)(2,1)S(1)}, bf16[176,384]{1,0:T(8,128)(2,1)S(1)}, u32[]{:S(2)}, u32[]{:S(2)}) collective-permute-start(bf16[176,384]{1,0:T(8,128)(2,1)S(1)} %pad_maximum_fusion.6), channel_id=1, source_target_pairs={{0,8},{1,5},{2,10},{3,7},{4,12},{5,1},{6,14},{7,3},{8,0},{9,13},{1... | collective-permute-start | bytes 405512 | tf_op jit(solution)/shard_map/ppermute | solution.py:843
  106.6 9.5 %collective-permute-start.18 = (bf16[128,384]{1,0:T(8,128)(2,1)S(1)}, bf16[128,384]{1,0:T(8,128)(2,1)S(1)}, u32[]{:S(2)}, u32[]{:S(2)}) collective-permute-start(bf16[128,384]{1,0:T(8,128)(2,1)S(1)} %add_convert_fusion.10), channel_id=1, source_target_pairs={{0,16},{1,17},{2,18},{3,19},{4,20},{5,21},{6,22},{7,23},{8,24},{9,... | collective-permute-start | bytes 294920 | tf_op jit(solution)/shard_map/ppermute | solution.py:843
  109.4 9.2 %collective-permute-start.26 = (bf16[128,384]{1,0:T(8,128)(2,1)S(1)}, bf16[128,384]{1,0:T(8,128)(2,1)S(1)}, u32[]{:S(2)}, u32[]{:S(2)}) collective-permute-start(bf16[128,384]{1,0:T(8,128)(2,1)S(1)} %add_convert_fusion.13), channel_id=1, source_target_pairs={{0,16},{1,17},{2,18},{3,19},{4,20},{5,21},{6,22},{7,23},{8,24},{9,... | collective-permute-start | bytes 294920 | tf_op jit(solution)/shard_map/ppermute | solution.py:843
  111.6 8.8 %collective-permute-start.19 = (bf16[176,384]{1,0:T(8,128)(2,1)S(1)}, bf16[176,384]{1,0:T(8,128)(2,1)S(1)}, u32[]{:S(2)}, u32[]{:S(2)}) collective-permute-start(bf16[176,384]{1,0:T(8,128)(2,1)S(1)} %pad_maximum_fusion.7), channel_id=1, source_target_pairs={{0,16},{1,17},{2,18},{3,19},{4,20},{5,21},{6,22},{7,23},{8,24},{9,... | collective-permute-start | bytes 405512 | tf_op jit(solution)/shard_map/ppermute | solution.py:843
  118.7 4.7 %collective-permute-start.27 = (bf16[128,384]{1,0:T(8,128)(2,1)S(1)}, bf16[128,384]{1,0:T(8,128)(2,1)S(1)}, u32[]{:S(2)}, u32[]{:S(2)}) collective-permute-start(bf16[128,384]{1,0:T(8,128)(2,1)S(1)} %add_convert_fusion.7), channel_id=1, source_target_pairs={{0,4},{1,3},{2,6},{3,1},{4,0},{5,7},{6,2},{7,5},{8,12},{9,11},{10,... | collective-permute-start | bytes 294920 | tf_op jit(solution)/shard_map/ppermute | solution.py:843
  120.5 5.1 %collective-permute-start.21 = (bf16[176,384]{1,0:T(8,128)(2,1)S(1)}, bf16[176,384]{1,0:T(8,128)(2,1)S(1)}, u32[]{:S(2)}, u32[]{:S(2)}) collective-permute-start(bf16[176,384]{1,0:T(8,128)(2,1)S(1)} %pad_maximum_fusion.8), channel_id=1, source_target_pairs={{0,2},{1,9},{2,0},{3,11},{4,6},{5,13},{6,4},{7,15},{8,10},{9,1},{1... | collective-permute-start | bytes 405512 | tf_op jit(solution)/shard_map/ppermute | solution.py:843
  121.1 4.7 %collective-permute-start.20 = (bf16[128,384]{1,0:T(8,128)(2,1)S(1)}, bf16[128,384]{1,0:T(8,128)(2,1)S(1)}, u32[]{:S(2)}, u32[]{:S(2)}) collective-permute-start(bf16[128,384]{1,0:T(8,128)(2,1)S(1)} %add_convert_fusion.8), channel_id=1, source_target_pairs={{0,8},{1,5},{2,10},{3,7},{4,12},{5,1},{6,14},{7,3},{8,0},{9,13},{1... | collective-permute-start | bytes 294920 | tf_op jit(solution)/shard_map/ppermute | solution.py:843
  123.4 6.8 %collective-permute-start.28 = (bf16[256,384]{1,0:T(8,128)(2,1)S(1)}, bf16[256,384]{1,0:T(8,128)(2,1)S(1)}, u32[]{:S(2)}, u32[]{:S(2)}) collective-permute-start(bf16[256,384]{1,0:T(8,128)(2,1)S(1)} %pad_maximum_fusion.5), channel_id=1, source_target_pairs={{0,2},{1,9},{2,0},{3,11},{4,6},{5,13},{6,4},{7,15},{8,10},{9,1},{1... | collective-permute-start | bytes 589832 | tf_op jit(solution)/shard_map/ppermute | solution.py:843
  125.6 5.7 %collective-permute-start.24 = (bf16[256,384]{1,0:T(8,128)(2,1)S(1)}, bf16[256,384]{1,0:T(8,128)(2,1)S(1)}, u32[]{:S(2)}, u32[]{:S(2)}) collective-permute-start(bf16[256,384]{1,0:T(8,128)(2,1)S(1)} %pad_maximum_fusion.4), channel_id=1, source_target_pairs={{0,8},{1,5},{2,10},{3,7},{4,12},{5,1},{6,14},{7,3},{8,0},{9,13},{1... | collective-permute-start | bytes 589832 | tf_op jit(solution)/shard_map/ppermute | solution.py:843
  125.8 8.3 %collective-permute-start.22 = (bf16[304,384]{1,0:T(8,128)(2,1)S(1)}, bf16[304,384]{1,0:T(8,128)(2,1)S(1)}, u32[]{:S(2)}, u32[]{:S(2)}) collective-permute-start(bf16[304,384]{1,0:T(8,128)(2,1)S(1)} %pad_maximum_fusion.3), channel_id=1, source_target_pairs={{0,4},{1,3},{2,6},{3,1},{4,0},{5,7},{6,2},{7,5},{8,12},{9,11},{10,... | collective-permute-start | bytes 700424 | tf_op jit(solution)/shard_map/ppermute | solution.py:843
  130.2 5.4 %collective-permute-start.32 = (bf16[512,384]{1,0:T(8,128)(2,1)S(1)}, bf16[512,384]{1,0:T(8,128)(2,1)S(1)}, u32[]{:S(2)}, u32[]{:S(2)}) collective-permute-start(bf16[512,384]{1,0:T(8,128)(2,1)S(1)} %pad_maximum_fusion.2.refs_4_), channel_id=1, source_target_pairs={{0,1},{1,0},{2,3},{3,2},{4,5},{5,4},{6,7},{7,6},{8,9},{9,8},{10,11... | collective-permute-start | bytes 1179656 | tf_op jit(solution)/shard_map/ppermute | solution.py:835
  130.3 11.3 %collective-permute-start.29 = (bf16[512,384]{1,0:T(8,128)(2,1)S(1)}, bf16[512,384]{1,0:T(8,128)(2,1)S(1)}, u32[]{:S(2)}, u32[]{:S(2)}) collective-permute-start(bf16[512,384]{1,0:T(8,128)(2,1)S(1)} %pad_maximum_fusion.2.refs_4_), channel_id=1, source_target_pairs={{0,8},{1,5},{2,10},{3,7},{4,12},{5,1},{6,14},{7,3},{8,0},{9,13},{1... | collective-permute-start | bytes 1179656 | tf_op jit(solution)/shard_map/ppermute | solution.py:843
  131.4 5.2 %collective-permute-start.31 = (bf16[512,384]{1,0:T(8,128)(2,1)S(1)}, bf16[512,384]{1,0:T(8,128)(2,1)S(1)}, u32[]{:S(2)}, u32[]{:S(2)}) collective-permute-start(bf16[512,384]{1,0:T(8,128)(2,1)S(1)} %pad_maximum_fusion.1.refs_2_), channel_id=1, source_target_pairs={{0,1},{1,0},{2,3},{3,2},{4,5},{5,4},{6,7},{7,6},{8,9},{9,8},{10,11... | collective-permute-start | bytes 1179656 | tf_op jit(solution)/shard_map/ppermute | solution.py:835
  132.0 9.8 %collective-permute-start.25 = (bf16[512,384]{1,0:T(8,128)(2,1)S(1)}, bf16[512,384]{1,0:T(8,128)(2,1)S(1)}, u32[]{:S(2)}, u32[]{:S(2)}) collective-permute-start(bf16[512,384]{1,0:T(8,128)(2,1)S(1)} %pad_maximum_fusion.1.refs_2_), channel_id=1, source_target_pairs={{0,4},{1,3},{2,6},{3,1},{4,0},{5,7},{6,2},{7,5},{8,12},{9,11},{10,... | collective-permute-start | bytes 1179656 | tf_op jit(solution)/shard_map/ppermute | solution.py:843
  135.6 7.8 %collective-permute-start.23 = (bf16[512,384]{1,0:T(8,128)(2,1)S(1)}, bf16[512,384]{1,0:T(8,128)(2,1)S(1)}, u32[]{:S(2)}, u32[]{:S(2)}) collective-permute-start(bf16[512,384]{1,0:T(8,128)(2,1)S(1)} %pad_maximum_fusion.refs_0_), channel_id=1, source_target_pairs={{0,2},{1,9},{2,0},{3,11},{4,6},{5,13},{6,4},{7,15},{8,10},{9,1},{1... | collective-permute-start | bytes 1179656 | tf_op jit(solution)/shard_map/ppermute | solution.py:843
  (23 other events, 175.3 us)

commit v8 on v7

--- a/solution.py
+++ b/solution.py
@@ -1000,6 +1000,9 @@
         flops=3000000000,
         scratch=[pltpu.VMEM((width, part), BF16)] * 3 + [pltpu.SemaphoreType.DMA((3,))],
     )
+    act, cot_other, mixed_other, middle_other = lax.optimization_barrier(
+        (act, cot_other, mixed_other, middle_other)
+    )
     chunk = hidden // 2
     steps = 2 * hidden // chunk
     hid_own, pre_own, sent, bundle, grad_slots, produced, router_part = call(

time: 149 us -> 149 us (level)
  no operation moved by 1% of the time
where the time goes in v8:
time: 149 us; the launch traced here: 148 us
  starting transfers between devices  49 us (33%)
  Pallas kernels  48 us (32%)
  waiting for transfers between devices  44.4 us (30%)
  other arithmetic  3.03 us (2%)
    pallas_call x7, Pallas kernels, call(): pl.pallas_call(kernel, out_shape=[jax.ShapeDtypeStruct(s, d) for s, d in...  39.1 us
    ppermute x21, starting transfers between devices, flip(): return lax.ppermute(x, ('expert', 'ffn'), pairs)  28.2 us
    ppermute x21, waiting for transfers between devices, flip(): return lax.ppermute(x, ('expert', 'ffn'), pairs)  21.9 us
    all_to_all x1, waiting for transfers between devices, shards(): arrived = lax.all_to_all(outgoing, 'expert', 0, 0, tiled=True)  15 us
    pallas_call x1, Pallas kernels, expert_weights(): pl.pallas_call(expert_weights_kernel, grid=(steps,), out_shape=[jax.Shape...  8.9 us
    all_to_all x1, starting transfers between devices, shards(): arrived = lax.all_to_all(outgoing, 'expert', 0, 0, tiled=True)  8.29 us
    all_to_all x1, starting transfers between devices, shards(): grad_returned = lax.all_to_all(grad_slots, 'expert', 0, 0, tiled=True)  5.26 us
    all_to_all x1, waiting for transfers between devices, shards(): grad_returned = lax.all_to_all(grad_slots, 'expert', 0, 0, tiled=True)  4.32 us
  transfers between devices with their start and end apart: 41, of which 19 were waited for; matrix products, arithmetic and copies ran while one was open for 3% of the time, Pallas kernels for 20%

profile of v8, /device:TPU:0, one launch (start us, length us, event | category | flops | bytes accessed | tf_op | source)
XLA Modules:
  0.0 147.8 jit_solution(15787405836583193290)
XLA Ops:
  2.6 7.1 %shard_map.237 = (f32[128,768]{1,0:T(8,128)}, f32[128,128]{1,0:T(8,128)}, bf16[256,1664]{1,0:T(8,128)(2,1)}, bf16[128,768]{1,0:T(8,128)(2,1)}, f32[12,768]{1,0:T...) custom-call(bf16[128,768]{1,0:T(8,128)(2,1)} %refs_17_.1, ...), custom_call_target="tpu_custom_call" | custom-call | flops 3000000000 | bytes 1000000 | tf_op jit(solution)/shard_map/pallas_call | solution.py:101
  10.2 8.3 %all-to-all-start = ((bf16[16,16,1664]{2,1,0:T(8,128)(2,1)}), bf16[16,16,1664]{2,1,0:T(8,128)(2,1)}, u32[]{:S(2)}, u32[]{:S(2)}) async-start(bf16[16,16,1664]{2,1,0:T(8,128)(2,1)} %bitcast.16), calls=%async_computation | async-start | bytes 1703936 | tf_op jit(solution)/shard_map/all_to_all | solution.py:982
  19.2 5.5 %shard_map.238 = (bf16[256,768]{1,0:T(8,128)(2,1)}, bf16[256,384]{1,0:T(8,128)(2,1)}, bf16[256,384]{1,0:T(8,128)(2,1)}, bf16[256,384]{1,0:T(8,128)(2,1)}, f32[6,256,256]{2,1,0:T(8,128)}) custom-call(bf16[128,768]{1,0:T(8,128)(2,1)} %refs_17_.1, bf16[128,768]{1,0:T(8,128)(2,1)} %collective-permute-done.refs_1_.refs_18_, f32[768]{0:T(1024)} %refs_2_.3, ...), custom_call_target="tpu_custom_call" | custom-call | flops 3000000000 | bytes 1000000 | tf_op jit(solution)/shard_map/pallas_call | solution.py:101
  24.8 15.0 %all-to-all-done = bf16[16,16,1664]{2,1,0:T(8,128)(2,1)} async-done(((bf16[16,16,1664]{2,1,0:T(8,128)(2,1)}), bf16[16,16,1664]{2,1,0:T(8,128)(2,1)}, u32[]{:S(2)}, u32[]{:S(2)}) %all-to-all-start) | async-done | bytes 852000 | tf_op jit(solution)/shard_map/all_to_all | solution.py:982
  39.7 9.3 %shard_map.239 = (bf16[256,1536]{1,0:T(8,128)(2,1)}, bf16[256,1536]{1,0:T(8,128)(2,1)}, bf16[256,768]{1,0:T(8,128)(2,1)}, bf16[256,4608]{1,0:T(8,128)(2,1)}, bf1...) custom-call(bf16[256,1664]{1,0:T(8,128)(2,1)} %bitcast.4.refs_0_.flat_own, ...), custom_call_target="tpu_custom_call" | custom-call | flops 6000000000 | bytes 1000000 | tf_op jit(solution)/shard_map/pallas_call | solution.py:101
  49.1 5.3 %all-to-all-start.1 = ((bf16[16,16,768]{2,1,0:T(8,128)(2,1)}), bf16[16,16,768]{2,1,0:T(8,128)(2,1)}, u32[]{:S(2)}, u32[]{:S(2)}) async-start(bf16[16,16,768]{2,1,0:T(8,128)(2,1)} %bitcast.18), calls=%async_computation.1 | async-start | bytes 786432 | tf_op jit(solution)/shard_map/all_to_all | solution.py:1031
  54.4 8.9 %shard_map.240 = (f32[1,768,1536]{2,1,0:T(8,128)}, f32[1,1536,768]{2,1,0:T(8,128)}) custom-call(bf16[256,1664]{1,0:T(8,128)(2,1)} %bitcast.4.refs_0_.flat_own, bf16[256,768]{1,0:T(8,128)(2,1)} %get-tuple-element.107.sent_own, bf16[256,1536]{1,0:T(8,128)(2,1)} %get-tuple-element.108.hid_own, bf16[256,1536]{1,0:T(8,128)(2,1)} %get-tuple-element.109.pre_own, ...), custom_call_target="tpu_custom_call" | custom-call | flops 2415919104 | bytes 14000000 | tf_op jit(solution)/shard_map/pallas_call | solution.py:488
  63.3 4.3 %all-to-all-done.1 = bf16[16,16,768]{2,1,0:T(8,128)(2,1)} async-done(((bf16[16,16,768]{2,1,0:T(8,128)(2,1)}), bf16[16,16,768]{2,1,0:T(8,128)(2,1)}, u32[]{:S(2)}, u32[]{:S(2)}) %all-to-all-start.1) | async-done | bytes 393248 | tf_op jit(solution)/shard_map/all_to_all | solution.py:1031
  67.7 3.8 %all-to-all-start.2 = ((bf16[16,16,768]{2,1,0:T(8,128)(2,1)}), bf16[16,16,768]{2,1,0:T(8,128)(2,1)S(1)}, u32[]{:S(2)}, u32[]{:S(2)}) async-start(bf16[16,16,768]{2,1,0:T(8,128)(2,1)} %bitcast.17), calls=%async_computation.2 | async-start | bytes 786432 | tf_op jit(solution)/shard_map/all_to_all | solution.py:1036
  72.2 8.3 %shard_map.241 = (bf16[512,384]{1,0:T(8,128)(2,1)}, bf16[512,384]{1,0:T(8,128)(2,1)}, bf16[512,384]{1,0:T(8,128)(2,1)}, bf16[512,384]{1,0:T(8,128)(2,1)}, bf16[5...) custom-call(bf16[256,768]{1,0:T(8,128)(2,1)} %bitcast.8.refs_0_, ...), custom_call_target="tpu_custom_call" | custom-call | flops 4000000000 | bytes 1000000 | tf_op jit(solution)/shard_map/pallas_call | solution.py:101
  80.6 1.9 %collective-permute-start.15 = (bf16[512,384]{1,0:T(8,128)(2,1)}, bf16[512,384]{1,0:T(8,128)(2,1)S(1)}, u32[]{:S(2)}, u32[]{:S(2)}) collective-permute-start(bf16[512,384]{1,0:T(8,128)(2,1)} %get-tuple-element.138), channel_id=1, source_target_pairs={{0,4},{1,3},{2,6},{3,1},{4,0},{5,7},{6,2},{7,5},{8,12},{9,11},{10,... | collective-permute-start | bytes 1179656 | tf_op jit(solution)/shard_map/ppermute | solution.py:843
  82.7 1.5 %collective-permute-start.12 = (bf16[512,384]{1,0:T(8,128)(2,1)}, bf16[512,384]{1,0:T(8,128)(2,1)S(1)}, u32[]{:S(2)}, u32[]{:S(2)}) collective-permute-start(bf16[512,384]{1,0:T(8,128)(2,1)} %get-tuple-element.136), channel_id=1, source_target_pairs={{0,8},{1,5},{2,10},{3,7},{4,12},{5,1},{6,14},{7,3},{8,0},{9,13},{1... | collective-permute-start | bytes 1179656 | tf_op jit(solution)/shard_map/ppermute | solution.py:843
  86.8 5.4 %collective-permute-done.15 = bf16[512,384]{1,0:T(8,128)(2,1)S(1)} collective-permute-done((bf16[512,384]{1,0:T(8,128)(2,1)}, bf16[512,384]{1,0:T(8,128)(2,1)S(1)}, u32[]{:S(2)}, u32[]{:S(2)}) %collective-permute-start.15) | collective-permute-done | bytes 393248 | tf_op jit(solution)/shard_map/ppermute | solution.py:843
  93.3 2.1 %collective-permute-start.16 = (bf16[256,384]{1,0:T(8,128)(2,1)S(1)}, bf16[256,384]{1,0:T(8,128)(2,1)S(1)}, u32[]{:S(2)}, u32[]{:S(2)}) collective-permute-start(bf16[256,384]{1,0:T(8,128)(2,1)S(1)} %get-tuple-element.176), channel_id=1, source_target_pairs={{0,8},{1,5},{2,10},{3,7},{4,12},{5,1},{6,14},{7,3},{8,0},{9,13},{1... | collective-permute-start | bytes 589832 | tf_op jit(solution)/shard_map/ppermute | solution.py:843
  95.5 1.6 %collective-permute-start.13 = (bf16[256,384]{1,0:T(8,128)(2,1)S(1)}, bf16[256,384]{1,0:T(8,128)(2,1)S(1)}, u32[]{:S(2)}, u32[]{:S(2)}) collective-permute-start(bf16[256,384]{1,0:T(8,128)(2,1)S(1)} %get-tuple-element.178), channel_id=1, source_target_pairs={{0,2},{1,9},{2,0},{3,11},{4,6},{5,13},{6,4},{7,15},{8,10},{9,1},{1... | collective-permute-start | bytes 589832 | tf_op jit(solution)/shard_map/ppermute | solution.py:843
  97.2 1.5 %collective-permute-start.10 = (bf16[256,384]{1,0:T(8,128)(2,1)S(1)}, bf16[256,384]{1,0:T(8,128)(2,1)S(1)}, u32[]{:S(2)}, u32[]{:S(2)}) collective-permute-start(bf16[256,384]{1,0:T(8,128)(2,1)S(1)} %get-tuple-element.180), channel_id=1, source_target_pairs={{0,4},{1,3},{2,6},{3,1},{4,0},{5,7},{6,2},{7,5},{8,12},{9,11},{10,... | collective-permute-start | bytes 589832 | tf_op jit(solution)/shard_map/ppermute | solution.py:843
  98.9 2.1 %collective-permute-done.16 = bf16[256,384]{1,0:T(8,128)(2,1)S(1)} collective-permute-done((bf16[256,384]{1,0:T(8,128)(2,1)S(1)}, bf16[256,384]{1,0:T(8,128)(2,1)S(1)}, u32[]{:S(2)}, u32[]{:S(2)}) %collective-permute-start.16) | collective-permute-done | bytes 196640 | tf_op jit(solution)/shard_map/ppermute | solution.py:843
  101.1 1.6 %collective-permute-start.17 = (bf16[128,384]{1,0:T(8,128)(2,1)S(1)}, bf16[128,384]{1,0:T(8,128)(2,1)S(1)}, u32[]{:S(2)}, u32[]{:S(2)}) collective-permute-start(bf16[128,384]{1,0:T(8,128)(2,1)S(1)} %add_convert_fusion.11), channel_id=1, source_target_pairs={{0,2},{1,9},{2,0},{3,11},{4,6},{5,13},{6,4},{7,15},{8,10},{9,1},{1... | collective-permute-start | bytes 294920 | tf_op jit(solution)/shard_map/ppermute | solution.py:843
  103.9 1.6 %collective-permute-start.11 = (bf16[176,384]{1,0:T(8,128)(2,1)S(1)}, bf16[176,384]{1,0:T(8,128)(2,1)S(1)}, u32[]{:S(2)}, u32[]{:S(2)}) collective-permute-start(bf16[176,384]{1,0:T(8,128)(2,1)S(1)} %pad_maximum_fusion.6), channel_id=1, source_target_pairs={{0,8},{1,5},{2,10},{3,7},{4,12},{5,1},{6,14},{7,3},{8,0},{9,13},{1... | collective-permute-start | bytes 405512 | tf_op jit(solution)/shard_map/ppermute | solution.py:843
  105.8 2.7 %collective-permute-start.18 = (bf16[128,384]{1,0:T(8,128)(2,1)S(1)}, bf16[128,384]{1,0:T(8,128)(2,1)S(1)}, u32[]{:S(2)}, u32[]{:S(2)}) collective-permute-start(bf16[128,384]{1,0:T(8,128)(2,1)S(1)} %add_convert_fusion.10), channel_id=1, source_target_pairs={{0,16},{1,17},{2,18},{3,19},{4,20},{5,21},{6,22},{7,23},{8,24},{9,... | collective-permute-start | bytes 294920 | tf_op jit(solution)/shard_map/ppermute | solution.py:843
  110.8 1.6 %collective-permute-start.19 = (bf16[176,384]{1,0:T(8,128)(2,1)S(1)}, bf16[176,384]{1,0:T(8,128)(2,1)S(1)}, u32[]{:S(2)}, u32[]{:S(2)}) collective-permute-start(bf16[176,384]{1,0:T(8,128)(2,1)S(1)} %pad_maximum_fusion.7), channel_id=1, source_target_pairs={{0,16},{1,17},{2,18},{3,19},{4,20},{5,21},{6,22},{7,23},{8,24},{9,... | collective-permute-start | bytes 405512 | tf_op jit(solution)/shard_map/ppermute | solution.py:843
  112.4 2.9 %collective-permute-done.18 = bf16[128,384]{1,0:T(8,128)(2,1)S(1)} collective-permute-done((bf16[128,384]{1,0:T(8,128)(2,1)S(1)}, bf16[128,384]{1,0:T(8,128)(2,1)S(1)}, u32[]{:S(2)}, u32[]{:S(2)}) %collective-permute-start.18) | collective-permute-done | bytes 98336 | tf_op jit(solution)/shard_map/ppermute | solution.py:843
  115.3 2.5 %collective-permute-done.26 = bf16[128,384]{1,0:T(8,128)(2,1)S(1)} collective-permute-done((bf16[128,384]{1,0:T(8,128)(2,1)S(1)}, bf16[128,384]{1,0:T(8,128)(2,1)S(1)}, u32[]{:S(2)}, u32[]{:S(2)}) %collective-permute-start.26) | collective-permute-done | bytes 98336 | tf_op jit(solution)/shard_map/ppermute | solution.py:843
  117.8 1.7 %collective-permute-start.27 = (bf16[128,384]{1,0:T(8,128)(2,1)S(1)}, bf16[128,384]{1,0:T(8,128)(2,1)S(1)}, u32[]{:S(2)}, u32[]{:S(2)}) collective-permute-start(bf16[128,384]{1,0:T(8,128)(2,1)S(1)} %add_convert_fusion.7), channel_id=1, source_target_pairs={{0,4},{1,3},{2,6},{3,1},{4,0},{5,7},{6,2},{7,5},{8,12},{9,11},{10,... | collective-permute-start | bytes 294920 | tf_op jit(solution)/shard_map/ppermute | solution.py:843
  120.6 2.0 %collective-permute-done.27 = bf16[128,384]{1,0:T(8,128)(2,1)S(1)} collective-permute-done((bf16[128,384]{1,0:T(8,128)(2,1)S(1)}, bf16[128,384]{1,0:T(8,128)(2,1)S(1)}, u32[]{:S(2)}, u32[]{:S(2)}) %collective-permute-start.27) | collective-permute-done | bytes 98336 | tf_op jit(solution)/shard_map/ppermute | solution.py:843
  125.0 2.6 %collective-permute-start.22 = (bf16[304,384]{1,0:T(8,128)(2,1)S(1)}, bf16[304,384]{1,0:T(8,128)(2,1)S(1)}, u32[]{:S(2)}, u32[]{:S(2)}) collective-permute-start(bf16[304,384]{1,0:T(8,128)(2,1)S(1)} %pad_maximum_fusion.3), channel_id=1, source_target_pairs={{0,4},{1,3},{2,6},{3,1},{4,0},{5,7},{6,2},{7,5},{8,12},{9,11},{10,... | collective-permute-start | bytes 700424 | tf_op jit(solution)/shard_map/ppermute | solution.py:843
  127.6 1.8 %collective-permute-done.28 = bf16[256,384]{1,0:T(8,128)(2,1)S(1)} collective-permute-done((bf16[256,384]{1,0:T(8,128)(2,1)S(1)}, bf16[256,384]{1,0:T(8,128)(2,1)S(1)}, u32[]{:S(2)}, u32[]{:S(2)}) %collective-permute-start.28) | collective-permute-done | bytes 196640 | tf_op jit(solution)/shard_map/ppermute | solution.py:843
  131.2 2.0 %collective-permute-start.25 = (bf16[512,384]{1,0:T(8,128)(2,1)S(1)}, bf16[512,384]{1,0:T(8,128)(2,1)S(1)}, u32[]{:S(2)}, u32[]{:S(2)}) collective-permute-start(bf16[512,384]{1,0:T(8,128)(2,1)S(1)} %pad_maximum_fusion.1.refs_2_), channel_id=1, source_target_pairs={{0,4},{1,3},{2,6},{3,1},{4,0},{5,7},{6,2},{7,5},{8,12},{9,11},{10,... | collective-permute-start | bytes 1179656 | tf_op jit(solution)/shard_map/ppermute | solution.py:843
  136.3 4.5 %shard_map.242 = (f32[768,768]{1,0:T(8,128)}, f32[768,768]{1,0:T(8,128)}, f32[768,768]{1,0:T(8,128)}, f32[768,768]{1,0:T(8,128)}, f32[768]{0:T(1024)}, /*index=5...) custom-call(bf16[512,384]{1,0:T(8,128)(2,1)S(1)} %pad_maximum_fusion.refs_0_, ...), custom_call_target="tpu_custom_call" | custom-call | bytes 8000000 | tf_op jit(solution)/shard_map/pallas_call | solution.py:101
  141.0 1.6 %collective-permute-done.23.refs_0_ = bf16[512,384]{1,0:T(8,128)(2,1)S(1)} collective-permute-done((bf16[512,384]{1,0:T(8,128)(2,1)S(1)}, bf16[512,384]{1,0:T(8,128)(2,1)S(1)}, u32[]{:S(2)}, u32[]{:S(2)}) %collective-permute-start.23) | collective-permute-done | bytes 393248 | tf_op jit(solution)/shard_map/ppermute | solution.py:843
  143.1 2.2 %shard_map.243 = (f32[768,768]{1,0:T(8,128)}, f32[768,768]{1,0:T(8,128)}, f32[768,768]{1,0:T(8,128)}, f32[768,768]{1,0:T(8,128)}) custom-call(bf16[512,384]{1,0:T(8,128)(2,1)S(1)} %collective-permute-done.23.refs_0_, bf16[512,384]{1,0:T(8,128)(2,1)S(1)} %collective-permute-done.25.refs_1_, ...), custom_call_target="tpu_custom_call", output_to_operand_aliasing={{0}: (3, {}), {1}: (4, {}), {2}: (5, {}), {3}: (6, {})} | custom-call | bytes 8000000 | tf_op jit(solution)/shard_map/pallas_call | solution.py:101
  145.4 2.2 %shard_map.244 = (f32[768,768]{1,0:T(8,128)}, f32[768,768]{1,0:T(8,128)}, f32[768,768]{1,0:T(8,128)}, f32[768,768]{1,0:T(8,128)}) custom-call(bf16[512,384]{1,0:T(8,128)(2,1)S(1)} %collective-permute-done.35.refs_0_, bf16[512,384]{1,0:T(8,128)(2,1)S(1)} %collective-permute-done.36.refs_1_, ...), custom_call_target="tpu_custom_call", output_to_operand_aliasing={{0}: (3, {}), {1}: (4, {}), {2}: (5, {}), {3}: (6, {})} | custom-call | bytes 8000000 | tf_op jit(solution)/shard_map/pallas_call | solution.py:101
  (115 shorter events, 21.3 us)
Async XLA Ops:
  9.6 30.1 %collective-permute-start.2 = (bf16[768,1536]{1,0:T(8,128)(2,1)}, bf16[768,1536]{1,0:T(8,128)(2,1)}, u32[]{:S(2)}, u32[]{:S(2)}) collective-permute-start(bf16[768,1536]{1,0:T(8,128)(2,1)} %bitcast.19), channel_id=1, source_target_pairs={{0,1},{1,0},{2,3},{3,2},{4,5},{5,4},{6,7},{7,6},{8,9},{9,8},{10,11... | collective-permute-start | bytes 7077896 | tf_op jit(solution)/shard_map/ppermute | solution.py:835
  10.1 29.6 %collective-permute-start.3 = (bf16[1536,768]{1,0:T(8,128)(2,1)}, bf16[1536,768]{1,0:T(8,128)(2,1)}, u32[]{:S(2)}, u32[]{:S(2)}) collective-permute-start(bf16[1536,768]{1,0:T(8,128)(2,1)} %bitcast.21), channel_id=1, source_target_pairs={{0,1},{1,0},{2,3},{3,2},{4,5},{5,4},{6,7},{7,6},{8,9},{9,8},{10,11... | collective-permute-start | bytes 7077896 | tf_op jit(solution)/shard_map/ppermute | solution.py:835
  10.2 29.5 %all-to-all-start = ((bf16[16,16,1664]{2,1,0:T(8,128)(2,1)}), bf16[16,16,1664]{2,1,0:T(8,128)(2,1)}, u32[]{:S(2)}, u32[]{:S(2)}) async-start(bf16[16,16,1664]{2,1,0:T(8,128)(2,1)} %bitcast.16), calls=%async_computation | async-start | bytes 1703936 | tf_op jit(solution)/shard_map/all_to_all | solution.py:982
  18.5 6.2 %collective-permute-start.6 = (f32[128,768]{1,0:T(8,128)}, f32[128,768]{1,0:T(8,128)}, u32[]{:S(2)}, u32[]{:S(2)}) collective-permute-start(f32[128,768]{1,0:T(8,128)} %get-tuple-element.103.refs_4_), channel_id=1, source_target_pairs={{0,1},{1,0},{2,3},{3,2},{4,5},{5,4},{6,7},{7,6},{8,9},{9,8},{10,11... | collective-permute-start | bytes 1179656 | tf_op jit(solution)/shard_map/ppermute | solution.py:835
  18.6 6.1 %collective-permute-start.4 = (bf16[128,768]{1,0:T(8,128)(2,1)}, bf16[128,768]{1,0:T(8,128)(2,1)}, u32[]{:S(2)}, u32[]{:S(2)}) collective-permute-start(bf16[128,768]{1,0:T(8,128)(2,1)} %refs_6_.2), channel_id=1, source_target_pairs={{0,1},{1,0},{2,3},{3,2},{4,5},{5,4},{6,7},{7,6},{8,9},{9,8},{10,11... | collective-permute-start | bytes 589832 | tf_op jit(solution)/shard_map/ppermute | solution.py:835
  19.1 5.7 %collective-permute-start.5 = (bf16[128,768]{1,0:T(8,128)(2,1)}, bf16[128,768]{1,0:T(8,128)(2,1)}, u32[]{:S(2)}, u32[]{:S(2)}) collective-permute-start(bf16[128,768]{1,0:T(8,128)(2,1)} %get-tuple-element.102.refs_9_), channel_id=1, source_target_pairs={{0,1},{1,0},{2,3},{3,2},{4,5},{5,4},{6,7},{7,6},{8,9},{9,8},{10,11... | collective-permute-start | bytes 589832 | tf_op jit(solution)/shard_map/ppermute | solution.py:835
  49.1 5.4 %collective-permute-start.7 = (bf16[256,4608]{1,0:T(8,128)(2,1)}, bf16[256,4608]{1,0:T(8,128)(2,1)}, u32[]{:S(2)}, u32[]{:S(2)}) collective-permute-start(bf16[256,4608]{1,0:T(8,128)(2,1)} %get-tuple-element.110), channel_id=1, source_target_pairs={{0,1},{1,0},{2,3},{3,2},{4,5},{5,4},{6,7},{7,6},{8,9},{9,8},{10,11... | collective-permute-start | bytes 7077896 | tf_op jit(solution)/shard_map/ppermute | solution.py:835
  49.1 18.5 %all-to-all-start.1 = ((bf16[16,16,768]{2,1,0:T(8,128)(2,1)}), bf16[16,16,768]{2,1,0:T(8,128)(2,1)}, u32[]{:S(2)}, u32[]{:S(2)}) async-start(bf16[16,16,768]{2,1,0:T(8,128)(2,1)} %bitcast.18), calls=%async_computation.1 | async-start | bytes 786432 | tf_op jit(solution)/shard_map/all_to_all | solution.py:1031
  67.7 18.0 %all-to-all-start.2 = ((bf16[16,16,768]{2,1,0:T(8,128)(2,1)}), bf16[16,16,768]{2,1,0:T(8,128)(2,1)S(1)}, u32[]{:S(2)}, u32[]{:S(2)}) async-start(bf16[16,16,768]{2,1,0:T(8,128)(2,1)} %bitcast.17), calls=%async_computation.2 | async-start | bytes 786432 | tf_op jit(solution)/shard_map/all_to_all | solution.py:1036
  80.6 11.6 %collective-permute-start.15 = (bf16[512,384]{1,0:T(8,128)(2,1)}, bf16[512,384]{1,0:T(8,128)(2,1)S(1)}, u32[]{:S(2)}, u32[]{:S(2)}) collective-permute-start(bf16[512,384]{1,0:T(8,128)(2,1)} %get-tuple-element.138), channel_id=1, source_target_pairs={{0,4},{1,3},{2,6},{3,1},{4,0},{5,7},{6,2},{7,5},{8,12},{9,11},{10,... | collective-permute-start | bytes 1179656 | tf_op jit(solution)/shard_map/ppermute | solution.py:843
  82.7 12.7 %collective-permute-start.12 = (bf16[512,384]{1,0:T(8,128)(2,1)}, bf16[512,384]{1,0:T(8,128)(2,1)S(1)}, u32[]{:S(2)}, u32[]{:S(2)}) collective-permute-start(bf16[512,384]{1,0:T(8,128)(2,1)} %get-tuple-element.136), channel_id=1, source_target_pairs={{0,8},{1,5},{2,10},{3,7},{4,12},{5,1},{6,14},{7,3},{8,0},{9,13},{1... | collective-permute-start | bytes 1179656 | tf_op jit(solution)/shard_map/ppermute | solution.py:843
  84.2 12.9 %collective-permute-start.9 = (bf16[512,384]{1,0:T(8,128)(2,1)}, bf16[512,384]{1,0:T(8,128)(2,1)S(1)}, u32[]{:S(2)}, u32[]{:S(2)}) collective-permute-start(bf16[512,384]{1,0:T(8,128)(2,1)} %get-tuple-element.133), channel_id=1, source_target_pairs={{0,2},{1,9},{2,0},{3,11},{4,6},{5,13},{6,4},{7,15},{8,10},{9,1},{1... | collective-permute-start | bytes 1179656 | tf_op jit(solution)/shard_map/ppermute | solution.py:843
  85.7 13.0 %collective-permute-start.34 = (bf16[128,768]{1,0:T(8,128)(2,1)}, bf16[128,768]{1,0:T(8,128)(2,1)S(1)}, u32[]{:S(2)}, u32[]{:S(2)}) collective-permute-start(bf16[128,768]{1,0:T(8,128)(2,1)} %get-tuple-element.151), channel_id=1, source_target_pairs={{0,1},{1,0},{2,3},{3,2},{4,5},{5,4},{6,7},{7,6},{8,9},{9,8},{10,11... | collective-permute-start | bytes 589832 | tf_op jit(solution)/shard_map/ppermute | solution.py:835
  93.3 7.8 %collective-permute-start.16 = (bf16[256,384]{1,0:T(8,128)(2,1)S(1)}, bf16[256,384]{1,0:T(8,128)(2,1)S(1)}, u32[]{:S(2)}, u32[]{:S(2)}) collective-permute-start(bf16[256,384]{1,0:T(8,128)(2,1)S(1)} %get-tuple-element.176), channel_id=1, source_target_pairs={{0,8},{1,5},{2,10},{3,7},{4,12},{5,1},{6,14},{7,3},{8,0},{9,13},{1... | collective-permute-start | bytes 589832 | tf_op jit(solution)/shard_map/ppermute | solution.py:843
  95.5 7.1 %collective-permute-start.13 = (bf16[256,384]{1,0:T(8,128)(2,1)S(1)}, bf16[256,384]{1,0:T(8,128)(2,1)S(1)}, u32[]{:S(2)}, u32[]{:S(2)}) collective-permute-start(bf16[256,384]{1,0:T(8,128)(2,1)S(1)} %get-tuple-element.178), channel_id=1, source_target_pairs={{0,2},{1,9},{2,0},{3,11},{4,6},{5,13},{6,4},{7,15},{8,10},{9,1},{1... | collective-permute-start | bytes 589832 | tf_op jit(solution)/shard_map/ppermute | solution.py:843
  97.2 6.6 %collective-permute-start.10 = (bf16[256,384]{1,0:T(8,128)(2,1)S(1)}, bf16[256,384]{1,0:T(8,128)(2,1)S(1)}, u32[]{:S(2)}, u32[]{:S(2)}) collective-permute-start(bf16[256,384]{1,0:T(8,128)(2,1)S(1)} %get-tuple-element.180), channel_id=1, source_target_pairs={{0,4},{1,3},{2,6},{3,1},{4,0},{5,7},{6,2},{7,5},{8,12},{9,11},{10,... | collective-permute-start | bytes 589832 | tf_op jit(solution)/shard_map/ppermute | solution.py:843
  101.1 4.7 %collective-permute-start.17 = (bf16[128,384]{1,0:T(8,128)(2,1)S(1)}, bf16[128,384]{1,0:T(8,128)(2,1)S(1)}, u32[]{:S(2)}, u32[]{:S(2)}) collective-permute-start(bf16[128,384]{1,0:T(8,128)(2,1)S(1)} %add_convert_fusion.11), channel_id=1, source_target_pairs={{0,2},{1,9},{2,0},{3,11},{4,6},{5,13},{6,4},{7,15},{8,10},{9,1},{1... | collective-permute-start | bytes 294920 | tf_op jit(solution)/shard_map/ppermute | solution.py:843
  102.7 5.8 %collective-permute-start.14 = (bf16[128,384]{1,0:T(8,128)(2,1)S(1)}, bf16[128,384]{1,0:T(8,128)(2,1)S(1)}, u32[]{:S(2)}, u32[]{:S(2)}) collective-permute-start(bf16[128,384]{1,0:T(8,128)(2,1)S(1)} %add_convert_fusion.14), channel_id=1, source_target_pairs={{0,4},{1,3},{2,6},{3,1},{4,0},{5,7},{6,2},{7,5},{8,12},{9,11},{10,... | collective-permute-start | bytes 294920 | tf_op jit(solution)/shard_map/ppermute | solution.py:843
  103.9 6.8 %collective-permute-start.11 = (bf16[176,384]{1,0:T(8,128)(2,1)S(1)}, bf16[176,384]{1,0:T(8,128)(2,1)S(1)}, u32[]{:S(2)}, u32[]{:S(2)}) collective-permute-start(bf16[176,384]{1,0:T(8,128)(2,1)S(1)} %pad_maximum_fusion.6), channel_id=1, source_target_pairs={{0,8},{1,5},{2,10},{3,7},{4,12},{5,1},{6,14},{7,3},{8,0},{9,13},{1... | collective-permute-start | bytes 405512 | tf_op jit(solution)/shard_map/ppermute | solution.py:843
  105.8 9.5 %collective-permute-start.18 = (bf16[128,384]{1,0:T(8,128)(2,1)S(1)}, bf16[128,384]{1,0:T(8,128)(2,1)S(1)}, u32[]{:S(2)}, u32[]{:S(2)}) collective-permute-start(bf16[128,384]{1,0:T(8,128)(2,1)S(1)} %add_convert_fusion.10), channel_id=1, source_target_pairs={{0,16},{1,17},{2,18},{3,19},{4,20},{5,21},{6,22},{7,23},{8,24},{9,... | collective-permute-start | bytes 294920 | tf_op jit(solution)/shard_map/ppermute | solution.py:843
  108.6 9.3 %collective-permute-start.26 = (bf16[128,384]{1,0:T(8,128)(2,1)S(1)}, bf16[128,384]{1,0:T(8,128)(2,1)S(1)}, u32[]{:S(2)}, u32[]{:S(2)}) collective-permute-start(bf16[128,384]{1,0:T(8,128)(2,1)S(1)} %add_convert_fusion.13), channel_id=1, source_target_pairs={{0,16},{1,17},{2,18},{3,19},{4,20},{5,21},{6,22},{7,23},{8,24},{9,... | collective-permute-start | bytes 294920 | tf_op jit(solution)/shard_map/ppermute | solution.py:843
  110.8 8.8 %collective-permute-start.19 = (bf16[176,384]{1,0:T(8,128)(2,1)S(1)}, bf16[176,384]{1,0:T(8,128)(2,1)S(1)}, u32[]{:S(2)}, u32[]{:S(2)}) collective-permute-start(bf16[176,384]{1,0:T(8,128)(2,1)S(1)} %pad_maximum_fusion.7), channel_id=1, source_target_pairs={{0,16},{1,17},{2,18},{3,19},{4,20},{5,21},{6,22},{7,23},{8,24},{9,... | collective-permute-start | bytes 405512 | tf_op jit(solution)/shard_map/ppermute | solution.py:843
  117.8 4.7 %collective-permute-start.27 = (bf16[128,384]{1,0:T(8,128)(2,1)S(1)}, bf16[128,384]{1,0:T(8,128)(2,1)S(1)}, u32[]{:S(2)}, u32[]{:S(2)}) collective-permute-start(bf16[128,384]{1,0:T(8,128)(2,1)S(1)} %add_convert_fusion.7), channel_id=1, source_target_pairs={{0,4},{1,3},{2,6},{3,1},{4,0},{5,7},{6,2},{7,5},{8,12},{9,11},{10,... | collective-permute-start | bytes 294920 | tf_op jit(solution)/shard_map/ppermute | solution.py:843
  119.6 5.1 %collective-permute-start.21 = (bf16[176,384]{1,0:T(8,128)(2,1)S(1)}, bf16[176,384]{1,0:T(8,128)(2,1)S(1)}, u32[]{:S(2)}, u32[]{:S(2)}) collective-permute-start(bf16[176,384]{1,0:T(8,128)(2,1)S(1)} %pad_maximum_fusion.8), channel_id=1, source_target_pairs={{0,2},{1,9},{2,0},{3,11},{4,6},{5,13},{6,4},{7,15},{8,10},{9,1},{1... | collective-permute-start | bytes 405512 | tf_op jit(solution)/shard_map/ppermute | solution.py:843
  122.6 6.8 %collective-permute-start.28 = (bf16[256,384]{1,0:T(8,128)(2,1)S(1)}, bf16[256,384]{1,0:T(8,128)(2,1)S(1)}, u32[]{:S(2)}, u32[]{:S(2)}) collective-permute-start(bf16[256,384]{1,0:T(8,128)(2,1)S(1)} %pad_maximum_fusion.5), channel_id=1, source_target_pairs={{0,2},{1,9},{2,0},{3,11},{4,6},{5,13},{6,4},{7,15},{8,10},{9,1},{1... | collective-permute-start | bytes 589832 | tf_op jit(solution)/shard_map/ppermute | solution.py:843
  124.8 5.7 %collective-permute-start.24 = (bf16[256,384]{1,0:T(8,128)(2,1)S(1)}, bf16[256,384]{1,0:T(8,128)(2,1)S(1)}, u32[]{:S(2)}, u32[]{:S(2)}) collective-permute-start(bf16[256,384]{1,0:T(8,128)(2,1)S(1)} %pad_maximum_fusion.4), channel_id=1, source_target_pairs={{0,8},{1,5},{2,10},{3,7},{4,12},{5,1},{6,14},{7,3},{8,0},{9,13},{1... | collective-permute-start | bytes 589832 | tf_op jit(solution)/shard_map/ppermute | solution.py:843
  125.0 8.3 %collective-permute-start.22 = (bf16[304,384]{1,0:T(8,128)(2,1)S(1)}, bf16[304,384]{1,0:T(8,128)(2,1)S(1)}, u32[]{:S(2)}, u32[]{:S(2)}) collective-permute-start(bf16[304,384]{1,0:T(8,128)(2,1)S(1)} %pad_maximum_fusion.3), channel_id=1, source_target_pairs={{0,4},{1,3},{2,6},{3,1},{4,0},{5,7},{6,2},{7,5},{8,12},{9,11},{10,... | collective-permute-start | bytes 700424 | tf_op jit(solution)/shard_map/ppermute | solution.py:843
  129.4 5.4 %collective-permute-start.32 = (bf16[512,384]{1,0:T(8,128)(2,1)S(1)}, bf16[512,384]{1,0:T(8,128)(2,1)S(1)}, u32[]{:S(2)}, u32[]{:S(2)}) collective-permute-start(bf16[512,384]{1,0:T(8,128)(2,1)S(1)} %pad_maximum_fusion.2.refs_4_), channel_id=1, source_target_pairs={{0,1},{1,0},{2,3},{3,2},{4,5},{5,4},{6,7},{7,6},{8,9},{9,8},{10,11... | collective-permute-start | bytes 1179656 | tf_op jit(solution)/shard_map/ppermute | solution.py:835
  129.5 11.3 %collective-permute-start.29 = (bf16[512,384]{1,0:T(8,128)(2,1)S(1)}, bf16[512,384]{1,0:T(8,128)(2,1)S(1)}, u32[]{:S(2)}, u32[]{:S(2)}) collective-permute-start(bf16[512,384]{1,0:T(8,128)(2,1)S(1)} %pad_maximum_fusion.2.refs_4_), channel_id=1, source_target_pairs={{0,8},{1,5},{2,10},{3,7},{4,12},{5,1},{6,14},{7,3},{8,0},{9,13},{1... | collective-permute-start | bytes 1179656 | tf_op jit(solution)/shard_map/ppermute | solution.py:843
  130.5 5.2 %collective-permute-start.31 = (bf16[512,384]{1,0:T(8,128)(2,1)S(1)}, bf16[512,384]{1,0:T(8,128)(2,1)S(1)}, u32[]{:S(2)}, u32[]{:S(2)}) collective-permute-start(bf16[512,384]{1,0:T(8,128)(2,1)S(1)} %pad_maximum_fusion.1.refs_2_), channel_id=1, source_target_pairs={{0,1},{1,0},{2,3},{3,2},{4,5},{5,4},{6,7},{7,6},{8,9},{9,8},{10,11... | collective-permute-start | bytes 1179656 | tf_op jit(solution)/shard_map/ppermute | solution.py:835
  131.2 9.8 %collective-permute-start.25 = (bf16[512,384]{1,0:T(8,128)(2,1)S(1)}, bf16[512,384]{1,0:T(8,128)(2,1)S(1)}, u32[]{:S(2)}, u32[]{:S(2)}) collective-permute-start(bf16[512,384]{1,0:T(8,128)(2,1)S(1)} %pad_maximum_fusion.1.refs_2_), channel_id=1, source_target_pairs={{0,4},{1,3},{2,6},{3,1},{4,0},{5,7},{6,2},{7,5},{8,12},{9,11},{10,... | collective-permute-start | bytes 1179656 | tf_op jit(solution)/shard_map/ppermute | solution.py:843
  134.8 7.8 %collective-permute-start.23 = (bf16[512,384]{1,0:T(8,128)(2,1)S(1)}, bf16[512,384]{1,0:T(8,128)(2,1)S(1)}, u32[]{:S(2)}, u32[]{:S(2)}) collective-permute-start(bf16[512,384]{1,0:T(8,128)(2,1)S(1)} %pad_maximum_fusion.refs_0_), channel_id=1, source_target_pairs={{0,2},{1,9},{2,0},{3,11},{4,6},{5,13},{6,4},{7,15},{8,10},{9,1},{1... | collective-permute-start | bytes 1179656 | tf_op jit(solution)/shard_map/ppermute | solution.py:843
  (21 other events, 173.7 us)

commit v9 on v8

--- a/solution.py
+++ b/solution.py
@@ -333,7 +333,7 @@
             )
             probs_ref[head] = attend(
                 queries[:, lanes], keys[:, lanes], scale, bias, side, low_half
-            )
+            ).astype(BF16)
 
 
 def expert_kernel(
@@ -563,8 +563,7 @@
     query_ref,
     act_ref,
     hot_ref,
-    own_ref,
-    other_ref,
+    gain_first_ref,
     router_ref,
     after_ref,
     wo_ref,
@@ -651,7 +650,7 @@
     flush(6)
     grad_low = jnp.concatenate([grad_own, grad_other], axis=0).astype(BF16)
     grad_mixed = cols_by_cols(grad_low, wo_half[...]).astype(BF16)
-    for i in range(9, 20):
+    for i in range(9, 19):
         wait(i)
     for copy in copies[1:]:
         copy.wait()
@@ -667,11 +666,12 @@
         grad_pair = grad_mixed[:, lanes]
         got_q, got_k, got_v = [], [], []
         for side in range(2):
-            probs = probs_ref[2 * pair + side]
+            probs_low = probs_ref[2 * pair + side]
+            probs = probs_low.astype(F32)
             keep_lanes = low_half if side == 0 else jnp.logical_not(low_half)
             own_grad = jnp.where(keep_lanes, grad_pair, 0).astype(BF16)
             grad_probs = cols_by_cols(own_grad, value)
-            got_v.append(rows_by_rows(probs.astype(BF16), grad_pair))
+            got_v.append(rows_by_rows(probs_low, grad_pair))
             inner = jnp.sum(probs * grad_probs, axis=-1, keepdims=True)
             grad_scores = probs * (grad_probs - inner)
             same.append(
@@ -703,15 +703,10 @@
     )
     input_other_ref[...] = grad_act[rows:].astype(BF16)
     flush(9)
-    input_own_ref[...] = grad_act[:rows]
+    input_own_ref[...] = grad_act[:rows].astype(BF16)
     flush(8)
-    x = own_ref[...].astype(F32)
-    y = other_ref[...].astype(F32)
-    gain_first = jnp.sum(
-        grad_act[:rows] * (x * root_mean(x)) + grad_act[rows:] * (y * root_mean(y)),
-        axis=0,
-        keepdims=True,
-    )
+    gain_first = jnp.sum(grad_act * act.astype(F32), axis=0, keepdims=True)
+    gain_first = gain_first / gain_first_ref[...].reshape(1, width)
     sums = jnp.concatenate(
         [jnp.concatenate(part_sums, axis=0) for part_sums in (same, ahead, behind)], axis=1
     )
@@ -992,7 +987,7 @@
             ((2 * rows, part), BF16),
             ((2 * rows, part), BF16),
             ((2 * rows, part), BF16),
-            ((heads // 2, 2 * rows, 2 * rows), F32),
+            ((heads // 2, 2 * rows, 2 * rows), BF16),
         ],
         (tokens, other, norm_first, w_query, w_key, w_value, windows, gate),
         "hhhrrrhr" + "hhhhh",
@@ -1049,7 +1044,7 @@
         + [
             ((rows, width), F32),
             ((16 + 2 * experts, part), BF16),
-            ((rows, width), F32),
+            ((rows, width), BF16),
             ((rows, width), BF16),
         ],
         (
@@ -1070,8 +1065,7 @@
             queries,
             act,
             hot,
-            tokens,
-            other,
+            norm_first,
             router_part,
             grad_w_in,
             w_out,
@@ -1079,7 +1073,7 @@
             w_key,
             w_value,
         ),
-        "l" * 20 + "rrrrr" + "rrrrrr" + "hhhh",
+        "l" * 19 + "rrrrr" + "rrrrrr" + "hhhh",
         vmem=56,
         flops=4000000000,
         scratch=[
@@ -1102,7 +1096,7 @@
     grad_middle, input_own, input_swapped, produced_returned = beside
     root = root[:, :1]
     scaled = tokens.astype(F32) * root
-    up = norm_first * (input_own + input_swapped.astype(F32))
+    up = norm_first * (input_own.astype(F32) + input_swapped.astype(F32))
     grad_input = grad_middle + root * (
         up - scaled * jnp.mean(up * scaled, axis=-1, keepdims=True)
     )

time: 149 us -> 148 us (level)
  no operation moved by 1% of the time
where the time goes in v9:
time: 148 us; the launch traced here: 147 us
  starting transfers between devices  49 us (33%)
  Pallas kernels  47.4 us (32%)
  waiting for transfers between devices  44.7 us (30%)
  other arithmetic  3.06 us (2%)
    pallas_call x7, Pallas kernels, call(): pl.pallas_call(kernel, out_shape=[jax.ShapeDtypeStruct(s, d) for s, d in...  38.5 us
    ppermute x21, starting transfers between devices, flip(): return lax.ppermute(x, ('expert', 'ffn'), pairs)  28.2 us
    ppermute x21, waiting for transfers between devices, flip(): return lax.ppermute(x, ('expert', 'ffn'), pairs)  21.9 us
    all_to_all x1, waiting for transfers between devices, shards(): arrived = lax.all_to_all(outgoing, 'expert', 0, 0, tiled=True)  15.2 us
    pallas_call x1, Pallas kernels, expert_weights(): pl.pallas_call(expert_weights_kernel, grid=(steps,), out_shape=[jax.Shape...  8.9 us
    all_to_all x1, starting transfers between devices, shards(): arrived = lax.all_to_all(outgoing, 'expert', 0, 0, tiled=True)  8.29 us
    all_to_all x1, starting transfers between devices, shards(): grad_returned = lax.all_to_all(grad_slots, 'expert', 0, 0, tiled=True)  5.26 us
    all_to_all x1, waiting for transfers between devices, shards(): grad_returned = lax.all_to_all(grad_slots, 'expert', 0, 0, tiled=True)  4.32 us
  transfers between devices with their start and end apart: 41, of which 19 were waited for; matrix products, arithmetic and copies ran while one was open for 3% of the time, Pallas kernels for 20%

profile of v9, /device:TPU:0, one launch (start us, length us, event | category | flops | bytes accessed | tf_op | source)
XLA Modules:
  0.0 147.5 jit_solution(7054705755202053708)
XLA Ops:
  2.6 7.1 %shard_map.237 = (f32[128,768]{1,0:T(8,128)}, f32[128,128]{1,0:T(8,128)}, bf16[256,1664]{1,0:T(8,128)(2,1)}, bf16[128,768]{1,0:T(8,128)(2,1)}, f32[12,768]{1,0:T...) custom-call(bf16[128,768]{1,0:T(8,128)(2,1)} %refs_0_.3, ...), custom_call_target="tpu_custom_call" | custom-call | flops 3000000000 | bytes 1000000 | tf_op jit(solution)/shard_map/pallas_call | solution.py:101
  10.2 8.3 %all-to-all-start = ((bf16[16,16,1664]{2,1,0:T(8,128)(2,1)}), bf16[16,16,1664]{2,1,0:T(8,128)(2,1)}, u32[]{:S(2)}, u32[]{:S(2)}) async-start(bf16[16,16,1664]{2,1,0:T(8,128)(2,1)} %bitcast.16), calls=%async_computation | async-start | bytes 1703936 | tf_op jit(solution)/shard_map/all_to_all | solution.py:977
  19.2 5.3 %shard_map.238 = (bf16[256,768]{1,0:T(8,128)(2,1)}, bf16[256,384]{1,0:T(8,128)(2,1)}, bf16[256,384]{1,0:T(8,128)(2,1)}, bf16[256,384]{1,0:T(8,128)(2,1)}, bf16[6,256,256]{2,1,0:T(8,128)(2,1)}) custom-call(bf16[128,768]{1,0:T(8,128)(2,1)} %refs_0_.3, bf16[128,768]{1,0:T(8,128)(2,1)} %collective-permute-done.refs_1_, f32[768]{0:T(1024)} %refs_17_.1, ...), custom_call_target="tpu_custom_call" | custom-call | flops 3000000000 | bytes 1000000 | tf_op jit(solution)/shard_map/pallas_call | solution.py:101
  24.5 15.2 %all-to-all-done = bf16[16,16,1664]{2,1,0:T(8,128)(2,1)} async-done(((bf16[16,16,1664]{2,1,0:T(8,128)(2,1)}), bf16[16,16,1664]{2,1,0:T(8,128)(2,1)}, u32[]{:S(2)}, u32[]{:S(2)}) %all-to-all-start) | async-done | bytes 852000 | tf_op jit(solution)/shard_map/all_to_all | solution.py:977
  39.7 9.3 %shard_map.239 = (bf16[256,1536]{1,0:T(8,128)(2,1)}, bf16[256,1536]{1,0:T(8,128)(2,1)}, bf16[256,768]{1,0:T(8,128)(2,1)}, bf16[256,4608]{1,0:T(8,128)(2,1)}, bf1...) custom-call(bf16[256,1664]{1,0:T(8,128)(2,1)} %bitcast.4.refs_0_.flat_own, ...), custom_call_target="tpu_custom_call" | custom-call | flops 6000000000 | bytes 1000000 | tf_op jit(solution)/shard_map/pallas_call | solution.py:101
  49.1 5.3 %all-to-all-start.1 = ((bf16[16,16,768]{2,1,0:T(8,128)(2,1)}), bf16[16,16,768]{2,1,0:T(8,128)(2,1)}, u32[]{:S(2)}, u32[]{:S(2)}) async-start(bf16[16,16,768]{2,1,0:T(8,128)(2,1)} %bitcast.18), calls=%async_computation.1 | async-start | bytes 786432 | tf_op jit(solution)/shard_map/all_to_all | solution.py:1026
  54.4 8.9 %shard_map.240 = (f32[1,768,1536]{2,1,0:T(8,128)}, f32[1,1536,768]{2,1,0:T(8,128)}) custom-call(bf16[256,1664]{1,0:T(8,128)(2,1)} %bitcast.4.refs_0_.flat_own, bf16[256,768]{1,0:T(8,128)(2,1)} %get-tuple-element.107.sent_own, bf16[256,1536]{1,0:T(8,128)(2,1)} %get-tuple-element.108.hid_own, bf16[256,1536]{1,0:T(8,128)(2,1)} %get-tuple-element.109.pre_own, ...), custom_call_target="tpu_custom_call" | custom-call | flops 2415919104 | bytes 14000000 | tf_op jit(solution)/shard_map/pallas_call | solution.py:488
  63.3 4.3 %all-to-all-done.1 = bf16[16,16,768]{2,1,0:T(8,128)(2,1)} async-done(((bf16[16,16,768]{2,1,0:T(8,128)(2,1)}), bf16[16,16,768]{2,1,0:T(8,128)(2,1)}, u32[]{:S(2)}, u32[]{:S(2)}) %all-to-all-start.1) | async-done | bytes 393248 | tf_op jit(solution)/shard_map/all_to_all | solution.py:1026
  67.7 3.8 %all-to-all-start.2 = ((bf16[16,16,768]{2,1,0:T(8,128)(2,1)}), bf16[16,16,768]{2,1,0:T(8,128)(2,1)S(1)}, u32[]{:S(2)}, u32[]{:S(2)}) async-start(bf16[16,16,768]{2,1,0:T(8,128)(2,1)} %bitcast.17), calls=%async_computation.2 | async-start | bytes 786432 | tf_op jit(solution)/shard_map/all_to_all | solution.py:1031
  72.2 8.0 %shard_map.241 = (bf16[512,384]{1,0:T(8,128)(2,1)}, bf16[512,384]{1,0:T(8,128)(2,1)}, bf16[512,384]{1,0:T(8,128)(2,1)}, bf16[512,384]{1,0:T(8,128)(2,1)}, bf16[5...) custom-call(bf16[256,768]{1,0:T(8,128)(2,1)} %bitcast.8.refs_0_, ...), custom_call_target="tpu_custom_call" | custom-call | flops 4000000000 | bytes 1000000 | tf_op jit(solution)/shard_map/pallas_call | solution.py:101
  80.3 1.9 %collective-permute-start.15 = (bf16[512,384]{1,0:T(8,128)(2,1)}, bf16[512,384]{1,0:T(8,128)(2,1)S(1)}, u32[]{:S(2)}, u32[]{:S(2)}) collective-permute-start(bf16[512,384]{1,0:T(8,128)(2,1)} %get-tuple-element.138), channel_id=1, source_target_pairs={{0,4},{1,3},{2,6},{3,1},{4,0},{5,7},{6,2},{7,5},{8,12},{9,11},{10,... | collective-permute-start | bytes 1179656 | tf_op jit(solution)/shard_map/ppermute | solution.py:838
  82.4 1.5 %collective-permute-start.12 = (bf16[512,384]{1,0:T(8,128)(2,1)}, bf16[512,384]{1,0:T(8,128)(2,1)S(1)}, u32[]{:S(2)}, u32[]{:S(2)}) collective-permute-start(bf16[512,384]{1,0:T(8,128)(2,1)} %get-tuple-element.136), channel_id=1, source_target_pairs={{0,8},{1,5},{2,10},{3,7},{4,12},{5,1},{6,14},{7,3},{8,0},{9,13},{1... | collective-permute-start | bytes 1179656 | tf_op jit(solution)/shard_map/ppermute | solution.py:838
  86.5 5.4 %collective-permute-done.15 = bf16[512,384]{1,0:T(8,128)(2,1)S(1)} collective-permute-done((bf16[512,384]{1,0:T(8,128)(2,1)}, bf16[512,384]{1,0:T(8,128)(2,1)S(1)}, u32[]{:S(2)}, u32[]{:S(2)}) %collective-permute-start.15) | collective-permute-done | bytes 393248 | tf_op jit(solution)/shard_map/ppermute | solution.py:838
  93.0 2.1 %collective-permute-start.16 = (bf16[256,384]{1,0:T(8,128)(2,1)S(1)}, bf16[256,384]{1,0:T(8,128)(2,1)S(1)}, u32[]{:S(2)}, u32[]{:S(2)}) collective-permute-start(bf16[256,384]{1,0:T(8,128)(2,1)S(1)} %get-tuple-element.176), channel_id=1, source_target_pairs={{0,8},{1,5},{2,10},{3,7},{4,12},{5,1},{6,14},{7,3},{8,0},{9,13},{1... | collective-permute-start | bytes 589832 | tf_op jit(solution)/shard_map/ppermute | solution.py:838
  95.2 1.6 %collective-permute-start.13 = (bf16[256,384]{1,0:T(8,128)(2,1)S(1)}, bf16[256,384]{1,0:T(8,128)(2,1)S(1)}, u32[]{:S(2)}, u32[]{:S(2)}) collective-permute-start(bf16[256,384]{1,0:T(8,128)(2,1)S(1)} %get-tuple-element.178), channel_id=1, source_target_pairs={{0,2},{1,9},{2,0},{3,11},{4,6},{5,13},{6,4},{7,15},{8,10},{9,1},{1... | collective-permute-start | bytes 589832 | tf_op jit(solution)/shard_map/ppermute | solution.py:838
  96.9 1.5 %collective-permute-start.10 = (bf16[256,384]{1,0:T(8,128)(2,1)S(1)}, bf16[256,384]{1,0:T(8,128)(2,1)S(1)}, u32[]{:S(2)}, u32[]{:S(2)}) collective-permute-start(bf16[256,384]{1,0:T(8,128)(2,1)S(1)} %get-tuple-element.180), channel_id=1, source_target_pairs={{0,4},{1,3},{2,6},{3,1},{4,0},{5,7},{6,2},{7,5},{8,12},{9,11},{10,... | collective-permute-start | bytes 589832 | tf_op jit(solution)/shard_map/ppermute | solution.py:838
  98.6 2.1 %collective-permute-done.16 = bf16[256,384]{1,0:T(8,128)(2,1)S(1)} collective-permute-done((bf16[256,384]{1,0:T(8,128)(2,1)S(1)}, bf16[256,384]{1,0:T(8,128)(2,1)S(1)}, u32[]{:S(2)}, u32[]{:S(2)}) %collective-permute-start.16) | collective-permute-done | bytes 196640 | tf_op jit(solution)/shard_map/ppermute | solution.py:838
  100.8 1.6 %collective-permute-start.17 = (bf16[128,384]{1,0:T(8,128)(2,1)S(1)}, bf16[128,384]{1,0:T(8,128)(2,1)S(1)}, u32[]{:S(2)}, u32[]{:S(2)}) collective-permute-start(bf16[128,384]{1,0:T(8,128)(2,1)S(1)} %add_convert_fusion.11), channel_id=1, source_target_pairs={{0,2},{1,9},{2,0},{3,11},{4,6},{5,13},{6,4},{7,15},{8,10},{9,1},{1... | collective-permute-start | bytes 294920 | tf_op jit(solution)/shard_map/ppermute | solution.py:838
  103.6 1.6 %collective-permute-start.11 = (bf16[176,384]{1,0:T(8,128)(2,1)S(1)}, bf16[176,384]{1,0:T(8,128)(2,1)S(1)}, u32[]{:S(2)}, u32[]{:S(2)}) collective-permute-start(bf16[176,384]{1,0:T(8,128)(2,1)S(1)} %pad_maximum_fusion.6), channel_id=1, source_target_pairs={{0,8},{1,5},{2,10},{3,7},{4,12},{5,1},{6,14},{7,3},{8,0},{9,13},{1... | collective-permute-start | bytes 405512 | tf_op jit(solution)/shard_map/ppermute | solution.py:838
  105.5 2.7 %collective-permute-start.18 = (bf16[128,384]{1,0:T(8,128)(2,1)S(1)}, bf16[128,384]{1,0:T(8,128)(2,1)S(1)}, u32[]{:S(2)}, u32[]{:S(2)}) collective-permute-start(bf16[128,384]{1,0:T(8,128)(2,1)S(1)} %add_convert_fusion.10), channel_id=1, source_target_pairs={{0,16},{1,17},{2,18},{3,19},{4,20},{5,21},{6,22},{7,23},{8,24},{9,... | collective-permute-start | bytes 294920 | tf_op jit(solution)/shard_map/ppermute | solution.py:838
  110.5 1.7 %collective-permute-start.19 = (bf16[176,384]{1,0:T(8,128)(2,1)S(1)}, bf16[176,384]{1,0:T(8,128)(2,1)S(1)}, u32[]{:S(2)}, u32[]{:S(2)}) collective-permute-start(bf16[176,384]{1,0:T(8,128)(2,1)S(1)} %pad_maximum_fusion.7), channel_id=1, source_target_pairs={{0,16},{1,17},{2,18},{3,19},{4,20},{5,21},{6,22},{7,23},{8,24},{9,... | collective-permute-start | bytes 405512 | tf_op jit(solution)/shard_map/ppermute | solution.py:838
  112.1 2.9 %collective-permute-done.18 = bf16[128,384]{1,0:T(8,128)(2,1)S(1)} collective-permute-done((bf16[128,384]{1,0:T(8,128)(2,1)S(1)}, bf16[128,384]{1,0:T(8,128)(2,1)S(1)}, u32[]{:S(2)}, u32[]{:S(2)}) %collective-permute-start.18) | collective-permute-done | bytes 98336 | tf_op jit(solution)/shard_map/ppermute | solution.py:838
  115.0 2.5 %collective-permute-done.26 = bf16[128,384]{1,0:T(8,128)(2,1)S(1)} collective-permute-done((bf16[128,384]{1,0:T(8,128)(2,1)S(1)}, bf16[128,384]{1,0:T(8,128)(2,1)S(1)}, u32[]{:S(2)}, u32[]{:S(2)}) %collective-permute-start.26) | collective-permute-done | bytes 98336 | tf_op jit(solution)/shard_map/ppermute | solution.py:838
  117.5 1.8 %collective-permute-start.27 = (bf16[128,384]{1,0:T(8,128)(2,1)S(1)}, bf16[128,384]{1,0:T(8,128)(2,1)S(1)}, u32[]{:S(2)}, u32[]{:S(2)}) collective-permute-start(bf16[128,384]{1,0:T(8,128)(2,1)S(1)} %add_convert_fusion.7), channel_id=1, source_target_pairs={{0,4},{1,3},{2,6},{3,1},{4,0},{5,7},{6,2},{7,5},{8,12},{9,11},{10,... | collective-permute-start | bytes 294920 | tf_op jit(solution)/shard_map/ppermute | solution.py:838
  120.3 1.9 %collective-permute-done.27 = bf16[128,384]{1,0:T(8,128)(2,1)S(1)} collective-permute-done((bf16[128,384]{1,0:T(8,128)(2,1)S(1)}, bf16[128,384]{1,0:T(8,128)(2,1)S(1)}, u32[]{:S(2)}, u32[]{:S(2)}) %collective-permute-start.27) | collective-permute-done | bytes 98336 | tf_op jit(solution)/shard_map/ppermute | solution.py:838
  124.7 2.6 %collective-permute-start.22 = (bf16[304,384]{1,0:T(8,128)(2,1)S(1)}, bf16[304,384]{1,0:T(8,128)(2,1)S(1)}, u32[]{:S(2)}, u32[]{:S(2)}) collective-permute-start(bf16[304,384]{1,0:T(8,128)(2,1)S(1)} %pad_maximum_fusion.3), channel_id=1, source_target_pairs={{0,4},{1,3},{2,6},{3,1},{4,0},{5,7},{6,2},{7,5},{8,12},{9,11},{10,... | collective-permute-start | bytes 700424 | tf_op jit(solution)/shard_map/ppermute | solution.py:838
  127.3 1.8 %collective-permute-done.28 = bf16[256,384]{1,0:T(8,128)(2,1)S(1)} collective-permute-done((bf16[256,384]{1,0:T(8,128)(2,1)S(1)}, bf16[256,384]{1,0:T(8,128)(2,1)S(1)}, u32[]{:S(2)}, u32[]{:S(2)}) %collective-permute-start.28) | collective-permute-done | bytes 196640 | tf_op jit(solution)/shard_map/ppermute | solution.py:838
  130.9 2.1 %collective-permute-start.25 = (bf16[512,384]{1,0:T(8,128)(2,1)S(1)}, bf16[512,384]{1,0:T(8,128)(2,1)S(1)}, u32[]{:S(2)}, u32[]{:S(2)}) collective-permute-start(bf16[512,384]{1,0:T(8,128)(2,1)S(1)} %pad_maximum_fusion.1.refs_2_), channel_id=1, source_target_pairs={{0,4},{1,3},{2,6},{3,1},{4,0},{5,7},{6,2},{7,5},{8,12},{9,11},{10,... | collective-permute-start | bytes 1179656 | tf_op jit(solution)/shard_map/ppermute | solution.py:838
  136.1 4.5 %shard_map.242 = (f32[768,768]{1,0:T(8,128)}, f32[768,768]{1,0:T(8,128)}, f32[768,768]{1,0:T(8,128)}, f32[768,768]{1,0:T(8,128)}, f32[768]{0:T(1024)}, /*index=5...) custom-call(bf16[512,384]{1,0:T(8,128)(2,1)S(1)} %pad_maximum_fusion.refs_0_, ...), custom_call_target="tpu_custom_call" | custom-call | bytes 8000000 | tf_op jit(solution)/shard_map/pallas_call | solution.py:101
  140.7 1.6 %collective-permute-done.23.refs_0_ = bf16[512,384]{1,0:T(8,128)(2,1)S(1)} collective-permute-done((bf16[512,384]{1,0:T(8,128)(2,1)S(1)}, bf16[512,384]{1,0:T(8,128)(2,1)S(1)}, u32[]{:S(2)}, u32[]{:S(2)}) %collective-permute-start.23) | collective-permute-done | bytes 393248 | tf_op jit(solution)/shard_map/ppermute | solution.py:838
  142.8 2.2 %shard_map.243 = (f32[768,768]{1,0:T(8,128)}, f32[768,768]{1,0:T(8,128)}, f32[768,768]{1,0:T(8,128)}, f32[768,768]{1,0:T(8,128)}) custom-call(bf16[512,384]{1,0:T(8,128)(2,1)S(1)} %collective-permute-done.23.refs_0_, bf16[512,384]{1,0:T(8,128)(2,1)S(1)} %collective-permute-done.25.refs_1_, ...), custom_call_target="tpu_custom_call", output_to_operand_aliasing={{0}: (3, {}), {1}: (4, {}), {2}: (5, {}), {3}: (6, {})} | custom-call | bytes 8000000 | tf_op jit(solution)/shard_map/pallas_call | solution.py:101
  145.1 2.2 %shard_map.244 = (f32[768,768]{1,0:T(8,128)}, f32[768,768]{1,0:T(8,128)}, f32[768,768]{1,0:T(8,128)}, f32[768,768]{1,0:T(8,128)}) custom-call(bf16[512,384]{1,0:T(8,128)(2,1)S(1)} %collective-permute-done.35.refs_0_, bf16[512,384]{1,0:T(8,128)(2,1)S(1)} %collective-permute-done.36.refs_1_, ...), custom_call_target="tpu_custom_call", output_to_operand_aliasing={{0}: (3, {}), {1}: (4, {}), {2}: (5, {}), {3}: (6, {})} | custom-call | bytes 8000000 | tf_op jit(solution)/shard_map/pallas_call | solution.py:101
  (115 shorter events, 21.3 us)
Async XLA Ops:
  9.6 30.1 %collective-permute-start.2 = (bf16[768,1536]{1,0:T(8,128)(2,1)}, bf16[768,1536]{1,0:T(8,128)(2,1)}, u32[]{:S(2)}, u32[]{:S(2)}) collective-permute-start(bf16[768,1536]{1,0:T(8,128)(2,1)} %bitcast.19), channel_id=1, source_target_pairs={{0,1},{1,0},{2,3},{3,2},{4,5},{5,4},{6,7},{7,6},{8,9},{9,8},{10,11... | collective-permute-start | bytes 7077896 | tf_op jit(solution)/shard_map/ppermute | solution.py:830
  10.1 29.6 %collective-permute-start.3 = (bf16[1536,768]{1,0:T(8,128)(2,1)}, bf16[1536,768]{1,0:T(8,128)(2,1)}, u32[]{:S(2)}, u32[]{:S(2)}) collective-permute-start(bf16[1536,768]{1,0:T(8,128)(2,1)} %bitcast.21), channel_id=1, source_target_pairs={{0,1},{1,0},{2,3},{3,2},{4,5},{5,4},{6,7},{7,6},{8,9},{9,8},{10,11... | collective-permute-start | bytes 7077896 | tf_op jit(solution)/shard_map/ppermute | solution.py:830
  10.2 29.5 %all-to-all-start = ((bf16[16,16,1664]{2,1,0:T(8,128)(2,1)}), bf16[16,16,1664]{2,1,0:T(8,128)(2,1)}, u32[]{:S(2)}, u32[]{:S(2)}) async-start(bf16[16,16,1664]{2,1,0:T(8,128)(2,1)} %bitcast.16), calls=%async_computation | async-start | bytes 1703936 | tf_op jit(solution)/shard_map/all_to_all | solution.py:977
  18.5 6.0 %collective-permute-start.6 = (f32[128,768]{1,0:T(8,128)}, f32[128,768]{1,0:T(8,128)}, u32[]{:S(2)}, u32[]{:S(2)}) collective-permute-start(f32[128,768]{1,0:T(8,128)} %get-tuple-element.103.refs_4_), channel_id=1, source_target_pairs={{0,1},{1,0},{2,3},{3,2},{4,5},{5,4},{6,7},{7,6},{8,9},{9,8},{10,11... | collective-permute-start | bytes 1179656 | tf_op jit(solution)/shard_map/ppermute | solution.py:830
  18.6 5.9 %collective-permute-start.4 = (bf16[128,768]{1,0:T(8,128)(2,1)}, bf16[128,768]{1,0:T(8,128)(2,1)}, u32[]{:S(2)}, u32[]{:S(2)}) collective-permute-start(bf16[128,768]{1,0:T(8,128)(2,1)} %refs_6_.2), channel_id=1, source_target_pairs={{0,1},{1,0},{2,3},{3,2},{4,5},{5,4},{6,7},{7,6},{8,9},{9,8},{10,11... | collective-permute-start | bytes 589832 | tf_op jit(solution)/shard_map/ppermute | solution.py:830
  19.1 5.4 %collective-permute-start.5 = (bf16[128,768]{1,0:T(8,128)(2,1)}, bf16[128,768]{1,0:T(8,128)(2,1)}, u32[]{:S(2)}, u32[]{:S(2)}) collective-permute-start(bf16[128,768]{1,0:T(8,128)(2,1)} %get-tuple-element.102.refs_9_), channel_id=1, source_target_pairs={{0,1},{1,0},{2,3},{3,2},{4,5},{5,4},{6,7},{7,6},{8,9},{9,8},{10,11... | collective-permute-start | bytes 589832 | tf_op jit(solution)/shard_map/ppermute | solution.py:830
  49.1 5.4 %collective-permute-start.7 = (bf16[256,4608]{1,0:T(8,128)(2,1)}, bf16[256,4608]{1,0:T(8,128)(2,1)}, u32[]{:S(2)}, u32[]{:S(2)}) collective-permute-start(bf16[256,4608]{1,0:T(8,128)(2,1)} %get-tuple-element.110), channel_id=1, source_target_pairs={{0,1},{1,0},{2,3},{3,2},{4,5},{5,4},{6,7},{7,6},{8,9},{9,8},{10,11... | collective-permute-start | bytes 7077896 | tf_op jit(solution)/shard_map/ppermute | solution.py:830
  49.1 18.5 %all-to-all-start.1 = ((bf16[16,16,768]{2,1,0:T(8,128)(2,1)}), bf16[16,16,768]{2,1,0:T(8,128)(2,1)}, u32[]{:S(2)}, u32[]{:S(2)}) async-start(bf16[16,16,768]{2,1,0:T(8,128)(2,1)} %bitcast.18), calls=%async_computation.1 | async-start | bytes 786432 | tf_op jit(solution)/shard_map/all_to_all | solution.py:1026
  67.7 17.7 %all-to-all-start.2 = ((bf16[16,16,768]{2,1,0:T(8,128)(2,1)}), bf16[16,16,768]{2,1,0:T(8,128)(2,1)S(1)}, u32[]{:S(2)}, u32[]{:S(2)}) async-start(bf16[16,16,768]{2,1,0:T(8,128)(2,1)} %bitcast.17), calls=%async_computation.2 | async-start | bytes 786432 | tf_op jit(solution)/shard_map/all_to_all | solution.py:1031
  80.3 11.6 %collective-permute-start.15 = (bf16[512,384]{1,0:T(8,128)(2,1)}, bf16[512,384]{1,0:T(8,128)(2,1)S(1)}, u32[]{:S(2)}, u32[]{:S(2)}) collective-permute-start(bf16[512,384]{1,0:T(8,128)(2,1)} %get-tuple-element.138), channel_id=1, source_target_pairs={{0,4},{1,3},{2,6},{3,1},{4,0},{5,7},{6,2},{7,5},{8,12},{9,11},{10,... | collective-permute-start | bytes 1179656 | tf_op jit(solution)/shard_map/ppermute | solution.py:838
  82.4 12.7 %collective-permute-start.12 = (bf16[512,384]{1,0:T(8,128)(2,1)}, bf16[512,384]{1,0:T(8,128)(2,1)S(1)}, u32[]{:S(2)}, u32[]{:S(2)}) collective-permute-start(bf16[512,384]{1,0:T(8,128)(2,1)} %get-tuple-element.136), channel_id=1, source_target_pairs={{0,8},{1,5},{2,10},{3,7},{4,12},{5,1},{6,14},{7,3},{8,0},{9,13},{1... | collective-permute-start | bytes 1179656 | tf_op jit(solution)/shard_map/ppermute | solution.py:838
  83.9 12.9 %collective-permute-start.9 = (bf16[512,384]{1,0:T(8,128)(2,1)}, bf16[512,384]{1,0:T(8,128)(2,1)S(1)}, u32[]{:S(2)}, u32[]{:S(2)}) collective-permute-start(bf16[512,384]{1,0:T(8,128)(2,1)} %get-tuple-element.133), channel_id=1, source_target_pairs={{0,2},{1,9},{2,0},{3,11},{4,6},{5,13},{6,4},{7,15},{8,10},{9,1},{1... | collective-permute-start | bytes 1179656 | tf_op jit(solution)/shard_map/ppermute | solution.py:838
  85.4 13.0 %collective-permute-start.34 = (bf16[128,768]{1,0:T(8,128)(2,1)}, bf16[128,768]{1,0:T(8,128)(2,1)S(1)}, u32[]{:S(2)}, u32[]{:S(2)}) collective-permute-start(bf16[128,768]{1,0:T(8,128)(2,1)} %get-tuple-element.151), channel_id=1, source_target_pairs={{0,1},{1,0},{2,3},{3,2},{4,5},{5,4},{6,7},{7,6},{8,9},{9,8},{10,11... | collective-permute-start | bytes 589832 | tf_op jit(solution)/shard_map/ppermute | solution.py:830
  93.0 7.7 %collective-permute-start.16 = (bf16[256,384]{1,0:T(8,128)(2,1)S(1)}, bf16[256,384]{1,0:T(8,128)(2,1)S(1)}, u32[]{:S(2)}, u32[]{:S(2)}) collective-permute-start(bf16[256,384]{1,0:T(8,128)(2,1)S(1)} %get-tuple-element.176), channel_id=1, source_target_pairs={{0,8},{1,5},{2,10},{3,7},{4,12},{5,1},{6,14},{7,3},{8,0},{9,13},{1... | collective-permute-start | bytes 589832 | tf_op jit(solution)/shard_map/ppermute | solution.py:838
  95.2 7.1 %collective-permute-start.13 = (bf16[256,384]{1,0:T(8,128)(2,1)S(1)}, bf16[256,384]{1,0:T(8,128)(2,1)S(1)}, u32[]{:S(2)}, u32[]{:S(2)}) collective-permute-start(bf16[256,384]{1,0:T(8,128)(2,1)S(1)} %get-tuple-element.178), channel_id=1, source_target_pairs={{0,2},{1,9},{2,0},{3,11},{4,6},{5,13},{6,4},{7,15},{8,10},{9,1},{1... | collective-permute-start | bytes 589832 | tf_op jit(solution)/shard_map/ppermute | solution.py:838
  96.9 6.6 %collective-permute-start.10 = (bf16[256,384]{1,0:T(8,128)(2,1)S(1)}, bf16[256,384]{1,0:T(8,128)(2,1)S(1)}, u32[]{:S(2)}, u32[]{:S(2)}) collective-permute-start(bf16[256,384]{1,0:T(8,128)(2,1)S(1)} %get-tuple-element.180), channel_id=1, source_target_pairs={{0,4},{1,3},{2,6},{3,1},{4,0},{5,7},{6,2},{7,5},{8,12},{9,11},{10,... | collective-permute-start | bytes 589832 | tf_op jit(solution)/shard_map/ppermute | solution.py:838
  100.8 4.7 %collective-permute-start.17 = (bf16[128,384]{1,0:T(8,128)(2,1)S(1)}, bf16[128,384]{1,0:T(8,128)(2,1)S(1)}, u32[]{:S(2)}, u32[]{:S(2)}) collective-permute-start(bf16[128,384]{1,0:T(8,128)(2,1)S(1)} %add_convert_fusion.11), channel_id=1, source_target_pairs={{0,2},{1,9},{2,0},{3,11},{4,6},{5,13},{6,4},{7,15},{8,10},{9,1},{1... | collective-permute-start | bytes 294920 | tf_op jit(solution)/shard_map/ppermute | solution.py:838
  102.4 5.8 %collective-permute-start.14 = (bf16[128,384]{1,0:T(8,128)(2,1)S(1)}, bf16[128,384]{1,0:T(8,128)(2,1)S(1)}, u32[]{:S(2)}, u32[]{:S(2)}) collective-permute-start(bf16[128,384]{1,0:T(8,128)(2,1)S(1)} %add_convert_fusion.14), channel_id=1, source_target_pairs={{0,4},{1,3},{2,6},{3,1},{4,0},{5,7},{6,2},{7,5},{8,12},{9,11},{10,... | collective-permute-start | bytes 294920 | tf_op jit(solution)/shard_map/ppermute | solution.py:838
  103.6 6.8 %collective-permute-start.11 = (bf16[176,384]{1,0:T(8,128)(2,1)S(1)}, bf16[176,384]{1,0:T(8,128)(2,1)S(1)}, u32[]{:S(2)}, u32[]{:S(2)}) collective-permute-start(bf16[176,384]{1,0:T(8,128)(2,1)S(1)} %pad_maximum_fusion.6), channel_id=1, source_target_pairs={{0,8},{1,5},{2,10},{3,7},{4,12},{5,1},{6,14},{7,3},{8,0},{9,13},{1... | collective-permute-start | bytes 405512 | tf_op jit(solution)/shard_map/ppermute | solution.py:838
  105.5 9.5 %collective-permute-start.18 = (bf16[128,384]{1,0:T(8,128)(2,1)S(1)}, bf16[128,384]{1,0:T(8,128)(2,1)S(1)}, u32[]{:S(2)}, u32[]{:S(2)}) collective-permute-start(bf16[128,384]{1,0:T(8,128)(2,1)S(1)} %add_convert_fusion.10), channel_id=1, source_target_pairs={{0,16},{1,17},{2,18},{3,19},{4,20},{5,21},{6,22},{7,23},{8,24},{9,... | collective-permute-start | bytes 294920 | tf_op jit(solution)/shard_map/ppermute | solution.py:838
  108.3 9.3 %collective-permute-start.26 = (bf16[128,384]{1,0:T(8,128)(2,1)S(1)}, bf16[128,384]{1,0:T(8,128)(2,1)S(1)}, u32[]{:S(2)}, u32[]{:S(2)}) collective-permute-start(bf16[128,384]{1,0:T(8,128)(2,1)S(1)} %add_convert_fusion.13), channel_id=1, source_target_pairs={{0,16},{1,17},{2,18},{3,19},{4,20},{5,21},{6,22},{7,23},{8,24},{9,... | collective-permute-start | bytes 294920 | tf_op jit(solution)/shard_map/ppermute | solution.py:838
  110.5 8.8 %collective-permute-start.19 = (bf16[176,384]{1,0:T(8,128)(2,1)S(1)}, bf16[176,384]{1,0:T(8,128)(2,1)S(1)}, u32[]{:S(2)}, u32[]{:S(2)}) collective-permute-start(bf16[176,384]{1,0:T(8,128)(2,1)S(1)} %pad_maximum_fusion.7), channel_id=1, source_target_pairs={{0,16},{1,17},{2,18},{3,19},{4,20},{5,21},{6,22},{7,23},{8,24},{9,... | collective-permute-start | bytes 405512 | tf_op jit(solution)/shard_map/ppermute | solution.py:838
  117.5 4.7 %collective-permute-start.27 = (bf16[128,384]{1,0:T(8,128)(2,1)S(1)}, bf16[128,384]{1,0:T(8,128)(2,1)S(1)}, u32[]{:S(2)}, u32[]{:S(2)}) collective-permute-start(bf16[128,384]{1,0:T(8,128)(2,1)S(1)} %add_convert_fusion.7), channel_id=1, source_target_pairs={{0,4},{1,3},{2,6},{3,1},{4,0},{5,7},{6,2},{7,5},{8,12},{9,11},{10,... | collective-permute-start | bytes 294920 | tf_op jit(solution)/shard_map/ppermute | solution.py:838
  119.4 5.1 %collective-permute-start.21 = (bf16[176,384]{1,0:T(8,128)(2,1)S(1)}, bf16[176,384]{1,0:T(8,128)(2,1)S(1)}, u32[]{:S(2)}, u32[]{:S(2)}) collective-permute-start(bf16[176,384]{1,0:T(8,128)(2,1)S(1)} %pad_maximum_fusion.8), channel_id=1, source_target_pairs={{0,2},{1,9},{2,0},{3,11},{4,6},{5,13},{6,4},{7,15},{8,10},{9,1},{1... | collective-permute-start | bytes 405512 | tf_op jit(solution)/shard_map/ppermute | solution.py:838
  122.3 6.8 %collective-permute-start.28 = (bf16[256,384]{1,0:T(8,128)(2,1)S(1)}, bf16[256,384]{1,0:T(8,128)(2,1)S(1)}, u32[]{:S(2)}, u32[]{:S(2)}) collective-permute-start(bf16[256,384]{1,0:T(8,128)(2,1)S(1)} %pad_maximum_fusion.5), channel_id=1, source_target_pairs={{0,2},{1,9},{2,0},{3,11},{4,6},{5,13},{6,4},{7,15},{8,10},{9,1},{1... | collective-permute-start | bytes 589832 | tf_op jit(solution)/shard_map/ppermute | solution.py:838
  124.5 5.7 %collective-permute-start.24 = (bf16[256,384]{1,0:T(8,128)(2,1)S(1)}, bf16[256,384]{1,0:T(8,128)(2,1)S(1)}, u32[]{:S(2)}, u32[]{:S(2)}) collective-permute-start(bf16[256,384]{1,0:T(8,128)(2,1)S(1)} %pad_maximum_fusion.4), channel_id=1, source_target_pairs={{0,8},{1,5},{2,10},{3,7},{4,12},{5,1},{6,14},{7,3},{8,0},{9,13},{1... | collective-permute-start | bytes 589832 | tf_op jit(solution)/shard_map/ppermute | solution.py:838
  124.7 8.3 %collective-permute-start.22 = (bf16[304,384]{1,0:T(8,128)(2,1)S(1)}, bf16[304,384]{1,0:T(8,128)(2,1)S(1)}, u32[]{:S(2)}, u32[]{:S(2)}) collective-permute-start(bf16[304,384]{1,0:T(8,128)(2,1)S(1)} %pad_maximum_fusion.3), channel_id=1, source_target_pairs={{0,4},{1,3},{2,6},{3,1},{4,0},{5,7},{6,2},{7,5},{8,12},{9,11},{10,... | collective-permute-start | bytes 700424 | tf_op jit(solution)/shard_map/ppermute | solution.py:838
  129.1 5.4 %collective-permute-start.32 = (bf16[512,384]{1,0:T(8,128)(2,1)S(1)}, bf16[512,384]{1,0:T(8,128)(2,1)S(1)}, u32[]{:S(2)}, u32[]{:S(2)}) collective-permute-start(bf16[512,384]{1,0:T(8,128)(2,1)S(1)} %pad_maximum_fusion.2.refs_4_), channel_id=1, source_target_pairs={{0,1},{1,0},{2,3},{3,2},{4,5},{5,4},{6,7},{7,6},{8,9},{9,8},{10,11... | collective-permute-start | bytes 1179656 | tf_op jit(solution)/shard_map/ppermute | solution.py:830
  129.2 11.4 %collective-permute-start.29 = (bf16[512,384]{1,0:T(8,128)(2,1)S(1)}, bf16[512,384]{1,0:T(8,128)(2,1)S(1)}, u32[]{:S(2)}, u32[]{:S(2)}) collective-permute-start(bf16[512,384]{1,0:T(8,128)(2,1)S(1)} %pad_maximum_fusion.2.refs_4_), channel_id=1, source_target_pairs={{0,8},{1,5},{2,10},{3,7},{4,12},{5,1},{6,14},{7,3},{8,0},{9,13},{1... | collective-permute-start | bytes 1179656 | tf_op jit(solution)/shard_map/ppermute | solution.py:838
  130.3 5.2 %collective-permute-start.31 = (bf16[512,384]{1,0:T(8,128)(2,1)S(1)}, bf16[512,384]{1,0:T(8,128)(2,1)S(1)}, u32[]{:S(2)}, u32[]{:S(2)}) collective-permute-start(bf16[512,384]{1,0:T(8,128)(2,1)S(1)} %pad_maximum_fusion.1.refs_2_), channel_id=1, source_target_pairs={{0,1},{1,0},{2,3},{3,2},{4,5},{5,4},{6,7},{7,6},{8,9},{9,8},{10,11... | collective-permute-start | bytes 1179656 | tf_op jit(solution)/shard_map/ppermute | solution.py:830
  130.9 9.8 %collective-permute-start.25 = (bf16[512,384]{1,0:T(8,128)(2,1)S(1)}, bf16[512,384]{1,0:T(8,128)(2,1)S(1)}, u32[]{:S(2)}, u32[]{:S(2)}) collective-permute-start(bf16[512,384]{1,0:T(8,128)(2,1)S(1)} %pad_maximum_fusion.1.refs_2_), channel_id=1, source_target_pairs={{0,4},{1,3},{2,6},{3,1},{4,0},{5,7},{6,2},{7,5},{8,12},{9,11},{10,... | collective-permute-start | bytes 1179656 | tf_op jit(solution)/shard_map/ppermute | solution.py:838
  134.5 7.8 %collective-permute-start.23 = (bf16[512,384]{1,0:T(8,128)(2,1)S(1)}, bf16[512,384]{1,0:T(8,128)(2,1)S(1)}, u32[]{:S(2)}, u32[]{:S(2)}) collective-permute-start(bf16[512,384]{1,0:T(8,128)(2,1)S(1)} %pad_maximum_fusion.refs_0_), channel_id=1, source_target_pairs={{0,2},{1,9},{2,0},{3,11},{4,6},{5,13},{6,4},{7,15},{8,10},{9,1},{1... | collective-permute-start | bytes 1179656 | tf_op jit(solution)/shard_map/ppermute | solution.py:838
  (21 other events, 172.5 us)
